TPU v7x, 512 devices: a whole 4x4x16 slice. The times are simulated.
512 devices in a mesh: tm: 16 (over z_hi, x, core), space: 32 (over z_lo, y).
Axes of the slice: x: 4, y: 4, z: 16 (z_hi: 2, z_lo: 8; z = z_hi * 8 + z_lo), core: 2. Of those that a mesh axis runs over, the one named last changes fastest.
Arguments:
- initial: float32 [256, 128, 128], P('space'), may hold values from -6 to 6
- guess: float32 [16, 256, 128, 128], P('tm', 'space'), may hold values from -6 to 6
- conductivity: float32 [256, 128, 128], P('space'), may hold values from 0.5 to 2
- source: float32 [256, 128, 128], P('space'), may hold values from -4 to 4
Outputs:
- corrected: float32 [16, 256, 128, 128], P('tm', 'space')
- residual: float32 [16, 256, 128, 128], P('tm', 'space')
All inputs are finite; a program needn't handle non-finite values.
Results may differ from a plain program's by a relative error of at most 0.0001.
Values sent between devices are 32-bit elements; how exact they have to be, the bound alone decides.
No kernel may reach another device: no remote copies, remote signals or barrier semaphores. Data moves between devices by JAX's collectives and lax.ppermute only.
A program may use at most 64 MiB of HBM per device.

v0:
```python
import jax
import jax.numpy as jnp
from jax import lax
from jax.sharding import PartitionSpec as P

STEPS = 4


ALONG_FIRST = 0.1
ALONG_SECOND = 0.1
ALONG_THIRD = 0.0125
RIM_DEPTH = 4


def padded_2(shard, sides, width):
    for axis, dim in sides:
        peers, length = (lax.axis_size(axis), shard.shape[dim])
        up = [(i, (i + 1) % peers) for i in range(peers - 1)]
        down = [(j, i) for i, j in up]
        last = lax.slice_in_dim(shard, length - width, length, axis=dim)
        first = lax.slice_in_dim(shard, 0, width, axis=dim)
        before = lax.ppermute(last, axis, up)
        after = lax.ppermute(first, axis, down)
        shard = jnp.concatenate([before, shard, after], axis=dim)
    return shard


def passed_along(block, axis, distance):
    devices = range(lax.axis_size(axis))
    route = [(i - distance, i) for i in devices if i - distance in devices]
    return lax.ppermute(block, axis, route)


def laplace(field_ext, kappa_ext, first_w, second_w, third_w):
    centre = field_ext[1:-1]
    kcentre = kappa_ext[1:-1]
    flux_one = first_w * (
        0.5 * (kcentre + kappa_ext[2:]) * (field_ext[2:] - centre)
        - 0.5 * (kcentre + kappa_ext[:-2]) * (centre - field_ext[:-2])
    )
    side_pad = jnp.pad(centre, ((0, 0), (1, 1), (0, 0)))
    kside_pad = jnp.pad(kcentre, ((0, 0), (1, 1), (0, 0)))
    flux_two = second_w * (
        0.5 * (kcentre + kside_pad[:, 2:]) * (side_pad[:, 2:] - centre)
        - 0.5 * (kcentre + kside_pad[:, :-2]) * (centre - side_pad[:, :-2])
    )
    deep_pad = jnp.pad(centre, ((0, 0), (0, 0), (1, 1)))
    kdeep_pad = jnp.pad(kcentre, ((0, 0), (0, 0), (1, 1)))
    flux_three = third_w * (
        0.5 * (kcentre + kdeep_pad[:, :, 2:]) * (deep_pad[:, :, 2:] - centre)
        - 0.5 * (kcentre + kdeep_pad[:, :, :-2]) * (centre - deep_pad[:, :, :-2])
    )
    return flux_one + flux_two + flux_three


def fine_step(field_ext, kappa_ext, heat):
    return (
        field_ext[1:-1]
        + laplace(field_ext, kappa_ext, ALONG_FIRST, ALONG_SECOND, ALONG_THIRD)
        + heat
    )


def per_device(initial, guess, conductivity, source):
    rows = conductivity.shape[0]
    width_two = conductivity.shape[1]
    width_three = conductivity.shape[2]
    current = guess[0]
    stacked = padded_2(jnp.stack([conductivity, source]), (("space", 1),), RIM_DEPTH)
    kappa_wide = stacked[0]
    source_wide = stacked[1]
    time_index = lax.axis_index("tm")
    first_slice = time_index == 0

    def widen(array, margin):
        return array[RIM_DEPTH - margin : array.shape[0] - RIM_DEPTH + margin]

    def sweep(padded):
        result = fine_step(padded, widen(kappa_wide, 1), widen(source_wide, 0))
        return result

    def advance(field):
        for repeat in range(STEPS):
            padded = padded_2(field, (("space", 0),), 1)
            field = sweep(padded)
        return field

    def predecessor_of(field):
        before = passed_along(field, "tm", 1)
        return jnp.where(first_slice, initial, before)

    def restrict(field):
        return field.reshape(rows // 2, 2, width_two // 2, 2, width_three).mean(axis=(1, 3))

    first = advance(predecessor_of(current))
    second = advance(predecessor_of(first))
    before_third = predecessor_of(second)
    residual = advance(before_third) - second
    coarse_kappa = restrict(conductivity)
    coarse_kappa_ext = padded_2(coarse_kappa, (("space", 0),), 1)
    coarse_rhs = restrict(residual)
    coarse_now = restrict(second)
    coarse_base = restrict(before_third)

    def coarse_step(field):
        padded = padded_2(field, (("space", 0),), 1)
        return field + laplace(
            padded, coarse_kappa_ext, ALONG_FIRST, ALONG_SECOND, 4.0 * ALONG_THIRD
        )

    tau = coarse_rhs + coarse_now - coarse_step(coarse_base)
    start_state = jnp.where(first_slice, coarse_rhs + coarse_now, tau)

    def link(index, state):
        moved = passed_along(state, "tm", 1)
        fresh = tau + coarse_step(moved)
        return jnp.where(time_index == index + 1, fresh, state)

    coarse_state = lax.fori_loop(0, lax.axis_size("tm") - 1, link, start_state)
    finer = jnp.repeat(jnp.repeat(coarse_state - coarse_now, 2, axis=0), 2, axis=1)
    corrected = second + finer
    return (corrected[None], residual[None])


def solution(mesh):
    in_specs = (
        P("space", None, None),
        P("tm", "space", None, None),
        P("space", None, None),
        P("space", None, None),
    )
    out_specs = (P("tm", "space", None, None), P("tm", "space", None, None))
    return jax.shard_map(
        per_device, mesh=mesh, in_specs=in_specs, out_specs=out_specs, check_vma=False
    )
```

profile of v0, /device:TPU:376, one launch (start us, length us, event | category | flops | bytes accessed | tf_op | source)
XLA Modules:
  0.0 698.8 jit_solution(6310450097789559146)
XLA Ops:
  13.9 19.6 %collective-permute-done.3 = f32[8,128,128]{2,1,0:T(8,128)S(1)} collective-permute-done((f32[8,128,128]{2,1,0:T(8,128)}, f32[8,128,128]{2,1,0:T(8,128)S(1)}, u32[]{:S(2)}, u32[]{:S(2)}) %collective-permute-start.3) | collective-permute-done | bytes 524320 | tf_op jit(solution)/shard_map/ppermute | solution.py:31
  36.4 6.5 collective-permute-start.7
  48.4 7.6 %collective-permute-start.9 = (f32[1,128,128]{2,1,0:T(8,128)S(1)}, f32[1,128,128]{2,1,0:T(8,128)S(1)}, u32[]{:S(2)}, u32[]{:S(2)}) collective-permute-start(f32[1,128,128]{2,1,0:T(8,128)S(1)} %get-tuple-element.213), channel_id=1, source_target_pairs={{0,1},{1,2},{2,3},{3,4},{4,5},{5,6},{6,7},{7,8},{8,9},{9,10},{10,1... | collective-permute-start | bytes 196616 | tf_op jit(solution)/shard_map/ppermute | solution.py:22
  60.4 7.6 %collective-permute-start.11 = (f32[1,128,128]{2,1,0:T(8,128)S(1)}, f32[1,128,128]{2,1,0:T(8,128)S(1)}, u32[]{:S(2)}, u32[]{:S(2)}) collective-permute-start(f32[1,128,128]{2,1,0:T(8,128)S(1)} %get-tuple-element.211), channel_id=1, source_target_pairs={{0,1},{1,2},{2,3},{3,4},{4,5},{5,6},{6,7},{7,8},{8,9},{9,10},{10,1... | collective-permute-start | bytes 196616 | tf_op jit(solution)/shard_map/ppermute | solution.py:22
  72.4 7.7 %collective-permute-start.13 = (f32[1,128,128]{2,1,0:T(8,128)S(1)}, f32[1,128,128]{2,1,0:T(8,128)S(1)}, u32[]{:S(2)}, u32[]{:S(2)}) collective-permute-start(f32[1,128,128]{2,1,0:T(8,128)S(1)} %get-tuple-element.209), channel_id=1, source_target_pairs={{0,1},{1,2},{2,3},{3,4},{4,5},{5,6},{6,7},{7,8},{8,9},{9,10},{10,1... | collective-permute-start | bytes 196616 | tf_op jit(solution)/shard_map/ppermute | solution.py:22
  84.4 29.9 %collective-permute-done.14 = f32[8,128,128]{2,1,0:T(8,128)S(1)} collective-permute-done((f32[8,128,128]{2,1,0:T(8,128)S(1)}, f32[8,128,128]{2,1,0:T(8,128)S(1)}, u32[]{:S(2)}, u32[]{:S(2)}) %collective-permute-start.14) | collective-permute-done | bytes 524320 | tf_op jit(solution)/shard_map/ppermute | solution.py:31
  116.3 7.2 %collective-permute-start.16 = (f32[1,128,128]{2,1,0:T(8,128)S(1)}, f32[1,128,128]{2,1,0:T(8,128)S(1)}, u32[]{:S(2)}, u32[]{:S(2)}) collective-permute-start(f32[1,128,128]{2,1,0:T(8,128)S(1)} %get-tuple-element.207), channel_id=1, source_target_pairs={{0,1},{1,2},{2,3},{3,4},{4,5},{5,6},{6,7},{7,8},{8,9},{9,10},{10,1... | collective-permute-start | bytes 196616 | tf_op jit(solution)/shard_map/ppermute | solution.py:22
  140.3 7.2 %collective-permute-start.20 = (f32[1,128,128]{2,1,0:T(8,128)S(1)}, f32[1,128,128]{2,1,0:T(8,128)S(1)}, u32[]{:S(2)}, u32[]{:S(2)}) collective-permute-start(f32[1,128,128]{2,1,0:T(8,128)S(1)} %get-tuple-element.203), channel_id=1, source_target_pairs={{0,1},{1,2},{2,3},{3,4},{4,5},{5,6},{6,7},{7,8},{8,9},{9,10},{10,1... | collective-permute-start | bytes 196616 | tf_op jit(solution)/shard_map/ppermute | solution.py:22
  151.8 7.6 %collective-permute-start.22 = (f32[1,128,128]{2,1,0:T(8,128)S(1)}, f32[1,128,128]{2,1,0:T(8,128)S(1)}, u32[]{:S(2)}, u32[]{:S(2)}) collective-permute-start(f32[1,128,128]{2,1,0:T(8,128)S(1)} %get-tuple-element.201), channel_id=1, source_target_pairs={{0,1},{1,2},{2,3},{3,4},{4,5},{5,6},{6,7},{7,8},{8,9},{9,10},{10,1... | collective-permute-start | bytes 196616 | tf_op jit(solution)/shard_map/ppermute | solution.py:22
  166.0 25.6 %collective-permute-done.23 = f32[8,128,128]{2,1,0:T(8,128)} collective-permute-done((f32[8,128,128]{2,1,0:T(8,128)}, f32[8,128,128]{2,1,0:T(8,128)}, u32[]{:S(2)}, u32[]{:S(2)}) %collective-permute-start.23) | collective-permute-done | bytes 524320 | tf_op jit(solution)/shard_map/ppermute | solution.py:31
  204.5 7.2 %collective-permute-start.34 = (f32[1,64,128]{2,1,0:T(8,128)}, f32[1,64,128]{2,1,0:T(8,128)}, u32[]{:S(2)}, u32[]{:S(2)}) collective-permute-start(f32[1,64,128]{2,1,0:T(8,128)} %get-tuple-element.218), channel_id=1, source_target_pairs={{0,1},{1,2},{2,3},{3,4},{4,5},{5,6},{6,7},{7,8},{8,9},{9,10},{10,1... | collective-permute-start | bytes 98312 | tf_op jit(solution)/shard_map/ppermute | solution.py:22
  214.9 7.2 %collective-permute-start.27 = (f32[1,128,128]{2,1,0:T(8,128)}, f32[1,128,128]{2,1,0:T(8,128)}, u32[]{:S(2)}, u32[]{:S(2)}) collective-permute-start(f32[1,128,128]{2,1,0:T(8,128)} %get-tuple-element.197), channel_id=1, source_target_pairs={{0,1},{1,2},{2,3},{3,4},{4,5},{5,6},{6,7},{7,8},{8,9},{9,10},{10,1... | collective-permute-start | bytes 196616 | tf_op jit(solution)/shard_map/ppermute | solution.py:22
  231.6 7.2 %collective-permute-start.29 = (f32[1,128,128]{2,1,0:T(8,128)S(1)}, f32[1,128,128]{2,1,0:T(8,128)S(1)}, u32[]{:S(2)}, u32[]{:S(2)}) collective-permute-start(f32[1,128,128]{2,1,0:T(8,128)S(1)} %get-tuple-element.195), channel_id=1, source_target_pairs={{0,1},{1,2},{2,3},{3,4},{4,5},{5,6},{6,7},{7,8},{8,9},{9,10},{10,1... | collective-permute-start | bytes 196616 | tf_op jit(solution)/shard_map/ppermute | solution.py:22
  243.2 7.6 %collective-permute-start.31 = (f32[1,128,128]{2,1,0:T(8,128)S(1)}, f32[1,128,128]{2,1,0:T(8,128)S(1)}, u32[]{:S(2)}, u32[]{:S(2)}) collective-permute-start(f32[1,128,128]{2,1,0:T(8,128)S(1)} %get-tuple-element.193), channel_id=1, source_target_pairs={{0,1},{1,2},{2,3},{3,4},{4,5},{5,6},{6,7},{7,8},{8,9},{9,10},{10,1... | collective-permute-start | bytes 196616 | tf_op jit(solution)/shard_map/ppermute | solution.py:22
  253.4 7.2 %collective-permute-start.35 = (f32[1,64,128]{2,1,0:T(8,128)}, f32[1,64,128]{2,1,0:T(8,128)}, u32[]{:S(2)}, u32[]{:S(2)}) collective-permute-start(f32[1,64,128]{2,1,0:T(8,128)} %get-tuple-element.220), channel_id=1, source_target_pairs={{0,1},{1,2},{2,3},{3,4},{4,5},{5,6},{6,7},{7,8},{8,9},{9,10},{10,1... | collective-permute-start | bytes 98312 | tf_op jit(solution)/shard_map/ppermute | solution.py:22
  265.6 431.1 %while.15 = (s32[]{:T(128)}, f32[4,64,128]{2,1,0:T(8,128)S(1)}, s32[]{:T(128)}, f32[4,64,128]{2,1,0:T(8,128)S(1)}, f32[4,64,128]{2,1,0:T(8,128)S(1)}, /*index=5*...) while((s32[]{:T(128)}, f32[4,64,128]{2,1,0:T(8,128)S(1)}, s32[]{:T(128)}, ...), condition=%wide.region_5.6_spmd, body=%wide.region_4.5_spmd.sunk | while | flops 1114115 | bytes 1900759 | solution.py:119
  267.5 16.3 %collective-permute-done = f32[4,64,128]{2,1,0:T(8,128)S(1)} collective-permute-done((f32[4,64,128]{2,1,0:T(8,128)S(1)}, f32[4,64,128]{2,1,0:T(8,128)S(1)}, u32[]{:S(2)}, u32[]{:S(2)}) %collective-permute-start) | collective-permute-done | bytes 131104 | tf_op jit(solution)/shard_map/while/body/eval_jaxpr/ppermute | solution.py:31
  291.6 7.2 %collective-permute-done.2 = f32[1,64,128]{2,1,0:T(8,128)S(1)} collective-permute-done((f32[1,64,128]{2,1,0:T(8,128)S(1)}, f32[1,64,128]{2,1,0:T(8,128)S(1)}, u32[]{:S(2)}, u32[]{:S(2)}) %collective-permute-start.2) | collective-permute-done | bytes 32800 | tf_op jit(solution)/shard_map/while/body/eval_jaxpr/ppermute | solution.py:23
  300.9 15.2 %collective-permute-done = f32[4,64,128]{2,1,0:T(8,128)S(1)} collective-permute-done((f32[4,64,128]{2,1,0:T(8,128)S(1)}, f32[4,64,128]{2,1,0:T(8,128)S(1)}, u32[]{:S(2)}, u32[]{:S(2)}) %collective-permute-start) | collective-permute-done | bytes 131104 | tf_op jit(solution)/shard_map/while/body/eval_jaxpr/ppermute | solution.py:31
  329.3 15.2 %collective-permute-done = f32[4,64,128]{2,1,0:T(8,128)S(1)} collective-permute-done((f32[4,64,128]{2,1,0:T(8,128)S(1)}, f32[4,64,128]{2,1,0:T(8,128)S(1)}, u32[]{:S(2)}, u32[]{:S(2)}) %collective-permute-start) | collective-permute-done | bytes 131104 | tf_op jit(solution)/shard_map/while/body/eval_jaxpr/ppermute | solution.py:31
  357.7 15.2 %collective-permute-done = f32[4,64,128]{2,1,0:T(8,128)S(1)} collective-permute-done((f32[4,64,128]{2,1,0:T(8,128)S(1)}, f32[4,64,128]{2,1,0:T(8,128)S(1)}, u32[]{:S(2)}, u32[]{:S(2)}) %collective-permute-start) | collective-permute-done | bytes 131104 | tf_op jit(solution)/shard_map/while/body/eval_jaxpr/ppermute | solution.py:31
  386.1 15.2 %collective-permute-done = f32[4,64,128]{2,1,0:T(8,128)S(1)} collective-permute-done((f32[4,64,128]{2,1,0:T(8,128)S(1)}, f32[4,64,128]{2,1,0:T(8,128)S(1)}, u32[]{:S(2)}, u32[]{:S(2)}) %collective-permute-start) | collective-permute-done | bytes 131104 | tf_op jit(solution)/shard_map/while/body/eval_jaxpr/ppermute | solution.py:31
  414.6 15.2 %collective-permute-done = f32[4,64,128]{2,1,0:T(8,128)S(1)} collective-permute-done((f32[4,64,128]{2,1,0:T(8,128)S(1)}, f32[4,64,128]{2,1,0:T(8,128)S(1)}, u32[]{:S(2)}, u32[]{:S(2)}) %collective-permute-start) | collective-permute-done | bytes 131104 | tf_op jit(solution)/shard_map/while/body/eval_jaxpr/ppermute | solution.py:31
  443.0 15.2 %collective-permute-done = f32[4,64,128]{2,1,0:T(8,128)S(1)} collective-permute-done((f32[4,64,128]{2,1,0:T(8,128)S(1)}, f32[4,64,128]{2,1,0:T(8,128)S(1)}, u32[]{:S(2)}, u32[]{:S(2)}) %collective-permute-start) | collective-permute-done | bytes 131104 | tf_op jit(solution)/shard_map/while/body/eval_jaxpr/ppermute | solution.py:31
  471.4 15.2 %collective-permute-done = f32[4,64,128]{2,1,0:T(8,128)S(1)} collective-permute-done((f32[4,64,128]{2,1,0:T(8,128)S(1)}, f32[4,64,128]{2,1,0:T(8,128)S(1)}, u32[]{:S(2)}, u32[]{:S(2)}) %collective-permute-start) | collective-permute-done | bytes 131104 | tf_op jit(solution)/shard_map/while/body/eval_jaxpr/ppermute | solution.py:31
  499.8 15.2 %collective-permute-done = f32[4,64,128]{2,1,0:T(8,128)S(1)} collective-permute-done((f32[4,64,128]{2,1,0:T(8,128)S(1)}, f32[4,64,128]{2,1,0:T(8,128)S(1)}, u32[]{:S(2)}, u32[]{:S(2)}) %collective-permute-start) | collective-permute-done | bytes 131104 | tf_op jit(solution)/shard_map/while/body/eval_jaxpr/ppermute | solution.py:31
  528.2 15.2 %collective-permute-done = f32[4,64,128]{2,1,0:T(8,128)S(1)} collective-permute-done((f32[4,64,128]{2,1,0:T(8,128)S(1)}, f32[4,64,128]{2,1,0:T(8,128)S(1)}, u32[]{:S(2)}, u32[]{:S(2)}) %collective-permute-start) | collective-permute-done | bytes 131104 | tf_op jit(solution)/shard_map/while/body/eval_jaxpr/ppermute | solution.py:31
  556.6 15.2 %collective-permute-done = f32[4,64,128]{2,1,0:T(8,128)S(1)} collective-permute-done((f32[4,64,128]{2,1,0:T(8,128)S(1)}, f32[4,64,128]{2,1,0:T(8,128)S(1)}, u32[]{:S(2)}, u32[]{:S(2)}) %collective-permute-start) | collective-permute-done | bytes 131104 | tf_op jit(solution)/shard_map/while/body/eval_jaxpr/ppermute | solution.py:31
  585.0 15.2 %collective-permute-done = f32[4,64,128]{2,1,0:T(8,128)S(1)} collective-permute-done((f32[4,64,128]{2,1,0:T(8,128)S(1)}, f32[4,64,128]{2,1,0:T(8,128)S(1)}, u32[]{:S(2)}, u32[]{:S(2)}) %collective-permute-start) | collective-permute-done | bytes 131104 | tf_op jit(solution)/shard_map/while/body/eval_jaxpr/ppermute | solution.py:31
  613.4 15.2 %collective-permute-done = f32[4,64,128]{2,1,0:T(8,128)S(1)} collective-permute-done((f32[4,64,128]{2,1,0:T(8,128)S(1)}, f32[4,64,128]{2,1,0:T(8,128)S(1)}, u32[]{:S(2)}, u32[]{:S(2)}) %collective-permute-start) | collective-permute-done | bytes 131104 | tf_op jit(solution)/shard_map/while/body/eval_jaxpr/ppermute | solution.py:31
  641.8 15.2 %collective-permute-done = f32[4,64,128]{2,1,0:T(8,128)S(1)} collective-permute-done((f32[4,64,128]{2,1,0:T(8,128)S(1)}, f32[4,64,128]{2,1,0:T(8,128)S(1)}, u32[]{:S(2)}, u32[]{:S(2)}) %collective-permute-start) | collective-permute-done | bytes 131104 | tf_op jit(solution)/shard_map/while/body/eval_jaxpr/ppermute | solution.py:31
  670.2 15.2 %collective-permute-done = f32[4,64,128]{2,1,0:T(8,128)S(1)} collective-permute-done((f32[4,64,128]{2,1,0:T(8,128)S(1)}, f32[4,64,128]{2,1,0:T(8,128)S(1)}, u32[]{:S(2)}, u32[]{:S(2)}) %collective-permute-start) | collective-permute-done | bytes 131104 | tf_op jit(solution)/shard_map/while/body/eval_jaxpr/ppermute | solution.py:31
  (229 shorter events, 297.4 us)
Async XLA Ops:
  0.6 32.9 %collective-permute-start.3 = (f32[8,128,128]{2,1,0:T(8,128)}, f32[8,128,128]{2,1,0:T(8,128)S(1)}, u32[]{:S(2)}, u32[]{:S(2)}) collective-permute-start(f32[8,128,128]{2,1,0:T(8,128)} %bitcast.36), channel_id=1, source_target_pairs={{0,32},{32,64},{64,96},{96,128},{128,160},{160,192},{192,224},{224... | collective-permute-start | bytes 1572872 | tf_op jit(solution)/shard_map/ppermute | solution.py:31
  4.7 38.2 %collective-permute-start.4 = (f32[2,4,128,128]{3,2,1,0:T(8,128)}, f32[2,4,128,128]{3,2,1,0:T(8,128)S(1)}, u32[]{:S(2)}, u32[]{:S(2)}) collective-permute-start(f32[2,4,128,128]{3,2,1,0:T(8,128)} %get-tuple-element.191), channel_id=1, source_target_pairs={{1,0},{2,1},{3,2},{4,3},{5,4},{6,5},{7,6},{8,7},{9,8},{10,9},{11,1... | collective-permute-start | bytes 1572872 | tf_op jit(solution)/shard_map/ppermute | solution.py:23
  7.4 35.6 %collective-permute-start.6 = (f32[2,4,128,128]{3,2,1,0:T(8,128)S(1)}, f32[2,4,128,128]{3,2,1,0:T(8,128)S(1)}, u32[]{:S(2)}, u32[]{:S(2)}) collective-permute-start(f32[2,4,128,128]{3,2,1,0:T(8,128)S(1)} %get-tuple-element.190), channel_id=1, source_target_pairs={{0,1},{1,2},{2,3},{3,4},{4,5},{5,6},{6,7},{7,8},{8,9},{9,10},{10,1... | collective-permute-start | bytes 1572872 | tf_op jit(solution)/shard_map/ppermute | solution.py:22
  46.5 9.8 %collective-permute-start.8 = (f32[1,128,128]{2,1,0:T(8,128)S(1)}, f32[1,128,128]{2,1,0:T(8,128)S(1)}, u32[]{:S(2)}, u32[]{:S(2)}) collective-permute-start(f32[1,128,128]{2,1,0:T(8,128)S(1)} %get-tuple-element.212), channel_id=1, source_target_pairs={{1,0},{2,1},{3,2},{4,3},{5,4},{6,5},{7,6},{8,7},{9,8},{10,9},{11,1... | collective-permute-start | bytes 196616 | tf_op jit(solution)/shard_map/ppermute | solution.py:23
  82.5 31.8 %collective-permute-start.14 = (f32[8,128,128]{2,1,0:T(8,128)S(1)}, f32[8,128,128]{2,1,0:T(8,128)S(1)}, u32[]{:S(2)}, u32[]{:S(2)}) collective-permute-start(f32[8,128,128]{2,1,0:T(8,128)S(1)} %fusion.71), channel_id=1, source_target_pairs={{0,32},{32,64},{64,96},{96,128},{128,160},{160,192},{192,224},{224... | collective-permute-start | bytes 1572872 | tf_op jit(solution)/shard_map/ppermute | solution.py:31
  126.0 9.8 %collective-permute-start.17 = (f32[1,128,128]{2,1,0:T(8,128)S(1)}, f32[1,128,128]{2,1,0:T(8,128)S(1)}, u32[]{:S(2)}, u32[]{:S(2)}) collective-permute-start(f32[1,128,128]{2,1,0:T(8,128)S(1)} %get-tuple-element.204), channel_id=1, source_target_pairs={{1,0},{2,1},{3,2},{4,3},{5,4},{6,5},{7,6},{8,7},{9,8},{10,9},{11,1... | collective-permute-start | bytes 196616 | tf_op jit(solution)/shard_map/ppermute | solution.py:23
  162.6 28.9 %collective-permute-start.23 = (f32[8,128,128]{2,1,0:T(8,128)}, f32[8,128,128]{2,1,0:T(8,128)}, u32[]{:S(2)}, u32[]{:S(2)}) collective-permute-start(f32[8,128,128]{2,1,0:T(8,128)} %fusion.111), channel_id=1, source_target_pairs={{0,32},{32,64},{64,96},{96,128},{128,160},{160,192},{192,224},{224... | collective-permute-start | bytes 1572872 | tf_op jit(solution)/shard_map/ppermute | solution.py:31
  192.8 19.0 %collective-permute-start.24 = (f32[1,128,128]{2,1,0:T(8,128)S(1)}, f32[1,128,128]{2,1,0:T(8,128)S(1)}, u32[]{:S(2)}, u32[]{:S(2)}) collective-permute-start(f32[1,128,128]{2,1,0:T(8,128)S(1)} %get-tuple-element.198), channel_id=1, source_target_pairs={{1,0},{2,1},{3,2},{4,3},{5,4},{6,5},{7,6},{8,7},{9,8},{10,9},{11,1... | collective-permute-start | bytes 196616 | tf_op jit(solution)/shard_map/ppermute | solution.py:23
  196.8 14.9 %collective-permute-start.25 = (f32[1,128,128]{2,1,0:T(8,128)S(1)}, f32[1,128,128]{2,1,0:T(8,128)S(1)}, u32[]{:S(2)}, u32[]{:S(2)}) collective-permute-start(f32[1,128,128]{2,1,0:T(8,128)S(1)} %get-tuple-element.199), channel_id=1, source_target_pairs={{0,1},{1,2},{2,3},{3,4},{4,5},{5,6},{6,7},{7,8},{8,9},{9,10},{10,1... | collective-permute-start | bytes 196616 | tf_op jit(solution)/shard_map/ppermute | solution.py:22
  202.5 19.6 %collective-permute-start.32 = (f32[1,64,128]{2,1,0:T(8,128)S(1)}, f32[1,64,128]{2,1,0:T(8,128)S(1)}, u32[]{:S(2)}, u32[]{:S(2)}) collective-permute-start(f32[1,64,128]{2,1,0:T(8,128)S(1)} %get-tuple-element.217), channel_id=1, source_target_pairs={{1,0},{2,1},{3,2},{4,3},{5,4},{6,5},{7,6},{8,7},{9,8},{10,9},{11,1... | collective-permute-start | bytes 98312 | tf_op jit(solution)/shard_map/ppermute | solution.py:23
  204.5 60.1 %collective-permute-start.34 = (f32[1,64,128]{2,1,0:T(8,128)}, f32[1,64,128]{2,1,0:T(8,128)}, u32[]{:S(2)}, u32[]{:S(2)}) collective-permute-start(f32[1,64,128]{2,1,0:T(8,128)} %get-tuple-element.218), channel_id=1, source_target_pairs={{0,1},{1,2},{2,3},{3,4},{4,5},{5,6},{6,7},{7,8},{8,9},{9,10},{10,1... | collective-permute-start | bytes 98312 | tf_op jit(solution)/shard_map/ppermute | solution.py:22
  213.0 13.3 %collective-permute-start.26 = (f32[1,128,128]{2,1,0:T(8,128)}, f32[1,128,128]{2,1,0:T(8,128)}, u32[]{:S(2)}, u32[]{:S(2)}) collective-permute-start(f32[1,128,128]{2,1,0:T(8,128)} %get-tuple-element.196), channel_id=1, source_target_pairs={{1,0},{2,1},{3,2},{4,3},{5,4},{6,5},{7,6},{8,7},{9,8},{10,9},{11,1... | collective-permute-start | bytes 196616 | tf_op jit(solution)/shard_map/ppermute | solution.py:23
  214.9 11.4 %collective-permute-start.27 = (f32[1,128,128]{2,1,0:T(8,128)}, f32[1,128,128]{2,1,0:T(8,128)}, u32[]{:S(2)}, u32[]{:S(2)}) collective-permute-start(f32[1,128,128]{2,1,0:T(8,128)} %get-tuple-element.197), channel_id=1, source_target_pairs={{0,1},{1,2},{2,3},{3,4},{4,5},{5,6},{6,7},{7,8},{8,9},{9,10},{10,1... | collective-permute-start | bytes 196616 | tf_op jit(solution)/shard_map/ppermute | solution.py:22
  241.3 19.3 %collective-permute-start.30 = (f32[1,128,128]{2,1,0:T(8,128)S(1)}, f32[1,128,128]{2,1,0:T(8,128)S(1)}, u32[]{:S(2)}, u32[]{:S(2)}) collective-permute-start(f32[1,128,128]{2,1,0:T(8,128)S(1)} %get-tuple-element.192), channel_id=1, source_target_pairs={{1,0},{2,1},{3,2},{4,3},{5,4},{6,5},{7,6},{8,7},{9,8},{10,9},{11,1... | collective-permute-start | bytes 196616 | tf_op jit(solution)/shard_map/ppermute | solution.py:23
  243.2 17.4 %collective-permute-start.31 = (f32[1,128,128]{2,1,0:T(8,128)S(1)}, f32[1,128,128]{2,1,0:T(8,128)S(1)}, u32[]{:S(2)}, u32[]{:S(2)}) collective-permute-start(f32[1,128,128]{2,1,0:T(8,128)S(1)} %get-tuple-element.193), channel_id=1, source_target_pairs={{0,1},{1,2},{2,3},{3,4},{4,5},{5,6},{6,7},{7,8},{8,9},{9,10},{10,1... | collective-permute-start | bytes 196616 | tf_op jit(solution)/shard_map/ppermute | solution.py:22
  251.5 13.0 %collective-permute-start.33 = (f32[1,64,128]{2,1,0:T(8,128)}, f32[1,64,128]{2,1,0:T(8,128)}, u32[]{:S(2)}, u32[]{:S(2)}) collective-permute-start(f32[1,64,128]{2,1,0:T(8,128)} %get-tuple-element.219), channel_id=1, source_target_pairs={{1,0},{2,1},{3,2},{4,3},{5,4},{6,5},{7,6},{8,7},{9,8},{10,9},{11,1... | collective-permute-start | bytes 98312 | tf_op jit(solution)/shard_map/ppermute | solution.py:23
  253.4 11.1 %collective-permute-start.35 = (f32[1,64,128]{2,1,0:T(8,128)}, f32[1,64,128]{2,1,0:T(8,128)}, u32[]{:S(2)}, u32[]{:S(2)}) collective-permute-start(f32[1,64,128]{2,1,0:T(8,128)} %get-tuple-element.220), channel_id=1, source_target_pairs={{0,1},{1,2},{2,3},{3,4},{4,5},{5,6},{6,7},{7,8},{8,9},{9,10},{10,1... | collective-permute-start | bytes 98312 | tf_op jit(solution)/shard_map/ppermute | solution.py:22
  265.6 18.3 %collective-permute-start = (f32[4,64,128]{2,1,0:T(8,128)S(1)}, f32[4,64,128]{2,1,0:T(8,128)S(1)}, u32[]{:S(2)}, u32[]{:S(2)}) collective-permute-start(f32[4,64,128]{2,1,0:T(8,128)S(1)} %get-tuple-element.277), channel_id=1, source_target_pairs={{0,32},{32,64},{64,96},{96,128},{128,160},{160,192},{192,224},{224... | collective-permute-start | bytes 393224 | tf_op jit(solution)/shard_map/while/body/eval_jaxpr/ppermute | solution.py:31
  299.0 17.1 %collective-permute-start = (f32[4,64,128]{2,1,0:T(8,128)S(1)}, f32[4,64,128]{2,1,0:T(8,128)S(1)}, u32[]{:S(2)}, u32[]{:S(2)}) collective-permute-start(f32[4,64,128]{2,1,0:T(8,128)S(1)} %get-tuple-element.277), channel_id=1, source_target_pairs={{0,32},{32,64},{64,96},{96,128},{128,160},{160,192},{192,224},{224... | collective-permute-start | bytes 393224 | tf_op jit(solution)/shard_map/while/body/eval_jaxpr/ppermute | solution.py:31
  327.4 17.1 %collective-permute-start = (f32[4,64,128]{2,1,0:T(8,128)S(1)}, f32[4,64,128]{2,1,0:T(8,128)S(1)}, u32[]{:S(2)}, u32[]{:S(2)}) collective-permute-start(f32[4,64,128]{2,1,0:T(8,128)S(1)} %get-tuple-element.277), channel_id=1, source_target_pairs={{0,32},{32,64},{64,96},{96,128},{128,160},{160,192},{192,224},{224... | collective-permute-start | bytes 393224 | tf_op jit(solution)/shard_map/while/body/eval_jaxpr/ppermute | solution.py:31
  355.8 17.1 %collective-permute-start = (f32[4,64,128]{2,1,0:T(8,128)S(1)}, f32[4,64,128]{2,1,0:T(8,128)S(1)}, u32[]{:S(2)}, u32[]{:S(2)}) collective-permute-start(f32[4,64,128]{2,1,0:T(8,128)S(1)} %get-tuple-element.277), channel_id=1, source_target_pairs={{0,32},{32,64},{64,96},{96,128},{128,160},{160,192},{192,224},{224... | collective-permute-start | bytes 393224 | tf_op jit(solution)/shard_map/while/body/eval_jaxpr/ppermute | solution.py:31
  384.2 17.1 %collective-permute-start = (f32[4,64,128]{2,1,0:T(8,128)S(1)}, f32[4,64,128]{2,1,0:T(8,128)S(1)}, u32[]{:S(2)}, u32[]{:S(2)}) collective-permute-start(f32[4,64,128]{2,1,0:T(8,128)S(1)} %get-tuple-element.277), channel_id=1, source_target_pairs={{0,32},{32,64},{64,96},{96,128},{128,160},{160,192},{192,224},{224... | collective-permute-start | bytes 393224 | tf_op jit(solution)/shard_map/while/body/eval_jaxpr/ppermute | solution.py:31
  412.6 17.1 %collective-permute-start = (f32[4,64,128]{2,1,0:T(8,128)S(1)}, f32[4,64,128]{2,1,0:T(8,128)S(1)}, u32[]{:S(2)}, u32[]{:S(2)}) collective-permute-start(f32[4,64,128]{2,1,0:T(8,128)S(1)} %get-tuple-element.277), channel_id=1, source_target_pairs={{0,32},{32,64},{64,96},{96,128},{128,160},{160,192},{192,224},{224... | collective-permute-start | bytes 393224 | tf_op jit(solution)/shard_map/while/body/eval_jaxpr/ppermute | solution.py:31
  441.0 17.1 %collective-permute-start = (f32[4,64,128]{2,1,0:T(8,128)S(1)}, f32[4,64,128]{2,1,0:T(8,128)S(1)}, u32[]{:S(2)}, u32[]{:S(2)}) collective-permute-start(f32[4,64,128]{2,1,0:T(8,128)S(1)} %get-tuple-element.277), channel_id=1, source_target_pairs={{0,32},{32,64},{64,96},{96,128},{128,160},{160,192},{192,224},{224... | collective-permute-start | bytes 393224 | tf_op jit(solution)/shard_map/while/body/eval_jaxpr/ppermute | solution.py:31
  469.4 17.1 %collective-permute-start = (f32[4,64,128]{2,1,0:T(8,128)S(1)}, f32[4,64,128]{2,1,0:T(8,128)S(1)}, u32[]{:S(2)}, u32[]{:S(2)}) collective-permute-start(f32[4,64,128]{2,1,0:T(8,128)S(1)} %get-tuple-element.277), channel_id=1, source_target_pairs={{0,32},{32,64},{64,96},{96,128},{128,160},{160,192},{192,224},{224... | collective-permute-start | bytes 393224 | tf_op jit(solution)/shard_map/while/body/eval_jaxpr/ppermute | solution.py:31
  497.8 17.1 %collective-permute-start = (f32[4,64,128]{2,1,0:T(8,128)S(1)}, f32[4,64,128]{2,1,0:T(8,128)S(1)}, u32[]{:S(2)}, u32[]{:S(2)}) collective-permute-start(f32[4,64,128]{2,1,0:T(8,128)S(1)} %get-tuple-element.277), channel_id=1, source_target_pairs={{0,32},{32,64},{64,96},{96,128},{128,160},{160,192},{192,224},{224... | collective-permute-start | bytes 393224 | tf_op jit(solution)/shard_map/while/body/eval_jaxpr/ppermute | solution.py:31
  526.2 17.1 %collective-permute-start = (f32[4,64,128]{2,1,0:T(8,128)S(1)}, f32[4,64,128]{2,1,0:T(8,128)S(1)}, u32[]{:S(2)}, u32[]{:S(2)}) collective-permute-start(f32[4,64,128]{2,1,0:T(8,128)S(1)} %get-tuple-element.277), channel_id=1, source_target_pairs={{0,32},{32,64},{64,96},{96,128},{128,160},{160,192},{192,224},{224... | collective-permute-start | bytes 393224 | tf_op jit(solution)/shard_map/while/body/eval_jaxpr/ppermute | solution.py:31
  554.7 17.1 %collective-permute-start = (f32[4,64,128]{2,1,0:T(8,128)S(1)}, f32[4,64,128]{2,1,0:T(8,128)S(1)}, u32[]{:S(2)}, u32[]{:S(2)}) collective-permute-start(f32[4,64,128]{2,1,0:T(8,128)S(1)} %get-tuple-element.277), channel_id=1, source_target_pairs={{0,32},{32,64},{64,96},{96,128},{128,160},{160,192},{192,224},{224... | collective-permute-start | bytes 393224 | tf_op jit(solution)/shard_map/while/body/eval_jaxpr/ppermute | solution.py:31
  583.1 17.1 %collective-permute-start = (f32[4,64,128]{2,1,0:T(8,128)S(1)}, f32[4,64,128]{2,1,0:T(8,128)S(1)}, u32[]{:S(2)}, u32[]{:S(2)}) collective-permute-start(f32[4,64,128]{2,1,0:T(8,128)S(1)} %get-tuple-element.277), channel_id=1, source_target_pairs={{0,32},{32,64},{64,96},{96,128},{128,160},{160,192},{192,224},{224... | collective-permute-start | bytes 393224 | tf_op jit(solution)/shard_map/while/body/eval_jaxpr/ppermute | solution.py:31
  611.5 17.1 %collective-permute-start = (f32[4,64,128]{2,1,0:T(8,128)S(1)}, f32[4,64,128]{2,1,0:T(8,128)S(1)}, u32[]{:S(2)}, u32[]{:S(2)}) collective-permute-start(f32[4,64,128]{2,1,0:T(8,128)S(1)} %get-tuple-element.277), channel_id=1, source_target_pairs={{0,32},{32,64},{64,96},{96,128},{128,160},{160,192},{192,224},{224... | collective-permute-start | bytes 393224 | tf_op jit(solution)/shard_map/while/body/eval_jaxpr/ppermute | solution.py:31
  639.9 17.1 %collective-permute-start = (f32[4,64,128]{2,1,0:T(8,128)S(1)}, f32[4,64,128]{2,1,0:T(8,128)S(1)}, u32[]{:S(2)}, u32[]{:S(2)}) collective-permute-start(f32[4,64,128]{2,1,0:T(8,128)S(1)} %get-tuple-element.277), channel_id=1, source_target_pairs={{0,32},{32,64},{64,96},{96,128},{128,160},{160,192},{192,224},{224... | collective-permute-start | bytes 393224 | tf_op jit(solution)/shard_map/while/body/eval_jaxpr/ppermute | solution.py:31
  668.3 17.1 %collective-permute-start = (f32[4,64,128]{2,1,0:T(8,128)S(1)}, f32[4,64,128]{2,1,0:T(8,128)S(1)}, u32[]{:S(2)}, u32[]{:S(2)}) collective-permute-start(f32[4,64,128]{2,1,0:T(8,128)S(1)} %get-tuple-element.277), channel_id=1, source_target_pairs={{0,32},{32,64},{64,96},{96,128},{128,160},{160,192},{192,224},{224... | collective-permute-start | bytes 393224 | tf_op jit(solution)/shard_map/while/body/eval_jaxpr/ppermute | solution.py:31
  (62 other events, 677.4 us)
where the time goes:
time: 702 us; the launch traced here: 699 us
  waiting for transfers between devices  400 us (57%)
  starting transfers between devices  264 us (38%)
  other arithmetic  28.9 us (4%)
    ppermute x18, waiting for transfers between devices, passed_along(): return lax.ppermute(block, axis, route)  304 us
    ppermute x30, starting transfers between devices, padded_2(): before = lax.ppermute(last, axis, up)  138 us
    ppermute x30, starting transfers between devices, padded_2(): after = lax.ppermute(first, axis, down)  91.4 us
    ppermute x30, waiting for transfers between devices, padded_2(): after = lax.ppermute(first, axis, down)  82.2 us
    ppermute x18, starting transfers between devices, passed_along(): return lax.ppermute(block, axis, route)  34.6 us
  transfers between devices with their start and end apart: 78, of which 51 were waited for; matrix products, arithmetic and copies ran while one was open for 2% of the time, Pallas kernels for 0%

commit v1 on v0

v1 whole, which is shorter than its diff:
```python
import jax
import jax.numpy as jnp
from jax import lax
from jax.sharding import PartitionSpec as P

STEPS = 4
ALONG_FIRST = 0.1
ALONG_SECOND = 0.1
ALONG_THIRD = 0.0125
GROUP = 8


def laplace(field_ext, kappa_ext, first_w, second_w, third_w):
    centre = field_ext[1:-1]
    kcentre = kappa_ext[1:-1]
    flux_one = first_w * (
        0.5 * (kcentre + kappa_ext[2:]) * (field_ext[2:] - centre)
        - 0.5 * (kcentre + kappa_ext[:-2]) * (centre - field_ext[:-2])
    )
    side_pad = jnp.pad(centre, ((0, 0), (1, 1), (0, 0)))
    kside_pad = jnp.pad(kcentre, ((0, 0), (1, 1), (0, 0)))
    flux_two = second_w * (
        0.5 * (kcentre + kside_pad[:, 2:]) * (side_pad[:, 2:] - centre)
        - 0.5 * (kcentre + kside_pad[:, :-2]) * (centre - side_pad[:, :-2])
    )
    deep_pad = jnp.pad(centre, ((0, 0), (0, 0), (1, 1)))
    kdeep_pad = jnp.pad(kcentre, ((0, 0), (0, 0), (1, 1)))
    flux_three = third_w * (
        0.5 * (kcentre + kdeep_pad[:, :, 2:]) * (deep_pad[:, :, 2:] - centre)
        - 0.5 * (kcentre + kdeep_pad[:, :, :-2]) * (centre - deep_pad[:, :, :-2])
    )
    return flux_one + flux_two + flux_three


def per_device(initial, guess, conductivity, source):
    rows, width_two, width_three = conductivity.shape
    crows = rows // 2
    slabs = lax.axis_size("space")
    tm = lax.axis_index("tm")
    sp = lax.axis_index("space")
    local = tm % GROUP
    place = (local + 3) % GROUP

    def cut(array, have, want):
        return array[have - want : array.shape[0] - (have - want)]

    def inside(values, margin, block):
        first = sp * block - margin
        index = first + lax.broadcasted_iota(jnp.int32, (values.shape[0], 1, 1), 0)
        return jnp.where((index >= 0) & (index < slabs * block), values, 0.0)

    def route(block, pairs):
        return lax.ppermute(block, ("tm", "space"), pairs)

    def along_space(block, distance, times=range(2 * GROUP)):
        pairs = [
            (t * slabs + i, t * slabs + i + distance)
            for t in times
            for i in range(slabs)
            if 0 <= i + distance < slabs
        ]
        return route(block, pairs)

    def along_time(block, pairs):
        return lax.ppermute(block, "tm", pairs)

    def ring(shift, groups=(0, 1)):
        return [
            (g * GROUP + i, g * GROUP + (i + shift) % GROUP)
            for g in groups
            for i in range(GROUP)
        ]

    def fine(ext, kappa_wide, source_wide):
        margin = STEPS
        for _ in range(STEPS):
            margin -= 1
            ext = inside(
                ext[1:-1]
                + laplace(
                    ext,
                    cut(kappa_wide, STEPS, margin + 1),
                    ALONG_FIRST,
                    ALONG_SECOND,
                    ALONG_THIRD,
                )
                + cut(source_wide, STEPS - 1, margin),
                margin,
                rows,
            )
        return ext

    def restrict(field):
        return field.reshape(-1, 2, width_two // 2, 2, width_three).mean(axis=(1, 3))

    def coarse(ext, have, steps, kappa_c, kappa_have):
        for _ in range(steps):
            have -= 1
            ext = inside(
                ext[1:-1]
                + laplace(
                    ext,
                    cut(kappa_c, kappa_have, have + 1),
                    ALONG_FIRST,
                    ALONG_SECOND,
                    4.0 * ALONG_THIRD,
                ),
                have,
                crows,
            )
        return ext

    def widen(block, times, margin):
        far = margin - crows
        near = [along_space(block, 1, times), along_space(block, -1, times)]
        ends = [
            along_space(block[crows - far :], 2, times),
            along_space(block[:far], -2, times),
        ]
        return jnp.concatenate([ends[0], near[0], block, near[1], ends[1]], 0)

    current = guess[0]
    crossed = along_time(current, [(6, 14), (7, 15)])
    state = jnp.where(tm == 7, initial, jnp.where(tm >= 14, crossed, current))
    up = along_space(
        jnp.concatenate([state[-STEPS:], conductivity[-STEPS:], source[1 - STEPS :]]), 1
    )
    down = along_space(
        jnp.concatenate([state[:STEPS], conductivity[:STEPS], source[: STEPS - 1]]), -1
    )
    kappa_wide = jnp.concatenate(
        [up[STEPS : 2 * STEPS], conductivity, down[STEPS : 2 * STEPS]], 0
    )
    source_wide = jnp.concatenate([up[2 * STEPS :], source, down[2 * STEPS :]], 0)
    state = fine(
        jnp.concatenate([up[:STEPS], state, down[:STEPS]], 0), kappa_wide, source_wide
    )

    def exchange(field):
        before = along_space(field[-STEPS:], 1)
        after = along_space(field[:STEPS], -1)
        return jnp.concatenate([before, field, after], 0)

    state = jnp.where(tm == 6, initial, state)
    second = fine(exchange(state), kappa_wide, source_wide)
    crossed = along_time(second, [(5, 13)])
    second_home = along_time(second, ring(2))
    state = jnp.where(tm == 5, initial, jnp.where(tm == 13, crossed, second))
    before_third = exchange(state)
    third = fine(before_third, kappa_wide, source_wide)
    third_home = along_time(third, ring(3))

    kappa_c = restrict(kappa_wide)
    base = restrict(before_third[2:-2])
    image = coarse(base, 1, 1, kappa_c, 2)
    tau = restrict(third) - jnp.where(tm == 5, 0.0, image)

    def after(array, mark):
        return lax.optimization_barrier((array, mark))[0]

    low, high = range(GROUP), range(GROUP, 2 * GROUP)
    kappa_own = kappa_c[2:-2]
    tau_wide = widen(jnp.concatenate([tau, kappa_own], 1), low, crows * 2)
    kappa_wide_c = tau_wide[:, width_two // 2 :]
    low_sum = cut(tau_wide[:, : width_two // 2], 8, 7)
    got = along_time(low_sum, ring(4, (0,)))
    got = coarse(got, 7, 4, kappa_wide_c, 8)
    wrapped = jnp.where(place >= 4, 0.0, got)
    low_sum = cut(low_sum, 7, 3) + jnp.where(place >= 4, got, 0.0)
    have = 3
    for shift in (2, 1):
        got = along_time(jnp.stack([low_sum, wrapped]), ring(shift, (0,)))
        ahead = jnp.where(place >= shift, got[0], 0.0)
        around = jnp.where(place >= shift, got[1], got[0])
        ahead = coarse(ahead, have, shift, kappa_wide_c, 8)
        around = coarse(around, have, shift, kappa_wide_c, 8)
        low_sum = cut(low_sum, have, have - shift) + ahead
        wrapped = cut(wrapped, have, have - shift) + around
        have -= shift
    carry = wrapped + coarse(widen(low_sum, low, 8), 8, 8, kappa_wide_c, 8)
    carry_home = along_time(carry, [(i, GROUP + (i + 3) % GROUP) for i in range(GROUP)])
    tau = after(tau, carry)

    tau_wide = widen(jnp.concatenate([tau, kappa_own], 1), high, crows * 2)
    kappa_wide_c = tau_wide[:, width_two // 2 :]
    high_sum = cut(tau_wide[:, : width_two // 2], 8, 7)
    have = 7
    for shift in (4, 2, 1):
        got = along_time(high_sum, ring(shift, (1,)))
        got = coarse(jnp.where(place >= shift, got, 0.0), have, shift, kappa_wide_c, 8)
        high_sum = cut(high_sum, have, have - shift) + got
        have -= shift
    total = jnp.where(tm < GROUP, low_sum, high_sum)
    total_home = along_time(total, ring(3)) + carry_home

    residual = third_home - second_home
    change = total_home - restrict(second_home)
    finer = jnp.repeat(jnp.repeat(change, 2, axis=0), 2, axis=1)
    corrected = second_home + finer
    return (corrected[None], residual[None])


def solution(mesh):
    in_specs = (
        P("space", None, None),
        P("tm", "space", None, None),
        P("space", None, None),
        P("space", None, None),
    )
    out_specs = (P("tm", "space", None, None), P("tm", "space", None, None))
    return jax.shard_map(
        per_device, mesh=mesh, in_specs=in_specs, out_specs=out_specs, check_vma=False
    )
```

time: 702 us -> 292 us (0.42)
  the two profiles are of different devices: /device:TPU:376 before, /device:TPU:17 now
where the time goes in v1:
time: 292 us; the launch traced here: 291 us
  starting transfers between devices  142 us (49%)
  waiting for transfers between devices  74 us (25%)
  other arithmetic  46.1 us (16%)
  local copies, waits for them, and re-layouts  25.7 us (9%)
    ppermute x12, starting transfers between devices, along_time(): return lax.ppermute(block, 'tm', pairs)  91.8 us
    ppermute x18, starting transfers between devices, route(): return lax.ppermute(block, ('tm', 'space'), pairs)  50.4 us
    ppermute x18, waiting for transfers between devices, route(): return lax.ppermute(block, ('tm', 'space'), pairs)  39.4 us
    ppermute x12, waiting for transfers between devices, along_time(): return lax.ppermute(block, 'tm', pairs)  34.6 us
    select_n x26, other arithmetic, inside(): return jnp.where((index >= 0) & (index < slabs * block), values, 0.0)  23.4 us
    unnamed x152, local copies, waits for them, and re-layouts  16.9 us
  transfers between devices with their start and end apart: 30, of which 14 were waited for; matrix products, arithmetic and copies ran while one was open for 3% of the time, Pallas kernels for 0%

profile of v1, /device:TPU:17, one launch (start us, length us, event | category | flops | bytes accessed | tf_op | source)
XLA Modules:
  0.0 290.7 jit_solution(2016096567805785255)
XLA Ops:
  4.7 2.9 collective-permute-start.1
  8.5 2.5 collective-permute-start.2
  11.1 12.7 %collective-permute-done.1 = f32[11,128,128]{2,1,0:T(8,128)S(1)} collective-permute-done((f32[11,128,128]{2,1,0:T(8,128)}, f32[11,128,128]{2,1,0:T(8,128)S(1)}, u32[]{:S(2)}, u32[]{:S(2)}) %collective-permute-start.1) | collective-permute-done | bytes 720928 | tf_op jit(solution)/shard_map/ppermute | solution.py:53
  24.7 2.8 collective-permute-done.2
  38.5 5.3 %collective-permute-start.3 = (f32[4,128,128]{2,1,0:T(8,128)S(1)}, f32[4,128,128]{2,1,0:T(8,128)S(1)}, u32[]{:S(2)}, u32[]{:S(2)}) collective-permute-start(f32[4,128,128]{2,1,0:T(8,128)S(1)} %get-tuple-element.27), channel_id=1, source_target_pairs={{0,1},{1,2},{2,3},{3,4},{4,5},{5,6},{6,7},{7,8},{8,9},{9,10},{10,1... | collective-permute-start | bytes 786440 | tf_op jit(solution)/shard_map/ppermute | solution.py:53
  43.8 1.9 collective-permute-start.4
  47.6 3.8 %collective-permute-done.4 = f32[4,128,128]{2,1,0:T(8,128)S(1)} collective-permute-done((f32[4,128,128]{2,1,0:T(8,128)S(1)}, f32[4,128,128]{2,1,0:T(8,128)S(1)}, u32[]{:S(2)}, u32[]{:S(2)}) %collective-permute-start.4) | collective-permute-done | bytes 262176 | tf_op jit(solution)/shard_map/ppermute | solution.py:53
  61.9 4.3 %collective-permute-start.7 = (f32[4,128,128]{2,1,0:T(8,128)}, f32[4,128,128]{2,1,0:T(8,128)}, u32[]{:S(2)}, u32[]{:S(2)}) collective-permute-start(f32[4,128,128]{2,1,0:T(8,128)} %get-tuple-element.25), channel_id=1, source_target_pairs={{0,1},{1,2},{2,3},{3,4},{4,5},{5,6},{6,7},{7,8},{8,9},{9,10},{10,1... | collective-permute-start | bytes 786440 | tf_op jit(solution)/shard_map/ppermute | solution.py:53
  66.2 2.1 collective-permute-start.8
  71.6 2.1 collective-permute-done.8
  85.6 2.7 collective-permute-start.11
  88.3 4.3 %collective-permute-start.9 = (f32[4,128,128]{2,1,0:T(8,128)S(1)}, f32[4,128,128]{2,1,0:T(8,128)S(1)}, u32[]{:S(2)}, u32[]{:S(2)}) collective-permute-start(f32[4,128,128]{2,1,0:T(8,128)S(1)} %pad_maximum_fusion.22), channel_id=1, source_target_pairs={{0,1},{1,2},{2,3},{3,4},{4,5},{5,6},{6,7},{7,8},{8,9},{9,10},{10,1... | collective-permute-start | bytes 786440 | tf_op jit(solution)/shard_map/ppermute | solution.py:53
  92.6 2.1 collective-permute-start.10
  94.7 2.5 collective-permute-start.12
  98.2 2.4 collective-permute-done.10
  100.6 6.8 %collective-permute-done.12 = f32[4,128,128]{2,1,0:T(8,128)S(1)} collective-permute-done((f32[4,128,128]{2,1,0:T(8,128)S(1)}, f32[4,128,128]{2,1,0:T(8,128)S(1)}, u32[]{:S(2)}, u32[]{:S(2)}) %collective-permute-start.12) | collective-permute-done | bytes 262176 | tf_op jit(solution)/shard_map/ppermute | solution.py:53
  108.4 39.9 %collective-permute-start.13 = (f32[18,64,128]{2,1,0:T(8,128)S(1)}, f32[18,64,128]{2,1,0:T(8,128)S(1)}, u32[]{:S(2)}, u32[]{:S(2)}) collective-permute-start(f32[18,64,128]{2,1,0:T(8,128)S(1)} %get-tuple-element.10), channel_id=1, source_target_pairs={{0,128},{32,160},{64,192},{96,224},{128,0},{160,32},{192,64},{224,... | collective-permute-start | bytes 1769480 | tf_op jit(solution)/shard_map/ppermute | solution.py:65
  150.2 5.4 %collective-permute-done.13 = f32[18,64,128]{2,1,0:T(8,128)S(1)} collective-permute-done((f32[18,64,128]{2,1,0:T(8,128)S(1)}, f32[18,64,128]{2,1,0:T(8,128)S(1)}, u32[]{:S(2)}, u32[]{:S(2)}) %collective-permute-start.13) | collective-permute-done | bytes 589856 | tf_op jit(solution)/shard_map/ppermute | solution.py:65
  160.3 21.7 %collective-permute-start.14 = (f32[2,10,64,128]{3,2,1,0:T(8,128)}, f32[2,10,64,128]{3,2,1,0:T(8,128)}, u32[]{:S(2)}, u32[]{:S(2)}) collective-permute-start(f32[2,10,64,128]{3,2,1,0:T(8,128)} %pad_maximum_fusion.17), channel_id=1, source_target_pairs={{0,64},{32,96},{64,128},{96,160},{128,192},{160,224},{192,0},{224,... | collective-permute-start | bytes 1966088 | tf_op jit(solution)/shard_map/ppermute | solution.py:65
  183.2 9.3 %collective-permute-done.14 = f32[2,10,64,128]{3,2,1,0:T(8,128)} collective-permute-done((f32[2,10,64,128]{3,2,1,0:T(8,128)}, f32[2,10,64,128]{3,2,1,0:T(8,128)}, u32[]{:S(2)}, u32[]{:S(2)}) %collective-permute-start.14) | collective-permute-done | bytes 655392 | tf_op jit(solution)/shard_map/ppermute | solution.py:65
  195.8 9.7 %collective-permute-start.15 = (f32[2,6,64,128]{3,2,1,0:T(8,128)S(1)}, f32[2,6,64,128]{3,2,1,0:T(8,128)}, u32[]{:S(2)}, u32[]{:S(2)}) collective-permute-start(f32[2,6,64,128]{3,2,1,0:T(8,128)S(1)} %pad_maximum_fusion.20), channel_id=1, source_target_pairs={{0,32},{32,64},{64,96},{96,128},{128,160},{160,192},{192,224},{224... | collective-permute-start | bytes 1179656 | tf_op jit(solution)/shard_map/ppermute | solution.py:65
  205.6 4.7 %collective-permute-done.15 = f32[2,6,64,128]{3,2,1,0:T(8,128)} collective-permute-done((f32[2,6,64,128]{3,2,1,0:T(8,128)S(1)}, f32[2,6,64,128]{3,2,1,0:T(8,128)}, u32[]{:S(2)}, u32[]{:S(2)}) %collective-permute-start.15) | collective-permute-done | bytes 393248 | tf_op jit(solution)/shard_map/ppermute | solution.py:65
  212.6 9.9 %collective-permute-start.16 = (f32[4,64,128]{2,1,0:T(8,128)S(1)}, f32[4,64,128]{2,1,0:T(8,128)S(1)}, u32[]{:S(2)}, u32[]{:S(2)}) collective-permute-start(f32[4,64,128]{2,1,0:T(8,128)S(1)} %fusion.866), channel_id=1, source_target_pairs={{0,2},{1,3},{2,4},{3,5},{4,6},{5,7},{6,8},{7,9},{8,10},{9,11},{10,... | collective-permute-start | bytes 393224 | tf_op jit(solution)/shard_map/ppermute | solution.py:53
  222.5 1.9 collective-permute-start.17
  224.4 3.4 %collective-permute-start.18 = (f32[4,64,128]{2,1,0:T(8,128)S(1)}, f32[4,64,128]{2,1,0:T(8,128)S(1)}, u32[]{:S(2)}, u32[]{:S(2)}) collective-permute-start(f32[4,64,128]{2,1,0:T(8,128)S(1)} %fusion.866), channel_id=1, source_target_pairs={{1,0},{2,1},{3,2},{4,3},{5,4},{6,5},{7,6},{8,7},{9,8},{10,9},{11,1... | collective-permute-start | bytes 393224 | tf_op jit(solution)/shard_map/ppermute | solution.py:53
  227.8 1.9 collective-permute-start.19
  230.1 5.8 %collective-permute-done.19 = f32[4,64,128]{2,1,0:T(8,128)S(1)} collective-permute-done((f32[4,64,128]{2,1,0:T(8,128)S(1)}, f32[4,64,128]{2,1,0:T(8,128)S(1)}, u32[]{:S(2)}, u32[]{:S(2)}) %collective-permute-start.19) | collective-permute-done | bytes 131104 | tf_op jit(solution)/shard_map/ppermute | solution.py:53
  256.1 3.1 %collective-permute-start.5 = (f32[8,128,128]{2,1,0:T(8,128)}, f32[8,128,128]{2,1,0:T(8,128)S(1)}, u32[]{:S(2)}, u32[]{:S(2)}) collective-permute-start(f32[8,128,128]{2,1,0:T(8,128)} %fusion.281), channel_id=1, source_target_pairs={{0,64},{32,96},{64,128},{96,160},{128,192},{160,224},{192,0},{224,... | collective-permute-start | bytes 1572872 | tf_op jit(solution)/shard_map/ppermute | solution.py:65
  259.2 8.9 %collective-permute-start.29 = (f32[8,128,128]{2,1,0:T(8,128)S(1)}, f32[8,128,128]{2,1,0:T(8,128)S(1)}, u32[]{:S(2)}, u32[]{:S(2)}) collective-permute-start(f32[8,128,128]{2,1,0:T(8,128)S(1)} %copy-done.55), channel_id=1, source_target_pairs={{0,96},{32,128},{64,160},{96,192},{128,224},{160,0},{192,32},{224,... | collective-permute-start | bytes 1572872 | tf_op jit(solution)/shard_map/ppermute | solution.py:65
  268.1 1.9 collective-permute-start.28
  271.0 1.9 collective-permute-start.27
  273.3 15.2 %collective-permute-done.27 = f32[4,64,128]{2,1,0:T(8,128)S(1)} collective-permute-done((f32[4,64,128]{2,1,0:T(8,128)}, f32[4,64,128]{2,1,0:T(8,128)S(1)}, u32[]{:S(2)}, u32[]{:S(2)}) %collective-permute-start.27) | collective-permute-done | bytes 131104 | tf_op jit(solution)/shard_map/ppermute | solution.py:65
  (336 shorter events, 82.2 us)
Async XLA Ops:
  0.7 3.0 %collective-permute-start = (f32[8,128,128]{2,1,0:T(8,128)}, f32[8,128,128]{2,1,0:T(8,128)S(1)}, u32[]{:S(2)}, u32[]{:S(2)}) collective-permute-start(f32[8,128,128]{2,1,0:T(8,128)} %bitcast.106), channel_id=1, source_target_pairs={{192,448},{224,480},{193,449},{225,481},{194,450},{226,482},{195,4... | collective-permute-start | bytes 1572872 | tf_op jit(solution)/shard_map/ppermute | solution.py:65
  4.7 19.1 %collective-permute-start.1 = (f32[11,128,128]{2,1,0:T(8,128)}, f32[11,128,128]{2,1,0:T(8,128)S(1)}, u32[]{:S(2)}, u32[]{:S(2)}) collective-permute-start(f32[11,128,128]{2,1,0:T(8,128)} %pad_maximum_fusion.11), channel_id=1, source_target_pairs={{0,1},{1,2},{2,3},{3,4},{4,5},{5,6},{6,7},{7,8},{8,9},{9,10},{10,1... | collective-permute-start | bytes 2162696 | tf_op jit(solution)/shard_map/ppermute | solution.py:53
  8.5 18.9 %collective-permute-start.2 = (f32[11,128,128]{2,1,0:T(8,128)}, f32[11,128,128]{2,1,0:T(8,128)S(1)}, u32[]{:S(2)}, u32[]{:S(2)}) collective-permute-start(f32[11,128,128]{2,1,0:T(8,128)} %pad_maximum_fusion.12), channel_id=1, source_target_pairs={{1,0},{2,1},{3,2},{4,3},{5,4},{6,5},{7,6},{8,7},{9,8},{10,9},{11,1... | collective-permute-start | bytes 2162696 | tf_op jit(solution)/shard_map/ppermute | solution.py:53
  38.5 9.0 %collective-permute-start.3 = (f32[4,128,128]{2,1,0:T(8,128)S(1)}, f32[4,128,128]{2,1,0:T(8,128)S(1)}, u32[]{:S(2)}, u32[]{:S(2)}) collective-permute-start(f32[4,128,128]{2,1,0:T(8,128)S(1)} %get-tuple-element.27), channel_id=1, source_target_pairs={{0,1},{1,2},{2,3},{3,4},{4,5},{5,6},{6,7},{7,8},{8,9},{9,10},{10,1... | collective-permute-start | bytes 786440 | tf_op jit(solution)/shard_map/ppermute | solution.py:53
  43.8 7.5 %collective-permute-start.4 = (f32[4,128,128]{2,1,0:T(8,128)S(1)}, f32[4,128,128]{2,1,0:T(8,128)S(1)}, u32[]{:S(2)}, u32[]{:S(2)}) collective-permute-start(f32[4,128,128]{2,1,0:T(8,128)S(1)} %get-tuple-element.28), channel_id=1, source_target_pairs={{1,0},{2,1},{3,2},{4,3},{5,4},{6,5},{7,6},{8,7},{9,8},{10,9},{11,1... | collective-permute-start | bytes 786440 | tf_op jit(solution)/shard_map/ppermute | solution.py:53
  57.6 1.5 collective-permute-start.6
  61.9 9.0 %collective-permute-start.7 = (f32[4,128,128]{2,1,0:T(8,128)}, f32[4,128,128]{2,1,0:T(8,128)}, u32[]{:S(2)}, u32[]{:S(2)}) collective-permute-start(f32[4,128,128]{2,1,0:T(8,128)} %get-tuple-element.25), channel_id=1, source_target_pairs={{0,1},{1,2},{2,3},{3,4},{4,5},{5,6},{6,7},{7,8},{8,9},{9,10},{10,1... | collective-permute-start | bytes 786440 | tf_op jit(solution)/shard_map/ppermute | solution.py:53
  66.2 7.4 %collective-permute-start.8 = (f32[4,128,128]{2,1,0:T(8,128)}, f32[4,128,128]{2,1,0:T(8,128)}, u32[]{:S(2)}, u32[]{:S(2)}) collective-permute-start(f32[4,128,128]{2,1,0:T(8,128)} %get-tuple-element.26), channel_id=1, source_target_pairs={{1,0},{2,1},{3,2},{4,3},{5,4},{6,5},{7,6},{8,7},{9,8},{10,9},{11,1... | collective-permute-start | bytes 786440 | tf_op jit(solution)/shard_map/ppermute | solution.py:53
  85.6 11.6 %collective-permute-start.11 = (f32[4,128,128]{2,1,0:T(8,128)S(1)}, f32[4,128,128]{2,1,0:T(8,128)S(1)}, u32[]{:S(2)}, u32[]{:S(2)}) collective-permute-start(f32[4,128,128]{2,1,0:T(8,128)S(1)} %pad_maximum_fusion.22), channel_id=1, source_target_pairs={{0,2},{1,3},{2,4},{3,5},{4,6},{5,7},{6,8},{7,9},{8,10},{9,11},{10,... | collective-permute-start | bytes 786440 | tf_op jit(solution)/shard_map/ppermute | solution.py:53
  88.3 9.9 %collective-permute-start.9 = (f32[4,128,128]{2,1,0:T(8,128)S(1)}, f32[4,128,128]{2,1,0:T(8,128)S(1)}, u32[]{:S(2)}, u32[]{:S(2)}) collective-permute-start(f32[4,128,128]{2,1,0:T(8,128)S(1)} %pad_maximum_fusion.22), channel_id=1, source_target_pairs={{0,1},{1,2},{2,3},{3,4},{4,5},{5,6},{6,7},{7,8},{8,9},{9,10},{10,1... | collective-permute-start | bytes 786440 | tf_op jit(solution)/shard_map/ppermute | solution.py:53
  92.6 63.1 %copy-start.69 = (pred[16]{0:T(512)(128)(4,1)}, pred[16]{0:T(512)(128)(4,1)S(1)}, u32[]{:S(2)}) copy-start(pred[16]{0:T(512)(128)(4,1)S(1)} %compare_and_fusion.3) | copy-start | bytes 52
  92.6 8.0 %collective-permute-start.10 = (f32[4,128,128]{2,1,0:T(8,128)S(1)}, f32[4,128,128]{2,1,0:T(8,128)S(1)}, u32[]{:S(2)}, u32[]{:S(2)}) collective-permute-start(f32[4,128,128]{2,1,0:T(8,128)S(1)} %pad_maximum_fusion.22), channel_id=1, source_target_pairs={{1,0},{2,1},{3,2},{4,3},{5,4},{6,5},{7,6},{8,7},{9,8},{10,9},{11,1... | collective-permute-start | bytes 786440 | tf_op jit(solution)/shard_map/ppermute | solution.py:53
  94.7 12.8 %collective-permute-start.12 = (f32[4,128,128]{2,1,0:T(8,128)S(1)}, f32[4,128,128]{2,1,0:T(8,128)S(1)}, u32[]{:S(2)}, u32[]{:S(2)}) collective-permute-start(f32[4,128,128]{2,1,0:T(8,128)S(1)} %pad_maximum_fusion.22), channel_id=1, source_target_pairs={{2,0},{3,1},{4,2},{5,3},{6,4},{7,5},{8,6},{9,7},{10,8},{11,9},{12,... | collective-permute-start | bytes 786440 | tf_op jit(solution)/shard_map/ppermute | solution.py:53
  98.2 50.4 %copy-start.28 = (f32[4,128,128]{2,1,0:T(8,128)}, f32[4,128,128]{2,1,0:T(8,128)S(1)}, u32[]{:S(2)}) copy-start(f32[4,128,128]{2,1,0:T(8,128)S(1)} %collective-permute-done.9) | copy-start | bytes 786436
  108.4 47.2 %collective-permute-start.13 = (f32[18,64,128]{2,1,0:T(8,128)S(1)}, f32[18,64,128]{2,1,0:T(8,128)S(1)}, u32[]{:S(2)}, u32[]{:S(2)}) collective-permute-start(f32[18,64,128]{2,1,0:T(8,128)S(1)} %get-tuple-element.10), channel_id=1, source_target_pairs={{0,128},{32,160},{64,192},{96,224},{128,0},{160,32},{192,64},{224,... | collective-permute-start | bytes 1769480 | tf_op jit(solution)/shard_map/ppermute | solution.py:65
  160.3 32.2 %collective-permute-start.14 = (f32[2,10,64,128]{3,2,1,0:T(8,128)}, f32[2,10,64,128]{3,2,1,0:T(8,128)}, u32[]{:S(2)}, u32[]{:S(2)}) collective-permute-start(f32[2,10,64,128]{3,2,1,0:T(8,128)} %pad_maximum_fusion.17), channel_id=1, source_target_pairs={{0,64},{32,96},{64,128},{96,160},{128,192},{160,224},{192,0},{224,... | collective-permute-start | bytes 1966088 | tf_op jit(solution)/shard_map/ppermute | solution.py:65
  195.8 14.4 %collective-permute-start.15 = (f32[2,6,64,128]{3,2,1,0:T(8,128)S(1)}, f32[2,6,64,128]{3,2,1,0:T(8,128)}, u32[]{:S(2)}, u32[]{:S(2)}) collective-permute-start(f32[2,6,64,128]{3,2,1,0:T(8,128)S(1)} %pad_maximum_fusion.20), channel_id=1, source_target_pairs={{0,32},{32,64},{64,96},{96,128},{128,160},{160,192},{192,224},{224... | collective-permute-start | bytes 1179656 | tf_op jit(solution)/shard_map/ppermute | solution.py:65
  212.6 17.2 %collective-permute-start.16 = (f32[4,64,128]{2,1,0:T(8,128)S(1)}, f32[4,64,128]{2,1,0:T(8,128)S(1)}, u32[]{:S(2)}, u32[]{:S(2)}) collective-permute-start(f32[4,64,128]{2,1,0:T(8,128)S(1)} %fusion.866), channel_id=1, source_target_pairs={{0,2},{1,3},{2,4},{3,5},{4,6},{5,7},{6,8},{7,9},{8,10},{9,11},{10,... | collective-permute-start | bytes 393224 | tf_op jit(solution)/shard_map/ppermute | solution.py:53
  222.5 7.3 %collective-permute-start.17 = (f32[4,64,128]{2,1,0:T(8,128)S(1)}, f32[4,64,128]{2,1,0:T(8,128)S(1)}, u32[]{:S(2)}, u32[]{:S(2)}) collective-permute-start(f32[4,64,128]{2,1,0:T(8,128)S(1)} %fusion.866), channel_id=1, source_target_pairs={{0,1},{1,2},{2,3},{3,4},{4,5},{5,6},{6,7},{7,8},{8,9},{9,10},{10,1... | collective-permute-start | bytes 393224 | tf_op jit(solution)/shard_map/ppermute | solution.py:53
  224.4 5.7 %collective-permute-start.18 = (f32[4,64,128]{2,1,0:T(8,128)S(1)}, f32[4,64,128]{2,1,0:T(8,128)S(1)}, u32[]{:S(2)}, u32[]{:S(2)}) collective-permute-start(f32[4,64,128]{2,1,0:T(8,128)S(1)} %fusion.866), channel_id=1, source_target_pairs={{1,0},{2,1},{3,2},{4,3},{5,4},{6,5},{7,6},{8,7},{9,8},{10,9},{11,1... | collective-permute-start | bytes 393224 | tf_op jit(solution)/shard_map/ppermute | solution.py:53
  227.8 8.1 %collective-permute-start.19 = (f32[4,64,128]{2,1,0:T(8,128)S(1)}, f32[4,64,128]{2,1,0:T(8,128)S(1)}, u32[]{:S(2)}, u32[]{:S(2)}) collective-permute-start(f32[4,64,128]{2,1,0:T(8,128)S(1)} %fusion.866), channel_id=1, source_target_pairs={{2,0},{3,1},{4,2},{5,3},{6,4},{7,5},{8,6},{9,7},{10,8},{11,9},{12,... | collective-permute-start | bytes 393224 | tf_op jit(solution)/shard_map/ppermute | solution.py:53
  245.1 2.7 collective-permute-start.22
  245.8 2.1 collective-permute-start.20
  246.5 1.5 collective-permute-start.21
  247.2 0.8 collective-permute-start.23
  248.1 1.8 collective-permute-start.24
  253.5 1.1 collective-permute-start.25
  255.4 14.6 %collective-permute-start.26 = (f32[6,64,128]{2,1,0:T(8,128)S(1)}, f32[6,64,128]{2,1,0:T(8,128)S(1)}, u32[]{:S(2)}, u32[]{:S(2)}) collective-permute-start(f32[6,64,128]{2,1,0:T(8,128)S(1)} %fusion.788), channel_id=1, source_target_pairs={{256,288},{288,320},{320,352},{352,384},{384,416},{416,448},{448,4... | collective-permute-start | bytes 589832 | tf_op jit(solution)/shard_map/ppermute | solution.py:65
  256.1 16.8 %collective-permute-start.5 = (f32[8,128,128]{2,1,0:T(8,128)}, f32[8,128,128]{2,1,0:T(8,128)S(1)}, u32[]{:S(2)}, u32[]{:S(2)}) collective-permute-start(f32[8,128,128]{2,1,0:T(8,128)} %fusion.281), channel_id=1, source_target_pairs={{0,64},{32,96},{64,128},{96,160},{128,192},{160,224},{192,0},{224,... | collective-permute-start | bytes 1572872 | tf_op jit(solution)/shard_map/ppermute | solution.py:65
  259.2 30.2 %collective-permute-start.29 = (f32[8,128,128]{2,1,0:T(8,128)S(1)}, f32[8,128,128]{2,1,0:T(8,128)S(1)}, u32[]{:S(2)}, u32[]{:S(2)}) collective-permute-start(f32[8,128,128]{2,1,0:T(8,128)S(1)} %copy-done.55), channel_id=1, source_target_pairs={{0,96},{32,128},{64,160},{96,192},{128,224},{160,0},{192,32},{224,... | collective-permute-start | bytes 1572872 | tf_op jit(solution)/shard_map/ppermute | solution.py:65
  268.1 5.2 %collective-permute-start.28 = (f32[4,64,128]{2,1,0:T(8,128)}, f32[4,64,128]{2,1,0:T(8,128)}, u32[]{:S(2)}, u32[]{:S(2)}) collective-permute-start(f32[4,64,128]{2,1,0:T(8,128)} %fusion.878), channel_id=1, source_target_pairs={{0,352},{32,384},{64,416},{96,448},{128,480},{160,256},{192,288},{... | collective-permute-start | bytes 393224 | tf_op jit(solution)/shard_map/ppermute | solution.py:65
  271.0 17.5 %collective-permute-start.27 = (f32[4,64,128]{2,1,0:T(8,128)}, f32[4,64,128]{2,1,0:T(8,128)S(1)}, u32[]{:S(2)}, u32[]{:S(2)}) collective-permute-start(f32[4,64,128]{2,1,0:T(8,128)} %fusion.900), channel_id=1, source_target_pairs={{0,96},{32,128},{64,160},{96,192},{128,224},{160,0},{192,32},{224,... | collective-permute-start | bytes 393224 | tf_op jit(solution)/shard_map/ppermute | solution.py:65
  (71 other events, 501.2 us)

commit v2 on v1

--- a/solution.py
+++ b/solution.py
@@ -39,8 +39,6 @@
     tm = lax.axis_index("tm")
     sp = lax.axis_index("space")
     local = tm % GROUP
-    place = (local + 3) % GROUP
-
     def cut(array, have, want):
         return array[have - want : array.shape[0] - (have - want)]
 
@@ -119,14 +117,14 @@
         ]
         return jnp.concatenate([ends[0], near[0], block, near[1], ends[1]], 0)
 
-    current = guess[0]
-    crossed = along_time(current, [(6, 14), (7, 15)])
-    state = jnp.where(tm == 7, initial, jnp.where(tm >= 14, crossed, current))
-    up = along_space(
-        jnp.concatenate([state[-STEPS:], conductivity[-STEPS:], source[1 - STEPS :]]), 1
-    )
-    down = along_space(
-        jnp.concatenate([state[:STEPS], conductivity[:STEPS], source[: STEPS - 1]]), -1
+    def neighbours(block_first, block_last, times=range(2 * GROUP)):
+        return along_space(block_last, 1, times), along_space(block_first, -1, times)
+
+    kappa_own = restrict(conductivity)
+    state = jnp.where(tm == 15, initial, guess[0])
+    up, down = neighbours(
+        jnp.concatenate([state[:STEPS], conductivity[:STEPS], source[: STEPS - 1]]),
+        jnp.concatenate([state[-STEPS:], conductivity[-STEPS:], source[1 - STEPS :]]),
     )
     kappa_wide = jnp.concatenate(
         [up[STEPS : 2 * STEPS], conductivity, down[STEPS : 2 * STEPS]], 0
@@ -136,65 +134,91 @@
         jnp.concatenate([up[:STEPS], state, down[:STEPS]], 0), kappa_wide, source_wide
     )
 
-    def exchange(field):
-        before = along_space(field[-STEPS:], 1)
-        after = along_space(field[:STEPS], -1)
-        return jnp.concatenate([before, field, after], 0)
-
-    state = jnp.where(tm == 6, initial, state)
-    second = fine(exchange(state), kappa_wide, source_wide)
-    crossed = along_time(second, [(5, 13)])
-    second_home = along_time(second, ring(2))
-    state = jnp.where(tm == 5, initial, jnp.where(tm == 13, crossed, second))
-    before_third = exchange(state)
+    state = jnp.where(tm == 14, initial, state)
+    packed = kappa_own.reshape(crows // 2, width_two, width_three)
+    up, down = neighbours(
+        jnp.concatenate([state[:STEPS], packed]),
+        jnp.concatenate([state[-STEPS:], packed]),
+    )
+    shape_c = (crows, width_two // 2, width_three)
+    kappa_4 = jnp.concatenate(
+        [up[STEPS:].reshape(shape_c), kappa_own, down[STEPS:].reshape(shape_c)], 0
+    )
+    second = fine(
+        jnp.concatenate([up[:STEPS], state, down[:STEPS]], 0), kappa_wide, source_wide
+    )
+
+    state = jnp.where(tm == 13, initial, second)
+    up, down = neighbours(state[:STEPS], state[-STEPS:])
+    second_near = along_time(second, ring(2))
+    before_third = jnp.concatenate([up, state, down], 0)
     third = fine(before_third, kappa_wide, source_wide)
-    third_home = along_time(third, ring(3))
-
-    kappa_c = restrict(kappa_wide)
-    base = restrict(before_third[2:-2])
-    image = coarse(base, 1, 1, kappa_c, 2)
-    tau = restrict(third) - jnp.where(tm == 5, 0.0, image)
-
-    def after(array, mark):
-        return lax.optimization_barrier((array, mark))[0]
-
-    low, high = range(GROUP), range(GROUP, 2 * GROUP)
-    kappa_own = kappa_c[2:-2]
-    tau_wide = widen(jnp.concatenate([tau, kappa_own], 1), low, crows * 2)
-    kappa_wide_c = tau_wide[:, width_two // 2 :]
-    low_sum = cut(tau_wide[:, : width_two // 2], 8, 7)
-    got = along_time(low_sum, ring(4, (0,)))
-    got = coarse(got, 7, 4, kappa_wide_c, 8)
-    wrapped = jnp.where(place >= 4, 0.0, got)
-    low_sum = cut(low_sum, 7, 3) + jnp.where(place >= 4, got, 0.0)
-    have = 3
-    for shift in (2, 1):
-        got = along_time(jnp.stack([low_sum, wrapped]), ring(shift, (0,)))
-        ahead = jnp.where(place >= shift, got[0], 0.0)
-        around = jnp.where(place >= shift, got[1], got[0])
-        ahead = coarse(ahead, have, shift, kappa_wide_c, 8)
-        around = coarse(around, have, shift, kappa_wide_c, 8)
-        low_sum = cut(low_sum, have, have - shift) + ahead
-        wrapped = cut(wrapped, have, have - shift) + around
-        have -= shift
-    carry = wrapped + coarse(widen(low_sum, low, 8), 8, 8, kappa_wide_c, 8)
-    carry_home = along_time(carry, [(i, GROUP + (i + 3) % GROUP) for i in range(GROUP)])
-    tau = after(tau, carry)
-
-    tau_wide = widen(jnp.concatenate([tau, kappa_own], 1), high, crows * 2)
-    kappa_wide_c = tau_wide[:, width_two // 2 :]
-    high_sum = cut(tau_wide[:, : width_two // 2], 8, 7)
-    have = 7
-    for shift in (4, 2, 1):
-        got = along_time(high_sum, ring(shift, (1,)))
-        got = coarse(jnp.where(place >= shift, got, 0.0), have, shift, kappa_wide_c, 8)
-        high_sum = cut(high_sum, have, have - shift) + got
-        have -= shift
-    total = jnp.where(tm < GROUP, low_sum, high_sum)
-    total_home = along_time(total, ring(3)) + carry_home
+
+    image = coarse(restrict(before_third[2:-2]), 1, 1, kappa_4, 4)
+    tau = restrict(third) - jnp.where(tm == 13, 0.0, image)
+
+    up, down = neighbours(tau, tau)
+    second_cross = along_time(second_near, [(0, 8), (1, 9), (8, 0), (9, 1)])
+    tau_wide = jnp.concatenate([up, tau, down], 0)
+    high = tm >= GROUP
+    ahead, wrapped = 0.0, 0.0
+    got = [along_time(cut(tau_wide, 4, d), ring(d)) for d in (3, 2, 1)]
+    third_cross = along_time(third, [(i, i ^ 8) for i in (5, 6, 7, 13, 14, 15)])
+    for d, block in zip((3, 2, 1), got):
+        apart = high & (local >= 5) & (local < d + 5)
+        ahead = ahead + jnp.where((local >= d) & ~apart, block, 0.0)
+        wrapped = wrapped + jnp.where(local < d, block, 0.0)
+        ahead = coarse(ahead, d, 1, kappa_4, 4)
+        wrapped = coarse(wrapped, d, 1, kappa_4, 4)
+    ahead = ahead + tau
+
+    both = jnp.stack([ahead, wrapped])
+
+    def diagonal(distance):
+        pairs = [
+            (t * slabs + i, u * slabs + i + distance)
+            for t, u in ring(4)
+            for i in range(slabs)
+            if 0 <= i + distance < slabs
+        ]
+        return route(both, pairs)
+
+    got = jnp.concatenate([diagonal(1), diagonal(0), diagonal(-1)], 1)
+    more = jnp.where((local >= 4) & ~(high & (local >= 5)), got[0], 0.0)
+    behind = jnp.where(local >= 4, got[1], jnp.where(high & (local == 0), 0.0, got[0]))
+    ahead = ahead + coarse(more, 4, 4, kappa_4, 4)
+    wrapped = wrapped + coarse(behind, 4, 4, kappa_4, 4)
+
+    last = jnp.where(high & (local < 5), 0.0, ahead)
+    near = neighbours(last, last)
+    two = jnp.concatenate([last, kappa_own], 1)
+    far = (along_space(two, 2), along_space(two, -2))
+    half = width_two // 2
+    last_wide = jnp.concatenate(
+        [far[0][:, :half], near[0], last, near[1], far[1][:, :half]], 0
+    )
+    kappa_8 = jnp.concatenate([far[0][:, half:], kappa_4, far[1][:, half:]], 0)
+    carry = wrapped + coarse(last_wide, 8, 8, kappa_8, 8)
+    handed = along_time(
+        jnp.where(local >= 5, ahead, carry),
+        [
+            (g * GROUP + i, (1 - g) * GROUP + (i + 3) % GROUP)
+            for g in (0, 1)
+            for i in range(GROUP)
+        ],
+    )
+    twice = coarse(widen(carry, range(8, 13), 8), 8, 8, kappa_8, 8)
+    kept = jnp.where(
+        high,
+        jnp.where(local < 5, ahead + twice, carry),
+        jnp.where(local < 5, ahead, 0.0),
+    )
+    kept = along_time(kept, ring(3))
+    third_home = along_time(jnp.where(local >= 5, third_cross, third), ring(3))
+    second_home = jnp.where(local < 2, second_cross, second_near)
 
     residual = third_home - second_home
-    change = total_home - restrict(second_home)
+    change = handed + kept - restrict(second_home)
     finer = jnp.repeat(jnp.repeat(change, 2, axis=0), 2, axis=1)
     corrected = second_home + finer
     return (corrected[None], residual[None])

time: 292 us -> 280 us (0.959)
  the two profiles are of different devices: /device:TPU:17 before, /device:TPU:35 now
where the time goes in v2:
time: 280 us; the launch traced here: 278 us
  starting transfers between devices  148 us (53%)
  waiting for transfers between devices  45.3 us (16%)
  other arithmetic  43.4 us (16%)
  local copies, waits for them, and re-layouts  38.9 us (14%)
    ppermute x9, starting transfers between devices, along_time(): return lax.ppermute(block, 'tm', pairs)  85.9 us
    ppermute x19, starting transfers between devices, route(): return lax.ppermute(block, ('tm', 'space'), pairs)  62.2 us
    ppermute x19, waiting for transfers between devices, route(): return lax.ppermute(block, ('tm', 'space'), pairs)  32.6 us
    select_n x28, other arithmetic, inside(): return jnp.where((index >= 0) & (index < slabs * block), values, 0.0)  23.2 us
    unnamed x203, local copies, waits for them, and re-layouts  23.2 us
    ppermute x9, waiting for transfers between devices, along_time(): return lax.ppermute(block, 'tm', pairs)  12.6 us
  transfers between devices with their start and end apart: 28, of which 13 were waited for; matrix products, arithmetic and copies ran while one was open for 11% of the time, Pallas kernels for 0%

profile of v2, /device:TPU:35, one launch (start us, length us, event | category | flops | bytes accessed | tf_op | source)
XLA Modules:
  0.0 278.4 jit_solution(15568981560890579451)
XLA Ops:
  3.1 3.2 %collective-permute-start = (f32[11,128,128]{2,1,0:T(8,128)S(1)}, f32[11,128,128]{2,1,0:T(8,128)}, u32[]{:S(2)}, u32[]{:S(2)}) collective-permute-start(f32[11,128,128]{2,1,0:T(8,128)S(1)} %pad_maximum_fusion.5), channel_id=1, source_target_pairs={{0,1},{1,2},{2,3},{3,4},{4,5},{5,6},{6,7},{7,8},{8,9},{9,10},{10,1... | collective-permute-start | bytes 2162696 | tf_op jit(solution)/shard_map/ppermute | solution.py:51
  7.2 4.2 %collective-permute-start.1 = (f32[11,128,128]{2,1,0:T(8,128)}, f32[11,128,128]{2,1,0:T(8,128)S(1)}, u32[]{:S(2)}, u32[]{:S(2)}) collective-permute-start(f32[11,128,128]{2,1,0:T(8,128)} %pad_maximum_fusion.6), channel_id=1, source_target_pairs={{1,0},{2,1},{3,2},{4,3},{5,4},{6,5},{7,6},{8,7},{9,8},{10,9},{11,1... | collective-permute-start | bytes 2162696 | tf_op jit(solution)/shard_map/ppermute | solution.py:51
  11.9 12.3 %collective-permute-done = f32[11,128,128]{2,1,0:T(8,128)} collective-permute-done((f32[11,128,128]{2,1,0:T(8,128)S(1)}, f32[11,128,128]{2,1,0:T(8,128)}, u32[]{:S(2)}, u32[]{:S(2)}) %collective-permute-start) | collective-permute-done | bytes 720928 | tf_op jit(solution)/shard_map/ppermute | solution.py:51
  30.2 1.9 pad_maximum_fusion.4
  33.6 2.2 fusion.152
  38.8 3.0 %collective-permute-start.2 = (f32[6,128,128]{2,1,0:T(8,128)}, f32[6,128,128]{2,1,0:T(8,128)}, u32[]{:S(2)}, u32[]{:S(2)}) collective-permute-start(f32[6,128,128]{2,1,0:T(8,128)} %get-tuple-element.75), channel_id=1, source_target_pairs={{0,1},{1,2},{2,3},{3,4},{4,5},{5,6},{6,7},{7,8},{8,9},{9,10},{10,1... | collective-permute-start | bytes 1179656 | tf_op jit(solution)/shard_map/ppermute | solution.py:51
  41.8 5.0 %collective-permute-start.3 = (f32[6,128,128]{2,1,0:T(8,128)}, f32[6,128,128]{2,1,0:T(8,128)}, u32[]{:S(2)}, u32[]{:S(2)}) collective-permute-start(f32[6,128,128]{2,1,0:T(8,128)} %get-tuple-element.76), channel_id=1, source_target_pairs={{1,0},{2,1},{3,2},{4,3},{5,4},{6,5},{7,6},{8,7},{9,8},{10,9},{11,1... | collective-permute-start | bytes 1179656 | tf_op jit(solution)/shard_map/ppermute | solution.py:51
  46.9 5.9 %collective-permute-done.2 = f32[6,128,128]{2,1,0:T(8,128)} collective-permute-done((f32[6,128,128]{2,1,0:T(8,128)}, f32[6,128,128]{2,1,0:T(8,128)}, u32[]{:S(2)}, u32[]{:S(2)}) %collective-permute-start.2) | collective-permute-done | bytes 393248 | tf_op jit(solution)/shard_map/ppermute | solution.py:51
  56.1 1.8 fusion.23
  67.0 3.9 %collective-permute-start.6 = (f32[4,128,128]{2,1,0:T(8,128)}, f32[4,128,128]{2,1,0:T(8,128)}, u32[]{:S(2)}, u32[]{:S(2)}) collective-permute-start(f32[4,128,128]{2,1,0:T(8,128)} %get-tuple-element.55), channel_id=1, source_target_pairs={{0,1},{1,2},{2,3},{3,4},{4,5},{5,6},{6,7},{7,8},{8,9},{9,10},{10,1... | collective-permute-start | bytes 786440 | tf_op jit(solution)/shard_map/ppermute | solution.py:51
  70.9 4.4 %collective-permute-start.7 = (f32[4,128,128]{2,1,0:T(8,128)}, f32[4,128,128]{2,1,0:T(8,128)}, u32[]{:S(2)}, u32[]{:S(2)}) collective-permute-start(f32[4,128,128]{2,1,0:T(8,128)} %get-tuple-element.56), channel_id=1, source_target_pairs={{1,0},{2,1},{3,2},{4,3},{5,4},{6,5},{7,6},{8,7},{9,8},{10,9},{11,1... | collective-permute-start | bytes 786440 | tf_op jit(solution)/shard_map/ppermute | solution.py:51
  81.6 1.8 fusion.34
  91.4 3.7 %collective-permute-start.8 = (f32[4,64,128]{2,1,0:T(8,128)S(1)}, f32[4,64,128]{2,1,0:T(8,128)S(1)}, u32[]{:S(2)}, u32[]{:S(2)}) collective-permute-start(f32[4,64,128]{2,1,0:T(8,128)S(1)} %get-tuple-element.29), channel_id=1, source_target_pairs={{0,1},{1,2},{2,3},{3,4},{4,5},{5,6},{6,7},{7,8},{8,9},{9,10},{10,1... | collective-permute-start | bytes 393224 | tf_op jit(solution)/shard_map/ppermute | solution.py:51
  95.1 4.2 %collective-permute-start.9 = (f32[4,64,128]{2,1,0:T(8,128)S(1)}, f32[4,64,128]{2,1,0:T(8,128)S(1)}, u32[]{:S(2)}, u32[]{:S(2)}) collective-permute-start(f32[4,64,128]{2,1,0:T(8,128)S(1)} %get-tuple-element.29), channel_id=1, source_target_pairs={{1,0},{2,1},{3,2},{4,3},{5,4},{6,5},{7,6},{8,7},{9,8},{10,9},{11,1... | collective-permute-start | bytes 393224 | tf_op jit(solution)/shard_map/ppermute | solution.py:51
  101.3 8.6 %collective-permute-start.10 = (f32[10,64,128]{2,1,0:T(8,128)S(1)}, f32[10,64,128]{2,1,0:T(8,128)S(1)}, u32[]{:S(2)}, u32[]{:S(2)}) collective-permute-start(f32[10,64,128]{2,1,0:T(8,128)S(1)} %slice.2095), channel_id=1, source_target_pairs={{0,96},{32,128},{64,160},{96,192},{128,224},{160,0},{192,32},{224,... | collective-permute-start | bytes 983048 | tf_op jit(solution)/shard_map/ppermute | solution.py:63
  109.9 1.9 collective-permute-start.11
  114.5 7.7 %collective-permute-done.11 = f32[8,64,128]{2,1,0:T(8,128)S(1)} collective-permute-done((f32[8,64,128]{2,1,0:T(8,128)S(1)}, f32[8,64,128]{2,1,0:T(8,128)S(1)}, u32[]{:S(2)}, u32[]{:S(2)}) %collective-permute-start.11) | collective-permute-done | bytes 262176 | tf_op jit(solution)/shard_map/ppermute | solution.py:63
  126.5 5.7 %collective-permute-start.13 = (f32[2,4,64,128]{3,2,1,0:T(8,128)S(1)}, f32[2,4,64,128]{3,2,1,0:T(8,128)}, u32[]{:S(2)}, u32[]{:S(2)}) collective-permute-start(f32[2,4,64,128]{3,2,1,0:T(8,128)S(1)} %pad_maximum_fusion.15), channel_id=1, source_target_pairs={{0,129},{1,130},{2,131},{3,132},{4,133},{5,134},{6,135},{7,136},{8... | collective-permute-start | bytes 786440 | tf_op jit(solution)/shard_map/ppermute | solution.py:51
  132.3 2.6 collective-permute-start.14
  134.9 5.6 %collective-permute-start.15 = (f32[2,4,64,128]{3,2,1,0:T(8,128)S(1)}, f32[2,4,64,128]{3,2,1,0:T(8,128)}, u32[]{:S(2)}, u32[]{:S(2)}) collective-permute-start(f32[2,4,64,128]{3,2,1,0:T(8,128)S(1)} %pad_maximum_fusion.15), channel_id=1, source_target_pairs={{1,128},{2,129},{3,130},{4,131},{5,132},{6,133},{7,134},{8,135},{9... | collective-permute-start | bytes 786440 | tf_op jit(solution)/shard_map/ppermute | solution.py:51
  141.1 2.5 collective-permute-start.4
  144.6 5.2 %collective-permute-done.14 = f32[2,4,64,128]{3,2,1,0:T(8,128)} collective-permute-done((f32[2,4,64,128]{3,2,1,0:T(8,128)S(1)}, f32[2,4,64,128]{3,2,1,0:T(8,128)}, u32[]{:S(2)}, u32[]{:S(2)}) %collective-permute-start.14) | collective-permute-done | bytes 262176 | tf_op jit(solution)/shard_map/ppermute | solution.py:51
  160.4 3.7 %collective-permute-start.16 = (f32[4,128,128]{2,1,0:T(8,128)}, f32[4,128,128]{2,1,0:T(8,128)}, u32[]{:S(2)}, u32[]{:S(2)}) collective-permute-start(f32[4,128,128]{2,1,0:T(8,128)} %pad_maximum_fusion.16), channel_id=1, source_target_pairs={{0,2},{1,3},{2,4},{3,5},{4,6},{5,7},{6,8},{7,9},{8,10},{9,11},{10,... | collective-permute-start | bytes 786440 | tf_op jit(solution)/shard_map/ppermute | solution.py:51
  166.2 2.0 collective-permute-start.17
  168.2 5.4 %collective-permute-start.18 = (f32[4,64,128]{2,1,0:T(8,128)}, f32[4,64,128]{2,1,0:T(8,128)S(1)}, u32[]{:S(2)}, u32[]{:S(2)}) collective-permute-start(f32[4,64,128]{2,1,0:T(8,128)} %copy-done.86), channel_id=1, source_target_pairs={{1,0},{2,1},{3,2},{4,3},{5,4},{6,5},{7,6},{8,7},{9,8},{10,9},{11,1... | collective-permute-start | bytes 393224 | tf_op jit(solution)/shard_map/ppermute | solution.py:51
  174.6 3.1 %collective-permute-start.19 = (f32[4,128,128]{2,1,0:T(8,128)}, f32[4,128,128]{2,1,0:T(8,128)S(1)}, u32[]{:S(2)}, u32[]{:S(2)}) collective-permute-start(f32[4,128,128]{2,1,0:T(8,128)} %pad_maximum_fusion.16), channel_id=1, source_target_pairs={{2,0},{3,1},{4,2},{5,3},{6,4},{7,5},{8,6},{9,7},{10,8},{11,9},{12,... | collective-permute-start | bytes 786440 | tf_op jit(solution)/shard_map/ppermute | solution.py:51
  178.9 5.7 %collective-permute-done.19 = f32[4,128,128]{2,1,0:T(8,128)S(1)} collective-permute-done((f32[4,128,128]{2,1,0:T(8,128)}, f32[4,128,128]{2,1,0:T(8,128)S(1)}, u32[]{:S(2)}, u32[]{:S(2)}) %collective-permute-start.19) | collective-permute-done | bytes 262176 | tf_op jit(solution)/shard_map/ppermute | solution.py:51
  195.8 50.4 %collective-permute-start.27 = (f32[8,128,128]{2,1,0:T(8,128)S(1)}, f32[8,128,128]{2,1,0:T(8,128)S(1)}, u32[]{:S(2)}, u32[]{:S(2)}) collective-permute-start(f32[8,128,128]{2,1,0:T(8,128)S(1)} %broadcast_select_fusion), channel_id=1, source_target_pairs={{0,96},{32,128},{64,160},{96,192},{128,224},{160,0},{192,32},{224,... | collective-permute-start | bytes 1572872 | tf_op jit(solution)/shard_map/ppermute | solution.py:63
  247.6 11.7 %collective-permute-start.20 = (f32[4,64,128]{2,1,0:T(8,128)}, f32[4,64,128]{2,1,0:T(8,128)S(1)}, u32[]{:S(2)}, u32[]{:S(2)}) collective-permute-start(f32[4,64,128]{2,1,0:T(8,128)} %get-tuple-element.4), channel_id=1, source_target_pairs={{0,352},{32,384},{64,416},{96,448},{128,480},{160,256},{192,288},{... | collective-permute-start | bytes 393224 | tf_op jit(solution)/shard_map/ppermute | solution.py:63
  263.6 8.8 %collective-permute-start.25 = (f32[4,64,128]{2,1,0:T(8,128)S(1)}, f32[4,64,128]{2,1,0:T(8,128)S(1)}, u32[]{:S(2)}, u32[]{:S(2)}) collective-permute-start(f32[4,64,128]{2,1,0:T(8,128)S(1)} %fusion.903), channel_id=1, source_target_pairs={{0,96},{32,128},{64,160},{96,192},{128,224},{160,0},{192,32},{224,... | collective-permute-start | bytes 393224 | tf_op jit(solution)/shard_map/ppermute | solution.py:63
  272.4 1.9 subtract_bitcast_fusion
  274.8 2.6 collective-permute-done.20
  (382 shorter events, 83.2 us)
Async XLA Ops:
  3.1 21.1 %collective-permute-start = (f32[11,128,128]{2,1,0:T(8,128)S(1)}, f32[11,128,128]{2,1,0:T(8,128)}, u32[]{:S(2)}, u32[]{:S(2)}) collective-permute-start(f32[11,128,128]{2,1,0:T(8,128)S(1)} %pad_maximum_fusion.5), channel_id=1, source_target_pairs={{0,1},{1,2},{2,3},{3,4},{4,5},{5,6},{6,7},{7,8},{8,9},{9,10},{10,1... | collective-permute-start | bytes 2162696 | tf_op jit(solution)/shard_map/ppermute | solution.py:51
  7.2 19.0 %collective-permute-start.1 = (f32[11,128,128]{2,1,0:T(8,128)}, f32[11,128,128]{2,1,0:T(8,128)S(1)}, u32[]{:S(2)}, u32[]{:S(2)}) collective-permute-start(f32[11,128,128]{2,1,0:T(8,128)} %pad_maximum_fusion.6), channel_id=1, source_target_pairs={{1,0},{2,1},{3,2},{4,3},{5,4},{6,5},{7,6},{8,7},{9,8},{10,9},{11,1... | collective-permute-start | bytes 2162696 | tf_op jit(solution)/shard_map/ppermute | solution.py:51
  11.9 48.7 %copy-start.92 = (pred[10]{0:T(512)(128)(4,1)}, pred[10]{0:T(512)(128)(4,1)S(1)}, u32[]{:S(2)}) copy-start(pred[10]{0:T(512)(128)(4,1)S(1)} %compare_and_fusion.10) | copy-start | bytes 34
  11.9 25.9 %copy-start.15 = (f32[4,64,128]{2,1,0:T(8,128)}, f32[4,64,128]{2,1,0:T(8,128)S(1)}, u32[]{:S(2)}) copy-start(f32[4,64,128]{2,1,0:T(8,128)S(1)} %broadcast_multiply_fusion.1) | copy-start | bytes 393220
  38.8 14.0 %collective-permute-start.2 = (f32[6,128,128]{2,1,0:T(8,128)}, f32[6,128,128]{2,1,0:T(8,128)}, u32[]{:S(2)}, u32[]{:S(2)}) collective-permute-start(f32[6,128,128]{2,1,0:T(8,128)} %get-tuple-element.75), channel_id=1, source_target_pairs={{0,1},{1,2},{2,3},{3,4},{4,5},{5,6},{6,7},{7,8},{8,9},{9,10},{10,1... | collective-permute-start | bytes 1179656 | tf_op jit(solution)/shard_map/ppermute | solution.py:51
  41.8 11.9 %collective-permute-start.3 = (f32[6,128,128]{2,1,0:T(8,128)}, f32[6,128,128]{2,1,0:T(8,128)}, u32[]{:S(2)}, u32[]{:S(2)}) collective-permute-start(f32[6,128,128]{2,1,0:T(8,128)} %get-tuple-element.76), channel_id=1, source_target_pairs={{1,0},{2,1},{3,2},{4,3},{5,4},{6,5},{7,6},{8,7},{9,8},{10,9},{11,1... | collective-permute-start | bytes 1179656 | tf_op jit(solution)/shard_map/ppermute | solution.py:51
  67.0 11.4 %collective-permute-start.6 = (f32[4,128,128]{2,1,0:T(8,128)}, f32[4,128,128]{2,1,0:T(8,128)}, u32[]{:S(2)}, u32[]{:S(2)}) collective-permute-start(f32[4,128,128]{2,1,0:T(8,128)} %get-tuple-element.55), channel_id=1, source_target_pairs={{0,1},{1,2},{2,3},{3,4},{4,5},{5,6},{6,7},{7,8},{8,9},{9,10},{10,1... | collective-permute-start | bytes 786440 | tf_op jit(solution)/shard_map/ppermute | solution.py:51
  70.9 7.8 %collective-permute-start.7 = (f32[4,128,128]{2,1,0:T(8,128)}, f32[4,128,128]{2,1,0:T(8,128)}, u32[]{:S(2)}, u32[]{:S(2)}) collective-permute-start(f32[4,128,128]{2,1,0:T(8,128)} %get-tuple-element.56), channel_id=1, source_target_pairs={{1,0},{2,1},{3,2},{4,3},{5,4},{6,5},{7,6},{8,7},{9,8},{10,9},{11,1... | collective-permute-start | bytes 786440 | tf_op jit(solution)/shard_map/ppermute | solution.py:51
  91.4 20.5 %copy-start.80 = (f32[4,64,128]{2,1,0:T(8,128)}, f32[4,64,128]{2,1,0:T(8,128)S(1)}, u32[]{:S(2)}) copy-start(f32[4,64,128]{2,1,0:T(8,128)S(1)} %get-tuple-element.29) | copy-start | bytes 393220
  91.4 33.5 %copy-start.56 = (f32[4,64,128]{2,1,0:T(8,128)}, f32[4,64,128]{2,1,0:T(8,128)S(1)}, u32[]{:S(2)}) copy-start(f32[4,64,128]{2,1,0:T(8,128)S(1)} %get-tuple-element.30) | copy-start | bytes 393220
  91.4 8.3 %collective-permute-start.8 = (f32[4,64,128]{2,1,0:T(8,128)S(1)}, f32[4,64,128]{2,1,0:T(8,128)S(1)}, u32[]{:S(2)}, u32[]{:S(2)}) collective-permute-start(f32[4,64,128]{2,1,0:T(8,128)S(1)} %get-tuple-element.29), channel_id=1, source_target_pairs={{0,1},{1,2},{2,3},{3,4},{4,5},{5,6},{6,7},{7,8},{8,9},{9,10},{10,1... | collective-permute-start | bytes 393224 | tf_op jit(solution)/shard_map/ppermute | solution.py:51
  95.1 6.1 %collective-permute-start.9 = (f32[4,64,128]{2,1,0:T(8,128)S(1)}, f32[4,64,128]{2,1,0:T(8,128)S(1)}, u32[]{:S(2)}, u32[]{:S(2)}) collective-permute-start(f32[4,64,128]{2,1,0:T(8,128)S(1)} %get-tuple-element.29), channel_id=1, source_target_pairs={{1,0},{2,1},{3,2},{4,3},{5,4},{6,5},{7,6},{8,7},{9,8},{10,9},{11,1... | collective-permute-start | bytes 393224 | tf_op jit(solution)/shard_map/ppermute | solution.py:51
  101.3 13.1 %collective-permute-start.10 = (f32[10,64,128]{2,1,0:T(8,128)S(1)}, f32[10,64,128]{2,1,0:T(8,128)S(1)}, u32[]{:S(2)}, u32[]{:S(2)}) collective-permute-start(f32[10,64,128]{2,1,0:T(8,128)S(1)} %slice.2095), channel_id=1, source_target_pairs={{0,96},{32,128},{64,160},{96,192},{128,224},{160,0},{192,32},{224,... | collective-permute-start | bytes 983048 | tf_op jit(solution)/shard_map/ppermute | solution.py:63
  109.9 12.2 %collective-permute-start.11 = (f32[8,64,128]{2,1,0:T(8,128)S(1)}, f32[8,64,128]{2,1,0:T(8,128)S(1)}, u32[]{:S(2)}, u32[]{:S(2)}) collective-permute-start(f32[8,64,128]{2,1,0:T(8,128)S(1)} %slice.2102), channel_id=1, source_target_pairs={{0,64},{32,96},{64,128},{96,160},{128,192},{160,224},{192,0},{224,... | collective-permute-start | bytes 786440 | tf_op jit(solution)/shard_map/ppermute | solution.py:63
  111.9 11.6 %collective-permute-start.12 = (f32[6,64,128]{2,1,0:T(8,128)S(1)}, f32[6,64,128]{2,1,0:T(8,128)S(1)}, u32[]{:S(2)}, u32[]{:S(2)}) collective-permute-start(f32[6,64,128]{2,1,0:T(8,128)S(1)} %slice.2107), channel_id=1, source_target_pairs={{0,32},{32,64},{64,96},{96,128},{128,160},{160,192},{192,224},{224... | collective-permute-start | bytes 589832 | tf_op jit(solution)/shard_map/ppermute | solution.py:63
  126.5 17.1 %collective-permute-start.13 = (f32[2,4,64,128]{3,2,1,0:T(8,128)S(1)}, f32[2,4,64,128]{3,2,1,0:T(8,128)}, u32[]{:S(2)}, u32[]{:S(2)}) collective-permute-start(f32[2,4,64,128]{3,2,1,0:T(8,128)S(1)} %pad_maximum_fusion.15), channel_id=1, source_target_pairs={{0,129},{1,130},{2,131},{3,132},{4,133},{5,134},{6,135},{7,136},{8... | collective-permute-start | bytes 786440 | tf_op jit(solution)/shard_map/ppermute | solution.py:51
  132.3 17.5 %collective-permute-start.14 = (f32[2,4,64,128]{3,2,1,0:T(8,128)S(1)}, f32[2,4,64,128]{3,2,1,0:T(8,128)}, u32[]{:S(2)}, u32[]{:S(2)}) collective-permute-start(f32[2,4,64,128]{3,2,1,0:T(8,128)S(1)} %pad_maximum_fusion.15), channel_id=1, source_target_pairs={{0,128},{1,129},{2,130},{3,131},{4,132},{5,133},{6,134},{7,135},{8... | collective-permute-start | bytes 786440 | tf_op jit(solution)/shard_map/ppermute | solution.py:51
  134.9 16.3 %collective-permute-start.15 = (f32[2,4,64,128]{3,2,1,0:T(8,128)S(1)}, f32[2,4,64,128]{3,2,1,0:T(8,128)}, u32[]{:S(2)}, u32[]{:S(2)}) collective-permute-start(f32[2,4,64,128]{3,2,1,0:T(8,128)S(1)} %pad_maximum_fusion.15), channel_id=1, source_target_pairs={{1,128},{2,129},{3,130},{4,131},{5,132},{6,133},{7,134},{8,135},{9... | collective-permute-start | bytes 786440 | tf_op jit(solution)/shard_map/ppermute | solution.py:51
  141.1 24.4 %collective-permute-start.4 = (f32[8,128,128]{2,1,0:T(8,128)}, f32[8,128,128]{2,1,0:T(8,128)}, u32[]{:S(2)}, u32[]{:S(2)}) collective-permute-start(f32[8,128,128]{2,1,0:T(8,128)} %get-tuple-element.37), channel_id=1, source_target_pairs={{0,64},{32,96},{64,128},{96,160},{128,192},{160,224},{192,0},{224,... | collective-permute-start | bytes 1572872 | tf_op jit(solution)/shard_map/ppermute | solution.py:63
  160.4 14.2 %collective-permute-start.16 = (f32[4,128,128]{2,1,0:T(8,128)}, f32[4,128,128]{2,1,0:T(8,128)}, u32[]{:S(2)}, u32[]{:S(2)}) collective-permute-start(f32[4,128,128]{2,1,0:T(8,128)} %pad_maximum_fusion.16), channel_id=1, source_target_pairs={{0,2},{1,3},{2,4},{3,5},{4,6},{5,7},{6,8},{7,9},{8,10},{9,11},{10,... | collective-permute-start | bytes 786440 | tf_op jit(solution)/shard_map/ppermute | solution.py:51
  164.7 31.0 %collective-permute-start.26 = (f32[8,128,128]{2,1,0:T(8,128)}, f32[8,128,128]{2,1,0:T(8,128)S(1)}, u32[]{:S(2)}, u32[]{:S(2)}) collective-permute-start(f32[8,128,128]{2,1,0:T(8,128)} %copy-done.50), channel_id=1, source_target_pairs={{160,416},{192,448},{224,480},{416,160},{448,192},{480,224},{161,4... | collective-permute-start | bytes 1572872 | tf_op jit(solution)/shard_map/ppermute | solution.py:63
  165.5 106.9 %collective-permute-start.5 = (f32[8,128,128]{2,1,0:T(8,128)}, f32[8,128,128]{2,1,0:T(8,128)S(1)}, u32[]{:S(2)}, u32[]{:S(2)}) collective-permute-start(f32[8,128,128]{2,1,0:T(8,128)} %collective-permute-done.4), channel_id=1, source_target_pairs={{0,256},{32,288},{256,0},{288,32},{1,257},{33,289},{257,1},{289,33... | collective-permute-start | bytes 1572872 | tf_op jit(solution)/shard_map/ppermute | solution.py:63
  166.2 12.6 %collective-permute-start.17 = (f32[4,64,128]{2,1,0:T(8,128)}, f32[4,64,128]{2,1,0:T(8,128)S(1)}, u32[]{:S(2)}, u32[]{:S(2)}) collective-permute-start(f32[4,64,128]{2,1,0:T(8,128)} %copy-done.86), channel_id=1, source_target_pairs={{0,1},{1,2},{2,3},{3,4},{4,5},{5,6},{6,7},{7,8},{8,9},{9,10},{10,1... | collective-permute-start | bytes 393224 | tf_op jit(solution)/shard_map/ppermute | solution.py:51
  168.2 10.7 %collective-permute-start.18 = (f32[4,64,128]{2,1,0:T(8,128)}, f32[4,64,128]{2,1,0:T(8,128)S(1)}, u32[]{:S(2)}, u32[]{:S(2)}) collective-permute-start(f32[4,64,128]{2,1,0:T(8,128)} %copy-done.86), channel_id=1, source_target_pairs={{1,0},{2,1},{3,2},{4,3},{5,4},{6,5},{7,6},{8,7},{9,8},{10,9},{11,1... | collective-permute-start | bytes 393224 | tf_op jit(solution)/shard_map/ppermute | solution.py:51
  174.6 10.0 %collective-permute-start.19 = (f32[4,128,128]{2,1,0:T(8,128)}, f32[4,128,128]{2,1,0:T(8,128)S(1)}, u32[]{:S(2)}, u32[]{:S(2)}) collective-permute-start(f32[4,128,128]{2,1,0:T(8,128)} %pad_maximum_fusion.16), channel_id=1, source_target_pairs={{2,0},{3,1},{4,2},{5,3},{6,4},{7,5},{8,6},{9,7},{10,8},{11,9},{12,... | collective-permute-start | bytes 786440 | tf_op jit(solution)/shard_map/ppermute | solution.py:51
  194.3 52.5 %collective-permute-start.21 = (f32[4,64,128]{2,1,0:T(8,128)S(1)}, f32[4,64,128]{2,1,0:T(8,128)S(1)}, u32[]{:S(2)}, u32[]{:S(2)}) collective-permute-start(f32[4,64,128]{2,1,0:T(8,128)S(1)} %get-tuple-element.5), channel_id=1, source_target_pairs={{256,258},{257,259},{258,260},{259,261},{260,262},{261,263},{262,2... | collective-permute-start | bytes 393224 | tf_op jit(solution)/shard_map/ppermute | solution.py:51
  195.0 52.5 %collective-permute-start.22 = (f32[4,64,128]{2,1,0:T(8,128)S(1)}, f32[4,64,128]{2,1,0:T(8,128)S(1)}, u32[]{:S(2)}, u32[]{:S(2)}) collective-permute-start(f32[4,64,128]{2,1,0:T(8,128)S(1)} %get-tuple-element.5), channel_id=1, source_target_pairs={{256,257},{257,258},{258,259},{259,260},{260,261},{261,262},{262,2... | collective-permute-start | bytes 393224 | tf_op jit(solution)/shard_map/ppermute | solution.py:51
  195.8 76.7 %collective-permute-start.27 = (f32[8,128,128]{2,1,0:T(8,128)S(1)}, f32[8,128,128]{2,1,0:T(8,128)S(1)}, u32[]{:S(2)}, u32[]{:S(2)}) collective-permute-start(f32[8,128,128]{2,1,0:T(8,128)S(1)} %broadcast_select_fusion), channel_id=1, source_target_pairs={{0,96},{32,128},{64,160},{96,192},{128,224},{160,0},{192,32},{224,... | collective-permute-start | bytes 1572872 | tf_op jit(solution)/shard_map/ppermute | solution.py:63
  246.2 13.1 %collective-permute-start.23 = (f32[4,64,128]{2,1,0:T(8,128)S(1)}, f32[4,64,128]{2,1,0:T(8,128)S(1)}, u32[]{:S(2)}, u32[]{:S(2)}) collective-permute-start(f32[4,64,128]{2,1,0:T(8,128)S(1)} %get-tuple-element.5), channel_id=1, source_target_pairs={{257,256},{258,257},{259,258},{260,259},{261,260},{262,261},{263,2... | collective-permute-start | bytes 393224 | tf_op jit(solution)/shard_map/ppermute | solution.py:51
  246.9 12.4 %collective-permute-start.24 = (f32[4,64,128]{2,1,0:T(8,128)S(1)}, f32[4,64,128]{2,1,0:T(8,128)S(1)}, u32[]{:S(2)}, u32[]{:S(2)}) collective-permute-start(f32[4,64,128]{2,1,0:T(8,128)S(1)} %get-tuple-element.5), channel_id=1, source_target_pairs={{258,256},{259,257},{260,258},{261,259},{262,260},{263,261},{264,2... | collective-permute-start | bytes 393224 | tf_op jit(solution)/shard_map/ppermute | solution.py:51
  247.6 29.8 %collective-permute-start.20 = (f32[4,64,128]{2,1,0:T(8,128)}, f32[4,64,128]{2,1,0:T(8,128)S(1)}, u32[]{:S(2)}, u32[]{:S(2)}) collective-permute-start(f32[4,64,128]{2,1,0:T(8,128)} %get-tuple-element.4), channel_id=1, source_target_pairs={{0,352},{32,384},{64,416},{96,448},{128,480},{160,256},{192,288},{... | collective-permute-start | bytes 393224 | tf_op jit(solution)/shard_map/ppermute | solution.py:63
  263.6 13.7 %collective-permute-start.25 = (f32[4,64,128]{2,1,0:T(8,128)S(1)}, f32[4,64,128]{2,1,0:T(8,128)S(1)}, u32[]{:S(2)}, u32[]{:S(2)}) collective-permute-start(f32[4,64,128]{2,1,0:T(8,128)S(1)} %fusion.903), channel_id=1, source_target_pairs={{0,96},{32,128},{64,160},{96,192},{128,224},{160,0},{192,32},{224,... | collective-permute-start | bytes 393224 | tf_op jit(solution)/shard_map/ppermute | solution.py:63
  (96 other events, 201.7 us)

commit v3 on v2

v3 whole, which is shorter than its diff:
```python
import functools

import jax
import jax.numpy as jnp
from jax import lax
from jax.experimental import pallas as pl
from jax.experimental.pallas import tpu as pltpu
from jax.sharding import PartitionSpec as P

STEPS = 4
ALONG_FIRST = 0.1
ALONG_SECOND = 0.1
ALONG_THIRD = 0.0125
GROUP = 8
PAD = 8


def lane_mask(shape, *lanes):
    lane = lax.broadcasted_iota(jnp.int32, shape, 1)
    hit = lane == lanes[0]
    for other in lanes[1:]:
        hit = hit | (lane == other)
    return hit


def clear_edges(field):
    rows, wide, depth = field.shape
    zero = jnp.zeros((rows, PAD, depth), jnp.float32)
    field[:, :PAD] = zero
    field[:, wide - PAD :] = zero


def face_weights(kappa, weights, third):
    by_first, by_second, by_third, keep = weights
    rows, wide, depth = kappa.shape
    width = wide - 2 * PAD
    chunk = min(16, width)
    first_w, third_w = 0.5 * ALONG_FIRST, 0.5 * third
    for y in range(PAD, PAD + width, chunk):
        before = kappa[0, y : y + chunk]
        for row in range(rows):
            k = kappa[row, y : y + chunk]
            if row:
                by_first[row, y - PAD : y - PAD + chunk] = first_w * (before + k)
            beside = kappa[row, y - 1 : y - 1 + chunk]
            by_second[row, y : y + chunk] = first_w * (beside + k)
            deeper = pltpu.roll(k, depth - 1, 1)
            by_third[row, y - PAD : y - PAD + chunk] = jnp.where(
                lane_mask(k.shape, depth - 1), 0.0, third_w * (k + deeper)
            )
            keep[row, y - PAD : y - PAD + chunk] = jnp.where(
                lane_mask(k.shape, 0, depth - 1), 1.0 - third_w * k, 1.0
            )
            before = k
    for row in range(rows):
        edge = kappa[row, PAD + width - 1 : 2 * PAD + width - 1]
        by_second[row, PAD + width :] = first_w * edge


def sweep(src, dst, weights, heat, first, count, shift, inside, out=None):
    by_first, by_second, by_third, keep = weights
    wide, depth = src.shape[1:]
    width = wide - 2 * PAD
    chunk = min(16, width)
    for y in range(0, width, chunk):
        here = slice(y + PAD, y + PAD + chunk)
        flat = slice(y, y + chunk)
        v = src[first, here]
        flux = by_first[first + shift, flat] * (v - src[first - 1, here])
        for row in range(first, first + count):
            w = row + shift
            ahead = src[row + 1, here]
            flux_ahead = by_first[w + 1, flat] * (ahead - v)
            up = src[row, y + PAD + 1 : y + PAD + 1 + chunk]
            down = src[row, y + PAD - 1 : y + PAD - 1 + chunk]
            side = by_second[w, y + PAD + 1 : y + PAD + 1 + chunk] * (up - v)
            side = side - by_second[w, here] * (v - down)
            deep = by_third[w, flat] * (pltpu.roll(v, depth - 1, 1) - v)
            deep = deep - pltpu.roll(deep, 1, 1)
            total = keep[w, flat] * v + ((flux_ahead - flux) + side + deep)
            if heat is not None:
                total = total + heat(row, flat)
            mask = inside(row)
            if mask is not None:
                total = total * mask
            if out is None:
                dst[row, here] = total
            else:
                out(row - first, flat, total)
            v, flux = ahead, flux_ahead


def inside_of(place, slabs, margin, block):
    def inside(row):
        if row < margin:
            need = (margin - row + block - 1) // block
            return jnp.where(place >= need, 1.0, 0.0)
        if row >= margin + block:
            need = (row - margin) // block
            return jnp.where(place + need < slabs, 1.0, 0.0)
        return None

    return inside


def fill(field, pieces):
    width = field.shape[1] - 2 * PAD
    for ref, first, count, row in pieces:
        field[row : row + count, PAD : PAD + width] = ref[first : first + count]


def fine_scratch(rows, width, depth):
    high = rows + 2 * STEPS
    padded = pltpu.VMEM((high, width + 2 * PAD, depth), jnp.float32)
    plain = pltpu.VMEM((high, width, depth), jnp.float32)
    return [padded, padded, padded, plain, padded, plain, plain]


def four_steps(where, slabs, up_1, down_1, kappa, source, scratch, out):
    state, other, kappa_wide = scratch[:3]
    weights = scratch[3:7]
    rows = kappa.shape[0]
    for field in (other, kappa_wide):
        clear_edges(field)
    fill(
        kappa_wide,
        [
            (up_1, STEPS, STEPS, 0),
            (kappa, 0, rows, STEPS),
            (down_1, STEPS, STEPS, STEPS + rows),
        ],
    )
    face_weights(kappa_wide, weights, ALONG_THIRD)

    def heat(row, flat):
        if row < STEPS:
            return up_1[2 * STEPS + row - 1, flat]
        if row < STEPS + rows:
            return source[row - STEPS, flat]
        return down_1[2 * STEPS + row - STEPS - rows, flat]

    inside = inside_of(where[1], slabs, STEPS, rows)
    src, dst = state, other
    for step in range(1, STEPS + 1):
        count = rows + 2 * (STEPS - step)
        sweep(
            src, dst, weights, heat, step, count, 0, inside, out if step == STEPS else None
        )
        src, dst = dst, src


def phase_one_kernel(
    slabs, where, up_1, down_1, guess, initial, kappa, source, kappa_c,
    state_out, first_out, last_out, *scratch,
):
    state = scratch[0]
    rows = kappa.shape[0]
    clear_edges(state)
    fill(state, [(up_1, 0, STEPS, 0), (down_1, 0, STEPS, STEPS + rows)])

    @pl.when(where[0] == 15)
    def _():
        fill(state, [(initial, 0, rows, STEPS)])

    @pl.when(where[0] != 15)
    def _():
        fill(state, [(guess, 0, rows, STEPS)])

    def out(row, flat, value):
        state_out[row, flat] = value

    four_steps(where, slabs, up_1, down_1, kappa, source, scratch, out)

    @pl.when(where[0] == 14)
    def _():
        state_out[...] = initial[...]

    first_out[:STEPS] = state_out[:STEPS]
    last_out[:STEPS] = state_out[rows - STEPS :]
    half = kappa_c.shape[1]
    for row in range(rows // 2):
        at = (STEPS + row // 2, slice(row % 2 * half, (row % 2 + 1) * half))
        first_out[at] = kappa_c[row]
        last_out[at] = kappa_c[row]


def phase_two_kernel(
    slabs, where, up_1, down_1, up_2, down_2, before, initial, kappa, source,
    second_out, first_out, last_out, *scratch,
):
    state = scratch[0]
    rows = kappa.shape[0]
    clear_edges(state)
    fill(
        state,
        [
            (up_2, 0, STEPS, 0),
            (before, 0, rows, STEPS),
            (down_2, 0, STEPS, STEPS + rows),
        ],
    )

    def out(row, flat, value):
        second_out[row, flat] = value

    four_steps(where, slabs, up_1, down_1, kappa, source, scratch, out)

    @pl.when(where[0] == 13)
    def _():
        first_out[...] = initial[:STEPS]
        last_out[...] = initial[rows - STEPS :]

    @pl.when(where[0] != 13)
    def _():
        first_out[...] = second_out[:STEPS]
        last_out[...] = second_out[rows - STEPS :]


def coarse_kappa_4(field, up_2, down_2, kappa_c, at):
    block, half = kappa_c.shape[:2]
    clear_edges(field)
    fill(field, [(kappa_c, 0, block, at + block)])
    for row in range(block):
        piece = (STEPS + row // 2, slice(row % 2 * half, (row % 2 + 1) * half))
        field[at + row, PAD : PAD + half] = up_2[piece]
        field[at + 2 * block + row, PAD : PAD + half] = down_2[piece]


def coarse_scratch(rows, width, depth, fields):
    padded = pltpu.VMEM((rows, width + 2 * PAD, depth), jnp.float32)
    plain = pltpu.VMEM((rows, width, depth), jnp.float32)
    return [padded] * fields + [padded, plain, padded, plain, plain]


def phase_three_kernel(
    slabs, where, up_1, down_1, up_2, down_2, up_3, down_3, second, initial, kappa,
    source, kappa_c, third_out, tau_out, *scratch,
):
    state, other = scratch[:2]
    base, spare, kappa_wide, *weights = scratch[7:14]
    pair = scratch[14]
    rows, width = kappa.shape[:2]
    block, half = kappa_c.shape[:2]
    clear_edges(state)
    fill(state, [(up_3, 0, STEPS, 0), (down_3, 0, STEPS, STEPS + rows)])

    @pl.when(where[0] == 13)
    def _():
        fill(state, [(initial, 0, rows, STEPS)])

    @pl.when(where[0] != 13)
    def _():
        fill(state, [(second, 0, rows, STEPS)])

    clear_edges(base)
    for row in range(block + 2):
        fine_row = STEPS - 2 + 2 * row
        pair[...] = (
            state[fine_row, PAD : PAD + width] + state[fine_row + 1, PAD : PAD + width]
        )
        base[row, PAD : PAD + half] = 0.25 * (
            pair[pl.ds(0, half, stride=2), :] + pair[pl.ds(1, half, stride=2), :]
        )

    def out(row, flat, value):
        third_out[row, flat] = value

    four_steps(where, slabs, up_1, down_1, kappa, source, scratch, out)

    coarse_kappa_4(kappa_wide, up_2, down_2, kappa_c, 0)
    face_weights(kappa_wide, weights, 4.0 * ALONG_THIRD)

    def keep(row, flat, value):
        tau_out[row, flat] = value

    sweep(base, spare, weights, None, 1, block, block - 1, lambda row: None, keep)
    use = jnp.where(where[0] == 13, 0.0, 1.0)
    for row in range(block):
        pair[...] = third_out[2 * row] + third_out[2 * row + 1]
        now = 0.25 * (
            pair[pl.ds(0, half, stride=2), :] + pair[pl.ds(1, half, stride=2), :]
        )
        tau_out[row] = now - use * tau_out[row]


def near_sums_kernel(
    slabs, where, got_3, got_2, got_1, tau, up_2, down_2, kappa_c, both_out, *scratch
):
    ahead, wrapped, spare, kappa_wide, *weights = scratch
    block, half = kappa_c.shape[:2]
    local = lax.rem(where[0], GROUP)
    high = where[0] >= GROUP
    for field in (ahead, wrapped, spare):
        clear_edges(field)
    coarse_kappa_4(kappa_wide, up_2, down_2, kappa_c, 0)
    face_weights(kappa_wide, weights, 4.0 * ALONG_THIRD)
    inside = inside_of(where[1], slabs, block, block)
    for is_ahead in (True, False):
        src, dst = (ahead, spare) if is_ahead else (wrapped, spare)
        for distance, got in ((3, got_3), (2, got_2), (1, got_1)):
            apart = high & (local >= 5) & (local < distance + 5)
            use = (local >= distance) & ~apart if is_ahead else local < distance
            use = jnp.where(use, 1.0, 0.0)
            for row in range(block + 2 * distance):
                at = (row + block - distance, slice(PAD, PAD + half))
                value = use * got[row]
                src[at] = value if distance == 3 else src[at] + value
            if distance == 1:

                def out(row, flat, value, is_ahead=is_ahead):
                    if is_ahead:
                        both_out[0, row, flat] = value + tau[row, flat]
                    else:
                        both_out[1, row, flat] = value

            else:
                out = None
            sweep(
                src, dst, weights, None, block - distance + 1, block + 2 * distance - 2,
                0, inside, out,
            )
            src, dst = dst, src


def far_sums_kernel(
    slabs, where, got_up, got, got_down, both, up_2, down_2, kappa_c,
    ahead_out, wrapped_out, last_out, *scratch,
):
    field, spare, kappa_wide, *weights = scratch
    block, half = kappa_c.shape[:2]
    local = lax.rem(where[0], GROUP)
    high = where[0] >= GROUP
    clear_edges(field)
    clear_edges(spare)
    coarse_kappa_4(kappa_wide, up_2, down_2, kappa_c, 0)
    face_weights(kappa_wide, weights, 4.0 * ALONG_THIRD)
    inside = inside_of(where[1], slabs, block, block)
    late = local >= 4
    to_ahead = jnp.where(late & ~(high & (local >= 5)), 1.0, 0.0)
    from_wrapped = jnp.where(late, 1.0, 0.0)
    from_ahead = jnp.where(late | (high & (local == 0)), 0.0, 1.0)
    for index, result in ((0, ahead_out), (1, wrapped_out)):
        for piece, ref in enumerate((got_up, got, got_down)):
            for row in range(block):
                at = (piece * block + row, slice(PAD, PAD + half))
                if index == 0:
                    field[at] = to_ahead * ref[0, row]
                else:
                    field[at] = from_wrapped * ref[1, row] + from_ahead * ref[0, row]

        def out(row, flat, value, index=index, result=result):
            result[row, flat] = value + both[index, row, flat]

        src, dst = field, spare
        for step in range(1, block + 1):
            count = 3 * block - 2 * step
            sweep(
                src, dst, weights, None, step, count, 0, inside,
                out if step == block else None,
            )
            src, dst = dst, src
    hand_wrapped = high & (local < 5)

    @pl.when(hand_wrapped)
    def _():
        last_out[...] = wrapped_out[...]

    @pl.when(jnp.logical_not(hand_wrapped))
    def _():
        last_out[...] = ahead_out[...]


def hand_over_kernel(
    slabs, where, far_up, near_up, last, near_down, far_down, up_2, down_2, kappa_c,
    ahead, wrapped, handed_out, kept_out, *scratch,
):
    field, spare, kappa_wide, *weights = scratch
    block, half = kappa_c.shape[:2]
    local = lax.rem(where[0], GROUP)
    high = where[0] >= GROUP
    clear_edges(field)
    clear_edges(spare)
    coarse_kappa_4(kappa_wide, up_2, down_2, kappa_c, block)
    inner = slice(PAD, PAD + half)
    for row in range(block):
        kappa_wide[row, inner] = far_up[row, half:]
        kappa_wide[4 * block + row, inner] = far_down[row, half:]
        field[row, inner] = far_up[row, :half]
        field[4 * block + row, inner] = far_down[row, :half]
    fill(
        field,
        [
            (near_up, 0, block, block),
            (last, 0, block, 2 * block),
            (near_down, 0, block, 3 * block),
        ],
    )
    face_weights(kappa_wide, weights, 4.0 * ALONG_THIRD)
    inside = inside_of(where[1], slabs, 2 * block, block)
    early = local < 5

    def one(use):
        return jnp.where(use, 1.0, 0.0)

    hand_image = one(early & ~high)
    hand_wrapped = one(early)
    hand_ahead = one(~early)
    keep_image = one(high)
    keep_wrapped = one(high & ~early)
    keep_ahead = one(early)

    def out(row, flat, value):
        a, w = ahead[row, flat], wrapped[row, flat]
        handed_out[row, flat] = hand_image * value + hand_wrapped * w + hand_ahead * a
        kept_out[row, flat] = keep_image * value + keep_wrapped * w + keep_ahead * a

    src, dst = field, spare
    for step in range(1, 2 * block + 1):
        count = 5 * block - 2 * step
        sweep(
            src, dst, weights, None, step, count, 0, inside,
            out if step == 2 * block else None,
        )
        src, dst = dst, src


def call(kernel, slabs, outs, scratch, where, *args):
    vmem = pl.BlockSpec(memory_space=pltpu.VMEM)
    return pl.pallas_call(
        functools.partial(kernel, slabs),
        out_shape=[jax.ShapeDtypeStruct(shape, jnp.float32) for shape in outs],
        in_specs=[pl.BlockSpec(memory_space=pltpu.SMEM)] + [vmem] * len(args),
        out_specs=[vmem] * len(outs),
        scratch_shapes=scratch,
        compiler_params=pltpu.CompilerParams(vmem_limit_bytes=40 * 2**20),
        cost_estimate=pl.CostEstimate(flops=0, bytes_accessed=0, transcendentals=0),
    )(where, *args)


def per_device(initial, guess, conductivity, source):
    rows, width_two, width_three = conductivity.shape
    crows, half = rows // 2, width_two // 2
    slabs = lax.axis_size("space")
    tm = lax.axis_index("tm")
    sp = lax.axis_index("space")
    local = tm % GROUP
    where = jnp.stack([tm, sp]).astype(jnp.int32)

    def cut(array, have, want):
        return array[have - want : array.shape[0] - (have - want)]

    def route(block, pairs):
        return lax.ppermute(block, ("tm", "space"), pairs)

    def along_space(block, distance):
        pairs = [
            (i, i + distance) for i in range(slabs) if 0 <= i + distance < slabs
        ]
        return lax.ppermute(block, "space", pairs)

    def along_time(block, pairs):
        return lax.ppermute(block, "tm", pairs)

    def ring(shift):
        return [
            (g * GROUP + i, g * GROUP + (i + shift) % GROUP)
            for g in (0, 1)
            for i in range(GROUP)
        ]

    def restrict(field):
        return field.reshape(-1, 2, half, 2, width_three).mean(axis=(1, 3))

    def neighbours(block_first, block_last):
        return along_space(block_last, 1), along_space(block_first, -1)

    block_shape = (rows, width_two, width_three)
    coarse_shape = (crows, half, width_three)
    edge_shape = (STEPS, width_two, width_three)
    packed_shape = (STEPS + crows // 2, width_two, width_three)
    scratch = fine_scratch(rows, width_two, width_three)

    kappa_c = restrict(conductivity)
    ends = [
        jnp.where(tm == 15, initial[part], guess[0][part])
        for part in (slice(0, STEPS), slice(rows - STEPS, rows))
    ]
    sides = neighbours(
        jnp.concatenate([ends[0], conductivity[:STEPS], source[: STEPS - 1]]),
        jnp.concatenate([ends[1], conductivity[-STEPS:], source[1 - STEPS :]]),
    )
    state, first, last = call(
        phase_one_kernel, slabs, [block_shape, packed_shape, packed_shape], scratch,
        where, *sides, guess[0], initial, conductivity, source, kappa_c,
    )
    sides_2 = neighbours(first, last)
    second, first, last = call(
        phase_two_kernel, slabs, [block_shape, edge_shape, edge_shape], scratch,
        where, *sides, *sides_2, state, initial, conductivity, source,
    )
    sides_3 = neighbours(first, last)
    second_near = along_time(second, ring(2))
    third, tau = call(
        phase_three_kernel, slabs, [block_shape, coarse_shape],
        scratch
        + coarse_scratch(3 * crows, half, width_three, 2)
        + [pltpu.VMEM((width_two, width_three), jnp.float32)],
        where, *sides, *sides_2, *sides_3, second, initial, conductivity, source, kappa_c,
    )

    up, down = neighbours(tau, tau)
    second_cross = along_time(second_near, [(0, 8), (1, 9), (8, 0), (9, 1)])
    tau_wide = jnp.concatenate([up, tau, down], 0)
    got = [along_time(cut(tau_wide, crows, d), ring(d)) for d in (3, 2, 1)]
    third_cross = along_time(third, [(i, i ^ 8) for i in (5, 6, 7, 13, 14, 15)])
    (both,) = call(
        near_sums_kernel, slabs, [(2,) + coarse_shape],
        coarse_scratch(3 * crows, half, width_three, 3),
        where, *got, tau, *sides_2, kappa_c,
    )

    def diagonal(distance):
        pairs = [
            (t * slabs + i, u * slabs + i + distance)
            for t, u in ring(4)
            for i in range(slabs)
            if 0 <= i + distance < slabs
        ]
        return route(both, pairs)

    got = [diagonal(1), diagonal(0), diagonal(-1)]
    ahead, wrapped, last = call(
        far_sums_kernel, slabs, [coarse_shape] * 3,
        coarse_scratch(3 * crows, half, width_three, 2),
        where, *got, both, *sides_2, kappa_c,
    )

    near = neighbours(last, last)
    two = jnp.concatenate([last, kappa_c], 1)
    far = (along_space(two, 2), along_space(two, -2))
    handed, kept = call(
        hand_over_kernel, slabs, [coarse_shape] * 2,
        coarse_scratch(5 * crows, half, width_three, 2),
        where, far[0], near[0], last, near[1], far[1], *sides_2, kappa_c, ahead, wrapped,
    )
    handed = along_time(
        handed,
        [
            (g * GROUP + i, (1 - g) * GROUP + (i + 3) % GROUP)
            for g in (0, 1)
            for i in range(GROUP)
        ],
    )
    kept = along_time(kept, ring(3))
    third_home = along_time(jnp.where(local >= 5, third_cross, third), ring(3))
    second_home = jnp.where(local < 2, second_cross, second_near)

    residual = third_home - second_home
    change = handed + kept - restrict(second_home)
    finer = jnp.repeat(jnp.repeat(change, 2, axis=0), 2, axis=1)
    corrected = second_home + finer
    return (corrected[None], residual[None])


def solution(mesh):
    in_specs = (
        P("space", None, None),
        P("tm", "space", None, None),
        P("space", None, None),
        P("space", None, None),
    )
    out_specs = (P("tm", "space", None, None), P("tm", "space", None, None))
    return jax.shard_map(
        per_device, mesh=mesh, in_specs=in_specs, out_specs=out_specs, check_vma=False
    )
```

time: 280 us -> 327 us (1.17)
  the two profiles are of different devices: /device:TPU:35 before, /device:TPU:116 now
where the time goes in v3:
time: 327 us; the launch traced here: 326 us
  Pallas kernels  122 us (37%)
  starting transfers between devices  102 us (31%)
  waiting for transfers between devices  89.2 us (27%)
  other arithmetic  8.08 us (2%)
  local copies, waits for them, and re-layouts  3.92 us (1%)
    pallas_call x6, Pallas kernels, call(): pl.pallas_call(functools.partial(kernel, slabs), out_shape=[jax.ShapeDtyp...  122 us
    ppermute x12, waiting for transfers between devices, along_space(): return lax.ppermute(block, 'space', pairs)  52.8 us
    ppermute x12, starting transfers between devices, along_space(): return lax.ppermute(block, 'space', pairs)  41 us
    ppermute x3, starting transfers between devices, route(): return lax.ppermute(block, ('tm', 'space'), pairs)  37.5 us
    ppermute x9, starting transfers between devices, along_time(): return lax.ppermute(block, 'tm', pairs)  23.5 us
    ppermute x9, waiting for transfers between devices, along_time(): return lax.ppermute(block, 'tm', pairs)  19.3 us
    ppermute x3, waiting for transfers between devices, route(): return lax.ppermute(block, ('tm', 'space'), pairs)  17.2 us
  transfers between devices with their start and end apart: 24, of which 13 were waited for; matrix products, arithmetic and copies ran while one was open for 2% of the time, Pallas kernels for 13%

profile of v3, /device:TPU:116, one launch (start us, length us, event | category | flops | bytes accessed | tf_op | source)
XLA Modules:
  0.0 326.1 jit_solution(7471926168397411416)
XLA Ops:
  4.1 2.3 collective-permute-start.1
  7.4 3.6 %collective-permute-start = (f32[11,128,128]{2,1,0:T(8,128)}, f32[11,128,128]{2,1,0:T(8,128)S(1)}, u32[]{:S(2)}, u32[]{:S(2)}) collective-permute-start(f32[11,128,128]{2,1,0:T(8,128)} %pad_maximum_fusion), channel_id=1, source_target_pairs={{0,1},{1,2},{2,3},{3,4},{4,5},{5,6},{6,7},{7,8},{8,9},{9,10},{10,1... | collective-permute-start | bytes 2162696 | tf_op jit(solution)/shard_map/ppermute | solution.py:459
  11.5 12.6 %collective-permute-done.1.down_1 = f32[11,128,128]{2,1,0:T(8,128)S(1)} collective-permute-done((f32[11,128,128]{2,1,0:T(8,128)}, f32[11,128,128]{2,1,0:T(8,128)S(1)}, u32[]{:S(2)}, u32[]{:S(2)}) %collective-permute-start.1) | collective-permute-done | bytes 720928 | tf_op jit(solution)/shard_map/ppermute | solution.py:459
  24.1 3.1 collective-permute-done.up_1
  28.5 25.1 %shard_map.59 = (f32[8,128,128]{2,1,0:T(8,128)S(1)}, f32[6,128,128]{2,1,0:T(8,128)S(1)}, f32[6,128,128]{2,1,0:T(8,128)S(1)}) custom-call(s32[2]{0:T(128)S(1)} %pad_add_fusion.where, f32[11,128,128]{2,1,0:T(8,128)S(1)} %collective-permute-done.up_1, f32[11,128,128]{2,1,0:T(8,128)S(1)} %collective-permute-done.1.down_1, f32[8,128,128]{2,1,0:T(8,128)S(1)} %bitcast.16, ...), custom_call_target="tpu_custom_call" | custom-call | tf_op jit(solution)/shard_map/pallas_call | solution.py:429
  53.6 5.7 %collective-permute-start.2 = (f32[6,128,128]{2,1,0:T(8,128)S(1)}, f32[6,128,128]{2,1,0:T(8,128)S(1)}, u32[]{:S(2)}, u32[]{:S(2)}) collective-permute-start(f32[6,128,128]{2,1,0:T(8,128)S(1)} %get-tuple-element.15), channel_id=1, source_target_pairs={{0,1},{1,2},{2,3},{3,4},{4,5},{5,6},{6,7},{7,8},{8,9},{9,10},{10,1... | collective-permute-start | bytes 1179656 | tf_op jit(solution)/shard_map/ppermute | solution.py:459
  61.3 5.2 %collective-permute-done.2.up_2 = f32[6,128,128]{2,1,0:T(8,128)S(1)} collective-permute-done((f32[6,128,128]{2,1,0:T(8,128)S(1)}, f32[6,128,128]{2,1,0:T(8,128)S(1)}, u32[]{:S(2)}, u32[]{:S(2)}) %collective-permute-start.2) | collective-permute-done | bytes 393248 | tf_op jit(solution)/shard_map/ppermute | solution.py:459
  66.5 8.1 %collective-permute-done.3.down_2 = f32[6,128,128]{2,1,0:T(8,128)S(1)} collective-permute-done((f32[6,128,128]{2,1,0:T(8,128)S(1)}, f32[6,128,128]{2,1,0:T(8,128)S(1)}, u32[]{:S(2)}, u32[]{:S(2)}) %collective-permute-start.3) | collective-permute-done | bytes 393248 | tf_op jit(solution)/shard_map/ppermute | solution.py:459
  75.7 25.8 %shard_map.60 = (f32[8,128,128]{2,1,0:T(8,128)}, f32[4,128,128]{2,1,0:T(8,128)S(1)}, f32[4,128,128]{2,1,0:T(8,128)S(1)}) custom-call(s32[2]{0:T(128)S(1)} %pad_add_fusion.where, f32[11,128,128]{2,1,0:T(8,128)S(1)} %copy-done.4, f32[11,128,128]{2,1,0:T(8,128)S(1)} %collective-permute-done.1.down_1, f32[6,128,128]{2,1,0:T(8,128)S(1)} %collective-permute-done.2.up_2, ...), custom_call_target="tpu_custom_call" | custom-call | tf_op jit(solution)/shard_map/pallas_call | solution.py:429
  101.5 7.0 %collective-permute-start.6 = (f32[4,128,128]{2,1,0:T(8,128)S(1)}, f32[4,128,128]{2,1,0:T(8,128)S(1)}, u32[]{:S(2)}, u32[]{:S(2)}) collective-permute-start(f32[4,128,128]{2,1,0:T(8,128)S(1)} %get-tuple-element.19), channel_id=1, source_target_pairs={{0,1},{1,2},{2,3},{3,4},{4,5},{5,6},{6,7},{7,8},{8,9},{9,10},{10,1... | collective-permute-start | bytes 786440 | tf_op jit(solution)/shard_map/ppermute | solution.py:459
  110.4 1.9 collective-permute-done.6.up_3
  112.3 4.4 %collective-permute-done.7.down_3 = f32[4,128,128]{2,1,0:T(8,128)S(1)} collective-permute-done((f32[4,128,128]{2,1,0:T(8,128)S(1)}, f32[4,128,128]{2,1,0:T(8,128)S(1)}, u32[]{:S(2)}, u32[]{:S(2)}) %collective-permute-start.7) | collective-permute-done | bytes 262176 | tf_op jit(solution)/shard_map/ppermute | solution.py:459
  116.7 27.8 %shard_map.61 = (f32[8,128,128]{2,1,0:T(8,128)}, f32[4,64,128]{2,1,0:T(8,128)S(1)}) custom-call(s32[2]{0:T(128)S(1)} %pad_add_fusion.where, f32[11,128,128]{2,1,0:T(8,128)S(1)} %copy-done.5, f32[11,128,128]{2,1,0:T(8,128)S(1)} %collective-permute-done.1.down_1, f32[6,128,128]{2,1,0:T(8,128)S(1)} %collective-permute-done.2.up_2, ...), custom_call_target="tpu_custom_call" | custom-call | tf_op jit(solution)/shard_map/pallas_call | solution.py:429
  144.6 5.2 %collective-permute-start.8 = (f32[4,64,128]{2,1,0:T(8,128)S(1)}, f32[4,64,128]{2,1,0:T(8,128)S(1)}, u32[]{:S(2)}, u32[]{:S(2)}) collective-permute-start(f32[4,64,128]{2,1,0:T(8,128)S(1)} %get-tuple-element.21.tau), channel_id=1, source_target_pairs={{0,1},{1,2},{2,3},{3,4},{4,5},{5,6},{6,7},{7,8},{8,9},{9,10},{10,1... | collective-permute-start | bytes 393224 | tf_op jit(solution)/shard_map/ppermute | solution.py:459
  149.8 3.1 collective-permute-start.4
  155.6 4.2 %collective-permute-done.9 = f32[4,64,128]{2,1,0:T(8,128)S(1)} collective-permute-done((f32[4,64,128]{2,1,0:T(8,128)S(1)}, f32[4,64,128]{2,1,0:T(8,128)S(1)}, u32[]{:S(2)}, u32[]{:S(2)}) %collective-permute-start.9) | collective-permute-done | bytes 131104 | tf_op jit(solution)/shard_map/ppermute | solution.py:459
  159.8 5.6 %collective-permute-start.10 = (f32[10,64,128]{2,1,0:T(8,128)S(1)}, f32[10,64,128]{2,1,0:T(8,128)S(1)}, u32[]{:S(2)}, u32[]{:S(2)}) collective-permute-start(f32[10,64,128]{2,1,0:T(8,128)S(1)} %slice.52), channel_id=1, source_target_pairs={{0,96},{32,128},{64,160},{96,192},{128,224},{160,0},{192,32},{224,... | collective-permute-start | bytes 983048 | tf_op jit(solution)/shard_map/ppermute | solution.py:462
  165.5 6.9 %collective-permute-start.11 = (f32[8,64,128]{2,1,0:T(8,128)S(1)}, f32[8,64,128]{2,1,0:T(8,128)S(1)}, u32[]{:S(2)}, u32[]{:S(2)}) collective-permute-start(f32[8,64,128]{2,1,0:T(8,128)S(1)} %slice.53), channel_id=1, source_target_pairs={{0,64},{32,96},{64,128},{96,160},{128,192},{160,224},{192,0},{224,... | collective-permute-start | bytes 786440 | tf_op jit(solution)/shard_map/ppermute | solution.py:462
  173.9 8.2 %collective-permute-done.12.got_1 = f32[6,64,128]{2,1,0:T(8,128)S(1)} collective-permute-done((f32[6,64,128]{2,1,0:T(8,128)S(1)}, f32[6,64,128]{2,1,0:T(8,128)S(1)}, u32[]{:S(2)}, u32[]{:S(2)}) %collective-permute-start.12) | collective-permute-done | bytes 196640 | tf_op jit(solution)/shard_map/ppermute | solution.py:462
  182.1 6.3 %shard_map.62.both = f32[2,4,64,128]{3,2,1,0:T(8,128)S(1)} custom-call(s32[2]{0:T(128)S(1)} %pad_add_fusion.where, f32[10,64,128]{2,1,0:T(8,128)S(1)} %collective-permute-done.10.got_3, f32[8,64,128]{2,1,0:T(8,128)S(1)} %collective-permute-done.11.got_2, f32[6,64,128]{2,1,0:T(8,128)S(1)} %collective-permute-done.12.got_1, ...), custom_call_target="tpu_custom_call" | custom-call | tf_op jit(solution)/shard_map/pallas_call | solution.py:429
  188.4 30.8 %collective-permute-start.13 = (f32[2,4,64,128]{3,2,1,0:T(8,128)S(1)}, f32[2,4,64,128]{3,2,1,0:T(8,128)S(1)}, u32[]{:S(2)}, u32[]{:S(2)}) collective-permute-start(f32[2,4,64,128]{3,2,1,0:T(8,128)S(1)} %shard_map.62.both), channel_id=1, source_target_pairs={{0,129},{1,130},{2,131},{3,132},{4,133},{5,134},{6,135},{7,136},{8... | collective-permute-start | bytes 786440 | tf_op jit(solution)/shard_map/ppermute | solution.py:453
  219.2 4.8 %collective-permute-start.14 = (f32[2,4,64,128]{3,2,1,0:T(8,128)S(1)}, f32[2,4,64,128]{3,2,1,0:T(8,128)S(1)}, u32[]{:S(2)}, u32[]{:S(2)}) collective-permute-start(f32[2,4,64,128]{3,2,1,0:T(8,128)S(1)} %shard_map.62.both), channel_id=1, source_target_pairs={{0,128},{1,129},{2,130},{3,131},{4,132},{5,133},{6,134},{7,135},{8... | collective-permute-start | bytes 786440 | tf_op jit(solution)/shard_map/ppermute | solution.py:453
  229.0 4.4 %collective-permute-done.14.got = f32[2,4,64,128]{3,2,1,0:T(8,128)S(1)} collective-permute-done((f32[2,4,64,128]{3,2,1,0:T(8,128)S(1)}, f32[2,4,64,128]{3,2,1,0:T(8,128)S(1)}, u32[]{:S(2)}, u32[]{:S(2)}) %collective-permute-start.14) | collective-permute-done | bytes 262176 | tf_op jit(solution)/shard_map/ppermute | solution.py:453
  233.4 12.8 %collective-permute-done.15.got_down = f32[2,4,64,128]{3,2,1,0:T(8,128)S(1)} collective-permute-done((f32[2,4,64,128]{3,2,1,0:T(8,128)S(1)}, f32[2,4,64,128]{3,2,1,0:T(8,128)S(1)}, u32[]{:S(2)}, u32[]{:S(2)}) %collective-permute-start.15) | collective-permute-done | bytes 262176 | tf_op jit(solution)/shard_map/ppermute | solution.py:453
  246.1 13.6 %shard_map.63 = (f32[4,64,128]{2,1,0:T(8,128)S(1)}, f32[4,64,128]{2,1,0:T(8,128)S(1)}, f32[4,64,128]{2,1,0:T(8,128)S(1)}) custom-call(s32[2]{0:T(128)S(1)} %pad_add_fusion.where, f32[2,4,64,128]{3,2,1,0:T(8,128)S(1)} %collective-permute-done.13.got_up, f32[2,4,64,128]{3,2,1,0:T(8,128)S(1)} %collective-permute-done.14.got, ...), custom_call_target="tpu_custom_call" | custom-call | tf_op jit(solution)/shard_map/pallas_call | solution.py:429
  263.6 5.4 %collective-permute-start.19 = (f32[4,128,128]{2,1,0:T(8,128)S(1)}, f32[4,128,128]{2,1,0:T(8,128)S(1)}, u32[]{:S(2)}, u32[]{:S(2)}) collective-permute-start(f32[4,128,128]{2,1,0:T(8,128)S(1)} %pad_maximum_fusion.2), channel_id=1, source_target_pairs={{2,0},{3,1},{4,2},{5,3},{6,4},{7,5},{8,6},{9,7},{10,8},{11,9},{12,... | collective-permute-start | bytes 786440 | tf_op jit(solution)/shard_map/ppermute | solution.py:459
  269.0 8.5 %collective-permute-done.17.near_up = f32[4,64,128]{2,1,0:T(8,128)S(1)} collective-permute-done((f32[4,64,128]{2,1,0:T(8,128)S(1)}, f32[4,64,128]{2,1,0:T(8,128)S(1)}, u32[]{:S(2)}, u32[]{:S(2)}) %collective-permute-start.17) | collective-permute-done | bytes 131104 | tf_op jit(solution)/shard_map/ppermute | solution.py:459
  277.5 2.1 collective-permute-start.18
  279.7 4.7 %collective-permute-done.18.near_down = f32[4,64,128]{2,1,0:T(8,128)S(1)} collective-permute-done((f32[4,64,128]{2,1,0:T(8,128)S(1)}, f32[4,64,128]{2,1,0:T(8,128)S(1)}, u32[]{:S(2)}, u32[]{:S(2)}) %collective-permute-start.18) | collective-permute-done | bytes 131104 | tf_op jit(solution)/shard_map/ppermute | solution.py:459
  284.4 23.3 %shard_map.64 = (f32[4,64,128]{2,1,0:T(8,128)S(1)}, f32[4,64,128]{2,1,0:T(8,128)S(1)}) custom-call(s32[2]{0:T(128)S(1)} %pad_add_fusion.where, f32[4,128,128]{2,1,0:T(8,128)S(1)} %collective-permute-done.16.far_up, f32[4,64,128]{2,1,0:T(8,128)S(1)} %collective-permute-done.17.near_up, f32[4,64,128]{2,1,0:T(8,128)S(1)} %get-tuple-element.22.last, ...), custom_call_target="tpu_custom_call" | custom-call | tf_op jit(solution)/shard_map/pallas_call | solution.py:429
  311.5 2.1 subtract_bitcast_fusion
  314.0 11.1 %collective-permute-done.20 = f32[4,64,128]{2,1,0:T(8,128)S(1)} collective-permute-done((f32[4,64,128]{2,1,0:T(8,128)S(1)}, f32[4,64,128]{2,1,0:T(8,128)S(1)}, u32[]{:S(2)}, u32[]{:S(2)}) %collective-permute-start.20) | collective-permute-done | bytes 131104 | tf_op jit(solution)/shard_map/ppermute | solution.py:462
  (57 shorter events, 29.4 us)
Async XLA Ops:
  0.6 1.2 copy-start
  4.1 20.0 %collective-permute-start.1 = (f32[11,128,128]{2,1,0:T(8,128)}, f32[11,128,128]{2,1,0:T(8,128)S(1)}, u32[]{:S(2)}, u32[]{:S(2)}) collective-permute-start(f32[11,128,128]{2,1,0:T(8,128)} %pad_maximum_fusion.1), channel_id=1, source_target_pairs={{1,0},{2,1},{3,2},{4,3},{5,4},{6,5},{7,6},{8,7},{9,8},{10,9},{11,1... | collective-permute-start | bytes 2162696 | tf_op jit(solution)/shard_map/ppermute | solution.py:459
  6.5 20.8 %copy-start.2 = (f32[8,128,128]{2,1,0:T(8,128)S(1)}, f32[8,128,128]{2,1,0:T(8,128)}, u32[]{:S(2)}) copy-start(f32[8,128,128]{2,1,0:T(8,128)} %source.5) | copy-start | bytes 1572868
  7.4 19.8 %copy-start.1 = (f32[8,128,128]{2,1,0:T(8,128)S(1)}, f32[8,128,128]{2,1,0:T(8,128)}, u32[]{:S(2)}) copy-start(f32[8,128,128]{2,1,0:T(8,128)} %initial.5) | copy-start | bytes 1572868
  7.4 19.8 %collective-permute-start = (f32[11,128,128]{2,1,0:T(8,128)}, f32[11,128,128]{2,1,0:T(8,128)S(1)}, u32[]{:S(2)}, u32[]{:S(2)}) collective-permute-start(f32[11,128,128]{2,1,0:T(8,128)} %pad_maximum_fusion), channel_id=1, source_target_pairs={{0,1},{1,2},{2,3},{3,4},{4,5},{5,6},{6,7},{7,8},{8,9},{9,10},{10,1... | collective-permute-start | bytes 2162696 | tf_op jit(solution)/shard_map/ppermute | solution.py:459
  27.2 26.4 %copy-start.3 = (f32[11,128,128]{2,1,0:T(8,128)}, f32[11,128,128]{2,1,0:T(8,128)S(1)}, u32[]{:S(2)}) copy-start(f32[11,128,128]{2,1,0:T(8,128)S(1)} %collective-permute-done.up_1) | copy-start | bytes 2162692
  27.2 1.3 copy-start.6
  53.6 12.9 %collective-permute-start.2 = (f32[6,128,128]{2,1,0:T(8,128)S(1)}, f32[6,128,128]{2,1,0:T(8,128)S(1)}, u32[]{:S(2)}, u32[]{:S(2)}) collective-permute-start(f32[6,128,128]{2,1,0:T(8,128)S(1)} %get-tuple-element.15), channel_id=1, source_target_pairs={{0,1},{1,2},{2,3},{3,4},{4,5},{5,6},{6,7},{7,8},{8,9},{9,10},{10,1... | collective-permute-start | bytes 1179656 | tf_op jit(solution)/shard_map/ppermute | solution.py:459
  59.3 15.2 %collective-permute-start.3 = (f32[6,128,128]{2,1,0:T(8,128)S(1)}, f32[6,128,128]{2,1,0:T(8,128)S(1)}, u32[]{:S(2)}, u32[]{:S(2)}) collective-permute-start(f32[6,128,128]{2,1,0:T(8,128)S(1)} %get-tuple-element.16), channel_id=1, source_target_pairs={{1,0},{2,1},{3,2},{4,3},{5,4},{6,5},{7,6},{8,7},{9,8},{10,9},{11,1... | collective-permute-start | bytes 1179656 | tf_op jit(solution)/shard_map/ppermute | solution.py:459
  74.6 1.1 copy-start.4
  75.7 41.0 %copy-start.5 = (f32[11,128,128]{2,1,0:T(8,128)S(1)}, f32[11,128,128]{2,1,0:T(8,128)}, u32[]{:S(2)}) copy-start(f32[11,128,128]{2,1,0:T(8,128)} %copy-done.3) | copy-start | bytes 2162692
  101.5 10.8 %collective-permute-start.6 = (f32[4,128,128]{2,1,0:T(8,128)S(1)}, f32[4,128,128]{2,1,0:T(8,128)S(1)}, u32[]{:S(2)}, u32[]{:S(2)}) collective-permute-start(f32[4,128,128]{2,1,0:T(8,128)S(1)} %get-tuple-element.19), channel_id=1, source_target_pairs={{0,1},{1,2},{2,3},{3,4},{4,5},{5,6},{6,7},{7,8},{8,9},{9,10},{10,1... | collective-permute-start | bytes 786440 | tf_op jit(solution)/shard_map/ppermute | solution.py:459
  108.5 8.3 %collective-permute-start.7 = (f32[4,128,128]{2,1,0:T(8,128)S(1)}, f32[4,128,128]{2,1,0:T(8,128)S(1)}, u32[]{:S(2)}, u32[]{:S(2)}) collective-permute-start(f32[4,128,128]{2,1,0:T(8,128)S(1)} %get-tuple-element.20), channel_id=1, source_target_pairs={{1,0},{2,1},{3,2},{4,3},{5,4},{6,5},{7,6},{8,7},{9,8},{10,9},{11,1... | collective-permute-start | bytes 786440 | tf_op jit(solution)/shard_map/ppermute | solution.py:459
  144.6 11.0 %collective-permute-start.8 = (f32[4,64,128]{2,1,0:T(8,128)S(1)}, f32[4,64,128]{2,1,0:T(8,128)S(1)}, u32[]{:S(2)}, u32[]{:S(2)}) collective-permute-start(f32[4,64,128]{2,1,0:T(8,128)S(1)} %get-tuple-element.21.tau), channel_id=1, source_target_pairs={{0,1},{1,2},{2,3},{3,4},{4,5},{5,6},{6,7},{7,8},{8,9},{9,10},{10,1... | collective-permute-start | bytes 393224 | tf_op jit(solution)/shard_map/ppermute | solution.py:459
  149.8 22.6 %collective-permute-start.4 = (f32[8,128,128]{2,1,0:T(8,128)}, f32[8,128,128]{2,1,0:T(8,128)}, u32[]{:S(2)}, u32[]{:S(2)}) collective-permute-start(f32[8,128,128]{2,1,0:T(8,128)} %get-tuple-element.18.second), channel_id=1, source_target_pairs={{0,64},{32,96},{64,128},{96,160},{128,192},{160,224},{192,0},{224,... | collective-permute-start | bytes 1572872 | tf_op jit(solution)/shard_map/ppermute | solution.py:462
  152.9 6.9 %collective-permute-start.9 = (f32[4,64,128]{2,1,0:T(8,128)S(1)}, f32[4,64,128]{2,1,0:T(8,128)S(1)}, u32[]{:S(2)}, u32[]{:S(2)}) collective-permute-start(f32[4,64,128]{2,1,0:T(8,128)S(1)} %get-tuple-element.21.tau), channel_id=1, source_target_pairs={{1,0},{2,1},{3,2},{4,3},{5,4},{6,5},{7,6},{8,7},{9,8},{10,9},{11,1... | collective-permute-start | bytes 393224 | tf_op jit(solution)/shard_map/ppermute | solution.py:459
  154.8 71.1 %collective-permute-start.22 = (f32[8,128,128]{2,1,0:T(8,128)}, f32[8,128,128]{2,1,0:T(8,128)S(1)}, u32[]{:S(2)}, u32[]{:S(2)}) collective-permute-start(f32[8,128,128]{2,1,0:T(8,128)} %get-tuple-element.27), channel_id=1, source_target_pairs={{160,416},{192,448},{224,480},{416,160},{448,192},{480,224},{161,4... | collective-permute-start | bytes 1572872 | tf_op jit(solution)/shard_map/ppermute | solution.py:462
  159.8 22.3 %collective-permute-start.10 = (f32[10,64,128]{2,1,0:T(8,128)S(1)}, f32[10,64,128]{2,1,0:T(8,128)S(1)}, u32[]{:S(2)}, u32[]{:S(2)}) collective-permute-start(f32[10,64,128]{2,1,0:T(8,128)S(1)} %slice.52), channel_id=1, source_target_pairs={{0,96},{32,128},{64,160},{96,192},{128,224},{160,0},{192,32},{224,... | collective-permute-start | bytes 983048 | tf_op jit(solution)/shard_map/ppermute | solution.py:462
  165.5 16.7 %collective-permute-start.11 = (f32[8,64,128]{2,1,0:T(8,128)S(1)}, f32[8,64,128]{2,1,0:T(8,128)S(1)}, u32[]{:S(2)}, u32[]{:S(2)}) collective-permute-start(f32[8,64,128]{2,1,0:T(8,128)S(1)} %slice.53), channel_id=1, source_target_pairs={{0,64},{32,96},{64,128},{96,160},{128,192},{160,224},{192,0},{224,... | collective-permute-start | bytes 786440 | tf_op jit(solution)/shard_map/ppermute | solution.py:462
  172.3 9.8 %collective-permute-start.12 = (f32[6,64,128]{2,1,0:T(8,128)S(1)}, f32[6,64,128]{2,1,0:T(8,128)S(1)}, u32[]{:S(2)}, u32[]{:S(2)}) collective-permute-start(f32[6,64,128]{2,1,0:T(8,128)S(1)} %slice.54), channel_id=1, source_target_pairs={{0,32},{32,64},{64,96},{96,128},{128,160},{160,192},{192,224},{224... | collective-permute-start | bytes 589832 | tf_op jit(solution)/shard_map/ppermute | solution.py:462
  172.4 139.1 %collective-permute-start.5 = (f32[8,128,128]{2,1,0:T(8,128)}, f32[8,128,128]{2,1,0:T(8,128)}, u32[]{:S(2)}, u32[]{:S(2)}) collective-permute-start(f32[8,128,128]{2,1,0:T(8,128)} %collective-permute-done.4), channel_id=1, source_target_pairs={{0,256},{32,288},{256,0},{288,32},{1,257},{33,289},{257,1},{289,33... | collective-permute-start | bytes 1572872 | tf_op jit(solution)/shard_map/ppermute | solution.py:462
  188.4 40.6 %collective-permute-start.13 = (f32[2,4,64,128]{3,2,1,0:T(8,128)S(1)}, f32[2,4,64,128]{3,2,1,0:T(8,128)S(1)}, u32[]{:S(2)}, u32[]{:S(2)}) collective-permute-start(f32[2,4,64,128]{3,2,1,0:T(8,128)S(1)} %shard_map.62.both), channel_id=1, source_target_pairs={{0,129},{1,130},{2,131},{3,132},{4,133},{5,134},{6,135},{7,136},{8... | collective-permute-start | bytes 786440 | tf_op jit(solution)/shard_map/ppermute | solution.py:453
  219.2 14.2 %collective-permute-start.14 = (f32[2,4,64,128]{3,2,1,0:T(8,128)S(1)}, f32[2,4,64,128]{3,2,1,0:T(8,128)S(1)}, u32[]{:S(2)}, u32[]{:S(2)}) collective-permute-start(f32[2,4,64,128]{3,2,1,0:T(8,128)S(1)} %shard_map.62.both), channel_id=1, source_target_pairs={{0,128},{1,129},{2,130},{3,131},{4,132},{5,133},{6,134},{7,135},{8... | collective-permute-start | bytes 786440 | tf_op jit(solution)/shard_map/ppermute | solution.py:453
  224.0 22.1 %collective-permute-start.15 = (f32[2,4,64,128]{3,2,1,0:T(8,128)S(1)}, f32[2,4,64,128]{3,2,1,0:T(8,128)S(1)}, u32[]{:S(2)}, u32[]{:S(2)}) collective-permute-start(f32[2,4,64,128]{3,2,1,0:T(8,128)S(1)} %shard_map.62.both), channel_id=1, source_target_pairs={{1,128},{2,129},{3,130},{4,131},{5,132},{6,133},{7,134},{8,135},{9... | collective-permute-start | bytes 786440 | tf_op jit(solution)/shard_map/ppermute | solution.py:453
  227.1 84.5 %collective-permute-start.23 = (f32[8,128,128]{2,1,0:T(8,128)S(1)}, f32[8,128,128]{2,1,0:T(8,128)}, u32[]{:S(2)}, u32[]{:S(2)}) collective-permute-start(f32[8,128,128]{2,1,0:T(8,128)S(1)} %broadcast_select_fusion), channel_id=1, source_target_pairs={{0,96},{32,128},{64,160},{96,192},{128,224},{160,0},{192,32},{224,... | collective-permute-start | bytes 1572872 | tf_op jit(solution)/shard_map/ppermute | solution.py:462
  259.7 17.8 %collective-permute-start.17 = (f32[4,64,128]{2,1,0:T(8,128)S(1)}, f32[4,64,128]{2,1,0:T(8,128)S(1)}, u32[]{:S(2)}, u32[]{:S(2)}) collective-permute-start(f32[4,64,128]{2,1,0:T(8,128)S(1)} %get-tuple-element.22.last), channel_id=1, source_target_pairs={{0,1},{1,2},{2,3},{3,4},{4,5},{5,6},{6,7},{7,8},{8,9},{9,10},{10,1... | collective-permute-start | bytes 393224 | tf_op jit(solution)/shard_map/ppermute | solution.py:459
  261.7 22.7 %collective-permute-start.16 = (f32[4,128,128]{2,1,0:T(8,128)S(1)}, f32[4,128,128]{2,1,0:T(8,128)S(1)}, u32[]{:S(2)}, u32[]{:S(2)}) collective-permute-start(f32[4,128,128]{2,1,0:T(8,128)S(1)} %pad_maximum_fusion.2), channel_id=1, source_target_pairs={{0,2},{1,3},{2,4},{3,5},{4,6},{5,7},{6,8},{7,9},{8,10},{9,11},{10,... | collective-permute-start | bytes 786440 | tf_op jit(solution)/shard_map/ppermute | solution.py:459
  263.6 20.8 %collective-permute-start.19 = (f32[4,128,128]{2,1,0:T(8,128)S(1)}, f32[4,128,128]{2,1,0:T(8,128)S(1)}, u32[]{:S(2)}, u32[]{:S(2)}) collective-permute-start(f32[4,128,128]{2,1,0:T(8,128)S(1)} %pad_maximum_fusion.2), channel_id=1, source_target_pairs={{2,0},{3,1},{4,2},{5,3},{6,4},{7,5},{8,6},{9,7},{10,8},{11,9},{12,... | collective-permute-start | bytes 786440 | tf_op jit(solution)/shard_map/ppermute | solution.py:459
  277.5 6.8 %collective-permute-start.18 = (f32[4,64,128]{2,1,0:T(8,128)S(1)}, f32[4,64,128]{2,1,0:T(8,128)S(1)}, u32[]{:S(2)}, u32[]{:S(2)}) collective-permute-start(f32[4,64,128]{2,1,0:T(8,128)S(1)} %get-tuple-element.22.last), channel_id=1, source_target_pairs={{1,0},{2,1},{3,2},{4,3},{5,4},{6,5},{7,6},{8,7},{9,8},{10,9},{11,1... | collective-permute-start | bytes 393224 | tf_op jit(solution)/shard_map/ppermute | solution.py:459
  307.6 17.4 %collective-permute-start.20 = (f32[4,64,128]{2,1,0:T(8,128)S(1)}, f32[4,64,128]{2,1,0:T(8,128)S(1)}, u32[]{:S(2)}, u32[]{:S(2)}) collective-permute-start(f32[4,64,128]{2,1,0:T(8,128)S(1)} %get-tuple-element.25), channel_id=1, source_target_pairs={{0,352},{32,384},{64,416},{96,448},{128,480},{160,256},{192,288},{... | collective-permute-start | bytes 393224 | tf_op jit(solution)/shard_map/ppermute | solution.py:462
  309.6 15.5 %collective-permute-start.21 = (f32[4,64,128]{2,1,0:T(8,128)S(1)}, f32[4,64,128]{2,1,0:T(8,128)S(1)}, u32[]{:S(2)}, u32[]{:S(2)}) collective-permute-start(f32[4,64,128]{2,1,0:T(8,128)S(1)} %get-tuple-element.26), channel_id=1, source_target_pairs={{0,96},{32,128},{64,160},{96,192},{128,224},{160,0},{192,32},{224,... | collective-permute-start | bytes 393224 | tf_op jit(solution)/shard_map/ppermute | solution.py:462

commit v4 on v3

--- a/solution.py
+++ b/solution.py
@@ -34,71 +34,69 @@
     by_first, by_second, by_third, keep = weights
     rows, wide, depth = kappa.shape
     width = wide - 2 * PAD
-    chunk = min(16, width)
     first_w, third_w = 0.5 * ALONG_FIRST, 0.5 * third
-    for y in range(PAD, PAD + width, chunk):
-        before = kappa[0, y : y + chunk]
-        for row in range(rows):
-            k = kappa[row, y : y + chunk]
-            if row:
-                by_first[row, y - PAD : y - PAD + chunk] = first_w * (before + k)
-            beside = kappa[row, y - 1 : y - 1 + chunk]
-            by_second[row, y : y + chunk] = first_w * (beside + k)
-            deeper = pltpu.roll(k, depth - 1, 1)
-            by_third[row, y - PAD : y - PAD + chunk] = jnp.where(
-                lane_mask(k.shape, depth - 1), 0.0, third_w * (k + deeper)
-            )
-            keep[row, y - PAD : y - PAD + chunk] = jnp.where(
-                lane_mask(k.shape, 0, depth - 1), 1.0 - third_w * k, 1.0
-            )
-            before = k
+    inner = slice(PAD, PAD + width)
     for row in range(rows):
-        edge = kappa[row, PAD + width - 1 : 2 * PAD + width - 1]
-        by_second[row, PAD + width :] = first_w * edge
+        k = kappa[row, inner]
+        if row:
+            by_first[row] = first_w * (kappa[row - 1, inner] + k)
+        by_second[row, inner] = first_w * (kappa[row, PAD - 1 : PAD - 1 + width] + k)
+        by_second[row, PAD + width :] = (
+            first_w * kappa[row, PAD + width - 1 : 2 * PAD + width - 1]
+        )
+        deeper = pltpu.roll(k, depth - 1, 1)
+        by_third[row] = jnp.where(
+            lane_mask(k.shape, depth - 1), 0.0, third_w * (k + deeper)
+        )
+        keep[row] = jnp.where(lane_mask(k.shape, 0, depth - 1), 1.0 - third_w * k, 1.0)
 
 
 def sweep(src, dst, weights, heat, first, count, shift, inside, out=None):
     by_first, by_second, by_third, keep = weights
     wide, depth = src.shape[1:]
     width = wide - 2 * PAD
-    chunk = min(16, width)
-    for y in range(0, width, chunk):
-        here = slice(y + PAD, y + PAD + chunk)
-        flat = slice(y, y + chunk)
-        v = src[first, here]
-        flux = by_first[first + shift, flat] * (v - src[first - 1, here])
-        for row in range(first, first + count):
-            w = row + shift
-            ahead = src[row + 1, here]
-            flux_ahead = by_first[w + 1, flat] * (ahead - v)
-            up = src[row, y + PAD + 1 : y + PAD + 1 + chunk]
-            down = src[row, y + PAD - 1 : y + PAD - 1 + chunk]
-            side = by_second[w, y + PAD + 1 : y + PAD + 1 + chunk] * (up - v)
-            side = side - by_second[w, here] * (v - down)
-            deep = by_third[w, flat] * (pltpu.roll(v, depth - 1, 1) - v)
-            deep = deep - pltpu.roll(deep, 1, 1)
-            total = keep[w, flat] * v + ((flux_ahead - flux) + side + deep)
-            if heat is not None:
-                total = total + heat(row, flat)
-            mask = inside(row)
-            if mask is not None:
-                total = total * mask
-            if out is None:
-                dst[row, here] = total
-            else:
-                out(row - first, flat, total)
-            v, flux = ahead, flux_ahead
+    most = max(1, 256 // width)
+    inner = slice(PAD, PAD + width)
+    upper = slice(PAD + 1, PAD + 1 + width)
+    lower = slice(PAD - 1, PAD - 1 + width)
+    row = first
+    while row < first + count:
+        key, mask = inside(row)
+        end = row + 1
+        while end < first + count and end - row < most and inside(end)[0] == key:
+            end += 1
+        here = slice(row, end)
+        w = slice(row + shift, end + shift)
+        v = src[here, inner]
+        total = by_first[row + shift + 1 : end + shift + 1] * (
+            src[row + 1 : end + 1, inner] - v
+        ) - by_first[w] * (v - src[row - 1 : end - 1, inner])
+        total = total + (
+            by_second[w, upper] * (src[here, upper] - v)
+            - by_second[w, inner] * (v - src[here, lower])
+        )
+        deep = by_third[w] * (pltpu.roll(v, depth - 1, 2) - v)
+        total = keep[w] * v + (total + (deep - pltpu.roll(deep, 1, 2)))
+        if heat is not None:
+            total = total + heat(row, end)
+        if mask is not None:
+            total = total * mask
+        if out is None:
+            dst[here, inner] = total
+        else:
+            out(slice(row - first, end - first), total)
+        row = end
 
 
 def inside_of(place, slabs, margin, block):
     def inside(row):
         if row < margin:
             need = (margin - row + block - 1) // block
-            return jnp.where(place >= need, 1.0, 0.0)
+            return -need, jnp.where(place >= need, 1.0, 0.0)
         if row >= margin + block:
             need = (row - margin) // block
-            return jnp.where(place + need < slabs, 1.0, 0.0)
-        return None
+            return need, jnp.where(place + need < slabs, 1.0, 0.0)
+        return 0, None
 
     return inside
 
@@ -132,12 +130,12 @@
     )
     face_weights(kappa_wide, weights, ALONG_THIRD)
 
-    def heat(row, flat):
+    def heat(row, end):
         if row < STEPS:
-            return up_1[2 * STEPS + row - 1, flat]
+            return up_1[2 * STEPS + row - 1 : 2 * STEPS + end - 1]
         if row < STEPS + rows:
-            return source[row - STEPS, flat]
-        return down_1[2 * STEPS + row - STEPS - rows, flat]
+            return source[row - STEPS : end - STEPS]
+        return down_1[STEPS + row - rows : STEPS + end - rows]
 
     inside = inside_of(where[1], slabs, STEPS, rows)
     src, dst = state, other
@@ -166,8 +164,8 @@
     def _():
         fill(state, [(guess, 0, rows, STEPS)])
 
-    def out(row, flat, value):
-        state_out[row, flat] = value
+    def out(rows, value):
+        state_out[rows] = value
 
     four_steps(where, slabs, up_1, down_1, kappa, source, scratch, out)
 
@@ -200,8 +198,8 @@
         ],
     )
 
-    def out(row, flat, value):
-        second_out[row, flat] = value
+    def out(rows, value):
+        second_out[rows] = value
 
     four_steps(where, slabs, up_1, down_1, kappa, source, scratch, out)
 
@@ -262,18 +260,18 @@
             pair[pl.ds(0, half, stride=2), :] + pair[pl.ds(1, half, stride=2), :]
         )
 
-    def out(row, flat, value):
-        third_out[row, flat] = value
+    def out(rows, value):
+        third_out[rows] = value
 
     four_steps(where, slabs, up_1, down_1, kappa, source, scratch, out)
 
     coarse_kappa_4(kappa_wide, up_2, down_2, kappa_c, 0)
     face_weights(kappa_wide, weights, 4.0 * ALONG_THIRD)
 
-    def keep(row, flat, value):
-        tau_out[row, flat] = value
-
-    sweep(base, spare, weights, None, 1, block, block - 1, lambda row: None, keep)
+    def keep(rows, value):
+        tau_out[rows] = value
+
+    sweep(base, spare, weights, None, 1, block, block - 1, lambda row: (0, None), keep)
     use = jnp.where(where[0] == 13, 0.0, 1.0)
     for row in range(block):
         pair[...] = third_out[2 * row] + third_out[2 * row + 1]
@@ -307,11 +305,11 @@
                 src[at] = value if distance == 3 else src[at] + value
             if distance == 1:
 
-                def out(row, flat, value, is_ahead=is_ahead):
+                def out(rows, value, is_ahead=is_ahead):
                     if is_ahead:
-                        both_out[0, row, flat] = value + tau[row, flat]
+                        both_out[0, rows] = value + tau[rows]
                     else:
-                        both_out[1, row, flat] = value
+                        both_out[1, rows] = value
 
             else:
                 out = None
@@ -348,8 +346,8 @@
                 else:
                     field[at] = from_wrapped * ref[1, row] + from_ahead * ref[0, row]
 
-        def out(row, flat, value, index=index, result=result):
-            result[row, flat] = value + both[index, row, flat]
+        def out(rows, value, index=index, result=result):
+            result[rows] = value + both[index, rows]
 
         src, dst = field, spare
         for step in range(1, block + 1):
@@ -409,10 +407,10 @@
     keep_wrapped = one(high & ~early)
     keep_ahead = one(early)
 
-    def out(row, flat, value):
-        a, w = ahead[row, flat], wrapped[row, flat]
-        handed_out[row, flat] = hand_image * value + hand_wrapped * w + hand_ahead * a
-        kept_out[row, flat] = keep_image * value + keep_wrapped * w + keep_ahead * a
+    def out(rows, value):
+        a, w = ahead[rows], wrapped[rows]
+        handed_out[rows] = hand_image * value + hand_wrapped * w + hand_ahead * a
+        kept_out[rows] = keep_image * value + keep_wrapped * w + keep_ahead * a
 
     src, dst = field, spare
     for step in range(1, 2 * block + 1):
@@ -499,7 +497,7 @@
         where, *sides, *sides_2, state, initial, conductivity, source,
     )
     sides_3 = neighbours(first, last)
-    second_near = along_time(second, ring(2))
+    second_far = along_time(second, [(6, 8), (7, 9), (14, 0), (15, 1)])
     third, tau = call(
         phase_three_kernel, slabs, [block_shape, coarse_shape],
         scratch
@@ -509,10 +507,10 @@
     )
 
     up, down = neighbours(tau, tau)
-    second_cross = along_time(second_near, [(0, 8), (1, 9), (8, 0), (9, 1)])
     tau_wide = jnp.concatenate([up, tau, down], 0)
     got = [along_time(cut(tau_wide, crows, d), ring(d)) for d in (3, 2, 1)]
-    third_cross = along_time(third, [(i, i ^ 8) for i in (5, 6, 7, 13, 14, 15)])
+    third_near = along_time(third, ring(3))
+    third_far = along_time(third_near, [(i, i ^ GROUP) for i in (0, 1, 2, 8, 9, 10)])
     (both,) = call(
         near_sums_kernel, slabs, [(2,) + coarse_shape],
         coarse_scratch(3 * crows, half, width_three, 3),
@@ -552,8 +550,10 @@
         ],
     )
     kept = along_time(kept, ring(3))
-    third_home = along_time(jnp.where(local >= 5, third_cross, third), ring(3))
-    second_home = jnp.where(local < 2, second_cross, second_near)
+    second_far, third_far = lax.optimization_barrier((second_far, third_far, kept))[:2]
+    second_near = along_time(second, ring(2))
+    third_home = jnp.where(local < 3, third_far, third_near)
+    second_home = jnp.where(local < 2, second_far, second_near)
 
     residual = third_home - second_home
     change = handed + kept - restrict(second_home)

time: 327 us -> 246 us (0.75)
  the two profiles are of different devices: /device:TPU:116 before, /device:TPU:36 now
where the time goes in v4:
time: 246 us
  starting transfers between devices  128 us (52%)
  waiting for transfers between devices  87 us (35%)
  Pallas kernels  21.1 us (9%)
  other arithmetic  7.34 us (3%)
    ppermute x9, starting transfers between devices, along_time(): return lax.ppermute(block, 'tm', pairs)  63.8 us
    ppermute x12, starting transfers between devices, along_space(): return lax.ppermute(block, 'space', pairs)  47.7 us
    ppermute x12, waiting for transfers between devices, along_space(): return lax.ppermute(block, 'space', pairs)  41.8 us
    ppermute x9, waiting for transfers between devices, along_time(): return lax.ppermute(block, 'tm', pairs)  34.9 us
    pallas_call x6, Pallas kernels, call(): pl.pallas_call(functools.partial(kernel, slabs), out_shape=[jax.ShapeDtyp...  21.1 us
    ppermute x3, starting transfers between devices, route(): return lax.ppermute(block, ('tm', 'space'), pairs)  16.1 us
    ppermute x3, waiting for transfers between devices, route(): return lax.ppermute(block, ('tm', 'space'), pairs)  10.2 us
  transfers between devices with their start and end apart: 24, of which 15 were waited for; matrix products, arithmetic and copies ran while one was open for 2% of the time, Pallas kernels for 4%

profile of v4, /device:TPU:36, one launch (start us, length us, event | category | flops | bytes accessed | tf_op | source)
XLA Modules:
  0.0 245.5 jit_solution(5104957630070545031)
XLA Ops:
  4.1 4.5 %collective-permute-start.1 = (f32[11,128,128]{2,1,0:T(8,128)}, f32[11,128,128]{2,1,0:T(8,128)S(1)}, u32[]{:S(2)}, u32[]{:S(2)}) collective-permute-start(f32[11,128,128]{2,1,0:T(8,128)} %pad_maximum_fusion.1), channel_id=1, source_target_pairs={{1,0},{2,1},{3,2},{4,3},{5,4},{6,5},{7,6},{8,7},{9,8},{10,9},{11,1... | collective-permute-start | bytes 2162696 | tf_op jit(solution)/shard_map/ppermute | solution.py:457
  9.5 2.0 collective-permute-start
  13.6 10.7 %collective-permute-done.1.down_1 = f32[11,128,128]{2,1,0:T(8,128)S(1)} collective-permute-done((f32[11,128,128]{2,1,0:T(8,128)}, f32[11,128,128]{2,1,0:T(8,128)S(1)}, u32[]{:S(2)}, u32[]{:S(2)}) %collective-permute-start.1) | collective-permute-done | bytes 720928 | tf_op jit(solution)/shard_map/ppermute | solution.py:457
  24.2 7.2 %collective-permute-done.up_1 = f32[11,128,128]{2,1,0:T(8,128)S(1)} collective-permute-done((f32[11,128,128]{2,1,0:T(8,128)}, f32[11,128,128]{2,1,0:T(8,128)S(1)}, u32[]{:S(2)}, u32[]{:S(2)}) %collective-permute-start) | collective-permute-done | bytes 720928 | tf_op jit(solution)/shard_map/ppermute | solution.py:457
  31.4 3.9 %shard_map.59 = (f32[8,128,128]{2,1,0:T(8,128)S(1)}, f32[6,128,128]{2,1,0:T(8,128)S(1)}, f32[6,128,128]{2,1,0:T(8,128)S(1)}) custom-call(s32[2]{0:T(128)S(1)} %pad_add_fusion.where, f32[11,128,128]{2,1,0:T(8,128)S(1)} %collective-permute-done.up_1, f32[11,128,128]{2,1,0:T(8,128)S(1)} %collective-permute-done.1.down_1, f32[8,128,128]{2,1,0:T(8,128)S(1)} %bitcast.16, ...), custom_call_target="tpu_custom_call" | custom-call | tf_op jit(solution)/shard_map/pallas_call | solution.py:427
  37.3 6.0 %collective-permute-start.3 = (f32[6,128,128]{2,1,0:T(8,128)S(1)}, f32[6,128,128]{2,1,0:T(8,128)S(1)}, u32[]{:S(2)}, u32[]{:S(2)}) collective-permute-start(f32[6,128,128]{2,1,0:T(8,128)S(1)} %get-tuple-element.18), channel_id=1, source_target_pairs={{1,0},{2,1},{3,2},{4,3},{5,4},{6,5},{7,6},{8,7},{9,8},{10,9},{11,1... | collective-permute-start | bytes 1179656 | tf_op jit(solution)/shard_map/ppermute | solution.py:457
  43.3 5.7 %collective-permute-done.2.up_2 = f32[6,128,128]{2,1,0:T(8,128)S(1)} collective-permute-done((f32[6,128,128]{2,1,0:T(8,128)S(1)}, f32[6,128,128]{2,1,0:T(8,128)S(1)}, u32[]{:S(2)}, u32[]{:S(2)}) %collective-permute-start.2) | collective-permute-done | bytes 393248 | tf_op jit(solution)/shard_map/ppermute | solution.py:457
  50.2 3.9 %shard_map.60 = (f32[8,128,128]{2,1,0:T(8,128)S(1)}, f32[4,128,128]{2,1,0:T(8,128)S(1)}, f32[4,128,128]{2,1,0:T(8,128)S(1)}) custom-call(s32[2]{0:T(128)S(1)} %pad_add_fusion.where, f32[11,128,128]{2,1,0:T(8,128)S(1)} %collective-permute-done.up_1, f32[11,128,128]{2,1,0:T(8,128)S(1)} %collective-permute-done.1.down_1, ...), custom_call_target="tpu_custom_call" | custom-call | tf_op jit(solution)/shard_map/pallas_call | solution.py:427
  56.1 6.5 %collective-permute-start.6 = (f32[4,128,128]{2,1,0:T(8,128)S(1)}, f32[4,128,128]{2,1,0:T(8,128)S(1)}, u32[]{:S(2)}, u32[]{:S(2)}) collective-permute-start(f32[4,128,128]{2,1,0:T(8,128)S(1)} %get-tuple-element.22), channel_id=1, source_target_pairs={{1,0},{2,1},{3,2},{4,3},{5,4},{6,5},{7,6},{8,7},{9,8},{10,9},{11,1... | collective-permute-start | bytes 786440 | tf_op jit(solution)/shard_map/ppermute | solution.py:457
  62.6 2.4 collective-permute-done.5.up_3
  66.4 4.5 %shard_map.61 = (f32[8,128,128]{2,1,0:T(8,128)S(1)}, f32[4,64,128]{2,1,0:T(8,128)S(1)}) custom-call(s32[2]{0:T(128)S(1)} %pad_add_fusion.where, f32[11,128,128]{2,1,0:T(8,128)S(1)} %collective-permute-done.up_1, f32[11,128,128]{2,1,0:T(8,128)S(1)} %collective-permute-done.1.down_1, f32[6,128,128]{2,1,0:T(8,128)S(1)} %collective-permute-done.2.up_2, ...), custom_call_target="tpu_custom_call" | custom-call | tf_op jit(solution)/shard_map/pallas_call | solution.py:427
  70.9 4.2 %collective-permute-start.9 = (f32[4,64,128]{2,1,0:T(8,128)S(1)}, f32[4,64,128]{2,1,0:T(8,128)S(1)}, u32[]{:S(2)}, u32[]{:S(2)}) collective-permute-start(f32[4,64,128]{2,1,0:T(8,128)S(1)} %get-tuple-element.24.tau), channel_id=1, source_target_pairs={{0,1},{1,2},{2,3},{3,4},{4,5},{5,6},{6,7},{7,8},{8,9},{9,10},{10,1... | collective-permute-start | bytes 393224 | tf_op jit(solution)/shard_map/ppermute | solution.py:457
  75.2 4.2 %collective-permute-start.10 = (f32[4,64,128]{2,1,0:T(8,128)S(1)}, f32[4,64,128]{2,1,0:T(8,128)S(1)}, u32[]{:S(2)}, u32[]{:S(2)}) collective-permute-start(f32[4,64,128]{2,1,0:T(8,128)S(1)} %get-tuple-element.24.tau), channel_id=1, source_target_pairs={{1,0},{2,1},{3,2},{4,3},{5,4},{6,5},{7,6},{8,7},{9,8},{10,9},{11,1... | collective-permute-start | bytes 393224 | tf_op jit(solution)/shard_map/ppermute | solution.py:457
  84.0 3.1 %collective-permute-start.12 = (f32[8,64,128]{2,1,0:T(8,128)S(1)}, f32[8,64,128]{2,1,0:T(8,128)S(1)}, u32[]{:S(2)}, u32[]{:S(2)}) collective-permute-start(f32[8,64,128]{2,1,0:T(8,128)S(1)} %slice.53), channel_id=1, source_target_pairs={{0,64},{32,96},{64,128},{96,160},{128,192},{160,224},{192,0},{224,... | collective-permute-start | bytes 786440 | tf_op jit(solution)/shard_map/ppermute | solution.py:460
  87.2 4.8 %collective-permute-start.7 = (f32[8,128,128]{2,1,0:T(8,128)S(1)}, f32[8,128,128]{2,1,0:T(8,128)S(1)}, u32[]{:S(2)}, u32[]{:S(2)}) collective-permute-start(f32[8,128,128]{2,1,0:T(8,128)S(1)} %get-tuple-element.23), channel_id=1, source_target_pairs={{0,96},{32,128},{64,160},{96,192},{128,224},{160,0},{192,32},{224,... | collective-permute-start | bytes 1572872 | tf_op jit(solution)/shard_map/ppermute | solution.py:460
  92.0 11.7 %collective-permute-done.13.got_1 = f32[6,64,128]{2,1,0:T(8,128)S(1)} collective-permute-done((f32[6,64,128]{2,1,0:T(8,128)S(1)}, f32[6,64,128]{2,1,0:T(8,128)S(1)}, u32[]{:S(2)}, u32[]{:S(2)}) %collective-permute-start.13) | collective-permute-done | bytes 196640 | tf_op jit(solution)/shard_map/ppermute | solution.py:460
  103.7 2.1 shard_map.62.both
  105.8 7.3 %collective-permute-start.14 = (f32[2,4,64,128]{3,2,1,0:T(8,128)S(1)}, f32[2,4,64,128]{3,2,1,0:T(8,128)S(1)}, u32[]{:S(2)}, u32[]{:S(2)}) collective-permute-start(f32[2,4,64,128]{3,2,1,0:T(8,128)S(1)} %shard_map.62.both), channel_id=1, source_target_pairs={{0,129},{1,130},{2,131},{3,132},{4,133},{5,134},{6,135},{7,136},{8... | collective-permute-start | bytes 786440 | tf_op jit(solution)/shard_map/ppermute | solution.py:451
  115.1 6.9 %collective-permute-start.16 = (f32[2,4,64,128]{3,2,1,0:T(8,128)S(1)}, f32[2,4,64,128]{3,2,1,0:T(8,128)S(1)}, u32[]{:S(2)}, u32[]{:S(2)}) collective-permute-start(f32[2,4,64,128]{3,2,1,0:T(8,128)S(1)} %shard_map.62.both), channel_id=1, source_target_pairs={{1,128},{2,129},{3,130},{4,131},{5,132},{6,133},{7,134},{8,135},{9... | collective-permute-start | bytes 786440 | tf_op jit(solution)/shard_map/ppermute | solution.py:451
  122.0 3.1 %collective-permute-done.15.got = f32[2,4,64,128]{3,2,1,0:T(8,128)S(1)} collective-permute-done((f32[2,4,64,128]{3,2,1,0:T(8,128)S(1)}, f32[2,4,64,128]{3,2,1,0:T(8,128)S(1)}, u32[]{:S(2)}, u32[]{:S(2)}) %collective-permute-start.15) | collective-permute-done | bytes 262176 | tf_op jit(solution)/shard_map/ppermute | solution.py:451
  125.1 7.1 %collective-permute-done.16.got_down = f32[2,4,64,128]{3,2,1,0:T(8,128)S(1)} collective-permute-done((f32[2,4,64,128]{3,2,1,0:T(8,128)S(1)}, f32[2,4,64,128]{3,2,1,0:T(8,128)S(1)}, u32[]{:S(2)}, u32[]{:S(2)}) %collective-permute-start.16) | collective-permute-done | bytes 262176 | tf_op jit(solution)/shard_map/ppermute | solution.py:451
  132.2 2.8 %shard_map.63 = (f32[4,64,128]{2,1,0:T(8,128)S(1)}, f32[4,64,128]{2,1,0:T(8,128)S(1)}, f32[4,64,128]{2,1,0:T(8,128)S(1)}) custom-call(s32[2]{0:T(128)S(1)} %pad_add_fusion.where, f32[2,4,64,128]{3,2,1,0:T(8,128)S(1)} %collective-permute-done.14.got_up, f32[2,4,64,128]{3,2,1,0:T(8,128)S(1)} %collective-permute-done.15.got, ...), custom_call_target="tpu_custom_call" | custom-call | tf_op jit(solution)/shard_map/pallas_call | solution.py:427
  135.0 4.0 %collective-permute-start.18 = (f32[4,64,128]{2,1,0:T(8,128)S(1)}, f32[4,64,128]{2,1,0:T(8,128)S(1)}, u32[]{:S(2)}, u32[]{:S(2)}) collective-permute-start(f32[4,64,128]{2,1,0:T(8,128)S(1)} %get-tuple-element.25.last), channel_id=1, source_target_pairs={{0,1},{1,2},{2,3},{3,4},{4,5},{5,6},{6,7},{7,8},{8,9},{9,10},{10,1... | collective-permute-start | bytes 393224 | tf_op jit(solution)/shard_map/ppermute | solution.py:457
  139.0 3.9 %collective-permute-start.19 = (f32[4,64,128]{2,1,0:T(8,128)S(1)}, f32[4,64,128]{2,1,0:T(8,128)S(1)}, u32[]{:S(2)}, u32[]{:S(2)}) collective-permute-start(f32[4,64,128]{2,1,0:T(8,128)S(1)} %get-tuple-element.25.last), channel_id=1, source_target_pairs={{1,0},{2,1},{3,2},{4,3},{5,4},{6,5},{7,6},{8,7},{9,8},{10,9},{11,1... | collective-permute-start | bytes 393224 | tf_op jit(solution)/shard_map/ppermute | solution.py:457
  144.3 17.7 %collective-permute-start.22 = (f32[8,128,128]{2,1,0:T(8,128)S(1)}, f32[8,128,128]{2,1,0:T(8,128)S(1)}, u32[]{:S(2)}, u32[]{:S(2)}) collective-permute-start(f32[8,128,128]{2,1,0:T(8,128)S(1)} %get-tuple-element.20.second), channel_id=1, source_target_pairs={{0,64},{32,96},{64,128},{96,160},{128,192},{160,224},{192,0},{224,... | collective-permute-start | bytes 1572872 | tf_op jit(solution)/shard_map/ppermute | solution.py:460
  162.1 3.5 %collective-permute-start.17 = (f32[4,128,128]{2,1,0:T(8,128)S(1)}, f32[4,128,128]{2,1,0:T(8,128)S(1)}, u32[]{:S(2)}, u32[]{:S(2)}) collective-permute-start(f32[4,128,128]{2,1,0:T(8,128)S(1)} %pad_maximum_fusion.2), channel_id=1, source_target_pairs={{0,2},{1,3},{2,4},{3,5},{4,6},{5,7},{6,8},{7,9},{8,10},{9,11},{10,... | collective-permute-start | bytes 786440 | tf_op jit(solution)/shard_map/ppermute | solution.py:457
  165.6 5.0 %collective-permute-start.20 = (f32[4,128,128]{2,1,0:T(8,128)S(1)}, f32[4,128,128]{2,1,0:T(8,128)S(1)}, u32[]{:S(2)}, u32[]{:S(2)}) collective-permute-start(f32[4,128,128]{2,1,0:T(8,128)S(1)} %pad_maximum_fusion.2), channel_id=1, source_target_pairs={{2,0},{3,1},{4,2},{5,3},{6,4},{7,5},{8,6},{9,7},{10,8},{11,9},{12,... | collective-permute-start | bytes 786440 | tf_op jit(solution)/shard_map/ppermute | solution.py:457
  170.6 4.1 %collective-permute-done.17.far_up = f32[4,128,128]{2,1,0:T(8,128)S(1)} collective-permute-done((f32[4,128,128]{2,1,0:T(8,128)S(1)}, f32[4,128,128]{2,1,0:T(8,128)S(1)}, u32[]{:S(2)}, u32[]{:S(2)}) %collective-permute-start.17) | collective-permute-done | bytes 262176 | tf_op jit(solution)/shard_map/ppermute | solution.py:457
  174.7 6.5 %collective-permute-done.20.far_down = f32[4,128,128]{2,1,0:T(8,128)S(1)} collective-permute-done((f32[4,128,128]{2,1,0:T(8,128)S(1)}, f32[4,128,128]{2,1,0:T(8,128)S(1)}, u32[]{:S(2)}, u32[]{:S(2)}) %collective-permute-start.20) | collective-permute-done | bytes 262176 | tf_op jit(solution)/shard_map/ppermute | solution.py:457
  181.2 3.8 %shard_map.64 = (f32[4,64,128]{2,1,0:T(8,128)S(1)}, f32[4,64,128]{2,1,0:T(8,128)S(1)}) custom-call(s32[2]{0:T(128)S(1)} %pad_add_fusion.where, f32[4,128,128]{2,1,0:T(8,128)S(1)} %collective-permute-done.17.far_up, f32[4,64,128]{2,1,0:T(8,128)S(1)} %collective-permute-done.18.near_up, f32[4,64,128]{2,1,0:T(8,128)S(1)} %get-tuple-element.25.last, ...), custom_call_target="tpu_custom_call" | custom-call | tf_op jit(solution)/shard_map/pallas_call | solution.py:427
  185.0 32.9 %collective-permute-start.21 = (f32[4,64,128]{2,1,0:T(8,128)S(1)}, f32[4,64,128]{2,1,0:T(8,128)S(1)}, u32[]{:S(2)}, u32[]{:S(2)}) collective-permute-start(f32[4,64,128]{2,1,0:T(8,128)S(1)} %get-tuple-element.28), channel_id=1, source_target_pairs={{0,96},{32,128},{64,160},{96,192},{128,224},{160,0},{192,32},{224,... | collective-permute-start | bytes 393224 | tf_op jit(solution)/shard_map/ppermute | solution.py:460
  222.7 21.7 %collective-permute-done.23 = f32[4,64,128]{2,1,0:T(8,128)S(1)} collective-permute-done((f32[4,64,128]{2,1,0:T(8,128)S(1)}, f32[4,64,128]{2,1,0:T(8,128)S(1)}, u32[]{:S(2)}, u32[]{:S(2)}) %collective-permute-start.23) | collective-permute-done | bytes 131104 | tf_op jit(solution)/shard_map/ppermute | solution.py:460
  (50 shorter events, 26.7 us)
Async XLA Ops:
  0.6 1.2 copy-start
  4.1 20.2 %collective-permute-start.1 = (f32[11,128,128]{2,1,0:T(8,128)}, f32[11,128,128]{2,1,0:T(8,128)S(1)}, u32[]{:S(2)}, u32[]{:S(2)}) collective-permute-start(f32[11,128,128]{2,1,0:T(8,128)} %pad_maximum_fusion.1), channel_id=1, source_target_pairs={{1,0},{2,1},{3,2},{4,3},{5,4},{6,5},{7,6},{8,7},{9,8},{10,9},{11,1... | collective-permute-start | bytes 2162696 | tf_op jit(solution)/shard_map/ppermute | solution.py:457
  8.5 22.9 %copy-start.2 = (f32[8,128,128]{2,1,0:T(8,128)S(1)}, f32[8,128,128]{2,1,0:T(8,128)}, u32[]{:S(2)}) copy-start(f32[8,128,128]{2,1,0:T(8,128)} %source.5) | copy-start | bytes 1572868
  8.6 22.9 %copy-start.3 = (f32[1,8,128,128]{3,2,1,0:T(8,128)S(1)}, f32[1,8,128,128]{3,2,1,0:T(8,128)}, u32[]{:S(2)}) copy-start(f32[1,8,128,128]{3,2,1,0:T(8,128)} %param.5) | copy-start | bytes 1572868
  9.5 21.9 %copy-start.1 = (f32[8,128,128]{2,1,0:T(8,128)S(1)}, f32[8,128,128]{2,1,0:T(8,128)}, u32[]{:S(2)}) copy-start(f32[8,128,128]{2,1,0:T(8,128)} %initial.5) | copy-start | bytes 1572868
  9.5 21.9 %collective-permute-start = (f32[11,128,128]{2,1,0:T(8,128)}, f32[11,128,128]{2,1,0:T(8,128)S(1)}, u32[]{:S(2)}, u32[]{:S(2)}) collective-permute-start(f32[11,128,128]{2,1,0:T(8,128)} %pad_maximum_fusion), channel_id=1, source_target_pairs={{0,1},{1,2},{2,3},{3,4},{4,5},{5,6},{6,7},{7,8},{8,9},{9,10},{10,1... | collective-permute-start | bytes 2162696 | tf_op jit(solution)/shard_map/ppermute | solution.py:457
  35.4 13.7 %collective-permute-start.2 = (f32[6,128,128]{2,1,0:T(8,128)S(1)}, f32[6,128,128]{2,1,0:T(8,128)S(1)}, u32[]{:S(2)}, u32[]{:S(2)}) collective-permute-start(f32[6,128,128]{2,1,0:T(8,128)S(1)} %get-tuple-element.17), channel_id=1, source_target_pairs={{0,1},{1,2},{2,3},{3,4},{4,5},{5,6},{6,7},{7,8},{8,9},{9,10},{10,1... | collective-permute-start | bytes 1179656 | tf_op jit(solution)/shard_map/ppermute | solution.py:457
  37.3 12.9 %collective-permute-start.3 = (f32[6,128,128]{2,1,0:T(8,128)S(1)}, f32[6,128,128]{2,1,0:T(8,128)S(1)}, u32[]{:S(2)}, u32[]{:S(2)}) collective-permute-start(f32[6,128,128]{2,1,0:T(8,128)S(1)} %get-tuple-element.18), channel_id=1, source_target_pairs={{1,0},{2,1},{3,2},{4,3},{5,4},{6,5},{7,6},{8,7},{9,8},{10,9},{11,1... | collective-permute-start | bytes 1179656 | tf_op jit(solution)/shard_map/ppermute | solution.py:457
  54.1 10.8 %collective-permute-start.5 = (f32[4,128,128]{2,1,0:T(8,128)S(1)}, f32[4,128,128]{2,1,0:T(8,128)S(1)}, u32[]{:S(2)}, u32[]{:S(2)}) collective-permute-start(f32[4,128,128]{2,1,0:T(8,128)S(1)} %get-tuple-element.21), channel_id=1, source_target_pairs={{0,1},{1,2},{2,3},{3,4},{4,5},{5,6},{6,7},{7,8},{8,9},{9,10},{10,1... | collective-permute-start | bytes 786440 | tf_op jit(solution)/shard_map/ppermute | solution.py:457
  56.1 10.4 %collective-permute-start.6 = (f32[4,128,128]{2,1,0:T(8,128)S(1)}, f32[4,128,128]{2,1,0:T(8,128)S(1)}, u32[]{:S(2)}, u32[]{:S(2)}) collective-permute-start(f32[4,128,128]{2,1,0:T(8,128)S(1)} %get-tuple-element.22), channel_id=1, source_target_pairs={{1,0},{2,1},{3,2},{4,3},{5,4},{6,5},{7,6},{8,7},{9,8},{10,9},{11,1... | collective-permute-start | bytes 786440 | tf_op jit(solution)/shard_map/ppermute | solution.py:457
  70.9 9.4 %collective-permute-start.9 = (f32[4,64,128]{2,1,0:T(8,128)S(1)}, f32[4,64,128]{2,1,0:T(8,128)S(1)}, u32[]{:S(2)}, u32[]{:S(2)}) collective-permute-start(f32[4,64,128]{2,1,0:T(8,128)S(1)} %get-tuple-element.24.tau), channel_id=1, source_target_pairs={{0,1},{1,2},{2,3},{3,4},{4,5},{5,6},{6,7},{7,8},{8,9},{9,10},{10,1... | collective-permute-start | bytes 393224 | tf_op jit(solution)/shard_map/ppermute | solution.py:457
  75.2 6.9 %collective-permute-start.10 = (f32[4,64,128]{2,1,0:T(8,128)S(1)}, f32[4,64,128]{2,1,0:T(8,128)S(1)}, u32[]{:S(2)}, u32[]{:S(2)}) collective-permute-start(f32[4,64,128]{2,1,0:T(8,128)S(1)} %get-tuple-element.24.tau), channel_id=1, source_target_pairs={{1,0},{2,1},{3,2},{4,3},{5,4},{6,5},{7,6},{8,7},{9,8},{10,9},{11,1... | collective-permute-start | bytes 393224 | tf_op jit(solution)/shard_map/ppermute | solution.py:457
  82.1 21.6 %collective-permute-start.11 = (f32[10,64,128]{2,1,0:T(8,128)S(1)}, f32[10,64,128]{2,1,0:T(8,128)S(1)}, u32[]{:S(2)}, u32[]{:S(2)}) collective-permute-start(f32[10,64,128]{2,1,0:T(8,128)S(1)} %slice.52), channel_id=1, source_target_pairs={{0,96},{32,128},{64,160},{96,192},{128,224},{160,0},{192,32},{224,... | collective-permute-start | bytes 983048 | tf_op jit(solution)/shard_map/ppermute | solution.py:460
  84.0 19.7 %collective-permute-start.12 = (f32[8,64,128]{2,1,0:T(8,128)S(1)}, f32[8,64,128]{2,1,0:T(8,128)S(1)}, u32[]{:S(2)}, u32[]{:S(2)}) collective-permute-start(f32[8,64,128]{2,1,0:T(8,128)S(1)} %slice.53), channel_id=1, source_target_pairs={{0,64},{32,96},{64,128},{96,160},{128,192},{160,224},{192,0},{224,... | collective-permute-start | bytes 786440 | tf_op jit(solution)/shard_map/ppermute | solution.py:460
  87.2 56.5 %collective-permute-start.7 = (f32[8,128,128]{2,1,0:T(8,128)S(1)}, f32[8,128,128]{2,1,0:T(8,128)S(1)}, u32[]{:S(2)}, u32[]{:S(2)}) collective-permute-start(f32[8,128,128]{2,1,0:T(8,128)S(1)} %get-tuple-element.23), channel_id=1, source_target_pairs={{0,96},{32,128},{64,160},{96,192},{128,224},{160,0},{192,32},{224,... | collective-permute-start | bytes 1572872 | tf_op jit(solution)/shard_map/ppermute | solution.py:460
  92.0 11.7 %collective-permute-start.13 = (f32[6,64,128]{2,1,0:T(8,128)S(1)}, f32[6,64,128]{2,1,0:T(8,128)S(1)}, u32[]{:S(2)}, u32[]{:S(2)}) collective-permute-start(f32[6,64,128]{2,1,0:T(8,128)S(1)} %slice.54), channel_id=1, source_target_pairs={{0,32},{32,64},{64,96},{96,128},{128,160},{160,192},{192,224},{224... | collective-permute-start | bytes 589832 | tf_op jit(solution)/shard_map/ppermute | solution.py:460
  105.8 16.1 %collective-permute-start.14 = (f32[2,4,64,128]{3,2,1,0:T(8,128)S(1)}, f32[2,4,64,128]{3,2,1,0:T(8,128)S(1)}, u32[]{:S(2)}, u32[]{:S(2)}) collective-permute-start(f32[2,4,64,128]{3,2,1,0:T(8,128)S(1)} %shard_map.62.both), channel_id=1, source_target_pairs={{0,129},{1,130},{2,131},{3,132},{4,133},{5,134},{6,135},{7,136},{8... | collective-permute-start | bytes 786440 | tf_op jit(solution)/shard_map/ppermute | solution.py:451
  113.1 12.0 %collective-permute-start.15 = (f32[2,4,64,128]{3,2,1,0:T(8,128)S(1)}, f32[2,4,64,128]{3,2,1,0:T(8,128)S(1)}, u32[]{:S(2)}, u32[]{:S(2)}) collective-permute-start(f32[2,4,64,128]{3,2,1,0:T(8,128)S(1)} %shard_map.62.both), channel_id=1, source_target_pairs={{0,128},{1,129},{2,130},{3,131},{4,132},{5,133},{6,134},{7,135},{8... | collective-permute-start | bytes 786440 | tf_op jit(solution)/shard_map/ppermute | solution.py:451
  115.1 17.1 %collective-permute-start.16 = (f32[2,4,64,128]{3,2,1,0:T(8,128)S(1)}, f32[2,4,64,128]{3,2,1,0:T(8,128)S(1)}, u32[]{:S(2)}, u32[]{:S(2)}) collective-permute-start(f32[2,4,64,128]{3,2,1,0:T(8,128)S(1)} %shard_map.62.both), channel_id=1, source_target_pairs={{1,128},{2,129},{3,130},{4,131},{5,132},{6,133},{7,134},{8,135},{9... | collective-permute-start | bytes 786440 | tf_op jit(solution)/shard_map/ppermute | solution.py:451
  135.0 27.1 %collective-permute-start.18 = (f32[4,64,128]{2,1,0:T(8,128)S(1)}, f32[4,64,128]{2,1,0:T(8,128)S(1)}, u32[]{:S(2)}, u32[]{:S(2)}) collective-permute-start(f32[4,64,128]{2,1,0:T(8,128)S(1)} %get-tuple-element.25.last), channel_id=1, source_target_pairs={{0,1},{1,2},{2,3},{3,4},{4,5},{5,6},{6,7},{7,8},{8,9},{9,10},{10,1... | collective-permute-start | bytes 393224 | tf_op jit(solution)/shard_map/ppermute | solution.py:457
  139.0 26.6 %collective-permute-start.19 = (f32[4,64,128]{2,1,0:T(8,128)S(1)}, f32[4,64,128]{2,1,0:T(8,128)S(1)}, u32[]{:S(2)}, u32[]{:S(2)}) collective-permute-start(f32[4,64,128]{2,1,0:T(8,128)S(1)} %get-tuple-element.25.last), channel_id=1, source_target_pairs={{1,0},{2,1},{3,2},{4,3},{5,4},{6,5},{7,6},{8,7},{9,8},{10,9},{11,1... | collective-permute-start | bytes 393224 | tf_op jit(solution)/shard_map/ppermute | solution.py:457
  142.9 77.0 %collective-permute-start.4 = (f32[8,128,128]{2,1,0:T(8,128)S(1)}, f32[8,128,128]{2,1,0:T(8,128)S(1)}, u32[]{:S(2)}, u32[]{:S(2)}) collective-permute-start(f32[8,128,128]{2,1,0:T(8,128)S(1)} %get-tuple-element.20.second), channel_id=1, source_target_pairs={{192,256},{224,288},{448,0},{480,32},{193,257},{225,289},{449,1},{... | collective-permute-start | bytes 1572872 | tf_op jit(solution)/shard_map/ppermute | solution.py:460
  143.6 76.3 %collective-permute-start.8 = (f32[8,128,128]{2,1,0:T(8,128)S(1)}, f32[8,128,128]{2,1,0:T(8,128)S(1)}, u32[]{:S(2)}, u32[]{:S(2)}) collective-permute-start(f32[8,128,128]{2,1,0:T(8,128)S(1)} %collective-permute-done.7), channel_id=1, source_target_pairs={{0,256},{32,288},{64,320},{256,0},{288,32},{320,64},{1,257},{33,28... | collective-permute-start | bytes 1572872 | tf_op jit(solution)/shard_map/ppermute | solution.py:460
  144.3 77.1 %collective-permute-start.22 = (f32[8,128,128]{2,1,0:T(8,128)S(1)}, f32[8,128,128]{2,1,0:T(8,128)S(1)}, u32[]{:S(2)}, u32[]{:S(2)}) collective-permute-start(f32[8,128,128]{2,1,0:T(8,128)S(1)} %get-tuple-element.20.second), channel_id=1, source_target_pairs={{0,64},{32,96},{64,128},{96,160},{128,192},{160,224},{192,0},{224,... | collective-permute-start | bytes 1572872 | tf_op jit(solution)/shard_map/ppermute | solution.py:460
  162.1 12.6 %collective-permute-start.17 = (f32[4,128,128]{2,1,0:T(8,128)S(1)}, f32[4,128,128]{2,1,0:T(8,128)S(1)}, u32[]{:S(2)}, u32[]{:S(2)}) collective-permute-start(f32[4,128,128]{2,1,0:T(8,128)S(1)} %pad_maximum_fusion.2), channel_id=1, source_target_pairs={{0,2},{1,3},{2,4},{3,5},{4,6},{5,7},{6,8},{7,9},{8,10},{9,11},{10,... | collective-permute-start | bytes 786440 | tf_op jit(solution)/shard_map/ppermute | solution.py:457
  165.6 15.6 %collective-permute-start.20 = (f32[4,128,128]{2,1,0:T(8,128)S(1)}, f32[4,128,128]{2,1,0:T(8,128)S(1)}, u32[]{:S(2)}, u32[]{:S(2)}) collective-permute-start(f32[4,128,128]{2,1,0:T(8,128)S(1)} %pad_maximum_fusion.2), channel_id=1, source_target_pairs={{2,0},{3,1},{4,2},{5,3},{6,4},{7,5},{8,6},{9,7},{10,8},{11,9},{12,... | collective-permute-start | bytes 786440 | tf_op jit(solution)/shard_map/ppermute | solution.py:457
  185.0 36.4 %collective-permute-start.21 = (f32[4,64,128]{2,1,0:T(8,128)S(1)}, f32[4,64,128]{2,1,0:T(8,128)S(1)}, u32[]{:S(2)}, u32[]{:S(2)}) collective-permute-start(f32[4,64,128]{2,1,0:T(8,128)S(1)} %get-tuple-element.28), channel_id=1, source_target_pairs={{0,96},{32,128},{64,160},{96,192},{128,224},{160,0},{192,32},{224,... | collective-permute-start | bytes 393224 | tf_op jit(solution)/shard_map/ppermute | solution.py:460
  218.0 26.5 %collective-permute-start.23 = (f32[4,64,128]{2,1,0:T(8,128)S(1)}, f32[4,64,128]{2,1,0:T(8,128)S(1)}, u32[]{:S(2)}, u32[]{:S(2)}) collective-permute-start(f32[4,64,128]{2,1,0:T(8,128)S(1)} %get-tuple-element.30), channel_id=1, source_target_pairs={{0,352},{32,384},{64,416},{96,448},{128,480},{160,256},{192,288},{... | collective-permute-start | bytes 393224 | tf_op jit(solution)/shard_map/ppermute | solution.py:460

commit v5 on v4

--- a/solution.py
+++ b/solution.py
@@ -205,13 +205,16 @@
 
     @pl.when(where[0] == 13)
     def _():
-        first_out[...] = initial[:STEPS]
-        last_out[...] = initial[rows - STEPS :]
+        first_out[:STEPS] = initial[:STEPS]
+        last_out[:STEPS] = initial[rows - STEPS :]
 
     @pl.when(where[0] != 13)
     def _():
-        first_out[...] = second_out[:STEPS]
-        last_out[...] = second_out[rows - STEPS :]
+        first_out[:STEPS] = second_out[:STEPS]
+        last_out[:STEPS] = second_out[rows - STEPS :]
+
+    first_out[STEPS:] = down_2[STEPS:]
+    last_out[STEPS:] = up_2[STEPS:]
 
 
 def coarse_kappa_4(field, up_2, down_2, kappa_c, at):
@@ -232,7 +235,7 @@
 
 def phase_three_kernel(
     slabs, where, up_1, down_1, up_2, down_2, up_3, down_3, second, initial, kappa,
-    source, kappa_c, third_out, tau_out, *scratch,
+    source, kappa_c, _, third_out, tau_out, *scratch,
 ):
     state, other = scratch[:2]
     base, spare, kappa_wide, *weights = scratch[7:14]
@@ -369,8 +372,8 @@
 
 
 def hand_over_kernel(
-    slabs, where, far_up, near_up, last, near_down, far_down, up_2, down_2, kappa_c,
-    ahead, wrapped, handed_out, kept_out, *scratch,
+    slabs, where, far_up, near_up, last, near_down, far_down, up_2, down_2, up_3, down_3,
+    kappa_c, ahead, wrapped, handed_out, kept_out, *scratch,
 ):
     field, spare, kappa_wide, *weights = scratch
     block, half = kappa_c.shape[:2]
@@ -379,18 +382,18 @@
     clear_edges(field)
     clear_edges(spare)
     coarse_kappa_4(kappa_wide, up_2, down_2, kappa_c, block)
-    inner = slice(PAD, PAD + half)
     for row in range(block):
-        kappa_wide[row, inner] = far_up[row, half:]
-        kappa_wide[4 * block + row, inner] = far_down[row, half:]
-        field[row, inner] = far_up[row, :half]
-        field[4 * block + row, inner] = far_down[row, :half]
+        piece = (STEPS + row // 2, slice(row % 2 * half, (row % 2 + 1) * half))
+        kappa_wide[row, PAD : PAD + half] = up_3[piece]
+        kappa_wide[4 * block + row, PAD : PAD + half] = down_3[piece]
     fill(
         field,
         [
+            (far_up, 0, block, 0),
             (near_up, 0, block, block),
             (last, 0, block, 2 * block),
             (near_down, 0, block, 3 * block),
+            (far_down, 0, block, 4 * block),
         ],
     )
     face_weights(kappa_wide, weights, 4.0 * ALONG_THIRD)
@@ -422,12 +425,15 @@
         src, dst = dst, src
 
 
-def call(kernel, slabs, outs, scratch, where, *args):
+def call(kernel, slabs, outs, scratch, where, *args, unread=0):
     vmem = pl.BlockSpec(memory_space=pltpu.VMEM)
+    anywhere = pl.BlockSpec(memory_space=pl.ANY)
     return pl.pallas_call(
         functools.partial(kernel, slabs),
         out_shape=[jax.ShapeDtypeStruct(shape, jnp.float32) for shape in outs],
-        in_specs=[pl.BlockSpec(memory_space=pltpu.SMEM)] + [vmem] * len(args),
+        in_specs=[pl.BlockSpec(memory_space=pltpu.SMEM)]
+        + [vmem] * (len(args) - unread)
+        + [anywhere] * unread,
         out_specs=[vmem] * len(outs),
         scratch_shapes=scratch,
         compiler_params=pltpu.CompilerParams(vmem_limit_bytes=40 * 2**20),
@@ -474,7 +480,6 @@
 
     block_shape = (rows, width_two, width_three)
     coarse_shape = (crows, half, width_three)
-    edge_shape = (STEPS, width_two, width_three)
     packed_shape = (STEPS + crows // 2, width_two, width_three)
     scratch = fine_scratch(rows, width_two, width_three)
 
@@ -493,24 +498,27 @@
     )
     sides_2 = neighbours(first, last)
     second, first, last = call(
-        phase_two_kernel, slabs, [block_shape, edge_shape, edge_shape], scratch,
+        phase_two_kernel, slabs, [block_shape, packed_shape, packed_shape], scratch,
         where, *sides, *sides_2, state, initial, conductivity, source,
     )
     sides_3 = neighbours(first, last)
-    second_far = along_time(second, [(6, 8), (7, 9), (14, 0), (15, 1)])
+    second_near = along_time(second, ring(2))
+    second_far = along_time(second_near, [(0, 8), (1, 9), (8, 0), (9, 1)])
     third, tau = call(
         phase_three_kernel, slabs, [block_shape, coarse_shape],
         scratch
         + coarse_scratch(3 * crows, half, width_three, 2)
         + [pltpu.VMEM((width_two, width_three), jnp.float32)],
         where, *sides, *sides_2, *sides_3, second, initial, conductivity, source, kappa_c,
+        second_near, unread=1,
     )
 
     up, down = neighbours(tau, tau)
     tau_wide = jnp.concatenate([up, tau, down], 0)
     got = [along_time(cut(tau_wide, crows, d), ring(d)) for d in (3, 2, 1)]
-    third_near = along_time(third, ring(3))
-    third_far = along_time(third_near, [(i, i ^ GROUP) for i in (0, 1, 2, 8, 9, 10)])
+    third_far = along_time(
+        third, [(i, (i + 3) % (2 * GROUP)) for i in (5, 6, 7, 13, 14, 15)]
+    )
     (both,) = call(
         near_sums_kernel, slabs, [(2,) + coarse_shape],
         coarse_scratch(3 * crows, half, width_three, 3),
@@ -533,13 +541,14 @@
         where, *got, both, *sides_2, kappa_c,
     )
 
+    third_near = along_time(lax.optimization_barrier((third, last))[0], ring(3))
     near = neighbours(last, last)
-    two = jnp.concatenate([last, kappa_c], 1)
-    far = (along_space(two, 2), along_space(two, -2))
+    far = (along_space(last, 2), along_space(last, -2))
     handed, kept = call(
         hand_over_kernel, slabs, [coarse_shape] * 2,
         coarse_scratch(5 * crows, half, width_three, 2),
-        where, far[0], near[0], last, near[1], far[1], *sides_2, kappa_c, ahead, wrapped,
+        where, far[0], near[0], last, near[1], far[1], *sides_2, *sides_3, kappa_c,
+        ahead, wrapped,
     )
     handed = along_time(
         handed,
@@ -551,7 +560,6 @@
     )
     kept = along_time(kept, ring(3))
     second_far, third_far = lax.optimization_barrier((second_far, third_far, kept))[:2]
-    second_near = along_time(second, ring(2))
     third_home = jnp.where(local < 3, third_far, third_near)
     second_home = jnp.where(local < 2, second_far, second_near)
 

time: 246 us -> 235 us (0.955)
  starting transfers between devices: 128 us -> 104 us
  waiting for transfers between devices: 87 us -> 98.4 us
    ppermute x9, starting transfers between devices: 63.8 us -> 48.1 us  [along_time(): return lax.ppermute(block, 'tm', pairs)]
    ppermute x12, waiting for transfers between devices: 41.8 us -> 53.5 us  [along_space(): return lax.ppermute(block, 'space', pairs)]
    ppermute x12, starting transfers between devices: 47.7 us -> 41.8 us  [along_space(): return lax.ppermute(block, 'space', pairs)]
  transfers between devices with their start and end apart: 24 -> 24, of which waited for: 15 -> 17; matrix products, arithmetic and copies ran while one was open for 2% -> 2% of each run, Pallas kernels for 4% -> 3%
where the time goes in v5:
time: 235 us; the launch traced here: 234 us
  starting transfers between devices  104 us (44%)
  waiting for transfers between devices  98.4 us (42%)
  Pallas kernels  21.8 us (9%)
  other arithmetic  7.32 us (3%)
    ppermute x12, waiting for transfers between devices, along_space(): return lax.ppermute(block, 'space', pairs)  53.5 us
    ppermute x9, starting transfers between devices, along_time(): return lax.ppermute(block, 'tm', pairs)  48.1 us
    ppermute x12, starting transfers between devices, along_space(): return lax.ppermute(block, 'space', pairs)  41.8 us
    ppermute x9, waiting for transfers between devices, along_time(): return lax.ppermute(block, 'tm', pairs)  35.7 us
    pallas_call x6, Pallas kernels, call(): pl.pallas_call(functools.partial(kernel, slabs), out_shape=[jax.ShapeDtyp...  21.8 us
    ppermute x3, starting transfers between devices, route(): return lax.ppermute(block, ('tm', 'space'), pairs)  14 us
    ppermute x3, waiting for transfers between devices, route(): return lax.ppermute(block, ('tm', 'space'), pairs)  9.27 us
  transfers between devices with their start and end apart: 24, of which 17 were waited for; matrix products, arithmetic and copies ran while one was open for 2% of the time, Pallas kernels for 3%

profile of v5, /device:TPU:36, one launch (start us, length us, event | category | flops | bytes accessed | tf_op | source)
XLA Modules:
  0.0 233.9 jit_solution(193935235246130768)
XLA Ops:
  4.1 4.5 %collective-permute-start.1 = (f32[11,128,128]{2,1,0:T(8,128)}, f32[11,128,128]{2,1,0:T(8,128)S(1)}, u32[]{:S(2)}, u32[]{:S(2)}) collective-permute-start(f32[11,128,128]{2,1,0:T(8,128)} %pad_maximum_fusion.1), channel_id=1, source_target_pairs={{1,0},{2,1},{3,2},{4,3},{5,4},{6,5},{7,6},{8,7},{9,8},{10,9},{11,1... | collective-permute-start | bytes 2162696 | tf_op jit(solution)/shard_map/ppermute | solution.py:463
  9.5 2.0 collective-permute-start
  13.6 10.7 %collective-permute-done.1.down_1 = f32[11,128,128]{2,1,0:T(8,128)S(1)} collective-permute-done((f32[11,128,128]{2,1,0:T(8,128)}, f32[11,128,128]{2,1,0:T(8,128)S(1)}, u32[]{:S(2)}, u32[]{:S(2)}) %collective-permute-start.1) | collective-permute-done | bytes 720928 | tf_op jit(solution)/shard_map/ppermute | solution.py:463
  24.2 7.2 %collective-permute-done.up_1 = f32[11,128,128]{2,1,0:T(8,128)S(1)} collective-permute-done((f32[11,128,128]{2,1,0:T(8,128)}, f32[11,128,128]{2,1,0:T(8,128)S(1)}, u32[]{:S(2)}, u32[]{:S(2)}) %collective-permute-start) | collective-permute-done | bytes 720928 | tf_op jit(solution)/shard_map/ppermute | solution.py:463
  31.4 3.9 %shard_map.59 = (f32[8,128,128]{2,1,0:T(8,128)S(1)}, f32[6,128,128]{2,1,0:T(8,128)S(1)}, f32[6,128,128]{2,1,0:T(8,128)S(1)}) custom-call(s32[2]{0:T(128)S(1)} %pad_add_fusion.where, f32[11,128,128]{2,1,0:T(8,128)S(1)} %collective-permute-done.up_1, f32[11,128,128]{2,1,0:T(8,128)S(1)} %collective-permute-done.1.down_1, f32[8,128,128]{2,1,0:T(8,128)S(1)} %bitcast.16, ...), custom_call_target="tpu_custom_call" | custom-call | tf_op jit(solution)/shard_map/pallas_call | solution.py:431
  37.3 6.0 %collective-permute-start.3 = (f32[6,128,128]{2,1,0:T(8,128)S(1)}, f32[6,128,128]{2,1,0:T(8,128)S(1)}, u32[]{:S(2)}, u32[]{:S(2)}) collective-permute-start(f32[6,128,128]{2,1,0:T(8,128)S(1)} %get-tuple-element.19), channel_id=1, source_target_pairs={{1,0},{2,1},{3,2},{4,3},{5,4},{6,5},{7,6},{8,7},{9,8},{10,9},{11,1... | collective-permute-start | bytes 1179656 | tf_op jit(solution)/shard_map/ppermute | solution.py:463
  43.3 5.7 %collective-permute-done.2.up_2 = f32[6,128,128]{2,1,0:T(8,128)S(1)} collective-permute-done((f32[6,128,128]{2,1,0:T(8,128)S(1)}, f32[6,128,128]{2,1,0:T(8,128)S(1)}, u32[]{:S(2)}, u32[]{:S(2)}) %collective-permute-start.2) | collective-permute-done | bytes 393248 | tf_op jit(solution)/shard_map/ppermute | solution.py:463
  50.2 3.9 %shard_map.60 = (f32[8,128,128]{2,1,0:T(8,128)S(1)}, f32[6,128,128]{2,1,0:T(8,128)S(1)}, f32[6,128,128]{2,1,0:T(8,128)S(1)}) custom-call(s32[2]{0:T(128)S(1)} %pad_add_fusion.where, f32[11,128,128]{2,1,0:T(8,128)S(1)} %collective-permute-done.up_1, f32[11,128,128]{2,1,0:T(8,128)S(1)} %collective-permute-done.1.down_1, ...), custom_call_target="tpu_custom_call" | custom-call | tf_op jit(solution)/shard_map/pallas_call | solution.py:431
  54.2 3.1 %collective-permute-start.4 = (f32[8,128,128]{2,1,0:T(8,128)S(1)}, f32[8,128,128]{2,1,0:T(8,128)S(1)}, u32[]{:S(2)}, u32[]{:S(2)}) collective-permute-start(f32[8,128,128]{2,1,0:T(8,128)S(1)} %get-tuple-element.21.second), channel_id=1, source_target_pairs={{0,64},{32,96},{64,128},{96,160},{128,192},{160,224},{192,0},{224,... | collective-permute-start | bytes 1572872 | tf_op jit(solution)/shard_map/ppermute | solution.py:466
  59.2 6.5 %collective-permute-start.7 = (f32[6,128,128]{2,1,0:T(8,128)S(1)}, f32[6,128,128]{2,1,0:T(8,128)S(1)}, u32[]{:S(2)}, u32[]{:S(2)}) collective-permute-start(f32[6,128,128]{2,1,0:T(8,128)S(1)} %get-tuple-element.23), channel_id=1, source_target_pairs={{1,0},{2,1},{3,2},{4,3},{5,4},{6,5},{7,6},{8,7},{9,8},{10,9},{11,1... | collective-permute-start | bytes 1179656 | tf_op jit(solution)/shard_map/ppermute | solution.py:463
  65.7 4.5 %collective-permute-done.6.up_3 = f32[6,128,128]{2,1,0:T(8,128)S(1)} collective-permute-done((f32[6,128,128]{2,1,0:T(8,128)S(1)}, f32[6,128,128]{2,1,0:T(8,128)S(1)}, u32[]{:S(2)}, u32[]{:S(2)}) %collective-permute-start.6) | collective-permute-done | bytes 393248 | tf_op jit(solution)/shard_map/ppermute | solution.py:463
  71.4 5.2 %shard_map.61 = (f32[8,128,128]{2,1,0:T(8,128)}, f32[4,64,128]{2,1,0:T(8,128)S(1)}) custom-call(s32[2]{0:T(128)S(1)} %pad_add_fusion.where, f32[11,128,128]{2,1,0:T(8,128)S(1)} %collective-permute-done.up_1, f32[11,128,128]{2,1,0:T(8,128)S(1)} %collective-permute-done.1.down_1, f32[6,128,128]{2,1,0:T(8,128)S(1)} %collective-permute-done.2.up_2, ...), custom_call_target="tpu_custom_call" | custom-call | tf_op jit(solution)/shard_map/pallas_call | solution.py:431
  76.6 4.2 %collective-permute-start.9 = (f32[4,64,128]{2,1,0:T(8,128)S(1)}, f32[4,64,128]{2,1,0:T(8,128)S(1)}, u32[]{:S(2)}, u32[]{:S(2)}) collective-permute-start(f32[4,64,128]{2,1,0:T(8,128)S(1)} %get-tuple-element.25.tau), channel_id=1, source_target_pairs={{0,1},{1,2},{2,3},{3,4},{4,5},{5,6},{6,7},{7,8},{8,9},{9,10},{10,1... | collective-permute-start | bytes 393224 | tf_op jit(solution)/shard_map/ppermute | solution.py:463
  80.8 4.2 %collective-permute-start.10 = (f32[4,64,128]{2,1,0:T(8,128)S(1)}, f32[4,64,128]{2,1,0:T(8,128)S(1)}, u32[]{:S(2)}, u32[]{:S(2)}) collective-permute-start(f32[4,64,128]{2,1,0:T(8,128)S(1)} %get-tuple-element.25.tau), channel_id=1, source_target_pairs={{1,0},{2,1},{3,2},{4,3},{5,4},{6,5},{7,6},{8,7},{9,8},{10,9},{11,1... | collective-permute-start | bytes 393224 | tf_op jit(solution)/shard_map/ppermute | solution.py:463
  89.7 2.4 %collective-permute-start.12 = (f32[8,64,128]{2,1,0:T(8,128)S(1)}, f32[8,64,128]{2,1,0:T(8,128)S(1)}, u32[]{:S(2)}, u32[]{:S(2)}) collective-permute-start(f32[8,64,128]{2,1,0:T(8,128)S(1)} %slice.53), channel_id=1, source_target_pairs={{0,64},{32,96},{64,128},{96,160},{128,192},{160,224},{192,0},{224,... | collective-permute-start | bytes 786440 | tf_op jit(solution)/shard_map/ppermute | solution.py:466
  92.1 2.3 collective-permute-start.13
  94.4 12.4 %collective-permute-done.13.got_1 = f32[6,64,128]{2,1,0:T(8,128)S(1)} collective-permute-done((f32[6,64,128]{2,1,0:T(8,128)S(1)}, f32[6,64,128]{2,1,0:T(8,128)S(1)}, u32[]{:S(2)}, u32[]{:S(2)}) %collective-permute-start.13) | collective-permute-done | bytes 196640 | tf_op jit(solution)/shard_map/ppermute | solution.py:466
  106.8 2.1 shard_map.62.both
  108.9 5.2 %collective-permute-start.14 = (f32[2,4,64,128]{3,2,1,0:T(8,128)S(1)}, f32[2,4,64,128]{3,2,1,0:T(8,128)S(1)}, u32[]{:S(2)}, u32[]{:S(2)}) collective-permute-start(f32[2,4,64,128]{3,2,1,0:T(8,128)S(1)} %shard_map.62.both), channel_id=1, source_target_pairs={{0,129},{1,130},{2,131},{3,132},{4,133},{5,134},{6,135},{7,136},{8... | collective-permute-start | bytes 786440 | tf_op jit(solution)/shard_map/ppermute | solution.py:457
  114.1 3.7 %collective-permute-start.15 = (f32[2,4,64,128]{3,2,1,0:T(8,128)S(1)}, f32[2,4,64,128]{3,2,1,0:T(8,128)S(1)}, u32[]{:S(2)}, u32[]{:S(2)}) collective-permute-start(f32[2,4,64,128]{3,2,1,0:T(8,128)S(1)} %shard_map.62.both), channel_id=1, source_target_pairs={{0,128},{1,129},{2,130},{3,131},{4,132},{5,133},{6,134},{7,135},{8... | collective-permute-start | bytes 786440 | tf_op jit(solution)/shard_map/ppermute | solution.py:457
  117.8 5.1 %collective-permute-start.16 = (f32[2,4,64,128]{3,2,1,0:T(8,128)S(1)}, f32[2,4,64,128]{3,2,1,0:T(8,128)S(1)}, u32[]{:S(2)}, u32[]{:S(2)}) collective-permute-start(f32[2,4,64,128]{3,2,1,0:T(8,128)S(1)} %shard_map.62.both), channel_id=1, source_target_pairs={{1,128},{2,129},{3,130},{4,131},{5,132},{6,133},{7,134},{8,135},{9... | collective-permute-start | bytes 786440 | tf_op jit(solution)/shard_map/ppermute | solution.py:457
  124.3 7.8 %collective-permute-done.15.got = f32[2,4,64,128]{3,2,1,0:T(8,128)S(1)} collective-permute-done((f32[2,4,64,128]{3,2,1,0:T(8,128)S(1)}, f32[2,4,64,128]{3,2,1,0:T(8,128)S(1)}, u32[]{:S(2)}, u32[]{:S(2)}) %collective-permute-start.15) | collective-permute-done | bytes 262176 | tf_op jit(solution)/shard_map/ppermute | solution.py:457
  133.6 2.8 %shard_map.63 = (f32[4,64,128]{2,1,0:T(8,128)S(1)}, f32[4,64,128]{2,1,0:T(8,128)S(1)}, f32[4,64,128]{2,1,0:T(8,128)S(1)}) custom-call(s32[2]{0:T(128)S(1)} %pad_add_fusion.where, f32[2,4,64,128]{3,2,1,0:T(8,128)S(1)} %collective-permute-done.14.got_up, f32[2,4,64,128]{3,2,1,0:T(8,128)S(1)} %collective-permute-done.15.got, ...), custom_call_target="tpu_custom_call" | custom-call | tf_op jit(solution)/shard_map/pallas_call | solution.py:431
  136.4 9.7 %collective-permute-start.23 = (f32[8,128,128]{2,1,0:T(8,128)}, f32[8,128,128]{2,1,0:T(8,128)S(1)}, u32[]{:S(2)}, u32[]{:S(2)}) collective-permute-start(f32[8,128,128]{2,1,0:T(8,128)} %get-tuple-element.33), channel_id=1, source_target_pairs={{0,96},{32,128},{64,160},{96,192},{128,224},{160,0},{192,32},{224,... | collective-permute-start | bytes 1572872 | tf_op jit(solution)/shard_map/ppermute | solution.py:466
  146.1 3.3 %collective-permute-start.17 = (f32[4,64,128]{2,1,0:T(8,128)S(1)}, f32[4,64,128]{2,1,0:T(8,128)S(1)}, u32[]{:S(2)}, u32[]{:S(2)}) collective-permute-start(f32[4,64,128]{2,1,0:T(8,128)S(1)} %get-tuple-element.26.last), channel_id=1, source_target_pairs={{0,2},{1,3},{2,4},{3,5},{4,6},{5,7},{6,8},{7,9},{8,10},{9,11},{10,... | collective-permute-start | bytes 393224 | tf_op jit(solution)/shard_map/ppermute | solution.py:463
  149.3 3.4 %collective-permute-start.18 = (f32[4,64,128]{2,1,0:T(8,128)S(1)}, f32[4,64,128]{2,1,0:T(8,128)S(1)}, u32[]{:S(2)}, u32[]{:S(2)}) collective-permute-start(f32[4,64,128]{2,1,0:T(8,128)S(1)} %get-tuple-element.26.last), channel_id=1, source_target_pairs={{0,1},{1,2},{2,3},{3,4},{4,5},{5,6},{6,7},{7,8},{8,9},{9,10},{10,1... | collective-permute-start | bytes 393224 | tf_op jit(solution)/shard_map/ppermute | solution.py:463
  152.8 12.0 %collective-permute-done.17.far_up = f32[4,64,128]{2,1,0:T(8,128)S(1)} collective-permute-done((f32[4,64,128]{2,1,0:T(8,128)S(1)}, f32[4,64,128]{2,1,0:T(8,128)S(1)}, u32[]{:S(2)}, u32[]{:S(2)}) %collective-permute-start.17) | collective-permute-done | bytes 131104 | tf_op jit(solution)/shard_map/ppermute | solution.py:463
  171.6 5.4 %collective-permute-done.20.far_down = f32[4,64,128]{2,1,0:T(8,128)S(1)} collective-permute-done((f32[4,64,128]{2,1,0:T(8,128)S(1)}, f32[4,64,128]{2,1,0:T(8,128)S(1)}, u32[]{:S(2)}, u32[]{:S(2)}) %collective-permute-start.20) | collective-permute-done | bytes 131104 | tf_op jit(solution)/shard_map/ppermute | solution.py:463
  177.0 3.8 %shard_map.64 = (f32[4,64,128]{2,1,0:T(8,128)S(1)}, f32[4,64,128]{2,1,0:T(8,128)S(1)}) custom-call(s32[2]{0:T(128)S(1)} %pad_add_fusion.where, f32[4,64,128]{2,1,0:T(8,128)S(1)} %collective-permute-done.17.far_up, f32[4,64,128]{2,1,0:T(8,128)S(1)} %collective-permute-done.18.near_up, f32[4,64,128]{2,1,0:T(8,128)S(1)} %get-tuple-element.26.last, ...), custom_call_target="tpu_custom_call" | custom-call | tf_op jit(solution)/shard_map/pallas_call | solution.py:431
  180.9 25.2 %collective-permute-start.21 = (f32[4,64,128]{2,1,0:T(8,128)S(1)}, f32[4,64,128]{2,1,0:T(8,128)S(1)}, u32[]{:S(2)}, u32[]{:S(2)}) collective-permute-start(f32[4,64,128]{2,1,0:T(8,128)S(1)} %get-tuple-element.29), channel_id=1, source_target_pairs={{0,96},{32,128},{64,160},{96,192},{128,224},{160,0},{192,32},{224,... | collective-permute-start | bytes 393224 | tf_op jit(solution)/shard_map/ppermute | solution.py:466
  206.1 2.2 collective-permute-start.22
  210.2 22.6 %collective-permute-done.22 = f32[4,64,128]{2,1,0:T(8,128)S(1)} collective-permute-done((f32[4,64,128]{2,1,0:T(8,128)S(1)}, f32[4,64,128]{2,1,0:T(8,128)S(1)}, u32[]{:S(2)}, u32[]{:S(2)}) %collective-permute-start.22) | collective-permute-done | bytes 131104 | tf_op jit(solution)/shard_map/ppermute | solution.py:466
  (49 shorter events, 30.0 us)
Async XLA Ops:
  0.6 1.2 copy-start
  4.1 20.2 %collective-permute-start.1 = (f32[11,128,128]{2,1,0:T(8,128)}, f32[11,128,128]{2,1,0:T(8,128)S(1)}, u32[]{:S(2)}, u32[]{:S(2)}) collective-permute-start(f32[11,128,128]{2,1,0:T(8,128)} %pad_maximum_fusion.1), channel_id=1, source_target_pairs={{1,0},{2,1},{3,2},{4,3},{5,4},{6,5},{7,6},{8,7},{9,8},{10,9},{11,1... | collective-permute-start | bytes 2162696 | tf_op jit(solution)/shard_map/ppermute | solution.py:463
  8.5 22.9 %copy-start.2 = (f32[8,128,128]{2,1,0:T(8,128)S(1)}, f32[8,128,128]{2,1,0:T(8,128)}, u32[]{:S(2)}) copy-start(f32[8,128,128]{2,1,0:T(8,128)} %source.5) | copy-start | bytes 1572868
  8.6 22.9 %copy-start.3 = (f32[1,8,128,128]{3,2,1,0:T(8,128)S(1)}, f32[1,8,128,128]{3,2,1,0:T(8,128)}, u32[]{:S(2)}) copy-start(f32[1,8,128,128]{3,2,1,0:T(8,128)} %param.5) | copy-start | bytes 1572868
  9.5 21.9 %copy-start.1 = (f32[8,128,128]{2,1,0:T(8,128)S(1)}, f32[8,128,128]{2,1,0:T(8,128)}, u32[]{:S(2)}) copy-start(f32[8,128,128]{2,1,0:T(8,128)} %initial.5) | copy-start | bytes 1572868
  9.5 21.9 %collective-permute-start = (f32[11,128,128]{2,1,0:T(8,128)}, f32[11,128,128]{2,1,0:T(8,128)S(1)}, u32[]{:S(2)}, u32[]{:S(2)}) collective-permute-start(f32[11,128,128]{2,1,0:T(8,128)} %pad_maximum_fusion), channel_id=1, source_target_pairs={{0,1},{1,2},{2,3},{3,4},{4,5},{5,6},{6,7},{7,8},{8,9},{9,10},{10,1... | collective-permute-start | bytes 2162696 | tf_op jit(solution)/shard_map/ppermute | solution.py:463
  35.4 13.7 %collective-permute-start.2 = (f32[6,128,128]{2,1,0:T(8,128)S(1)}, f32[6,128,128]{2,1,0:T(8,128)S(1)}, u32[]{:S(2)}, u32[]{:S(2)}) collective-permute-start(f32[6,128,128]{2,1,0:T(8,128)S(1)} %get-tuple-element.18), channel_id=1, source_target_pairs={{0,1},{1,2},{2,3},{3,4},{4,5},{5,6},{6,7},{7,8},{8,9},{9,10},{10,1... | collective-permute-start | bytes 1179656 | tf_op jit(solution)/shard_map/ppermute | solution.py:463
  37.3 12.9 %collective-permute-start.3 = (f32[6,128,128]{2,1,0:T(8,128)S(1)}, f32[6,128,128]{2,1,0:T(8,128)S(1)}, u32[]{:S(2)}, u32[]{:S(2)}) collective-permute-start(f32[6,128,128]{2,1,0:T(8,128)S(1)} %get-tuple-element.19), channel_id=1, source_target_pairs={{1,0},{2,1},{3,2},{4,3},{5,4},{6,5},{7,6},{8,7},{9,8},{10,9},{11,1... | collective-permute-start | bytes 1179656 | tf_op jit(solution)/shard_map/ppermute | solution.py:463
  54.2 17.2 %collective-permute-start.4 = (f32[8,128,128]{2,1,0:T(8,128)S(1)}, f32[8,128,128]{2,1,0:T(8,128)S(1)}, u32[]{:S(2)}, u32[]{:S(2)}) collective-permute-start(f32[8,128,128]{2,1,0:T(8,128)S(1)} %get-tuple-element.21.second), channel_id=1, source_target_pairs={{0,64},{32,96},{64,128},{96,160},{128,192},{160,224},{192,0},{224,... | collective-permute-start | bytes 1572872 | tf_op jit(solution)/shard_map/ppermute | solution.py:466
  57.3 12.9 %collective-permute-start.6 = (f32[6,128,128]{2,1,0:T(8,128)S(1)}, f32[6,128,128]{2,1,0:T(8,128)S(1)}, u32[]{:S(2)}, u32[]{:S(2)}) collective-permute-start(f32[6,128,128]{2,1,0:T(8,128)S(1)} %get-tuple-element.22), channel_id=1, source_target_pairs={{0,1},{1,2},{2,3},{3,4},{4,5},{5,6},{6,7},{7,8},{8,9},{9,10},{10,1... | collective-permute-start | bytes 1179656 | tf_op jit(solution)/shard_map/ppermute | solution.py:463
  59.2 12.2 %collective-permute-start.7 = (f32[6,128,128]{2,1,0:T(8,128)S(1)}, f32[6,128,128]{2,1,0:T(8,128)S(1)}, u32[]{:S(2)}, u32[]{:S(2)}) collective-permute-start(f32[6,128,128]{2,1,0:T(8,128)S(1)} %get-tuple-element.23), channel_id=1, source_target_pairs={{1,0},{2,1},{3,2},{4,3},{5,4},{6,5},{7,6},{8,7},{9,8},{10,9},{11,1... | collective-permute-start | bytes 1179656 | tf_op jit(solution)/shard_map/ppermute | solution.py:463
  76.6 9.4 %collective-permute-start.9 = (f32[4,64,128]{2,1,0:T(8,128)S(1)}, f32[4,64,128]{2,1,0:T(8,128)S(1)}, u32[]{:S(2)}, u32[]{:S(2)}) collective-permute-start(f32[4,64,128]{2,1,0:T(8,128)S(1)} %get-tuple-element.25.tau), channel_id=1, source_target_pairs={{0,1},{1,2},{2,3},{3,4},{4,5},{5,6},{6,7},{7,8},{8,9},{9,10},{10,1... | collective-permute-start | bytes 393224 | tf_op jit(solution)/shard_map/ppermute | solution.py:463
  80.8 6.9 %collective-permute-start.10 = (f32[4,64,128]{2,1,0:T(8,128)S(1)}, f32[4,64,128]{2,1,0:T(8,128)S(1)}, u32[]{:S(2)}, u32[]{:S(2)}) collective-permute-start(f32[4,64,128]{2,1,0:T(8,128)S(1)} %get-tuple-element.25.tau), channel_id=1, source_target_pairs={{1,0},{2,1},{3,2},{4,3},{5,4},{6,5},{7,6},{8,7},{9,8},{10,9},{11,1... | collective-permute-start | bytes 393224 | tf_op jit(solution)/shard_map/ppermute | solution.py:463
  87.7 19.0 %collective-permute-start.11 = (f32[10,64,128]{2,1,0:T(8,128)S(1)}, f32[10,64,128]{2,1,0:T(8,128)S(1)}, u32[]{:S(2)}, u32[]{:S(2)}) collective-permute-start(f32[10,64,128]{2,1,0:T(8,128)S(1)} %slice.52), channel_id=1, source_target_pairs={{0,96},{32,128},{64,160},{96,192},{128,224},{160,0},{192,32},{224,... | collective-permute-start | bytes 983048 | tf_op jit(solution)/shard_map/ppermute | solution.py:466
  89.7 17.1 %collective-permute-start.12 = (f32[8,64,128]{2,1,0:T(8,128)S(1)}, f32[8,64,128]{2,1,0:T(8,128)S(1)}, u32[]{:S(2)}, u32[]{:S(2)}) collective-permute-start(f32[8,64,128]{2,1,0:T(8,128)S(1)} %slice.53), channel_id=1, source_target_pairs={{0,64},{32,96},{64,128},{96,160},{128,192},{160,224},{192,0},{224,... | collective-permute-start | bytes 786440 | tf_op jit(solution)/shard_map/ppermute | solution.py:466
  92.1 14.6 %collective-permute-start.13 = (f32[6,64,128]{2,1,0:T(8,128)S(1)}, f32[6,64,128]{2,1,0:T(8,128)S(1)}, u32[]{:S(2)}, u32[]{:S(2)}) collective-permute-start(f32[6,64,128]{2,1,0:T(8,128)S(1)} %slice.54), channel_id=1, source_target_pairs={{0,32},{32,64},{64,96},{96,128},{128,160},{160,192},{192,224},{224... | collective-permute-start | bytes 589832 | tf_op jit(solution)/shard_map/ppermute | solution.py:466
  108.9 15.4 %collective-permute-start.14 = (f32[2,4,64,128]{3,2,1,0:T(8,128)S(1)}, f32[2,4,64,128]{3,2,1,0:T(8,128)S(1)}, u32[]{:S(2)}, u32[]{:S(2)}) collective-permute-start(f32[2,4,64,128]{3,2,1,0:T(8,128)S(1)} %shard_map.62.both), channel_id=1, source_target_pairs={{0,129},{1,130},{2,131},{3,132},{4,133},{5,134},{6,135},{7,136},{8... | collective-permute-start | bytes 786440 | tf_op jit(solution)/shard_map/ppermute | solution.py:457
  114.1 18.0 %collective-permute-start.15 = (f32[2,4,64,128]{3,2,1,0:T(8,128)S(1)}, f32[2,4,64,128]{3,2,1,0:T(8,128)S(1)}, u32[]{:S(2)}, u32[]{:S(2)}) collective-permute-start(f32[2,4,64,128]{3,2,1,0:T(8,128)S(1)} %shard_map.62.both), channel_id=1, source_target_pairs={{0,128},{1,129},{2,130},{3,131},{4,132},{5,133},{6,134},{7,135},{8... | collective-permute-start | bytes 786440 | tf_op jit(solution)/shard_map/ppermute | solution.py:457
  117.8 15.8 %collective-permute-start.16 = (f32[2,4,64,128]{3,2,1,0:T(8,128)S(1)}, f32[2,4,64,128]{3,2,1,0:T(8,128)S(1)}, u32[]{:S(2)}, u32[]{:S(2)}) collective-permute-start(f32[2,4,64,128]{3,2,1,0:T(8,128)S(1)} %shard_map.62.both), channel_id=1, source_target_pairs={{1,128},{2,129},{3,130},{4,131},{5,132},{6,133},{7,134},{8,135},{9... | collective-permute-start | bytes 786440 | tf_op jit(solution)/shard_map/ppermute | solution.py:457
  122.9 85.3 %collective-permute-start.8 = (f32[8,128,128]{2,1,0:T(8,128)}, f32[8,128,128]{2,1,0:T(8,128)S(1)}, u32[]{:S(2)}, u32[]{:S(2)}) collective-permute-start(f32[8,128,128]{2,1,0:T(8,128)} %get-tuple-element.33), channel_id=1, source_target_pairs={{160,256},{192,288},{224,320},{416,0},{448,32},{480,64},{161,257},... | collective-permute-start | bytes 1572872 | tf_op jit(solution)/shard_map/ppermute | solution.py:466
  123.6 84.7 %collective-permute-start.5 = (f32[8,128,128]{2,1,0:T(8,128)S(1)}, f32[8,128,128]{2,1,0:T(8,128)S(1)}, u32[]{:S(2)}, u32[]{:S(2)}) collective-permute-start(f32[8,128,128]{2,1,0:T(8,128)S(1)} %collective-permute-done.4._), channel_id=1, source_target_pairs={{0,256},{32,288},{256,0},{288,32},{1,257},{33,289},{257,1},{289,33... | collective-permute-start | bytes 1572872 | tf_op jit(solution)/shard_map/ppermute | solution.py:466
  136.4 72.6 %collective-permute-start.23 = (f32[8,128,128]{2,1,0:T(8,128)}, f32[8,128,128]{2,1,0:T(8,128)S(1)}, u32[]{:S(2)}, u32[]{:S(2)}) collective-permute-start(f32[8,128,128]{2,1,0:T(8,128)} %get-tuple-element.33), channel_id=1, source_target_pairs={{0,96},{32,128},{64,160},{96,192},{128,224},{160,0},{192,32},{224,... | collective-permute-start | bytes 1572872 | tf_op jit(solution)/shard_map/ppermute | solution.py:466
  146.1 18.7 %collective-permute-start.17 = (f32[4,64,128]{2,1,0:T(8,128)S(1)}, f32[4,64,128]{2,1,0:T(8,128)S(1)}, u32[]{:S(2)}, u32[]{:S(2)}) collective-permute-start(f32[4,64,128]{2,1,0:T(8,128)S(1)} %get-tuple-element.26.last), channel_id=1, source_target_pairs={{0,2},{1,3},{2,4},{3,5},{4,6},{5,7},{6,8},{7,9},{8,10},{9,11},{10,... | collective-permute-start | bytes 393224 | tf_op jit(solution)/shard_map/ppermute | solution.py:463
  149.3 19.3 %collective-permute-start.18 = (f32[4,64,128]{2,1,0:T(8,128)S(1)}, f32[4,64,128]{2,1,0:T(8,128)S(1)}, u32[]{:S(2)}, u32[]{:S(2)}) collective-permute-start(f32[4,64,128]{2,1,0:T(8,128)S(1)} %get-tuple-element.26.last), channel_id=1, source_target_pairs={{0,1},{1,2},{2,3},{3,4},{4,5},{5,6},{6,7},{7,8},{8,9},{9,10},{10,1... | collective-permute-start | bytes 393224 | tf_op jit(solution)/shard_map/ppermute | solution.py:463
  164.8 6.8 %collective-permute-start.19 = (f32[4,64,128]{2,1,0:T(8,128)S(1)}, f32[4,64,128]{2,1,0:T(8,128)S(1)}, u32[]{:S(2)}, u32[]{:S(2)}) collective-permute-start(f32[4,64,128]{2,1,0:T(8,128)S(1)} %get-tuple-element.26.last), channel_id=1, source_target_pairs={{1,0},{2,1},{3,2},{4,3},{5,4},{6,5},{7,6},{8,7},{9,8},{10,9},{11,1... | collective-permute-start | bytes 393224 | tf_op jit(solution)/shard_map/ppermute | solution.py:463
  168.7 8.4 %collective-permute-start.20 = (f32[4,64,128]{2,1,0:T(8,128)S(1)}, f32[4,64,128]{2,1,0:T(8,128)S(1)}, u32[]{:S(2)}, u32[]{:S(2)}) collective-permute-start(f32[4,64,128]{2,1,0:T(8,128)S(1)} %get-tuple-element.26.last), channel_id=1, source_target_pairs={{2,0},{3,1},{4,2},{5,3},{6,4},{7,5},{8,6},{9,7},{10,8},{11,9},{12,... | collective-permute-start | bytes 393224 | tf_op jit(solution)/shard_map/ppermute | solution.py:463
  180.9 28.1 %collective-permute-start.21 = (f32[4,64,128]{2,1,0:T(8,128)S(1)}, f32[4,64,128]{2,1,0:T(8,128)S(1)}, u32[]{:S(2)}, u32[]{:S(2)}) collective-permute-start(f32[4,64,128]{2,1,0:T(8,128)S(1)} %get-tuple-element.29), channel_id=1, source_target_pairs={{0,96},{32,128},{64,160},{96,192},{128,224},{160,0},{192,32},{224,... | collective-permute-start | bytes 393224 | tf_op jit(solution)/shard_map/ppermute | solution.py:466
  206.1 26.7 %collective-permute-start.22 = (f32[4,64,128]{2,1,0:T(8,128)S(1)}, f32[4,64,128]{2,1,0:T(8,128)S(1)}, u32[]{:S(2)}, u32[]{:S(2)}) collective-permute-start(f32[4,64,128]{2,1,0:T(8,128)S(1)} %get-tuple-element.31), channel_id=1, source_target_pairs={{0,352},{32,384},{64,416},{96,448},{128,480},{160,256},{192,288},{... | collective-permute-start | bytes 393224 | tf_op jit(solution)/shard_map/ppermute | solution.py:466

commit v6 on v5

--- a/solution.py
+++ b/solution.py
@@ -147,6 +147,23 @@
         src, dst = dst, src
 
 
+def first_ends_kernel(where, guess, initial, kappa, source, first_out, last_out):
+    rows = kappa.shape[0]
+    start = where[0] == 15
+    for out, at, heat in ((first_out, 0, 0), (last_out, rows - STEPS, rows - STEPS + 1)):
+
+        @pl.when(start)
+        def _(out=out, at=at):
+            out[:STEPS] = initial[at : at + STEPS]
+
+        @pl.when(jnp.logical_not(start))
+        def _(out=out, at=at):
+            out[:STEPS] = guess[at : at + STEPS]
+
+        out[STEPS : 2 * STEPS] = kappa[at : at + STEPS]
+        out[2 * STEPS :] = source[heat : heat + STEPS - 1]
+
+
 def phase_one_kernel(
     slabs, where, up_1, down_1, guess, initial, kappa, source, kappa_c,
     state_out, first_out, last_out, *scratch,
@@ -235,7 +252,7 @@
 
 def phase_three_kernel(
     slabs, where, up_1, down_1, up_2, down_2, up_3, down_3, second, initial, kappa,
-    source, kappa_c, _, third_out, tau_out, *scratch,
+    source, kappa_c, second_near, third_out, tau_out, cross_out, *scratch,
 ):
     state, other = scratch[:2]
     base, spare, kappa_wide, *weights = scratch[7:14]
@@ -267,6 +284,14 @@
         third_out[rows] = value
 
     four_steps(where, slabs, up_1, down_1, kappa, source, scratch, out)
+
+    @pl.when(lax.rem(where[0], GROUP) < 2)
+    def _():
+        cross_out[...] = second_near[...]
+
+    @pl.when(lax.rem(where[0], GROUP) >= 2)
+    def _():
+        cross_out[...] = third_out[...]
 
     coarse_kappa_4(kappa_wide, up_2, down_2, kappa_c, 0)
     face_weights(kappa_wide, weights, 4.0 * ALONG_THIRD)
@@ -324,7 +349,7 @@
 
 
 def far_sums_kernel(
-    slabs, where, got_up, got, got_down, both, up_2, down_2, kappa_c,
+    slabs, where, got_up, got, got_down, both, up_2, down_2, kappa_c, _,
     ahead_out, wrapped_out, last_out, *scratch,
 ):
     field, spare, kappa_wide, *weights = scratch
@@ -429,7 +454,7 @@
     vmem = pl.BlockSpec(memory_space=pltpu.VMEM)
     anywhere = pl.BlockSpec(memory_space=pl.ANY)
     return pl.pallas_call(
-        functools.partial(kernel, slabs),
+        kernel if slabs is None else functools.partial(kernel, slabs),
         out_shape=[jax.ShapeDtypeStruct(shape, jnp.float32) for shape in outs],
         in_specs=[pl.BlockSpec(memory_space=pltpu.SMEM)]
         + [vmem] * (len(args) - unread)
@@ -484,14 +509,11 @@
     scratch = fine_scratch(rows, width_two, width_three)
 
     kappa_c = restrict(conductivity)
-    ends = [
-        jnp.where(tm == 15, initial[part], guess[0][part])
-        for part in (slice(0, STEPS), slice(rows - STEPS, rows))
-    ]
-    sides = neighbours(
-        jnp.concatenate([ends[0], conductivity[:STEPS], source[: STEPS - 1]]),
-        jnp.concatenate([ends[1], conductivity[-STEPS:], source[1 - STEPS :]]),
-    )
+    first, last = call(
+        first_ends_kernel, None, [(3 * STEPS - 1, width_two, width_three)] * 2, [],
+        where, guess[0], initial, conductivity, source,
+    )
+    sides = neighbours(first, last)
     state, first, last = call(
         phase_one_kernel, slabs, [block_shape, packed_shape, packed_shape], scratch,
         where, *sides, guess[0], initial, conductivity, source, kappa_c,
@@ -503,21 +525,21 @@
     )
     sides_3 = neighbours(first, last)
     second_near = along_time(second, ring(2))
-    second_far = along_time(second_near, [(0, 8), (1, 9), (8, 0), (9, 1)])
-    third, tau = call(
-        phase_three_kernel, slabs, [block_shape, coarse_shape],
+    third, tau, crossed = call(
+        phase_three_kernel, slabs, [block_shape, coarse_shape, block_shape],
         scratch
         + coarse_scratch(3 * crows, half, width_three, 2)
         + [pltpu.VMEM((width_two, width_three), jnp.float32)],
         where, *sides, *sides_2, *sides_3, second, initial, conductivity, source, kappa_c,
-        second_near, unread=1,
+        second_near,
     )
 
     up, down = neighbours(tau, tau)
     tau_wide = jnp.concatenate([up, tau, down], 0)
     got = [along_time(cut(tau_wide, crows, d), ring(d)) for d in (3, 2, 1)]
-    third_far = along_time(
-        third, [(i, (i + 3) % (2 * GROUP)) for i in (5, 6, 7, 13, 14, 15)]
+    crossed = along_time(
+        crossed,
+        [(i, i ^ GROUP) for i in range(2 * GROUP) if i % GROUP in (0, 1, 5, 6, 7)],
     )
     (both,) = call(
         near_sums_kernel, slabs, [(2,) + coarse_shape],
@@ -538,10 +560,13 @@
     ahead, wrapped, last = call(
         far_sums_kernel, slabs, [coarse_shape] * 3,
         coarse_scratch(3 * crows, half, width_three, 2),
-        where, *got, both, *sides_2, kappa_c,
-    )
-
-    third_near = along_time(lax.optimization_barrier((third, last))[0], ring(3))
+        where, *got, both, *sides_2, kappa_c, crossed, unread=1,
+    )
+
+    third_home = along_time(
+        lax.optimization_barrier((jnp.where(local >= 5, crossed, third), last))[0],
+        ring(3),
+    )
     near = neighbours(last, last)
     far = (along_space(last, 2), along_space(last, -2))
     handed, kept = call(
@@ -559,9 +584,7 @@
         ],
     )
     kept = along_time(kept, ring(3))
-    second_far, third_far = lax.optimization_barrier((second_far, third_far, kept))[:2]
-    third_home = jnp.where(local < 3, third_far, third_near)
-    second_home = jnp.where(local < 2, second_far, second_near)
+    second_home = jnp.where(local < 2, crossed, second_near)
 
     residual = third_home - second_home
     change = handed + kept - restrict(second_home)

time: 235 us -> 234 us (level)
  the two profiles are of different devices: /device:TPU:36 before, /device:TPU:81 now
where the time goes in v6:
time: 234 us; the launch traced here: 233 us
  starting transfers between devices  124 us (53%)
  waiting for transfers between devices  73.2 us (31%)
  Pallas kernels  23.4 us (10%)
  local copies, waits for them, and re-layouts  6.66 us (3%)
  other arithmetic  4.5 us (2%)
    ppermute x12, starting transfers between devices, along_space(): return lax.ppermute(block, 'space', pairs)  79 us
    ppermute x12, waiting for transfers between devices, along_space(): return lax.ppermute(block, 'space', pairs)  40.3 us
    ppermute x8, starting transfers between devices, along_time(): return lax.ppermute(block, 'tm', pairs)  34.5 us
    pallas_call x7, Pallas kernels, call(): pl.pallas_call(kernel if slabs is None else functools.partial(kernel, sla...  23.4 us
    ppermute x8, waiting for transfers between devices, along_time(): return lax.ppermute(block, 'tm', pairs)  19.5 us
    ppermute x3, waiting for transfers between devices, route(): return lax.ppermute(block, ('tm', 'space'), pairs)  13.3 us
    ppermute x3, starting transfers between devices, route(): return lax.ppermute(block, ('tm', 'space'), pairs)  11 us
    unnamed x40, local copies, waits for them, and re-layouts  6.39 us
  transfers between devices with their start and end apart: 23, of which 14 were waited for; matrix products, arithmetic and copies ran while one was open for 2% of the time, Pallas kernels for 2%

profile of v6, /device:TPU:81, one launch (start us, length us, event | category | flops | bytes accessed | tf_op | source)
XLA Modules:
  0.0 233.3 jit_solution(9993347295753167113)
XLA Ops:
  6.7 3.0 %collective-permute-start = (f32[11,128,128]{2,1,0:T(8,128)}, f32[11,128,128]{2,1,0:T(8,128)S(1)}, u32[]{:S(2)}, u32[]{:S(2)}) collective-permute-start(f32[11,128,128]{2,1,0:T(8,128)} %get-tuple-element.19), channel_id=1, source_target_pairs={{0,1},{1,2},{2,3},{3,4},{4,5},{5,6},{6,7},{7,8},{8,9},{9,10},{10,1... | collective-permute-start | bytes 2162696 | tf_op jit(solution)/shard_map/ppermute | solution.py:488
  9.7 2.4 %collective-permute-start.1 = (f32[11,128,128]{2,1,0:T(8,128)}, f32[11,128,128]{2,1,0:T(8,128)S(1)}, u32[]{:S(2)}, u32[]{:S(2)}) collective-permute-start(f32[11,128,128]{2,1,0:T(8,128)} %get-tuple-element.20), channel_id=1, source_target_pairs={{1,0},{2,1},{3,2},{4,3},{5,4},{6,5},{7,6},{8,7},{9,8},{10,9},{11,1... | collective-permute-start | bytes 2162696 | tf_op jit(solution)/shard_map/ppermute | solution.py:488
  12.5 13.4 %collective-permute-done.up_1 = f32[11,128,128]{2,1,0:T(8,128)S(1)} collective-permute-done((f32[11,128,128]{2,1,0:T(8,128)}, f32[11,128,128]{2,1,0:T(8,128)S(1)}, u32[]{:S(2)}, u32[]{:S(2)}) %collective-permute-start) | collective-permute-done | bytes 720928 | tf_op jit(solution)/shard_map/ppermute | solution.py:488
  25.9 2.6 %collective-permute-done.1.down_1 = f32[11,128,128]{2,1,0:T(8,128)S(1)} collective-permute-done((f32[11,128,128]{2,1,0:T(8,128)}, f32[11,128,128]{2,1,0:T(8,128)S(1)}, u32[]{:S(2)}, u32[]{:S(2)}) %collective-permute-start.1) | collective-permute-done | bytes 720928 | tf_op jit(solution)/shard_map/ppermute | solution.py:488
  29.5 3.9 %shard_map.60 = (f32[8,128,128]{2,1,0:T(8,128)S(1)}, f32[6,128,128]{2,1,0:T(8,128)S(1)}, f32[6,128,128]{2,1,0:T(8,128)S(1)}) custom-call(s32[2]{0:T(128)S(1)} %pad_add_fusion.where, f32[11,128,128]{2,1,0:T(8,128)S(1)} %collective-permute-done.up_1, f32[11,128,128]{2,1,0:T(8,128)S(1)} %collective-permute-done.1.down_1, f32[8,128,128]{2,1,0:T(8,128)S(1)} %bitcast.13, ...), custom_call_target="tpu_custom_call" | custom-call | tf_op jit(solution)/shard_map/pallas_call | solution.py:456
  33.5 5.3 %collective-permute-start.2 = (f32[6,128,128]{2,1,0:T(8,128)S(1)}, f32[6,128,128]{2,1,0:T(8,128)S(1)}, u32[]{:S(2)}, u32[]{:S(2)}) collective-permute-start(f32[6,128,128]{2,1,0:T(8,128)S(1)} %get-tuple-element.21), channel_id=1, source_target_pairs={{0,1},{1,2},{2,3},{3,4},{4,5},{5,6},{6,7},{7,8},{8,9},{9,10},{10,1... | collective-permute-start | bytes 1179656 | tf_op jit(solution)/shard_map/ppermute | solution.py:488
  40.7 4.6 %collective-permute-done.2.up_2 = f32[6,128,128]{2,1,0:T(8,128)S(1)} collective-permute-done((f32[6,128,128]{2,1,0:T(8,128)S(1)}, f32[6,128,128]{2,1,0:T(8,128)S(1)}, u32[]{:S(2)}, u32[]{:S(2)}) %collective-permute-start.2) | collective-permute-done | bytes 393248 | tf_op jit(solution)/shard_map/ppermute | solution.py:488
  45.3 3.8 %collective-permute-done.3.down_2 = f32[6,128,128]{2,1,0:T(8,128)S(1)} collective-permute-done((f32[6,128,128]{2,1,0:T(8,128)S(1)}, f32[6,128,128]{2,1,0:T(8,128)S(1)}, u32[]{:S(2)}, u32[]{:S(2)}) %collective-permute-start.3) | collective-permute-done | bytes 393248 | tf_op jit(solution)/shard_map/ppermute | solution.py:488
  50.3 3.9 %shard_map.61 = (f32[8,128,128]{2,1,0:T(8,128)S(1)}, f32[6,128,128]{2,1,0:T(8,128)S(1)}, f32[6,128,128]{2,1,0:T(8,128)S(1)}) custom-call(s32[2]{0:T(128)S(1)} %pad_add_fusion.where, f32[11,128,128]{2,1,0:T(8,128)S(1)} %collective-permute-done.up_1, f32[11,128,128]{2,1,0:T(8,128)S(1)} %copy-done.7, f32[6,128,128]{2,1,0:T(8,128)S(1)} %collective-permute-done.2.up_2, ...), custom_call_target="tpu_custom_call" | custom-call | tf_op jit(solution)/shard_map/pallas_call | solution.py:456
  54.2 3.1 %collective-permute-start.6 = (f32[8,128,128]{2,1,0:T(8,128)S(1)}, f32[8,128,128]{2,1,0:T(8,128)S(1)}, u32[]{:S(2)}, u32[]{:S(2)}) collective-permute-start(f32[8,128,128]{2,1,0:T(8,128)S(1)} %get-tuple-element.26.second), channel_id=1, source_target_pairs={{0,64},{32,96},{64,128},{96,160},{128,192},{160,224},{192,0},{224,... | collective-permute-start | bytes 1572872 | tf_op jit(solution)/shard_map/ppermute | solution.py:491
  57.4 4.3 %collective-permute-start.4 = (f32[6,128,128]{2,1,0:T(8,128)S(1)}, f32[6,128,128]{2,1,0:T(8,128)S(1)}, u32[]{:S(2)}, u32[]{:S(2)}) collective-permute-start(f32[6,128,128]{2,1,0:T(8,128)S(1)} %get-tuple-element.24), channel_id=1, source_target_pairs={{0,1},{1,2},{2,3},{3,4},{4,5},{5,6},{6,7},{7,8},{8,9},{9,10},{10,1... | collective-permute-start | bytes 1179656 | tf_op jit(solution)/shard_map/ppermute | solution.py:488
  63.6 3.4 %collective-permute-done.4.up_3 = f32[6,128,128]{2,1,0:T(8,128)S(1)} collective-permute-done((f32[6,128,128]{2,1,0:T(8,128)S(1)}, f32[6,128,128]{2,1,0:T(8,128)S(1)}, u32[]{:S(2)}, u32[]{:S(2)}) %collective-permute-start.4) | collective-permute-done | bytes 393248 | tf_op jit(solution)/shard_map/ppermute | solution.py:488
  67.0 3.8 %collective-permute-done.5.down_3 = f32[6,128,128]{2,1,0:T(8,128)S(1)} collective-permute-done((f32[6,128,128]{2,1,0:T(8,128)S(1)}, f32[6,128,128]{2,1,0:T(8,128)S(1)}, u32[]{:S(2)}, u32[]{:S(2)}) %collective-permute-start.5) | collective-permute-done | bytes 393248 | tf_op jit(solution)/shard_map/ppermute | solution.py:488
  70.9 5.2 %shard_map.62 = (f32[8,128,128]{2,1,0:T(8,128)S(1)}, f32[4,64,128]{2,1,0:T(8,128)S(1)}, f32[8,128,128]{2,1,0:T(8,128)}) custom-call(s32[2]{0:T(128)S(1)} %pad_add_fusion.where, f32[11,128,128]{2,1,0:T(8,128)S(1)} %collective-permute-done.up_1, f32[11,128,128]{2,1,0:T(8,128)S(1)} %copy-done.8, f32[6,128,128]{2,1,0:T(8,128)S(1)} %collective-permute-done.2.up_2, ...), custom_call_target="tpu_custom_call" | custom-call | tf_op jit(solution)/shard_map/pallas_call | solution.py:456
  76.1 4.5 %collective-permute-start.8 = (f32[4,64,128]{2,1,0:T(8,128)S(1)}, f32[4,64,128]{2,1,0:T(8,128)S(1)}, u32[]{:S(2)}, u32[]{:S(2)}) collective-permute-start(f32[4,64,128]{2,1,0:T(8,128)S(1)} %get-tuple-element.28.tau), channel_id=1, source_target_pairs={{0,1},{1,2},{2,3},{3,4},{4,5},{5,6},{6,7},{7,8},{8,9},{9,10},{10,1... | collective-permute-start | bytes 393224 | tf_op jit(solution)/shard_map/ppermute | solution.py:488
  82.5 12.6 %collective-permute-start.7 = (f32[8,128,128]{2,1,0:T(8,128)}, f32[8,128,128]{2,1,0:T(8,128)S(1)}, u32[]{:S(2)}, u32[]{:S(2)}) collective-permute-start(f32[8,128,128]{2,1,0:T(8,128)} %get-tuple-element.27), channel_id=1, source_target_pairs={{0,256},{32,288},{160,416},{192,448},{224,480},{256,0},{288,32},{4... | collective-permute-start | bytes 1572872 | tf_op jit(solution)/shard_map/ppermute | solution.py:491
  97.1 8.4 %collective-permute-start.11 = (f32[8,64,128]{2,1,0:T(8,128)S(1)}, f32[8,64,128]{2,1,0:T(8,128)S(1)}, u32[]{:S(2)}, u32[]{:S(2)}) collective-permute-start(f32[8,64,128]{2,1,0:T(8,128)S(1)} %slice.13), channel_id=1, source_target_pairs={{0,64},{32,96},{64,128},{96,160},{128,192},{160,224},{192,0},{224,... | collective-permute-start | bytes 786440 | tf_op jit(solution)/shard_map/ppermute | solution.py:491
  105.6 8.0 %collective-permute-done.12.got_1 = f32[6,64,128]{2,1,0:T(8,128)S(1)} collective-permute-done((f32[6,64,128]{2,1,0:T(8,128)S(1)}, f32[6,64,128]{2,1,0:T(8,128)S(1)}, u32[]{:S(2)}, u32[]{:S(2)}) %collective-permute-start.12) | collective-permute-done | bytes 196640 | tf_op jit(solution)/shard_map/ppermute | solution.py:491
  116.9 4.7 %collective-permute-start.13 = (f32[2,4,64,128]{3,2,1,0:T(8,128)S(1)}, f32[2,4,64,128]{3,2,1,0:T(8,128)S(1)}, u32[]{:S(2)}, u32[]{:S(2)}) collective-permute-start(f32[2,4,64,128]{3,2,1,0:T(8,128)S(1)} %shard_map.63.both), channel_id=1, source_target_pairs={{0,129},{1,130},{2,131},{3,132},{4,133},{5,134},{6,135},{7,136},{8... | collective-permute-start | bytes 786440 | tf_op jit(solution)/shard_map/ppermute | solution.py:482
  121.7 3.6 %collective-permute-start.14 = (f32[2,4,64,128]{3,2,1,0:T(8,128)S(1)}, f32[2,4,64,128]{3,2,1,0:T(8,128)S(1)}, u32[]{:S(2)}, u32[]{:S(2)}) collective-permute-start(f32[2,4,64,128]{3,2,1,0:T(8,128)S(1)} %shard_map.63.both), channel_id=1, source_target_pairs={{0,128},{1,129},{2,130},{3,131},{4,132},{5,133},{6,134},{7,135},{8... | collective-permute-start | bytes 786440 | tf_op jit(solution)/shard_map/ppermute | solution.py:482
  125.3 2.6 %collective-permute-start.15 = (f32[2,4,64,128]{3,2,1,0:T(8,128)S(1)}, f32[2,4,64,128]{3,2,1,0:T(8,128)S(1)}, u32[]{:S(2)}, u32[]{:S(2)}) collective-permute-start(f32[2,4,64,128]{3,2,1,0:T(8,128)S(1)} %shard_map.63.both), channel_id=1, source_target_pairs={{1,128},{2,129},{3,130},{4,131},{5,132},{6,133},{7,134},{8,135},{9... | collective-permute-start | bytes 786440 | tf_op jit(solution)/shard_map/ppermute | solution.py:482
  129.1 3.2 %collective-permute-done.14.got = f32[2,4,64,128]{3,2,1,0:T(8,128)S(1)} collective-permute-done((f32[2,4,64,128]{3,2,1,0:T(8,128)S(1)}, f32[2,4,64,128]{3,2,1,0:T(8,128)S(1)}, u32[]{:S(2)}, u32[]{:S(2)}) %collective-permute-start.14) | collective-permute-done | bytes 262176 | tf_op jit(solution)/shard_map/ppermute | solution.py:482
  132.3 10.1 %collective-permute-done.15.got_down = f32[2,4,64,128]{3,2,1,0:T(8,128)S(1)} collective-permute-done((f32[2,4,64,128]{3,2,1,0:T(8,128)S(1)}, f32[2,4,64,128]{3,2,1,0:T(8,128)S(1)}, u32[]{:S(2)}, u32[]{:S(2)}) %collective-permute-start.15) | collective-permute-done | bytes 262176 | tf_op jit(solution)/shard_map/ppermute | solution.py:482
  142.4 2.8 %shard_map.64 = (f32[4,64,128]{2,1,0:T(8,128)S(1)}, f32[4,64,128]{2,1,0:T(8,128)S(1)}, f32[4,64,128]{2,1,0:T(8,128)S(1)}) custom-call(s32[2]{0:T(128)S(1)} %pad_add_fusion.where, f32[2,4,64,128]{3,2,1,0:T(8,128)S(1)} %collective-permute-done.13.got_up, f32[2,4,64,128]{3,2,1,0:T(8,128)S(1)} %collective-permute-done.14.got, ...), custom_call_target="tpu_custom_call" | custom-call | tf_op jit(solution)/shard_map/pallas_call | solution.py:456
  147.3 13.6 %collective-permute-start.16 = (f32[4,64,128]{2,1,0:T(8,128)S(1)}, f32[4,64,128]{2,1,0:T(8,128)S(1)}, u32[]{:S(2)}, u32[]{:S(2)}) collective-permute-start(f32[4,64,128]{2,1,0:T(8,128)S(1)} %get-tuple-element.29.last), channel_id=1, source_target_pairs={{0,2},{1,3},{2,4},{3,5},{4,6},{5,7},{6,8},{7,9},{8,10},{9,11},{10,... | collective-permute-start | bytes 393224 | tf_op jit(solution)/shard_map/ppermute | solution.py:488
  160.9 36.3 %collective-permute-start.17 = (f32[4,64,128]{2,1,0:T(8,128)S(1)}, f32[4,64,128]{2,1,0:T(8,128)S(1)}, u32[]{:S(2)}, u32[]{:S(2)}) collective-permute-start(f32[4,64,128]{2,1,0:T(8,128)S(1)} %get-tuple-element.29.last), channel_id=1, source_target_pairs={{0,1},{1,2},{2,3},{3,4},{4,5},{5,6},{6,7},{7,8},{8,9},{9,10},{10,1... | collective-permute-start | bytes 393224 | tf_op jit(solution)/shard_map/ppermute | solution.py:488
  201.1 2.9 %collective-permute-done.18.near_down = f32[4,64,128]{2,1,0:T(8,128)S(1)} collective-permute-done((f32[4,64,128]{2,1,0:T(8,128)S(1)}, f32[4,64,128]{2,1,0:T(8,128)S(1)}, u32[]{:S(2)}, u32[]{:S(2)}) %collective-permute-start.18) | collective-permute-done | bytes 131104 | tf_op jit(solution)/shard_map/ppermute | solution.py:488
  203.9 5.8 %collective-permute-done.19.far_down = f32[4,64,128]{2,1,0:T(8,128)S(1)} collective-permute-done((f32[4,64,128]{2,1,0:T(8,128)S(1)}, f32[4,64,128]{2,1,0:T(8,128)S(1)}, u32[]{:S(2)}, u32[]{:S(2)}) %collective-permute-start.19) | collective-permute-done | bytes 131104 | tf_op jit(solution)/shard_map/ppermute | solution.py:488
  209.7 3.8 %shard_map.65 = (f32[4,64,128]{2,1,0:T(8,128)S(1)}, f32[4,64,128]{2,1,0:T(8,128)S(1)}) custom-call(s32[2]{0:T(128)S(1)} %pad_add_fusion.where, f32[4,64,128]{2,1,0:T(8,128)S(1)} %collective-permute-done.16.far_up, f32[4,64,128]{2,1,0:T(8,128)S(1)} %collective-permute-done.17.near_up, f32[4,64,128]{2,1,0:T(8,128)S(1)} %get-tuple-element.29.last, ...), custom_call_target="tpu_custom_call" | custom-call | tf_op jit(solution)/shard_map/pallas_call | solution.py:456
  213.5 4.0 %collective-permute-start.20 = (f32[4,64,128]{2,1,0:T(8,128)S(1)}, f32[4,64,128]{2,1,0:T(8,128)S(1)}, u32[]{:S(2)}, u32[]{:S(2)}) collective-permute-start(f32[4,64,128]{2,1,0:T(8,128)S(1)} %get-tuple-element.32), channel_id=1, source_target_pairs={{0,352},{32,384},{64,416},{96,448},{128,480},{160,256},{192,288},{... | collective-permute-start | bytes 393224 | tf_op jit(solution)/shard_map/ppermute | solution.py:491
  217.5 2.4 %collective-permute-start.21 = (f32[4,64,128]{2,1,0:T(8,128)S(1)}, f32[4,64,128]{2,1,0:T(8,128)S(1)}, u32[]{:S(2)}, u32[]{:S(2)}) collective-permute-start(f32[4,64,128]{2,1,0:T(8,128)S(1)} %get-tuple-element.33), channel_id=1, source_target_pairs={{0,96},{32,128},{64,160},{96,192},{128,224},{160,0},{192,32},{224,... | collective-permute-start | bytes 393224 | tf_op jit(solution)/shard_map/ppermute | solution.py:491
  222.2 9.9 %collective-permute-done.20 = f32[4,64,128]{2,1,0:T(8,128)S(1)} collective-permute-done((f32[4,64,128]{2,1,0:T(8,128)S(1)}, f32[4,64,128]{2,1,0:T(8,128)S(1)}, u32[]{:S(2)}, u32[]{:S(2)}) %collective-permute-start.20) | collective-permute-done | bytes 131104 | tf_op jit(solution)/shard_map/ppermute | solution.py:491
  (75 shorter events, 30.2 us)
Async XLA Ops:
  4.9 23.6 %copy-start.5 = (f32[8,128,128]{2,1,0:T(8,128)S(1)}, f32[8,128,128]{2,1,0:T(8,128)}, u32[]{:S(2)}) copy-start(f32[8,128,128]{2,1,0:T(8,128)} %source.7) | copy-start | bytes 1572868
  6.7 21.8 %copy-start.3 = (f32[8,128,128]{2,1,0:T(8,128)S(1)}, f32[8,128,128]{2,1,0:T(8,128)}, u32[]{:S(2)}) copy-start(f32[8,128,128]{2,1,0:T(8,128)} %initial.7) | copy-start | bytes 1572868
  6.7 19.2 %collective-permute-start = (f32[11,128,128]{2,1,0:T(8,128)}, f32[11,128,128]{2,1,0:T(8,128)S(1)}, u32[]{:S(2)}, u32[]{:S(2)}) collective-permute-start(f32[11,128,128]{2,1,0:T(8,128)} %get-tuple-element.19), channel_id=1, source_target_pairs={{0,1},{1,2},{2,3},{3,4},{4,5},{5,6},{6,7},{7,8},{8,9},{9,10},{10,1... | collective-permute-start | bytes 2162696 | tf_op jit(solution)/shard_map/ppermute | solution.py:488
  9.7 18.8 %collective-permute-start.1 = (f32[11,128,128]{2,1,0:T(8,128)}, f32[11,128,128]{2,1,0:T(8,128)S(1)}, u32[]{:S(2)}, u32[]{:S(2)}) collective-permute-start(f32[11,128,128]{2,1,0:T(8,128)} %get-tuple-element.20), channel_id=1, source_target_pairs={{1,0},{2,1},{3,2},{4,3},{5,4},{6,5},{7,6},{8,7},{9,8},{10,9},{11,1... | collective-permute-start | bytes 2162696 | tf_op jit(solution)/shard_map/ppermute | solution.py:488
  33.5 11.8 %collective-permute-start.2 = (f32[6,128,128]{2,1,0:T(8,128)S(1)}, f32[6,128,128]{2,1,0:T(8,128)S(1)}, u32[]{:S(2)}, u32[]{:S(2)}) collective-permute-start(f32[6,128,128]{2,1,0:T(8,128)S(1)} %get-tuple-element.21), channel_id=1, source_target_pairs={{0,1},{1,2},{2,3},{3,4},{4,5},{5,6},{6,7},{7,8},{8,9},{9,10},{10,1... | collective-permute-start | bytes 1179656 | tf_op jit(solution)/shard_map/ppermute | solution.py:488
  38.8 10.4 %collective-permute-start.3 = (f32[6,128,128]{2,1,0:T(8,128)S(1)}, f32[6,128,128]{2,1,0:T(8,128)S(1)}, u32[]{:S(2)}, u32[]{:S(2)}) collective-permute-start(f32[6,128,128]{2,1,0:T(8,128)S(1)} %get-tuple-element.22), channel_id=1, source_target_pairs={{1,0},{2,1},{3,2},{4,3},{5,4},{6,5},{7,6},{8,7},{9,8},{10,9},{11,1... | collective-permute-start | bytes 1179656 | tf_op jit(solution)/shard_map/ppermute | solution.py:488
  50.3 20.6 %copy-start.8 = (f32[11,128,128]{2,1,0:T(8,128)S(1)}, f32[11,128,128]{2,1,0:T(8,128)}, u32[]{:S(2)}) copy-start(f32[11,128,128]{2,1,0:T(8,128)} %copy-done.6) | copy-start | bytes 2162692
  54.2 16.6 %collective-permute-start.6 = (f32[8,128,128]{2,1,0:T(8,128)S(1)}, f32[8,128,128]{2,1,0:T(8,128)S(1)}, u32[]{:S(2)}, u32[]{:S(2)}) collective-permute-start(f32[8,128,128]{2,1,0:T(8,128)S(1)} %get-tuple-element.26.second), channel_id=1, source_target_pairs={{0,64},{32,96},{64,128},{96,160},{128,192},{160,224},{192,0},{224,... | collective-permute-start | bytes 1572872 | tf_op jit(solution)/shard_map/ppermute | solution.py:491
  57.4 9.6 %collective-permute-start.4 = (f32[6,128,128]{2,1,0:T(8,128)S(1)}, f32[6,128,128]{2,1,0:T(8,128)S(1)}, u32[]{:S(2)}, u32[]{:S(2)}) collective-permute-start(f32[6,128,128]{2,1,0:T(8,128)S(1)} %get-tuple-element.24), channel_id=1, source_target_pairs={{0,1},{1,2},{2,3},{3,4},{4,5},{5,6},{6,7},{7,8},{8,9},{9,10},{10,1... | collective-permute-start | bytes 1179656 | tf_op jit(solution)/shard_map/ppermute | solution.py:488
  61.7 9.2 %collective-permute-start.5 = (f32[6,128,128]{2,1,0:T(8,128)S(1)}, f32[6,128,128]{2,1,0:T(8,128)S(1)}, u32[]{:S(2)}, u32[]{:S(2)}) collective-permute-start(f32[6,128,128]{2,1,0:T(8,128)S(1)} %get-tuple-element.25), channel_id=1, source_target_pairs={{1,0},{2,1},{3,2},{4,3},{5,4},{6,5},{7,6},{8,7},{9,8},{10,9},{11,1... | collective-permute-start | bytes 1179656 | tf_op jit(solution)/shard_map/ppermute | solution.py:488
  67.0 9.0 %copy-start.13 = (f32[6,128,128]{2,1,0:T(8,128)}, f32[6,128,128]{2,1,0:T(8,128)S(1)}, u32[]{:S(2)}) copy-start(f32[6,128,128]{2,1,0:T(8,128)S(1)} %collective-permute-done.4.up_3) | copy-start | bytes 1179652
  76.0 19.1 %copy-start.17 = (f32[8,128,128]{2,1,0:T(8,128)}, f32[8,128,128]{2,1,0:T(8,128)S(1)}, u32[]{:S(2)}) copy-start(f32[8,128,128]{2,1,0:T(8,128)S(1)} %get-tuple-element.34) | copy-start | bytes 1572868
  76.1 19.0 %collective-permute-start.8 = (f32[4,64,128]{2,1,0:T(8,128)S(1)}, f32[4,64,128]{2,1,0:T(8,128)S(1)}, u32[]{:S(2)}, u32[]{:S(2)}) collective-permute-start(f32[4,64,128]{2,1,0:T(8,128)S(1)} %get-tuple-element.28.tau), channel_id=1, source_target_pairs={{0,1},{1,2},{2,3},{3,4},{4,5},{5,6},{6,7},{7,8},{8,9},{9,10},{10,1... | collective-permute-start | bytes 393224 | tf_op jit(solution)/shard_map/ppermute | solution.py:488
  80.5 14.6 %collective-permute-start.9 = (f32[4,64,128]{2,1,0:T(8,128)S(1)}, f32[4,64,128]{2,1,0:T(8,128)S(1)}, u32[]{:S(2)}, u32[]{:S(2)}) collective-permute-start(f32[4,64,128]{2,1,0:T(8,128)S(1)} %get-tuple-element.28.tau), channel_id=1, source_target_pairs={{1,0},{2,1},{3,2},{4,3},{5,4},{6,5},{7,6},{8,7},{9,8},{10,9},{11,1... | collective-permute-start | bytes 393224 | tf_op jit(solution)/shard_map/ppermute | solution.py:488
  82.5 45.8 %collective-permute-start.7 = (f32[8,128,128]{2,1,0:T(8,128)}, f32[8,128,128]{2,1,0:T(8,128)S(1)}, u32[]{:S(2)}, u32[]{:S(2)}) collective-permute-start(f32[8,128,128]{2,1,0:T(8,128)} %get-tuple-element.27), channel_id=1, source_target_pairs={{0,256},{32,288},{160,416},{192,448},{224,480},{256,0},{288,32},{4... | collective-permute-start | bytes 1572872 | tf_op jit(solution)/shard_map/ppermute | solution.py:491
  95.2 19.7 %collective-permute-start.10 = (f32[10,64,128]{2,1,0:T(8,128)S(1)}, f32[10,64,128]{2,1,0:T(8,128)S(1)}, u32[]{:S(2)}, u32[]{:S(2)}) collective-permute-start(f32[10,64,128]{2,1,0:T(8,128)S(1)} %slice.12), channel_id=1, source_target_pairs={{0,96},{32,128},{64,160},{96,192},{128,224},{160,0},{192,32},{224,... | collective-permute-start | bytes 983048 | tf_op jit(solution)/shard_map/ppermute | solution.py:491
  97.1 16.4 %collective-permute-start.11 = (f32[8,64,128]{2,1,0:T(8,128)S(1)}, f32[8,64,128]{2,1,0:T(8,128)S(1)}, u32[]{:S(2)}, u32[]{:S(2)}) collective-permute-start(f32[8,64,128]{2,1,0:T(8,128)S(1)} %slice.13), channel_id=1, source_target_pairs={{0,64},{32,96},{64,128},{96,160},{128,192},{160,224},{192,0},{224,... | collective-permute-start | bytes 786440 | tf_op jit(solution)/shard_map/ppermute | solution.py:491
  105.5 8.0 %collective-permute-start.12 = (f32[6,64,128]{2,1,0:T(8,128)S(1)}, f32[6,64,128]{2,1,0:T(8,128)S(1)}, u32[]{:S(2)}, u32[]{:S(2)}) collective-permute-start(f32[6,64,128]{2,1,0:T(8,128)S(1)} %slice.14), channel_id=1, source_target_pairs={{0,32},{32,64},{64,96},{96,128},{128,160},{160,192},{192,224},{224... | collective-permute-start | bytes 589832 | tf_op jit(solution)/shard_map/ppermute | solution.py:491
  105.6 22.7 %copy-start.18 = (f32[8,128,128]{2,1,0:T(8,128)S(1)}, f32[8,128,128]{2,1,0:T(8,128)}, u32[]{:S(2)}) copy-start(f32[8,128,128]{2,1,0:T(8,128)} %copy-done.17) | copy-start | bytes 1572868
  116.9 12.2 %collective-permute-start.13 = (f32[2,4,64,128]{3,2,1,0:T(8,128)S(1)}, f32[2,4,64,128]{3,2,1,0:T(8,128)S(1)}, u32[]{:S(2)}, u32[]{:S(2)}) collective-permute-start(f32[2,4,64,128]{3,2,1,0:T(8,128)S(1)} %shard_map.63.both), channel_id=1, source_target_pairs={{0,129},{1,130},{2,131},{3,132},{4,133},{5,134},{6,135},{7,136},{8... | collective-permute-start | bytes 786440 | tf_op jit(solution)/shard_map/ppermute | solution.py:482
  121.7 10.7 %collective-permute-start.14 = (f32[2,4,64,128]{3,2,1,0:T(8,128)S(1)}, f32[2,4,64,128]{3,2,1,0:T(8,128)S(1)}, u32[]{:S(2)}, u32[]{:S(2)}) collective-permute-start(f32[2,4,64,128]{3,2,1,0:T(8,128)S(1)} %shard_map.63.both), channel_id=1, source_target_pairs={{0,128},{1,129},{2,130},{3,131},{4,132},{5,133},{6,134},{7,135},{8... | collective-permute-start | bytes 786440 | tf_op jit(solution)/shard_map/ppermute | solution.py:482
  125.3 17.1 %collective-permute-start.15 = (f32[2,4,64,128]{3,2,1,0:T(8,128)S(1)}, f32[2,4,64,128]{3,2,1,0:T(8,128)S(1)}, u32[]{:S(2)}, u32[]{:S(2)}) collective-permute-start(f32[2,4,64,128]{3,2,1,0:T(8,128)S(1)} %shard_map.63.both), channel_id=1, source_target_pairs={{1,128},{2,129},{3,130},{4,131},{5,132},{6,133},{7,134},{8,135},{9... | collective-permute-start | bytes 786440 | tf_op jit(solution)/shard_map/ppermute | solution.py:482
  129.1 80.6 %copy-start.14 = (f32[6,128,128]{2,1,0:T(8,128)S(1)}, f32[6,128,128]{2,1,0:T(8,128)}, u32[]{:S(2)}) copy-start(f32[6,128,128]{2,1,0:T(8,128)} %copy-done.13) | copy-start | bytes 1179652
  129.1 80.6 %copy-start.16 = (f32[6,128,128]{2,1,0:T(8,128)S(1)}, f32[6,128,128]{2,1,0:T(8,128)}, u32[]{:S(2)}) copy-start(f32[6,128,128]{2,1,0:T(8,128)} %copy-done.15) | copy-start | bytes 1179652
  145.2 74.7 %collective-permute-start.22 = (f32[8,128,128]{2,1,0:T(8,128)}, f32[8,128,128]{2,1,0:T(8,128)}, u32[]{:S(2)}, u32[]{:S(2)}) collective-permute-start(f32[8,128,128]{2,1,0:T(8,128)} %broadcast_select_fusion), channel_id=1, source_target_pairs={{0,96},{32,128},{64,160},{96,192},{128,224},{160,0},{192,32},{224,... | collective-permute-start | bytes 1572872 | tf_op jit(solution)/shard_map/ppermute | solution.py:491
  147.3 53.8 %collective-permute-start.16 = (f32[4,64,128]{2,1,0:T(8,128)S(1)}, f32[4,64,128]{2,1,0:T(8,128)S(1)}, u32[]{:S(2)}, u32[]{:S(2)}) collective-permute-start(f32[4,64,128]{2,1,0:T(8,128)S(1)} %get-tuple-element.29.last), channel_id=1, source_target_pairs={{0,2},{1,3},{2,4},{3,5},{4,6},{5,7},{6,8},{7,9},{8,10},{9,11},{10,... | collective-permute-start | bytes 393224 | tf_op jit(solution)/shard_map/ppermute | solution.py:488
  160.9 40.2 %collective-permute-start.17 = (f32[4,64,128]{2,1,0:T(8,128)S(1)}, f32[4,64,128]{2,1,0:T(8,128)S(1)}, u32[]{:S(2)}, u32[]{:S(2)}) collective-permute-start(f32[4,64,128]{2,1,0:T(8,128)S(1)} %get-tuple-element.29.last), channel_id=1, source_target_pairs={{0,1},{1,2},{2,3},{3,4},{4,5},{5,6},{6,7},{7,8},{8,9},{9,10},{10,1... | collective-permute-start | bytes 393224 | tf_op jit(solution)/shard_map/ppermute | solution.py:488
  197.2 6.7 %collective-permute-start.18 = (f32[4,64,128]{2,1,0:T(8,128)S(1)}, f32[4,64,128]{2,1,0:T(8,128)S(1)}, u32[]{:S(2)}, u32[]{:S(2)}) collective-permute-start(f32[4,64,128]{2,1,0:T(8,128)S(1)} %get-tuple-element.29.last), channel_id=1, source_target_pairs={{1,0},{2,1},{3,2},{4,3},{5,4},{6,5},{7,6},{8,7},{9,8},{10,9},{11,1... | collective-permute-start | bytes 393224 | tf_op jit(solution)/shard_map/ppermute | solution.py:488
  199.1 10.6 %collective-permute-start.19 = (f32[4,64,128]{2,1,0:T(8,128)S(1)}, f32[4,64,128]{2,1,0:T(8,128)S(1)}, u32[]{:S(2)}, u32[]{:S(2)}) collective-permute-start(f32[4,64,128]{2,1,0:T(8,128)S(1)} %get-tuple-element.29.last), channel_id=1, source_target_pairs={{2,0},{3,1},{4,2},{5,3},{6,4},{7,5},{8,6},{9,7},{10,8},{11,9},{12,... | collective-permute-start | bytes 393224 | tf_op jit(solution)/shard_map/ppermute | solution.py:488
  209.7 10.2 %copy-start.12 = (f32[8,128,128]{2,1,0:T(8,128)S(1)}, f32[8,128,128]{2,1,0:T(8,128)}, u32[]{:S(2)}) copy-start(f32[8,128,128]{2,1,0:T(8,128)} %copy-done.11) | copy-start | bytes 1572868
  213.5 18.7 %collective-permute-start.20 = (f32[4,64,128]{2,1,0:T(8,128)S(1)}, f32[4,64,128]{2,1,0:T(8,128)S(1)}, u32[]{:S(2)}, u32[]{:S(2)}) collective-permute-start(f32[4,64,128]{2,1,0:T(8,128)S(1)} %get-tuple-element.32), channel_id=1, source_target_pairs={{0,352},{32,384},{64,416},{96,448},{128,480},{160,256},{192,288},{... | collective-permute-start | bytes 393224 | tf_op jit(solution)/shard_map/ppermute | solution.py:491
  217.5 14.7 %collective-permute-start.21 = (f32[4,64,128]{2,1,0:T(8,128)S(1)}, f32[4,64,128]{2,1,0:T(8,128)S(1)}, u32[]{:S(2)}, u32[]{:S(2)}) collective-permute-start(f32[4,64,128]{2,1,0:T(8,128)S(1)} %get-tuple-element.33), channel_id=1, source_target_pairs={{0,96},{32,128},{64,160},{96,192},{128,224},{160,0},{192,32},{224,... | collective-permute-start | bytes 393224 | tf_op jit(solution)/shard_map/ppermute | solution.py:491
  (10 other events, 27.9 us)

commit v7 on v6

--- a/solution.py
+++ b/solution.py
@@ -536,9 +536,10 @@
 
     up, down = neighbours(tau, tau)
     tau_wide = jnp.concatenate([up, tau, down], 0)
-    got = [along_time(cut(tau_wide, crows, d), ring(d)) for d in (3, 2, 1)]
+    sent = [cut(tau_wide, crows, d) for d in (3, 2, 1)]
+    got = [along_time(block, ring(d)) for d, block in zip((3, 2, 1), sent)]
     crossed = along_time(
-        crossed,
+        lax.optimization_barrier((crossed, got[2]))[0],
         [(i, i ^ GROUP) for i in range(2 * GROUP) if i % GROUP in (0, 1, 5, 6, 7)],
     )
     (both,) = call(

time: 234 us -> 223 us (0.953)
  the two profiles are of different devices: /device:TPU:81 before, /device:TPU:33 now
where the time goes in v7:
time: 223 us; the launch traced here: 222 us
  starting transfers between devices  107 us (48%)
  waiting for transfers between devices  78.6 us (35%)
  Pallas kernels  23.4 us (10%)
  local copies, waits for them, and re-layouts  6.66 us (3%)
  other arithmetic  4.5 us (2%)
    ppermute x8, starting transfers between devices, along_time(): return lax.ppermute(block, 'tm', pairs)  49.4 us
    ppermute x12, starting transfers between devices, along_space(): return lax.ppermute(block, 'space', pairs)  44.8 us
    ppermute x12, waiting for transfers between devices, along_space(): return lax.ppermute(block, 'space', pairs)  33.1 us
    ppermute x8, waiting for transfers between devices, along_time(): return lax.ppermute(block, 'tm', pairs)  27.2 us
    pallas_call x7, Pallas kernels, call(): pl.pallas_call(kernel if slabs is None else functools.partial(kernel, sla...  23.4 us
    ppermute x3, waiting for transfers between devices, route(): return lax.ppermute(block, ('tm', 'space'), pairs)  18.3 us
    ppermute x3, starting transfers between devices, route(): return lax.ppermute(block, ('tm', 'space'), pairs)  13 us
    unnamed x40, local copies, waits for them, and re-layouts  6.39 us
  transfers between devices with their start and end apart: 23, of which 14 were waited for; matrix products, arithmetic and copies ran while one was open for 2% of the time, Pallas kernels for 3%

profile of v7, /device:TPU:33, one launch (start us, length us, event | category | flops | bytes accessed | tf_op | source)
XLA Modules:
  0.0 221.5 jit_solution(3180999083589324413)
XLA Ops:
  6.7 3.3 %collective-permute-start = (f32[11,128,128]{2,1,0:T(8,128)}, f32[11,128,128]{2,1,0:T(8,128)S(1)}, u32[]{:S(2)}, u32[]{:S(2)}) collective-permute-start(f32[11,128,128]{2,1,0:T(8,128)} %get-tuple-element.20), channel_id=1, source_target_pairs={{0,1},{1,2},{2,3},{3,4},{4,5},{5,6},{6,7},{7,8},{8,9},{9,10},{10,1... | collective-permute-start | bytes 2162696 | tf_op jit(solution)/shard_map/ppermute | solution.py:488
  10.0 4.2 %collective-permute-start.1 = (f32[11,128,128]{2,1,0:T(8,128)}, f32[11,128,128]{2,1,0:T(8,128)S(1)}, u32[]{:S(2)}, u32[]{:S(2)}) collective-permute-start(f32[11,128,128]{2,1,0:T(8,128)} %get-tuple-element.21), channel_id=1, source_target_pairs={{1,0},{2,1},{3,2},{4,3},{5,4},{6,5},{7,6},{8,7},{9,8},{10,9},{11,1... | collective-permute-start | bytes 2162696 | tf_op jit(solution)/shard_map/ppermute | solution.py:488
  14.6 13.4 %collective-permute-done.up_1 = f32[11,128,128]{2,1,0:T(8,128)S(1)} collective-permute-done((f32[11,128,128]{2,1,0:T(8,128)}, f32[11,128,128]{2,1,0:T(8,128)S(1)}, u32[]{:S(2)}, u32[]{:S(2)}) %collective-permute-start) | collective-permute-done | bytes 720928 | tf_op jit(solution)/shard_map/ppermute | solution.py:488
  30.0 3.9 %shard_map.60 = (f32[8,128,128]{2,1,0:T(8,128)S(1)}, f32[6,128,128]{2,1,0:T(8,128)S(1)}, f32[6,128,128]{2,1,0:T(8,128)S(1)}) custom-call(s32[2]{0:T(128)S(1)} %pad_add_fusion.where, f32[11,128,128]{2,1,0:T(8,128)S(1)} %collective-permute-done.up_1, f32[11,128,128]{2,1,0:T(8,128)S(1)} %collective-permute-done.1.down_1, f32[8,128,128]{2,1,0:T(8,128)S(1)} %bitcast.13, ...), custom_call_target="tpu_custom_call" | custom-call | tf_op jit(solution)/shard_map/pallas_call | solution.py:456
  34.0 3.0 %collective-permute-start.2 = (f32[6,128,128]{2,1,0:T(8,128)S(1)}, f32[6,128,128]{2,1,0:T(8,128)S(1)}, u32[]{:S(2)}, u32[]{:S(2)}) collective-permute-start(f32[6,128,128]{2,1,0:T(8,128)S(1)} %get-tuple-element.22), channel_id=1, source_target_pairs={{0,1},{1,2},{2,3},{3,4},{4,5},{5,6},{6,7},{7,8},{8,9},{9,10},{10,1... | collective-permute-start | bytes 1179656 | tf_op jit(solution)/shard_map/ppermute | solution.py:488
  37.0 5.0 %collective-permute-start.3 = (f32[6,128,128]{2,1,0:T(8,128)S(1)}, f32[6,128,128]{2,1,0:T(8,128)S(1)}, u32[]{:S(2)}, u32[]{:S(2)}) collective-permute-start(f32[6,128,128]{2,1,0:T(8,128)S(1)} %get-tuple-element.23), channel_id=1, source_target_pairs={{1,0},{2,1},{3,2},{4,3},{5,4},{6,5},{7,6},{8,7},{9,8},{10,9},{11,1... | collective-permute-start | bytes 1179656 | tf_op jit(solution)/shard_map/ppermute | solution.py:488
  42.0 5.6 %collective-permute-done.2.up_2 = f32[6,128,128]{2,1,0:T(8,128)S(1)} collective-permute-done((f32[6,128,128]{2,1,0:T(8,128)S(1)}, f32[6,128,128]{2,1,0:T(8,128)S(1)}, u32[]{:S(2)}, u32[]{:S(2)}) %collective-permute-start.2) | collective-permute-done | bytes 393248 | tf_op jit(solution)/shard_map/ppermute | solution.py:488
  49.6 3.9 %shard_map.61 = (f32[8,128,128]{2,1,0:T(8,128)S(1)}, f32[6,128,128]{2,1,0:T(8,128)S(1)}, f32[6,128,128]{2,1,0:T(8,128)S(1)}) custom-call(s32[2]{0:T(128)S(1)} %pad_add_fusion.where, f32[11,128,128]{2,1,0:T(8,128)S(1)} %collective-permute-done.up_1, f32[11,128,128]{2,1,0:T(8,128)S(1)} %copy-done.7, f32[6,128,128]{2,1,0:T(8,128)S(1)} %collective-permute-done.2.up_2, ...), custom_call_target="tpu_custom_call" | custom-call | tf_op jit(solution)/shard_map/pallas_call | solution.py:456
  53.6 3.1 %collective-permute-start.6 = (f32[8,128,128]{2,1,0:T(8,128)S(1)}, f32[8,128,128]{2,1,0:T(8,128)S(1)}, u32[]{:S(2)}, u32[]{:S(2)}) collective-permute-start(f32[8,128,128]{2,1,0:T(8,128)S(1)} %get-tuple-element.27.second), channel_id=1, source_target_pairs={{0,64},{32,96},{64,128},{96,160},{128,192},{160,224},{192,0},{224,... | collective-permute-start | bytes 1572872 | tf_op jit(solution)/shard_map/ppermute | solution.py:491
  56.7 4.0 %collective-permute-start.4 = (f32[6,128,128]{2,1,0:T(8,128)S(1)}, f32[6,128,128]{2,1,0:T(8,128)S(1)}, u32[]{:S(2)}, u32[]{:S(2)}) collective-permute-start(f32[6,128,128]{2,1,0:T(8,128)S(1)} %get-tuple-element.25), channel_id=1, source_target_pairs={{0,1},{1,2},{2,3},{3,4},{4,5},{5,6},{6,7},{7,8},{8,9},{9,10},{10,1... | collective-permute-start | bytes 1179656 | tf_op jit(solution)/shard_map/ppermute | solution.py:488
  60.7 4.2 %collective-permute-start.5 = (f32[6,128,128]{2,1,0:T(8,128)S(1)}, f32[6,128,128]{2,1,0:T(8,128)S(1)}, u32[]{:S(2)}, u32[]{:S(2)}) collective-permute-start(f32[6,128,128]{2,1,0:T(8,128)S(1)} %get-tuple-element.26), channel_id=1, source_target_pairs={{1,0},{2,1},{3,2},{4,3},{5,4},{6,5},{7,6},{8,7},{9,8},{10,9},{11,1... | collective-permute-start | bytes 1179656 | tf_op jit(solution)/shard_map/ppermute | solution.py:488
  64.9 4.4 %collective-permute-done.4.up_3 = f32[6,128,128]{2,1,0:T(8,128)S(1)} collective-permute-done((f32[6,128,128]{2,1,0:T(8,128)S(1)}, f32[6,128,128]{2,1,0:T(8,128)S(1)}, u32[]{:S(2)}, u32[]{:S(2)}) %collective-permute-start.4) | collective-permute-done | bytes 393248 | tf_op jit(solution)/shard_map/ppermute | solution.py:488
  70.2 5.2 %shard_map.62 = (f32[8,128,128]{2,1,0:T(8,128)S(1)}, f32[4,64,128]{2,1,0:T(8,128)S(1)}, f32[8,128,128]{2,1,0:T(8,128)}) custom-call(s32[2]{0:T(128)S(1)} %pad_add_fusion.where, f32[11,128,128]{2,1,0:T(8,128)S(1)} %collective-permute-done.up_1, f32[11,128,128]{2,1,0:T(8,128)S(1)} %copy-done.8, f32[6,128,128]{2,1,0:T(8,128)S(1)} %collective-permute-done.2.up_2, ...), custom_call_target="tpu_custom_call" | custom-call | tf_op jit(solution)/shard_map/pallas_call | solution.py:456
  75.4 4.0 %collective-permute-start.7 = (f32[4,64,128]{2,1,0:T(8,128)S(1)}, f32[4,64,128]{2,1,0:T(8,128)S(1)}, u32[]{:S(2)}, u32[]{:S(2)}) collective-permute-start(f32[4,64,128]{2,1,0:T(8,128)S(1)} %get-tuple-element.29.tau), channel_id=1, source_target_pairs={{0,1},{1,2},{2,3},{3,4},{4,5},{5,6},{6,7},{7,8},{8,9},{9,10},{10,1... | collective-permute-start | bytes 393224 | tf_op jit(solution)/shard_map/ppermute | solution.py:488
  79.4 4.2 %collective-permute-start.8 = (f32[4,64,128]{2,1,0:T(8,128)S(1)}, f32[4,64,128]{2,1,0:T(8,128)S(1)}, u32[]{:S(2)}, u32[]{:S(2)}) collective-permute-start(f32[4,64,128]{2,1,0:T(8,128)S(1)} %get-tuple-element.29.tau), channel_id=1, source_target_pairs={{1,0},{2,1},{3,2},{4,3},{5,4},{6,5},{7,6},{8,7},{9,8},{10,9},{11,1... | collective-permute-start | bytes 393224 | tf_op jit(solution)/shard_map/ppermute | solution.py:488
  85.6 6.1 %collective-permute-start.9 = (f32[6,64,128]{2,1,0:T(8,128)S(1)}, f32[6,64,128]{2,1,0:T(8,128)S(1)}, u32[]{:S(2)}, u32[]{:S(2)}) collective-permute-start(f32[6,64,128]{2,1,0:T(8,128)S(1)} %slice.12), channel_id=1, source_target_pairs={{0,32},{32,64},{64,96},{96,128},{128,160},{160,192},{192,224},{224... | collective-permute-start | bytes 589832 | tf_op jit(solution)/shard_map/ppermute | solution.py:491
  94.3 14.4 %collective-permute-start.10 = (f32[8,128,128]{2,1,0:T(8,128)}, f32[8,128,128]{2,1,0:T(8,128)S(1)}, u32[]{:S(2)}, u32[]{:S(2)}) collective-permute-start(f32[8,128,128]{2,1,0:T(8,128)} %get-tuple-element.30), channel_id=1, source_target_pairs={{0,256},{32,288},{160,416},{192,448},{224,480},{256,0},{288,32},{4... | collective-permute-start | bytes 1572872 | tf_op jit(solution)/shard_map/ppermute | solution.py:491
  110.6 5.5 %collective-permute-start.12 = (f32[8,64,128]{2,1,0:T(8,128)S(1)}, f32[8,64,128]{2,1,0:T(8,128)S(1)}, u32[]{:S(2)}, u32[]{:S(2)}) collective-permute-start(f32[8,64,128]{2,1,0:T(8,128)S(1)} %slice.14), channel_id=1, source_target_pairs={{0,64},{32,96},{64,128},{96,160},{128,192},{160,224},{192,0},{224,... | collective-permute-start | bytes 786440 | tf_op jit(solution)/shard_map/ppermute | solution.py:491
  116.2 9.5 %collective-permute-done.12.got_2 = f32[8,64,128]{2,1,0:T(8,128)S(1)} collective-permute-done((f32[8,64,128]{2,1,0:T(8,128)S(1)}, f32[8,64,128]{2,1,0:T(8,128)S(1)}, u32[]{:S(2)}, u32[]{:S(2)}) %collective-permute-start.12) | collective-permute-done | bytes 262176 | tf_op jit(solution)/shard_map/ppermute | solution.py:491
  127.7 4.1 %collective-permute-start.13 = (f32[2,4,64,128]{3,2,1,0:T(8,128)S(1)}, f32[2,4,64,128]{3,2,1,0:T(8,128)S(1)}, u32[]{:S(2)}, u32[]{:S(2)}) collective-permute-start(f32[2,4,64,128]{3,2,1,0:T(8,128)S(1)} %shard_map.63.both), channel_id=1, source_target_pairs={{0,129},{1,130},{2,131},{3,132},{4,133},{5,134},{6,135},{7,136},{8... | collective-permute-start | bytes 786440 | tf_op jit(solution)/shard_map/ppermute | solution.py:482
  131.7 3.5 %collective-permute-start.14 = (f32[2,4,64,128]{3,2,1,0:T(8,128)S(1)}, f32[2,4,64,128]{3,2,1,0:T(8,128)S(1)}, u32[]{:S(2)}, u32[]{:S(2)}) collective-permute-start(f32[2,4,64,128]{3,2,1,0:T(8,128)S(1)} %shard_map.63.both), channel_id=1, source_target_pairs={{0,128},{1,129},{2,130},{3,131},{4,132},{5,133},{6,134},{7,135},{8... | collective-permute-start | bytes 786440 | tf_op jit(solution)/shard_map/ppermute | solution.py:482
  135.3 5.4 %collective-permute-start.15 = (f32[2,4,64,128]{3,2,1,0:T(8,128)S(1)}, f32[2,4,64,128]{3,2,1,0:T(8,128)S(1)}, u32[]{:S(2)}, u32[]{:S(2)}) collective-permute-start(f32[2,4,64,128]{3,2,1,0:T(8,128)S(1)} %shard_map.63.both), channel_id=1, source_target_pairs={{1,128},{2,129},{3,130},{4,131},{5,132},{6,133},{7,134},{8,135},{9... | collective-permute-start | bytes 786440 | tf_op jit(solution)/shard_map/ppermute | solution.py:482
  143.5 16.4 %collective-permute-done.15.got_down = f32[2,4,64,128]{3,2,1,0:T(8,128)S(1)} collective-permute-done((f32[2,4,64,128]{3,2,1,0:T(8,128)S(1)}, f32[2,4,64,128]{3,2,1,0:T(8,128)S(1)}, u32[]{:S(2)}, u32[]{:S(2)}) %collective-permute-start.15) | collective-permute-done | bytes 262176 | tf_op jit(solution)/shard_map/ppermute | solution.py:482
  159.9 2.8 %shard_map.64 = (f32[4,64,128]{2,1,0:T(8,128)S(1)}, f32[4,64,128]{2,1,0:T(8,128)S(1)}, f32[4,64,128]{2,1,0:T(8,128)S(1)}) custom-call(s32[2]{0:T(128)S(1)} %pad_add_fusion.where, f32[2,4,64,128]{3,2,1,0:T(8,128)S(1)} %collective-permute-done.13.got_up, f32[2,4,64,128]{3,2,1,0:T(8,128)S(1)} %collective-permute-done.14.got, ...), custom_call_target="tpu_custom_call" | custom-call | tf_op jit(solution)/shard_map/pallas_call | solution.py:456
  162.7 9.3 %collective-permute-start.22 = (f32[8,128,128]{2,1,0:T(8,128)}, f32[8,128,128]{2,1,0:T(8,128)}, u32[]{:S(2)}, u32[]{:S(2)}) collective-permute-start(f32[8,128,128]{2,1,0:T(8,128)} %broadcast_select_fusion), channel_id=1, source_target_pairs={{0,96},{32,128},{64,160},{96,192},{128,224},{160,0},{192,32},{224,... | collective-permute-start | bytes 1572872 | tf_op jit(solution)/shard_map/ppermute | solution.py:491
  175.9 5.5 %collective-permute-start.18 = (f32[4,64,128]{2,1,0:T(8,128)S(1)}, f32[4,64,128]{2,1,0:T(8,128)S(1)}, u32[]{:S(2)}, u32[]{:S(2)}) collective-permute-start(f32[4,64,128]{2,1,0:T(8,128)S(1)} %get-tuple-element.31.last), channel_id=1, source_target_pairs={{1,0},{2,1},{3,2},{4,3},{5,4},{6,5},{7,6},{8,7},{9,8},{10,9},{11,1... | collective-permute-start | bytes 393224 | tf_op jit(solution)/shard_map/ppermute | solution.py:488
  181.4 3.7 %collective-permute-start.19 = (f32[4,64,128]{2,1,0:T(8,128)S(1)}, f32[4,64,128]{2,1,0:T(8,128)S(1)}, u32[]{:S(2)}, u32[]{:S(2)}) collective-permute-start(f32[4,64,128]{2,1,0:T(8,128)S(1)} %get-tuple-element.31.last), channel_id=1, source_target_pairs={{2,0},{3,1},{4,2},{5,3},{6,4},{7,5},{8,6},{9,7},{10,8},{11,9},{12,... | collective-permute-start | bytes 393224 | tf_op jit(solution)/shard_map/ppermute | solution.py:488
  185.1 5.0 %collective-permute-done.19.far_down = f32[4,64,128]{2,1,0:T(8,128)S(1)} collective-permute-done((f32[4,64,128]{2,1,0:T(8,128)S(1)}, f32[4,64,128]{2,1,0:T(8,128)S(1)}, u32[]{:S(2)}, u32[]{:S(2)}) %collective-permute-start.19) | collective-permute-done | bytes 131104 | tf_op jit(solution)/shard_map/ppermute | solution.py:488
  190.1 3.8 %shard_map.65 = (f32[4,64,128]{2,1,0:T(8,128)S(1)}, f32[4,64,128]{2,1,0:T(8,128)S(1)}) custom-call(s32[2]{0:T(128)S(1)} %pad_add_fusion.where, f32[4,64,128]{2,1,0:T(8,128)S(1)} %collective-permute-done.16.far_up, f32[4,64,128]{2,1,0:T(8,128)S(1)} %collective-permute-done.17.near_up, f32[4,64,128]{2,1,0:T(8,128)S(1)} %get-tuple-element.31.last, ...), custom_call_target="tpu_custom_call" | custom-call | tf_op jit(solution)/shard_map/pallas_call | solution.py:456
  193.9 4.9 %collective-permute-start.20 = (f32[4,64,128]{2,1,0:T(8,128)S(1)}, f32[4,64,128]{2,1,0:T(8,128)S(1)}, u32[]{:S(2)}, u32[]{:S(2)}) collective-permute-start(f32[4,64,128]{2,1,0:T(8,128)S(1)} %get-tuple-element.34), channel_id=1, source_target_pairs={{0,352},{32,384},{64,416},{96,448},{128,480},{160,256},{192,288},{... | collective-permute-start | bytes 393224 | tf_op jit(solution)/shard_map/ppermute | solution.py:491
  198.8 4.1 %collective-permute-start.21 = (f32[4,64,128]{2,1,0:T(8,128)S(1)}, f32[4,64,128]{2,1,0:T(8,128)S(1)}, u32[]{:S(2)}, u32[]{:S(2)}) collective-permute-start(f32[4,64,128]{2,1,0:T(8,128)S(1)} %get-tuple-element.35), channel_id=1, source_target_pairs={{0,96},{32,128},{64,160},{96,192},{128,224},{160,0},{192,32},{224,... | collective-permute-start | bytes 393224 | tf_op jit(solution)/shard_map/ppermute | solution.py:491
  205.3 15.1 %collective-permute-done.20 = f32[4,64,128]{2,1,0:T(8,128)S(1)} collective-permute-done((f32[4,64,128]{2,1,0:T(8,128)S(1)}, f32[4,64,128]{2,1,0:T(8,128)S(1)}, u32[]{:S(2)}, u32[]{:S(2)}) %collective-permute-start.20) | collective-permute-done | bytes 131104 | tf_op jit(solution)/shard_map/ppermute | solution.py:491
  (75 shorter events, 29.9 us)
Async XLA Ops:
  4.9 9.3 %copy-start.1 = (f32[8,128,128]{2,1,0:T(8,128)S(1)}, f32[8,128,128]{2,1,0:T(8,128)}, u32[]{:S(2)}) copy-start(f32[8,128,128]{2,1,0:T(8,128)} %kappa.7) | copy-start | bytes 1572868
  4.9 24.1 %copy-start.5 = (f32[8,128,128]{2,1,0:T(8,128)S(1)}, f32[8,128,128]{2,1,0:T(8,128)}, u32[]{:S(2)}) copy-start(f32[8,128,128]{2,1,0:T(8,128)} %source.7) | copy-start | bytes 1572868
  6.7 22.3 %copy-start.3 = (f32[8,128,128]{2,1,0:T(8,128)S(1)}, f32[8,128,128]{2,1,0:T(8,128)}, u32[]{:S(2)}) copy-start(f32[8,128,128]{2,1,0:T(8,128)} %initial.7) | copy-start | bytes 1572868
  6.7 21.3 %collective-permute-start = (f32[11,128,128]{2,1,0:T(8,128)}, f32[11,128,128]{2,1,0:T(8,128)S(1)}, u32[]{:S(2)}, u32[]{:S(2)}) collective-permute-start(f32[11,128,128]{2,1,0:T(8,128)} %get-tuple-element.20), channel_id=1, source_target_pairs={{0,1},{1,2},{2,3},{3,4},{4,5},{5,6},{6,7},{7,8},{8,9},{9,10},{10,1... | collective-permute-start | bytes 2162696 | tf_op jit(solution)/shard_map/ppermute | solution.py:488
  10.0 19.0 %collective-permute-start.1 = (f32[11,128,128]{2,1,0:T(8,128)}, f32[11,128,128]{2,1,0:T(8,128)S(1)}, u32[]{:S(2)}, u32[]{:S(2)}) collective-permute-start(f32[11,128,128]{2,1,0:T(8,128)} %get-tuple-element.21), channel_id=1, source_target_pairs={{1,0},{2,1},{3,2},{4,3},{5,4},{6,5},{7,6},{8,7},{9,8},{10,9},{11,1... | collective-permute-start | bytes 2162696 | tf_op jit(solution)/shard_map/ppermute | solution.py:488
  34.0 13.7 %collective-permute-start.2 = (f32[6,128,128]{2,1,0:T(8,128)S(1)}, f32[6,128,128]{2,1,0:T(8,128)S(1)}, u32[]{:S(2)}, u32[]{:S(2)}) collective-permute-start(f32[6,128,128]{2,1,0:T(8,128)S(1)} %get-tuple-element.22), channel_id=1, source_target_pairs={{0,1},{1,2},{2,3},{3,4},{4,5},{5,6},{6,7},{7,8},{8,9},{9,10},{10,1... | collective-permute-start | bytes 1179656 | tf_op jit(solution)/shard_map/ppermute | solution.py:488
  37.0 11.5 %collective-permute-start.3 = (f32[6,128,128]{2,1,0:T(8,128)S(1)}, f32[6,128,128]{2,1,0:T(8,128)S(1)}, u32[]{:S(2)}, u32[]{:S(2)}) collective-permute-start(f32[6,128,128]{2,1,0:T(8,128)S(1)} %get-tuple-element.23), channel_id=1, source_target_pairs={{1,0},{2,1},{3,2},{4,3},{5,4},{6,5},{7,6},{8,7},{9,8},{10,9},{11,1... | collective-permute-start | bytes 1179656 | tf_op jit(solution)/shard_map/ppermute | solution.py:488
  49.6 20.6 %copy-start.8 = (f32[11,128,128]{2,1,0:T(8,128)S(1)}, f32[11,128,128]{2,1,0:T(8,128)}, u32[]{:S(2)}) copy-start(f32[11,128,128]{2,1,0:T(8,128)} %copy-done.6) | copy-start | bytes 2162692
  53.6 16.6 %collective-permute-start.6 = (f32[8,128,128]{2,1,0:T(8,128)S(1)}, f32[8,128,128]{2,1,0:T(8,128)S(1)}, u32[]{:S(2)}, u32[]{:S(2)}) collective-permute-start(f32[8,128,128]{2,1,0:T(8,128)S(1)} %get-tuple-element.27.second), channel_id=1, source_target_pairs={{0,64},{32,96},{64,128},{96,160},{128,192},{160,224},{192,0},{224,... | collective-permute-start | bytes 1572872 | tf_op jit(solution)/shard_map/ppermute | solution.py:491
  56.7 12.6 %collective-permute-start.4 = (f32[6,128,128]{2,1,0:T(8,128)S(1)}, f32[6,128,128]{2,1,0:T(8,128)S(1)}, u32[]{:S(2)}, u32[]{:S(2)}) collective-permute-start(f32[6,128,128]{2,1,0:T(8,128)S(1)} %get-tuple-element.25), channel_id=1, source_target_pairs={{0,1},{1,2},{2,3},{3,4},{4,5},{5,6},{6,7},{7,8},{8,9},{9,10},{10,1... | collective-permute-start | bytes 1179656 | tf_op jit(solution)/shard_map/ppermute | solution.py:488
  60.7 9.5 %collective-permute-start.5 = (f32[6,128,128]{2,1,0:T(8,128)S(1)}, f32[6,128,128]{2,1,0:T(8,128)S(1)}, u32[]{:S(2)}, u32[]{:S(2)}) collective-permute-start(f32[6,128,128]{2,1,0:T(8,128)S(1)} %get-tuple-element.26), channel_id=1, source_target_pairs={{1,0},{2,1},{3,2},{4,3},{5,4},{6,5},{7,6},{8,7},{9,8},{10,9},{11,1... | collective-permute-start | bytes 1179656 | tf_op jit(solution)/shard_map/ppermute | solution.py:488
  75.4 10.1 %copy-start.17 = (f32[8,128,128]{2,1,0:T(8,128)}, f32[8,128,128]{2,1,0:T(8,128)S(1)}, u32[]{:S(2)}) copy-start(f32[8,128,128]{2,1,0:T(8,128)S(1)} %get-tuple-element.36) | copy-start | bytes 1572868
  75.4 8.6 %collective-permute-start.7 = (f32[4,64,128]{2,1,0:T(8,128)S(1)}, f32[4,64,128]{2,1,0:T(8,128)S(1)}, u32[]{:S(2)}, u32[]{:S(2)}) collective-permute-start(f32[4,64,128]{2,1,0:T(8,128)S(1)} %get-tuple-element.29.tau), channel_id=1, source_target_pairs={{0,1},{1,2},{2,3},{3,4},{4,5},{5,6},{6,7},{7,8},{8,9},{9,10},{10,1... | collective-permute-start | bytes 393224 | tf_op jit(solution)/shard_map/ppermute | solution.py:488
  79.4 6.1 %collective-permute-start.8 = (f32[4,64,128]{2,1,0:T(8,128)S(1)}, f32[4,64,128]{2,1,0:T(8,128)S(1)}, u32[]{:S(2)}, u32[]{:S(2)}) collective-permute-start(f32[4,64,128]{2,1,0:T(8,128)S(1)} %get-tuple-element.29.tau), channel_id=1, source_target_pairs={{1,0},{2,1},{3,2},{4,3},{5,4},{6,5},{7,6},{8,7},{9,8},{10,9},{11,1... | collective-permute-start | bytes 393224 | tf_op jit(solution)/shard_map/ppermute | solution.py:488
  85.6 8.7 %collective-permute-start.9 = (f32[6,64,128]{2,1,0:T(8,128)S(1)}, f32[6,64,128]{2,1,0:T(8,128)S(1)}, u32[]{:S(2)}, u32[]{:S(2)}) collective-permute-start(f32[6,64,128]{2,1,0:T(8,128)S(1)} %slice.12), channel_id=1, source_target_pairs={{0,32},{32,64},{64,96},{96,128},{128,160},{160,192},{192,224},{224... | collective-permute-start | bytes 589832 | tf_op jit(solution)/shard_map/ppermute | solution.py:491
  94.3 46.4 %collective-permute-start.10 = (f32[8,128,128]{2,1,0:T(8,128)}, f32[8,128,128]{2,1,0:T(8,128)S(1)}, u32[]{:S(2)}, u32[]{:S(2)}) collective-permute-start(f32[8,128,128]{2,1,0:T(8,128)} %get-tuple-element.30), channel_id=1, source_target_pairs={{0,256},{32,288},{160,416},{192,448},{224,480},{256,0},{288,32},{4... | collective-permute-start | bytes 1572872 | tf_op jit(solution)/shard_map/ppermute | solution.py:491
  108.7 16.9 %collective-permute-start.11 = (f32[10,64,128]{2,1,0:T(8,128)S(1)}, f32[10,64,128]{2,1,0:T(8,128)S(1)}, u32[]{:S(2)}, u32[]{:S(2)}) collective-permute-start(f32[10,64,128]{2,1,0:T(8,128)S(1)} %slice.13), channel_id=1, source_target_pairs={{0,96},{32,128},{64,160},{96,192},{128,224},{160,0},{192,32},{224,... | collective-permute-start | bytes 983048 | tf_op jit(solution)/shard_map/ppermute | solution.py:491
  110.6 15.0 %collective-permute-start.12 = (f32[8,64,128]{2,1,0:T(8,128)S(1)}, f32[8,64,128]{2,1,0:T(8,128)S(1)}, u32[]{:S(2)}, u32[]{:S(2)}) collective-permute-start(f32[8,64,128]{2,1,0:T(8,128)S(1)} %slice.14), channel_id=1, source_target_pairs={{0,64},{32,96},{64,128},{96,160},{128,192},{160,224},{192,0},{224,... | collective-permute-start | bytes 786440 | tf_op jit(solution)/shard_map/ppermute | solution.py:491
  116.2 24.6 %copy-start.18 = (f32[8,128,128]{2,1,0:T(8,128)S(1)}, f32[8,128,128]{2,1,0:T(8,128)}, u32[]{:S(2)}) copy-start(f32[8,128,128]{2,1,0:T(8,128)} %copy-done.17) | copy-start | bytes 1572868
  127.7 13.9 %collective-permute-start.13 = (f32[2,4,64,128]{3,2,1,0:T(8,128)S(1)}, f32[2,4,64,128]{3,2,1,0:T(8,128)S(1)}, u32[]{:S(2)}, u32[]{:S(2)}) collective-permute-start(f32[2,4,64,128]{3,2,1,0:T(8,128)S(1)} %shard_map.63.both), channel_id=1, source_target_pairs={{0,129},{1,130},{2,131},{3,132},{4,133},{5,134},{6,135},{7,136},{8... | collective-permute-start | bytes 786440 | tf_op jit(solution)/shard_map/ppermute | solution.py:482
  131.7 11.7 %collective-permute-start.14 = (f32[2,4,64,128]{3,2,1,0:T(8,128)S(1)}, f32[2,4,64,128]{3,2,1,0:T(8,128)S(1)}, u32[]{:S(2)}, u32[]{:S(2)}) collective-permute-start(f32[2,4,64,128]{3,2,1,0:T(8,128)S(1)} %shard_map.63.both), channel_id=1, source_target_pairs={{0,128},{1,129},{2,130},{3,131},{4,132},{5,133},{6,134},{7,135},{8... | collective-permute-start | bytes 786440 | tf_op jit(solution)/shard_map/ppermute | solution.py:482
  135.3 24.6 %collective-permute-start.15 = (f32[2,4,64,128]{3,2,1,0:T(8,128)S(1)}, f32[2,4,64,128]{3,2,1,0:T(8,128)S(1)}, u32[]{:S(2)}, u32[]{:S(2)}) collective-permute-start(f32[2,4,64,128]{3,2,1,0:T(8,128)S(1)} %shard_map.63.both), channel_id=1, source_target_pairs={{1,128},{2,129},{3,130},{4,131},{5,132},{6,133},{7,134},{8,135},{9... | collective-permute-start | bytes 786440 | tf_op jit(solution)/shard_map/ppermute | solution.py:482
  141.6 48.5 %copy-start.14 = (f32[6,128,128]{2,1,0:T(8,128)S(1)}, f32[6,128,128]{2,1,0:T(8,128)}, u32[]{:S(2)}) copy-start(f32[6,128,128]{2,1,0:T(8,128)} %copy-done.13) | copy-start | bytes 1179652
  141.6 48.5 %copy-start.16 = (f32[6,128,128]{2,1,0:T(8,128)S(1)}, f32[6,128,128]{2,1,0:T(8,128)}, u32[]{:S(2)}) copy-start(f32[6,128,128]{2,1,0:T(8,128)} %copy-done.15) | copy-start | bytes 1179652
  162.7 40.2 %collective-permute-start.22 = (f32[8,128,128]{2,1,0:T(8,128)}, f32[8,128,128]{2,1,0:T(8,128)}, u32[]{:S(2)}, u32[]{:S(2)}) collective-permute-start(f32[8,128,128]{2,1,0:T(8,128)} %broadcast_select_fusion), channel_id=1, source_target_pairs={{0,96},{32,128},{64,160},{96,192},{128,224},{160,0},{192,32},{224,... | collective-permute-start | bytes 1572872 | tf_op jit(solution)/shard_map/ppermute | solution.py:491
  172.0 13.0 %collective-permute-start.16 = (f32[4,64,128]{2,1,0:T(8,128)S(1)}, f32[4,64,128]{2,1,0:T(8,128)S(1)}, u32[]{:S(2)}, u32[]{:S(2)}) collective-permute-start(f32[4,64,128]{2,1,0:T(8,128)S(1)} %get-tuple-element.31.last), channel_id=1, source_target_pairs={{0,2},{1,3},{2,4},{3,5},{4,6},{5,7},{6,8},{7,9},{8,10},{9,11},{10,... | collective-permute-start | bytes 393224 | tf_op jit(solution)/shard_map/ppermute | solution.py:488
  173.9 11.1 %collective-permute-start.17 = (f32[4,64,128]{2,1,0:T(8,128)S(1)}, f32[4,64,128]{2,1,0:T(8,128)S(1)}, u32[]{:S(2)}, u32[]{:S(2)}) collective-permute-start(f32[4,64,128]{2,1,0:T(8,128)S(1)} %get-tuple-element.31.last), channel_id=1, source_target_pairs={{0,1},{1,2},{2,3},{3,4},{4,5},{5,6},{6,7},{7,8},{8,9},{9,10},{10,1... | collective-permute-start | bytes 393224 | tf_op jit(solution)/shard_map/ppermute | solution.py:488
  175.9 9.2 %collective-permute-start.18 = (f32[4,64,128]{2,1,0:T(8,128)S(1)}, f32[4,64,128]{2,1,0:T(8,128)S(1)}, u32[]{:S(2)}, u32[]{:S(2)}) collective-permute-start(f32[4,64,128]{2,1,0:T(8,128)S(1)} %get-tuple-element.31.last), channel_id=1, source_target_pairs={{1,0},{2,1},{3,2},{4,3},{5,4},{6,5},{7,6},{8,7},{9,8},{10,9},{11,1... | collective-permute-start | bytes 393224 | tf_op jit(solution)/shard_map/ppermute | solution.py:488
  181.4 8.7 %collective-permute-start.19 = (f32[4,64,128]{2,1,0:T(8,128)S(1)}, f32[4,64,128]{2,1,0:T(8,128)S(1)}, u32[]{:S(2)}, u32[]{:S(2)}) collective-permute-start(f32[4,64,128]{2,1,0:T(8,128)S(1)} %get-tuple-element.31.last), channel_id=1, source_target_pairs={{2,0},{3,1},{4,2},{5,3},{6,4},{7,5},{8,6},{9,7},{10,8},{11,9},{12,... | collective-permute-start | bytes 393224 | tf_op jit(solution)/shard_map/ppermute | solution.py:488
  190.1 12.9 %copy-start.12 = (f32[8,128,128]{2,1,0:T(8,128)S(1)}, f32[8,128,128]{2,1,0:T(8,128)}, u32[]{:S(2)}) copy-start(f32[8,128,128]{2,1,0:T(8,128)} %copy-done.11) | copy-start | bytes 1572868
  193.9 26.6 %collective-permute-start.20 = (f32[4,64,128]{2,1,0:T(8,128)S(1)}, f32[4,64,128]{2,1,0:T(8,128)S(1)}, u32[]{:S(2)}, u32[]{:S(2)}) collective-permute-start(f32[4,64,128]{2,1,0:T(8,128)S(1)} %get-tuple-element.34), channel_id=1, source_target_pairs={{0,352},{32,384},{64,416},{96,448},{128,480},{160,256},{192,288},{... | collective-permute-start | bytes 393224 | tf_op jit(solution)/shard_map/ppermute | solution.py:491
  198.8 21.6 %collective-permute-start.21 = (f32[4,64,128]{2,1,0:T(8,128)S(1)}, f32[4,64,128]{2,1,0:T(8,128)S(1)}, u32[]{:S(2)}, u32[]{:S(2)}) collective-permute-start(f32[4,64,128]{2,1,0:T(8,128)S(1)} %get-tuple-element.35), channel_id=1, source_target_pairs={{0,96},{32,128},{64,160},{96,192},{128,224},{160,0},{192,32},{224,... | collective-permute-start | bytes 393224 | tf_op jit(solution)/shard_map/ppermute | solution.py:491
  (10 other events, 26.8 us)

commit v8 on v6

--- a/solution.py
+++ b/solution.py
@@ -147,21 +147,40 @@
         src, dst = dst, src
 
 
-def first_ends_kernel(where, guess, initial, kappa, source, first_out, last_out):
+def first_ends_kernel(
+    where, guess, initial, kappa, source, first_out, last_out, sems
+):
     rows = kappa.shape[0]
-    start = where[0] == 15
-    for out, at, heat in ((first_out, 0, 0), (last_out, rows - STEPS, rows - STEPS + 1)):
-
-        @pl.when(start)
-        def _(out=out, at=at):
-            out[:STEPS] = initial[at : at + STEPS]
-
-        @pl.when(jnp.logical_not(start))
-        def _(out=out, at=at):
-            out[:STEPS] = guess[at : at + STEPS]
-
-        out[STEPS : 2 * STEPS] = kappa[at : at + STEPS]
-        out[2 * STEPS :] = source[heat : heat + STEPS - 1]
+
+    def copies(state):
+        index = 0
+        for out, at, heat in (
+            (first_out, 0, 0),
+            (last_out, rows - STEPS, rows - STEPS + 1),
+        ):
+            for ref, first, count, row in (
+                (state, at, STEPS, 0),
+                (kappa, at, STEPS, STEPS),
+                (source, heat, STEPS - 1, 2 * STEPS),
+            ):
+                yield pltpu.make_async_copy(
+                    ref.at[pl.ds(first, count)], out.at[pl.ds(row, count)], sems.at[index]
+                )
+                index += 1
+
+    @pl.when(where[0] == 15)
+    def _():
+        for copy in copies(initial):
+            copy.start()
+        for copy in copies(initial):
+            copy.wait()
+
+    @pl.when(where[0] != 15)
+    def _():
+        for copy in copies(guess):
+            copy.start()
+        for copy in copies(guess):
+            copy.wait()
 
 
 def phase_one_kernel(
@@ -309,8 +328,55 @@
         tau_out[row] = now - use * tau_out[row]
 
 
+def coarse_kappa_8(field, up_2, down_2, up_3, down_3, kappa_c):
+    block, half = kappa_c.shape[:2]
+    coarse_kappa_4(field, up_2, down_2, kappa_c, block)
+    for row in range(block):
+        piece = (STEPS + row // 2, slice(row % 2 * half, (row % 2 + 1) * half))
+        field[row, PAD : PAD + half] = up_3[piece]
+        field[4 * block + row, PAD : PAD + half] = down_3[piece]
+
+
+def far_sums_kernel(
+    slabs, where, got_a, got_b, wide_a, wide_b, up_2, down_2, up_3, down_3, kappa_c,
+    ahead_out, wrapped_out, *scratch,
+):
+    field, spare, kappa_wide, *weights = scratch
+    block = kappa_c.shape[0]
+    deep = 2 * block - 1
+    rows = block + 2 * deep
+    part = rows // 2
+    local = lax.rem(where[0], GROUP)
+    high = where[0] >= GROUP
+    clear_edges(field)
+    clear_edges(spare)
+    coarse_kappa_8(kappa_wide, up_2, down_2, up_3, down_3, kappa_c)
+    face_weights(kappa_wide, weights, 4.0 * ALONG_THIRD)
+    fill(field, [(got_a, 1, part, 0), (got_b, 0, part, part)])
+    inside = inside_of(where[1], slabs, deep, block)
+    late = local >= 4
+    to_ahead = jnp.where(late & ~(high & (local >= 5)), 1.0, 0.0)
+    to_wrapped = jnp.where(late | (high & (local == 0)), 0.0, 1.0)
+
+    def out(rows, value):
+        ahead_out[rows] = to_ahead * value
+        wrapped_out[rows] = to_wrapped * value
+
+    src, dst = field, spare
+    for step in range(1, block + 1):
+        sweep(
+            src, dst, weights, None, step, rows - 2 * step, 1, inside,
+            out if step == block else None,
+        )
+        src, dst = dst, src
+    cut = part - block
+    ahead_out[:cut] = ahead_out[:cut] + wide_a[block + 1 :]
+    ahead_out[cut:] = ahead_out[cut:] + wide_b[: rows - 2 * block - cut]
+
+
 def near_sums_kernel(
-    slabs, where, got_3, got_2, got_1, tau, up_2, down_2, kappa_c, both_out, *scratch
+    slabs, where, got_3, got_2, got_1, behind_3, behind_2, behind_1, own_ahead,
+    own_wrapped, up_2, down_2, kappa_c, ahead_out, wrapped_out, last_out, *scratch,
 ):
     ahead, wrapped, spare, kappa_wide, *weights = scratch
     block, half = kappa_c.shape[:2]
@@ -321,23 +387,29 @@
     coarse_kappa_4(kappa_wide, up_2, down_2, kappa_c, 0)
     face_weights(kappa_wide, weights, 4.0 * ALONG_THIRD)
     inside = inside_of(where[1], slabs, block, block)
+    own = slice(block - 1, 2 * block - 1)
     for is_ahead in (True, False):
         src, dst = (ahead, spare) if is_ahead else (wrapped, spare)
-        for distance, got in ((3, got_3), (2, got_2), (1, got_1)):
+        for distance, got, behind in (
+            (3, got_3, behind_3), (2, got_2, behind_2), (1, got_1, behind_1),
+        ):
             apart = high & (local >= 5) & (local < distance + 5)
             use = (local >= distance) & ~apart if is_ahead else local < distance
-            use = jnp.where(use, 1.0, 0.0)
-            for row in range(block + 2 * distance):
-                at = (row + block - distance, slice(PAD, PAD + half))
-                value = use * got[row]
-                src[at] = value if distance == 3 else src[at] + value
+            value = jnp.where(use, 1.0, 0.0) * got[...]
+            if not is_ahead:
+                value = value + behind[...]
+            at = (
+                slice(block - distance, 2 * block + distance),
+                slice(PAD, PAD + half),
+            )
+            src[at] = value if distance == 3 else src[at] + value
             if distance == 1:
 
                 def out(rows, value, is_ahead=is_ahead):
-                    if is_ahead:
-                        both_out[0, rows] = value + tau[rows]
-                    else:
-                        both_out[1, rows] = value
+                    result, mine = (
+                        (ahead_out, own_ahead) if is_ahead else (wrapped_out, own_wrapped)
+                    )
+                    result[rows] = value + mine[own][rows]
 
             else:
                 out = None
@@ -346,11 +418,20 @@
                 0, inside, out,
             )
             src, dst = dst, src
-
-
-def far_sums_kernel(
-    slabs, where, got_up, got, got_down, both, up_2, down_2, kappa_c, _,
-    ahead_out, wrapped_out, last_out, *scratch,
+    hand_wrapped = high & (local < 5)
+
+    @pl.when(hand_wrapped)
+    def _():
+        last_out[...] = wrapped_out[...]
+
+    @pl.when(jnp.logical_not(hand_wrapped))
+    def _():
+        last_out[...] = ahead_out[...]
+
+
+def hand_over_kernel(
+    slabs, where, far_up, near_up, last, near_down, far_down, up_2, down_2, up_3, down_3,
+    kappa_c, ahead, wrapped, _, handed_out, kept_out, *scratch,
 ):
     field, spare, kappa_wide, *weights = scratch
     block, half = kappa_c.shape[:2]
@@ -358,59 +439,7 @@
     high = where[0] >= GROUP
     clear_edges(field)
     clear_edges(spare)
-    coarse_kappa_4(kappa_wide, up_2, down_2, kappa_c, 0)
-    face_weights(kappa_wide, weights, 4.0 * ALONG_THIRD)
-    inside = inside_of(where[1], slabs, block, block)
-    late = local >= 4
-    to_ahead = jnp.where(late & ~(high & (local >= 5)), 1.0, 0.0)
-    from_wrapped = jnp.where(late, 1.0, 0.0)
-    from_ahead = jnp.where(late | (high & (local == 0)), 0.0, 1.0)
-    for index, result in ((0, ahead_out), (1, wrapped_out)):
-        for piece, ref in enumerate((got_up, got, got_down)):
-            for row in range(block):
-                at = (piece * block + row, slice(PAD, PAD + half))
-                if index == 0:
-                    field[at] = to_ahead * ref[0, row]
-                else:
-                    field[at] = from_wrapped * ref[1, row] + from_ahead * ref[0, row]
-
-        def out(rows, value, index=index, result=result):
-            result[rows] = value + both[index, rows]
-
-        src, dst = field, spare
-        for step in range(1, block + 1):
-            count = 3 * block - 2 * step
-            sweep(
-                src, dst, weights, None, step, count, 0, inside,
-                out if step == block else None,
-            )
-            src, dst = dst, src
-    hand_wrapped = high & (local < 5)
-
-    @pl.when(hand_wrapped)
-    def _():
-        last_out[...] = wrapped_out[...]
-
-    @pl.when(jnp.logical_not(hand_wrapped))
-    def _():
-        last_out[...] = ahead_out[...]
-
-
-def hand_over_kernel(
-    slabs, where, far_up, near_up, last, near_down, far_down, up_2, down_2, up_3, down_3,
-    kappa_c, ahead, wrapped, handed_out, kept_out, *scratch,
-):
-    field, spare, kappa_wide, *weights = scratch
-    block, half = kappa_c.shape[:2]
-    local = lax.rem(where[0], GROUP)
-    high = where[0] >= GROUP
-    clear_edges(field)
-    clear_edges(spare)
-    coarse_kappa_4(kappa_wide, up_2, down_2, kappa_c, block)
-    for row in range(block):
-        piece = (STEPS + row // 2, slice(row % 2 * half, (row % 2 + 1) * half))
-        kappa_wide[row, PAD : PAD + half] = up_3[piece]
-        kappa_wide[4 * block + row, PAD : PAD + half] = down_3[piece]
+    coarse_kappa_8(kappa_wide, up_2, down_2, up_3, down_3, kappa_c)
     fill(
         field,
         [
@@ -450,7 +479,7 @@
         src, dst = dst, src
 
 
-def call(kernel, slabs, outs, scratch, where, *args, unread=0):
+def call(kernel, slabs, outs, scratch, where, *args, unread=0, room=40):
     vmem = pl.BlockSpec(memory_space=pltpu.VMEM)
     anywhere = pl.BlockSpec(memory_space=pl.ANY)
     return pl.pallas_call(
@@ -461,7 +490,7 @@
         + [anywhere] * unread,
         out_specs=[vmem] * len(outs),
         scratch_shapes=scratch,
-        compiler_params=pltpu.CompilerParams(vmem_limit_bytes=40 * 2**20),
+        compiler_params=pltpu.CompilerParams(vmem_limit_bytes=room * 2**20),
         cost_estimate=pl.CostEstimate(flops=0, bytes_accessed=0, transcendentals=0),
     )(where, *args)
 
@@ -478,9 +507,6 @@
     def cut(array, have, want):
         return array[have - want : array.shape[0] - (have - want)]
 
-    def route(block, pairs):
-        return lax.ppermute(block, ("tm", "space"), pairs)
-
     def along_space(block, distance):
         pairs = [
             (i, i + distance) for i in range(slabs) if 0 <= i + distance < slabs
@@ -510,8 +536,9 @@
 
     kappa_c = restrict(conductivity)
     first, last = call(
-        first_ends_kernel, None, [(3 * STEPS - 1, width_two, width_three)] * 2, [],
-        where, guess[0], initial, conductivity, source,
+        first_ends_kernel, None, [(3 * STEPS - 1, width_two, width_three)] * 2,
+        [pltpu.SemaphoreType.DMA((6,))],
+        where, guess[0], initial, conductivity, source, unread=4, room=60,
     )
     sides = neighbours(first, last)
     state, first, last = call(
@@ -534,47 +561,46 @@
         second_near,
     )
 
-    up, down = neighbours(tau, tau)
-    tau_wide = jnp.concatenate([up, tau, down], 0)
-    got = [along_time(cut(tau_wide, crows, d), ring(d)) for d in (3, 2, 1)]
+    deep = 2 * crows - 1
+    far = (along_space(tau, 2), along_space(tau, -2))
+    near = neighbours(tau, tau)
+    tau_wide = jnp.concatenate([far[0], near[0], tau, near[1], far[1]], 0)
+    part = tau_wide.shape[0] // 2
+    wide = (tau_wide[:part], tau_wide[part:])
+    got_a = along_time(wide[0], ring(4))
     crossed = along_time(
-        crossed,
+        lax.optimization_barrier((crossed, got_a))[0],
         [(i, i ^ GROUP) for i in range(2 * GROUP) if i % GROUP in (0, 1, 5, 6, 7)],
     )
-    (both,) = call(
-        near_sums_kernel, slabs, [(2,) + coarse_shape],
+    got_b = along_time(wide[1], ring(4))
+    wide_shape = (deep + 3,) + coarse_shape[1:]
+    ahead, wrapped = call(
+        far_sums_kernel, slabs, [wide_shape] * 2,
+        coarse_scratch(5 * crows, half, width_three, 2),
+        where, got_a, got_b, *wide, *sides_2, *sides_3, kappa_c,
+    )
+    behind_pairs = lambda d: [
+        (g * GROUP + i, g * GROUP + i + d) for g in (0, 1) for i in range(4)
+    ]
+    got = [along_time(cut(ahead, 3, d), ring(d)) for d in (3, 2, 1)]
+    behind = [along_time(cut(wrapped, 3, d), behind_pairs(d)) for d in (3, 2, 1)]
+    ahead, wrapped, last = call(
+        near_sums_kernel, slabs, [coarse_shape] * 3,
         coarse_scratch(3 * crows, half, width_three, 3),
-        where, *got, tau, *sides_2, kappa_c,
-    )
-
-    def diagonal(distance):
-        pairs = [
-            (t * slabs + i, u * slabs + i + distance)
-            for t, u in ring(4)
-            for i in range(slabs)
-            if 0 <= i + distance < slabs
-        ]
-        return route(both, pairs)
-
-    got = [diagonal(1), diagonal(0), diagonal(-1)]
-    ahead, wrapped, last = call(
-        far_sums_kernel, slabs, [coarse_shape] * 3,
-        coarse_scratch(3 * crows, half, width_three, 2),
-        where, *got, both, *sides_2, kappa_c, crossed, unread=1,
-    )
-
-    third_home = along_time(
-        lax.optimization_barrier((jnp.where(local >= 5, crossed, third), last))[0],
-        ring(3),
-    )
+        where, *got, *behind, ahead, wrapped, *sides_2, kappa_c,
+    )
+
     near = neighbours(last, last)
     far = (along_space(last, 2), along_space(last, -2))
     handed, kept = call(
         hand_over_kernel, slabs, [coarse_shape] * 2,
         coarse_scratch(5 * crows, half, width_three, 2),
         where, far[0], near[0], last, near[1], far[1], *sides_2, *sides_3, kappa_c,
-        ahead, wrapped,
-    )
+        ahead, wrapped, crossed, unread=1,
+    )
+    third = lax.optimization_barrier(
+        (jnp.where(local >= 5, crossed, third), handed)
+    )[0]
     handed = along_time(
         handed,
         [
@@ -584,6 +610,7 @@
         ],
     )
     kept = along_time(kept, ring(3))
+    third_home = along_time(third, ring(3))
     second_home = jnp.where(local < 2, crossed, second_near)
 
     residual = third_home - second_home

time: 234 us -> 214 us (0.915)
  the two profiles are of different devices: /device:TPU:81 before, /device:TPU:97 now
where the time goes in v8:
time: 214 us; the launch traced here: 213 us
  starting transfers between devices  116 us (54%)
  waiting for transfers between devices  59.7 us (28%)
  Pallas kernels  25.9 us (12%)
  local copies, waits for them, and re-layouts  7.11 us (3%)
  other arithmetic  4.02 us (2%)
    ppermute x13, starting transfers between devices, along_time(): return lax.ppermute(block, 'tm', pairs)  60.3 us
    ppermute x14, starting transfers between devices, along_space(): return lax.ppermute(block, 'space', pairs)  55.3 us
    ppermute x14, waiting for transfers between devices, along_space(): return lax.ppermute(block, 'space', pairs)  37.1 us
    pallas_call x7, Pallas kernels, call(): pl.pallas_call(kernel if slabs is None else functools.partial(kernel, sla...  25.9 us
    ppermute x13, waiting for transfers between devices, along_time(): return lax.ppermute(block, 'tm', pairs)  22.6 us
    unnamed x40, local copies, waits for them, and re-layouts  5.42 us
  transfers between devices with their start and end apart: 27, of which 14 were waited for; matrix products, arithmetic and copies ran while one was open for 2% of the time, Pallas kernels for 2%

profile of v8, /device:TPU:97, one launch (start us, length us, event | category | flops | bytes accessed | tf_op | source)
XLA Modules:
  0.0 213.4 jit_solution(1329469548565871681)
XLA Ops:
  1.2 3.3 %shard_map.59 = (f32[11,128,128]{2,1,0:T(8,128)}, f32[11,128,128]{2,1,0:T(8,128)}) custom-call(s32[2]{0:T(128)} %pad_add_fusion.where, f32[8,128,128]{2,1,0:T(8,128)} %bitcast.12, f32[8,128,128]{2,1,0:T(8,128)} %initial.7, f32[8,128,128]{2,1,0:T(8,128)} %kappa.7, f32[8,128,128]{2,1,0:T(8,128)} %source.7), custom_call_target="tpu_custom_call" | custom-call | tf_op jit(solution)/shard_map/pallas_call | solution.py:485
  4.5 3.3 %collective-permute-start = (f32[11,128,128]{2,1,0:T(8,128)}, f32[11,128,128]{2,1,0:T(8,128)S(1)}, u32[]{:S(2)}, u32[]{:S(2)}) collective-permute-start(f32[11,128,128]{2,1,0:T(8,128)} %get-tuple-element.22), channel_id=1, source_target_pairs={{0,1},{1,2},{2,3},{3,4},{4,5},{5,6},{6,7},{7,8},{8,9},{9,10},{10,1... | collective-permute-start | bytes 2162696 | tf_op jit(solution)/shard_map/ppermute | solution.py:514
  7.9 4.2 %collective-permute-start.1 = (f32[11,128,128]{2,1,0:T(8,128)}, f32[11,128,128]{2,1,0:T(8,128)S(1)}, u32[]{:S(2)}, u32[]{:S(2)}) collective-permute-start(f32[11,128,128]{2,1,0:T(8,128)} %get-tuple-element.23), channel_id=1, source_target_pairs={{1,0},{2,1},{3,2},{4,3},{5,4},{6,5},{7,6},{8,7},{9,8},{10,9},{11,1... | collective-permute-start | bytes 2162696 | tf_op jit(solution)/shard_map/ppermute | solution.py:514
  12.5 13.4 %collective-permute-done.up_1 = f32[11,128,128]{2,1,0:T(8,128)S(1)} collective-permute-done((f32[11,128,128]{2,1,0:T(8,128)}, f32[11,128,128]{2,1,0:T(8,128)S(1)}, u32[]{:S(2)}, u32[]{:S(2)}) %collective-permute-start) | collective-permute-done | bytes 720928 | tf_op jit(solution)/shard_map/ppermute | solution.py:514
  27.9 4.1 %shard_map.60 = (f32[8,128,128]{2,1,0:T(8,128)S(1)}, f32[6,128,128]{2,1,0:T(8,128)S(1)}, f32[6,128,128]{2,1,0:T(8,128)S(1)}) custom-call(s32[2]{0:T(128)S(1)} %copy-done.19, f32[11,128,128]{2,1,0:T(8,128)S(1)} %collective-permute-done.up_1, f32[11,128,128]{2,1,0:T(8,128)S(1)} %collective-permute-done.1.down_1, f32[8,128,128]{2,1,0:T(8,128)S(1)} %bitcast.13, ...), custom_call_target="tpu_custom_call" | custom-call | tf_op jit(solution)/shard_map/pallas_call | solution.py:485
  32.1 3.0 %collective-permute-start.2 = (f32[6,128,128]{2,1,0:T(8,128)S(1)}, f32[6,128,128]{2,1,0:T(8,128)S(1)}, u32[]{:S(2)}, u32[]{:S(2)}) collective-permute-start(f32[6,128,128]{2,1,0:T(8,128)S(1)} %get-tuple-element.24), channel_id=1, source_target_pairs={{0,1},{1,2},{2,3},{3,4},{4,5},{5,6},{6,7},{7,8},{8,9},{9,10},{10,1... | collective-permute-start | bytes 1179656 | tf_op jit(solution)/shard_map/ppermute | solution.py:514
  35.1 5.0 %collective-permute-start.3 = (f32[6,128,128]{2,1,0:T(8,128)S(1)}, f32[6,128,128]{2,1,0:T(8,128)S(1)}, u32[]{:S(2)}, u32[]{:S(2)}) collective-permute-start(f32[6,128,128]{2,1,0:T(8,128)S(1)} %get-tuple-element.25), channel_id=1, source_target_pairs={{1,0},{2,1},{3,2},{4,3},{5,4},{6,5},{7,6},{8,7},{9,8},{10,9},{11,1... | collective-permute-start | bytes 1179656 | tf_op jit(solution)/shard_map/ppermute | solution.py:514
  40.1 5.6 %collective-permute-done.2.up_2 = f32[6,128,128]{2,1,0:T(8,128)S(1)} collective-permute-done((f32[6,128,128]{2,1,0:T(8,128)S(1)}, f32[6,128,128]{2,1,0:T(8,128)S(1)}, u32[]{:S(2)}, u32[]{:S(2)}) %collective-permute-start.2) | collective-permute-done | bytes 393248 | tf_op jit(solution)/shard_map/ppermute | solution.py:514
  48.1 4.1 %shard_map.61 = (f32[8,128,128]{2,1,0:T(8,128)S(1)}, f32[6,128,128]{2,1,0:T(8,128)S(1)}, f32[6,128,128]{2,1,0:T(8,128)S(1)}) custom-call(s32[2]{0:T(128)S(1)} %copy-done.19, f32[11,128,128]{2,1,0:T(8,128)S(1)} %collective-permute-done.up_1, f32[11,128,128]{2,1,0:T(8,128)S(1)} %copy-done.4, f32[6,128,128]{2,1,0:T(8,128)S(1)} %collective-permute-done.2.up_2, ...), custom_call_target="tpu_custom_call" | custom-call | tf_op jit(solution)/shard_map/pallas_call | solution.py:485
  52.3 3.1 %collective-permute-start.6 = (f32[8,128,128]{2,1,0:T(8,128)S(1)}, f32[8,128,128]{2,1,0:T(8,128)S(1)}, u32[]{:S(2)}, u32[]{:S(2)}) collective-permute-start(f32[8,128,128]{2,1,0:T(8,128)S(1)} %get-tuple-element.29.second), channel_id=1, source_target_pairs={{0,64},{32,96},{64,128},{96,160},{128,192},{160,224},{192,0},{224,... | collective-permute-start | bytes 1572872 | tf_op jit(solution)/shard_map/ppermute | solution.py:517
  55.4 6.0 %collective-permute-start.4 = (f32[6,128,128]{2,1,0:T(8,128)S(1)}, f32[6,128,128]{2,1,0:T(8,128)S(1)}, u32[]{:S(2)}, u32[]{:S(2)}) collective-permute-start(f32[6,128,128]{2,1,0:T(8,128)S(1)} %get-tuple-element.27), channel_id=1, source_target_pairs={{0,1},{1,2},{2,3},{3,4},{4,5},{5,6},{6,7},{7,8},{8,9},{9,10},{10,1... | collective-permute-start | bytes 1179656 | tf_op jit(solution)/shard_map/ppermute | solution.py:514
  63.4 4.3 %collective-permute-done.4.up_3 = f32[6,128,128]{2,1,0:T(8,128)S(1)} collective-permute-done((f32[6,128,128]{2,1,0:T(8,128)S(1)}, f32[6,128,128]{2,1,0:T(8,128)S(1)}, u32[]{:S(2)}, u32[]{:S(2)}) %collective-permute-start.4) | collective-permute-done | bytes 393248 | tf_op jit(solution)/shard_map/ppermute | solution.py:514
  67.6 3.0 %collective-permute-done.5.down_3 = f32[6,128,128]{2,1,0:T(8,128)S(1)} collective-permute-done((f32[6,128,128]{2,1,0:T(8,128)S(1)}, f32[6,128,128]{2,1,0:T(8,128)S(1)}, u32[]{:S(2)}, u32[]{:S(2)}) %collective-permute-start.5) | collective-permute-done | bytes 393248 | tf_op jit(solution)/shard_map/ppermute | solution.py:514
  70.6 5.4 %shard_map.62 = (f32[8,128,128]{2,1,0:T(8,128)S(1)}, f32[4,64,128]{2,1,0:T(8,128)S(1)}, f32[8,128,128]{2,1,0:T(8,128)}) custom-call(s32[2]{0:T(128)S(1)} %copy-done.19, f32[11,128,128]{2,1,0:T(8,128)S(1)} %collective-permute-done.up_1, f32[11,128,128]{2,1,0:T(8,128)S(1)} %copy-done.5, f32[6,128,128]{2,1,0:T(8,128)S(1)} %collective-permute-done.2.up_2, ...), custom_call_target="tpu_custom_call" | custom-call | tf_op jit(solution)/shard_map/pallas_call | solution.py:485
  76.0 2.9 %collective-permute-start.12 = (f32[4,64,128]{2,1,0:T(8,128)S(1)}, f32[4,64,128]{2,1,0:T(8,128)S(1)}, u32[]{:S(2)}, u32[]{:S(2)}) collective-permute-start(f32[4,64,128]{2,1,0:T(8,128)S(1)} %get-tuple-element.31), channel_id=1, source_target_pairs={{2,0},{3,1},{4,2},{5,3},{6,4},{7,5},{8,6},{9,7},{10,8},{11,9},{12,... | collective-permute-start | bytes 393224 | tf_op jit(solution)/shard_map/ppermute | solution.py:514
  78.9 3.3 %collective-permute-start.11 = (f32[4,64,128]{2,1,0:T(8,128)S(1)}, f32[4,64,128]{2,1,0:T(8,128)S(1)}, u32[]{:S(2)}, u32[]{:S(2)}) collective-permute-start(f32[4,64,128]{2,1,0:T(8,128)S(1)} %get-tuple-element.31), channel_id=1, source_target_pairs={{1,0},{2,1},{3,2},{4,3},{5,4},{6,5},{7,6},{8,7},{9,8},{10,9},{11,1... | collective-permute-start | bytes 393224 | tf_op jit(solution)/shard_map/ppermute | solution.py:514
  82.2 3.1 %collective-permute-start.8 = (f32[4,64,128]{2,1,0:T(8,128)S(1)}, f32[4,64,128]{2,1,0:T(8,128)S(1)}, u32[]{:S(2)}, u32[]{:S(2)}) collective-permute-start(f32[4,64,128]{2,1,0:T(8,128)S(1)} %get-tuple-element.31), channel_id=1, source_target_pairs={{0,1},{1,2},{2,3},{3,4},{4,5},{5,6},{6,7},{7,8},{8,9},{9,10},{10,1... | collective-permute-start | bytes 393224 | tf_op jit(solution)/shard_map/ppermute | solution.py:514
  85.3 7.0 %collective-permute-start.7 = (f32[4,64,128]{2,1,0:T(8,128)S(1)}, f32[4,64,128]{2,1,0:T(8,128)S(1)}, u32[]{:S(2)}, u32[]{:S(2)}) collective-permute-start(f32[4,64,128]{2,1,0:T(8,128)S(1)} %get-tuple-element.31), channel_id=1, source_target_pairs={{0,2},{1,3},{2,4},{3,5},{4,6},{5,7},{6,8},{7,9},{8,10},{9,11},{10,... | collective-permute-start | bytes 393224 | tf_op jit(solution)/shard_map/ppermute | solution.py:514
  94.6 4.4 %collective-permute-start.9 = (f32[10,64,128]{2,1,0:T(8,128)S(1)}, f32[10,64,128]{2,1,0:T(8,128)S(1)}, u32[]{:S(2)}, u32[]{:S(2)}) collective-permute-start(f32[10,64,128]{2,1,0:T(8,128)S(1)} %get-tuple-element.45.wide_a), channel_id=1, source_target_pairs={{0,128},{32,160},{64,192},{96,224},{128,0},{160,32},{192,64},{224,... | collective-permute-start | bytes 983048 | tf_op jit(solution)/shard_map/ppermute | solution.py:517
  103.9 11.5 %collective-permute-start.10 = (f32[8,128,128]{2,1,0:T(8,128)}, f32[8,128,128]{2,1,0:T(8,128)S(1)}, u32[]{:S(2)}, u32[]{:S(2)}) collective-permute-start(f32[8,128,128]{2,1,0:T(8,128)} %get-tuple-element.32), channel_id=1, source_target_pairs={{0,256},{32,288},{160,416},{192,448},{224,480},{256,0},{288,32},{4... | collective-permute-start | bytes 1572872 | tf_op jit(solution)/shard_map/ppermute | solution.py:517
  120.8 3.3 %collective-permute-start.14 = (f32[10,64,128]{2,1,0:T(8,128)S(1)}, f32[10,64,128]{2,1,0:T(8,128)S(1)}, u32[]{:S(2)}, u32[]{:S(2)}) collective-permute-start(f32[10,64,128]{2,1,0:T(8,128)S(1)} %get-tuple-element.33.own_ahead), channel_id=1, source_target_pairs={{0,96},{32,128},{64,160},{96,192},{128,224},{160,0},{192,32},{224,... | collective-permute-start | bytes 983048 | tf_op jit(solution)/shard_map/ppermute | solution.py:517
  124.0 11.3 %collective-permute-start.17 = (f32[10,64,128]{2,1,0:T(8,128)S(1)}, f32[10,64,128]{2,1,0:T(8,128)S(1)}, u32[]{:S(2)}, u32[]{:S(2)}) collective-permute-start(f32[10,64,128]{2,1,0:T(8,128)S(1)} %get-tuple-element.34.own_wrapped), channel_id=1, source_target_pairs={{0,96},{32,128},{64,160},{96,192},{256,352},{288,384},{320,416},{3... | collective-permute-start | bytes 983048 | tf_op jit(solution)/shard_map/ppermute | solution.py:517
  142.1 5.9 %collective-permute-done.15.got_2 = f32[8,64,128]{2,1,0:T(8,128)S(1)} collective-permute-done((f32[8,64,128]{2,1,0:T(8,128)}, f32[8,64,128]{2,1,0:T(8,128)S(1)}, u32[]{:S(2)}, u32[]{:S(2)}) %collective-permute-start.15) | collective-permute-done | bytes 262176 | tf_op jit(solution)/shard_map/ppermute | solution.py:517
  148.1 4.5 %collective-permute-done.18.behind_2 = f32[8,64,128]{2,1,0:T(8,128)} collective-permute-done((f32[8,64,128]{2,1,0:T(8,128)}, f32[8,64,128]{2,1,0:T(8,128)}, u32[]{:S(2)}, u32[]{:S(2)}) %collective-permute-start.18) | collective-permute-done | bytes 262176 | tf_op jit(solution)/shard_map/ppermute | solution.py:517
  157.1 5.4 %collective-permute-start.20 = (f32[4,64,128]{2,1,0:T(8,128)S(1)}, f32[4,64,128]{2,1,0:T(8,128)S(1)}, u32[]{:S(2)}, u32[]{:S(2)}) collective-permute-start(f32[4,64,128]{2,1,0:T(8,128)S(1)} %get-tuple-element.35.last), channel_id=1, source_target_pairs={{0,2},{1,3},{2,4},{3,5},{4,6},{5,7},{6,8},{7,9},{8,10},{9,11},{10,... | collective-permute-start | bytes 393224 | tf_op jit(solution)/shard_map/ppermute | solution.py:514
  162.4 4.9 %collective-permute-start.21 = (f32[4,64,128]{2,1,0:T(8,128)S(1)}, f32[4,64,128]{2,1,0:T(8,128)S(1)}, u32[]{:S(2)}, u32[]{:S(2)}) collective-permute-start(f32[4,64,128]{2,1,0:T(8,128)S(1)} %get-tuple-element.35.last), channel_id=1, source_target_pairs={{0,1},{1,2},{2,3},{3,4},{4,5},{5,6},{6,7},{7,8},{8,9},{9,10},{10,1... | collective-permute-start | bytes 393224 | tf_op jit(solution)/shard_map/ppermute | solution.py:514
  175.4 4.5 %collective-permute-done.23.far_down = f32[4,64,128]{2,1,0:T(8,128)S(1)} collective-permute-done((f32[4,64,128]{2,1,0:T(8,128)S(1)}, f32[4,64,128]{2,1,0:T(8,128)S(1)}, u32[]{:S(2)}, u32[]{:S(2)}) %collective-permute-start.23) | collective-permute-done | bytes 131104 | tf_op jit(solution)/shard_map/ppermute | solution.py:514
  179.9 3.8 %shard_map.65 = (f32[4,64,128]{2,1,0:T(8,128)S(1)}, f32[4,64,128]{2,1,0:T(8,128)S(1)}) custom-call(s32[2]{0:T(128)S(1)} %copy-done.19, f32[4,64,128]{2,1,0:T(8,128)S(1)} %collective-permute-done.20.far_up, f32[4,64,128]{2,1,0:T(8,128)S(1)} %collective-permute-done.21.near_up, f32[4,64,128]{2,1,0:T(8,128)S(1)} %get-tuple-element.35.last, ...), custom_call_target="tpu_custom_call" | custom-call | tf_op jit(solution)/shard_map/pallas_call | solution.py:485
  183.7 6.3 %collective-permute-start.26 = (f32[8,128,128]{2,1,0:T(8,128)}, f32[8,128,128]{2,1,0:T(8,128)S(1)}, u32[]{:S(2)}, u32[]{:S(2)}) collective-permute-start(f32[8,128,128]{2,1,0:T(8,128)} %broadcast_select_fusion), channel_id=1, source_target_pairs={{0,96},{32,128},{64,160},{96,192},{128,224},{160,0},{192,32},{224,... | collective-permute-start | bytes 1572872 | tf_op jit(solution)/shard_map/ppermute | solution.py:517
  190.1 6.9 %collective-permute-start.24 = (f32[4,64,128]{2,1,0:T(8,128)S(1)}, f32[4,64,128]{2,1,0:T(8,128)S(1)}, u32[]{:S(2)}, u32[]{:S(2)}) collective-permute-start(f32[4,64,128]{2,1,0:T(8,128)S(1)} %get-tuple-element.38), channel_id=1, source_target_pairs={{0,352},{32,384},{64,416},{96,448},{128,480},{160,256},{192,288},{... | collective-permute-start | bytes 393224 | tf_op jit(solution)/shard_map/ppermute | solution.py:517
  197.0 4.5 %collective-permute-start.25 = (f32[4,64,128]{2,1,0:T(8,128)S(1)}, f32[4,64,128]{2,1,0:T(8,128)S(1)}, u32[]{:S(2)}, u32[]{:S(2)}) collective-permute-start(f32[4,64,128]{2,1,0:T(8,128)S(1)} %get-tuple-element.39), channel_id=1, source_target_pairs={{0,96},{32,128},{64,160},{96,192},{128,224},{160,0},{192,32},{224,... | collective-permute-start | bytes 393224 | tf_op jit(solution)/shard_map/ppermute | solution.py:517
  204.2 8.1 %collective-permute-done.24 = f32[4,64,128]{2,1,0:T(8,128)S(1)} collective-permute-done((f32[4,64,128]{2,1,0:T(8,128)S(1)}, f32[4,64,128]{2,1,0:T(8,128)S(1)}, u32[]{:S(2)}, u32[]{:S(2)}) %collective-permute-start.24) | collective-permute-done | bytes 131104 | tf_op jit(solution)/shard_map/ppermute | solution.py:517
  (84 shorter events, 42.8 us)
Async XLA Ops:
  1.2 25.6 %copy-start.2 = (f32[8,128,128]{2,1,0:T(8,128)S(1)}, f32[8,128,128]{2,1,0:T(8,128)}, u32[]{:S(2)}) copy-start(f32[8,128,128]{2,1,0:T(8,128)} %source.7) | copy-start | bytes 1572868
  4.5 21.4 %collective-permute-start = (f32[11,128,128]{2,1,0:T(8,128)}, f32[11,128,128]{2,1,0:T(8,128)S(1)}, u32[]{:S(2)}, u32[]{:S(2)}) collective-permute-start(f32[11,128,128]{2,1,0:T(8,128)} %get-tuple-element.22), channel_id=1, source_target_pairs={{0,1},{1,2},{2,3},{3,4},{4,5},{5,6},{6,7},{7,8},{8,9},{9,10},{10,1... | collective-permute-start | bytes 2162696 | tf_op jit(solution)/shard_map/ppermute | solution.py:514
  7.9 19.0 %collective-permute-start.1 = (f32[11,128,128]{2,1,0:T(8,128)}, f32[11,128,128]{2,1,0:T(8,128)S(1)}, u32[]{:S(2)}, u32[]{:S(2)}) collective-permute-start(f32[11,128,128]{2,1,0:T(8,128)} %get-tuple-element.23), channel_id=1, source_target_pairs={{1,0},{2,1},{3,2},{4,3},{5,4},{6,5},{7,6},{8,7},{9,8},{10,9},{11,1... | collective-permute-start | bytes 2162696 | tf_op jit(solution)/shard_map/ppermute | solution.py:514
  32.1 13.7 %collective-permute-start.2 = (f32[6,128,128]{2,1,0:T(8,128)S(1)}, f32[6,128,128]{2,1,0:T(8,128)S(1)}, u32[]{:S(2)}, u32[]{:S(2)}) collective-permute-start(f32[6,128,128]{2,1,0:T(8,128)S(1)} %get-tuple-element.24), channel_id=1, source_target_pairs={{0,1},{1,2},{2,3},{3,4},{4,5},{5,6},{6,7},{7,8},{8,9},{9,10},{10,1... | collective-permute-start | bytes 1179656 | tf_op jit(solution)/shard_map/ppermute | solution.py:514
  35.1 11.9 %collective-permute-start.3 = (f32[6,128,128]{2,1,0:T(8,128)S(1)}, f32[6,128,128]{2,1,0:T(8,128)S(1)}, u32[]{:S(2)}, u32[]{:S(2)}) collective-permute-start(f32[6,128,128]{2,1,0:T(8,128)S(1)} %get-tuple-element.25), channel_id=1, source_target_pairs={{1,0},{2,1},{3,2},{4,3},{5,4},{6,5},{7,6},{8,7},{9,8},{10,9},{11,1... | collective-permute-start | bytes 1179656 | tf_op jit(solution)/shard_map/ppermute | solution.py:514
  52.3 18.3 %collective-permute-start.6 = (f32[8,128,128]{2,1,0:T(8,128)S(1)}, f32[8,128,128]{2,1,0:T(8,128)S(1)}, u32[]{:S(2)}, u32[]{:S(2)}) collective-permute-start(f32[8,128,128]{2,1,0:T(8,128)S(1)} %get-tuple-element.29.second), channel_id=1, source_target_pairs={{0,64},{32,96},{64,128},{96,160},{128,192},{160,224},{192,0},{224,... | collective-permute-start | bytes 1572872 | tf_op jit(solution)/shard_map/ppermute | solution.py:517
  55.4 12.2 %collective-permute-start.4 = (f32[6,128,128]{2,1,0:T(8,128)S(1)}, f32[6,128,128]{2,1,0:T(8,128)S(1)}, u32[]{:S(2)}, u32[]{:S(2)}) collective-permute-start(f32[6,128,128]{2,1,0:T(8,128)S(1)} %get-tuple-element.27), channel_id=1, source_target_pairs={{0,1},{1,2},{2,3},{3,4},{4,5},{5,6},{6,7},{7,8},{8,9},{9,10},{10,1... | collective-permute-start | bytes 1179656 | tf_op jit(solution)/shard_map/ppermute | solution.py:514
  61.4 9.2 %collective-permute-start.5 = (f32[6,128,128]{2,1,0:T(8,128)S(1)}, f32[6,128,128]{2,1,0:T(8,128)S(1)}, u32[]{:S(2)}, u32[]{:S(2)}) collective-permute-start(f32[6,128,128]{2,1,0:T(8,128)S(1)} %get-tuple-element.28), channel_id=1, source_target_pairs={{1,0},{2,1},{3,2},{4,3},{5,4},{6,5},{7,6},{8,7},{9,8},{10,9},{11,1... | collective-permute-start | bytes 1179656 | tf_op jit(solution)/shard_map/ppermute | solution.py:514
  67.6 47.8 %copy-start.6 = (f32[6,128,128]{2,1,0:T(8,128)}, f32[6,128,128]{2,1,0:T(8,128)S(1)}, u32[]{:S(2)}) copy-start(f32[6,128,128]{2,1,0:T(8,128)S(1)} %collective-permute-done.4.up_3) | copy-start | bytes 1179652
  70.6 44.8 %copy-start.8 = (f32[6,128,128]{2,1,0:T(8,128)}, f32[6,128,128]{2,1,0:T(8,128)S(1)}, u32[]{:S(2)}) copy-start(f32[6,128,128]{2,1,0:T(8,128)S(1)} %collective-permute-done.5.down_3) | copy-start | bytes 1179652
  76.0 16.4 %collective-permute-start.12 = (f32[4,64,128]{2,1,0:T(8,128)S(1)}, f32[4,64,128]{2,1,0:T(8,128)S(1)}, u32[]{:S(2)}, u32[]{:S(2)}) collective-permute-start(f32[4,64,128]{2,1,0:T(8,128)S(1)} %get-tuple-element.31), channel_id=1, source_target_pairs={{2,0},{3,1},{4,2},{5,3},{6,4},{7,5},{8,6},{9,7},{10,8},{11,9},{12,... | collective-permute-start | bytes 393224 | tf_op jit(solution)/shard_map/ppermute | solution.py:514
  78.9 13.5 %collective-permute-start.11 = (f32[4,64,128]{2,1,0:T(8,128)S(1)}, f32[4,64,128]{2,1,0:T(8,128)S(1)}, u32[]{:S(2)}, u32[]{:S(2)}) collective-permute-start(f32[4,64,128]{2,1,0:T(8,128)S(1)} %get-tuple-element.31), channel_id=1, source_target_pairs={{1,0},{2,1},{3,2},{4,3},{5,4},{6,5},{7,6},{8,7},{9,8},{10,9},{11,1... | collective-permute-start | bytes 393224 | tf_op jit(solution)/shard_map/ppermute | solution.py:514
  82.2 10.2 %collective-permute-start.8 = (f32[4,64,128]{2,1,0:T(8,128)S(1)}, f32[4,64,128]{2,1,0:T(8,128)S(1)}, u32[]{:S(2)}, u32[]{:S(2)}) collective-permute-start(f32[4,64,128]{2,1,0:T(8,128)S(1)} %get-tuple-element.31), channel_id=1, source_target_pairs={{0,1},{1,2},{2,3},{3,4},{4,5},{5,6},{6,7},{7,8},{8,9},{9,10},{10,1... | collective-permute-start | bytes 393224 | tf_op jit(solution)/shard_map/ppermute | solution.py:514
  85.3 9.1 %collective-permute-start.7 = (f32[4,64,128]{2,1,0:T(8,128)S(1)}, f32[4,64,128]{2,1,0:T(8,128)S(1)}, u32[]{:S(2)}, u32[]{:S(2)}) collective-permute-start(f32[4,64,128]{2,1,0:T(8,128)S(1)} %get-tuple-element.31), channel_id=1, source_target_pairs={{0,2},{1,3},{2,4},{3,5},{4,6},{5,7},{6,8},{7,9},{8,10},{9,11},{10,... | collective-permute-start | bytes 393224 | tf_op jit(solution)/shard_map/ppermute | solution.py:514
  94.6 9.3 %collective-permute-start.9 = (f32[10,64,128]{2,1,0:T(8,128)S(1)}, f32[10,64,128]{2,1,0:T(8,128)S(1)}, u32[]{:S(2)}, u32[]{:S(2)}) collective-permute-start(f32[10,64,128]{2,1,0:T(8,128)S(1)} %get-tuple-element.45.wide_a), channel_id=1, source_target_pairs={{0,128},{32,160},{64,192},{96,224},{128,0},{160,32},{192,64},{224,... | collective-permute-start | bytes 983048 | tf_op jit(solution)/shard_map/ppermute | solution.py:517
  98.9 16.5 %collective-permute-start.13 = (f32[10,64,128]{2,1,0:T(8,128)S(1)}, f32[10,64,128]{2,1,0:T(8,128)S(1)}, u32[]{:S(2)}, u32[]{:S(2)}) collective-permute-start(f32[10,64,128]{2,1,0:T(8,128)S(1)} %get-tuple-element.44.wide_b), channel_id=1, source_target_pairs={{0,128},{32,160},{64,192},{96,224},{128,0},{160,32},{192,64},{224,... | collective-permute-start | bytes 983048 | tf_op jit(solution)/shard_map/ppermute | solution.py:517
  103.9 68.6 %collective-permute-start.10 = (f32[8,128,128]{2,1,0:T(8,128)}, f32[8,128,128]{2,1,0:T(8,128)S(1)}, u32[]{:S(2)}, u32[]{:S(2)}) collective-permute-start(f32[8,128,128]{2,1,0:T(8,128)} %get-tuple-element.32), channel_id=1, source_target_pairs={{0,256},{32,288},{160,416},{192,448},{224,480},{256,0},{288,32},{4... | collective-permute-start | bytes 1572872 | tf_op jit(solution)/shard_map/ppermute | solution.py:517
  118.0 18.8 %collective-permute-start.16 = (f32[6,64,128]{2,1,0:T(8,128)S(1)}, f32[6,64,128]{2,1,0:T(8,128)S(1)}, u32[]{:S(2)}, u32[]{:S(2)}) collective-permute-start(f32[6,64,128]{2,1,0:T(8,128)S(1)} %slice.23), channel_id=1, source_target_pairs={{0,32},{32,64},{64,96},{96,128},{128,160},{160,192},{192,224},{224... | collective-permute-start | bytes 589832 | tf_op jit(solution)/shard_map/ppermute | solution.py:517
  118.9 20.6 %collective-permute-start.19 = (f32[6,64,128]{2,1,0:T(8,128)S(1)}, f32[6,64,128]{2,1,0:T(8,128)S(1)}, u32[]{:S(2)}, u32[]{:S(2)}) collective-permute-start(f32[6,64,128]{2,1,0:T(8,128)S(1)} %slice.25), channel_id=1, source_target_pairs={{0,32},{32,64},{64,96},{96,128},{256,288},{288,320},{320,352},{352... | collective-permute-start | bytes 589832 | tf_op jit(solution)/shard_map/ppermute | solution.py:517
  120.8 31.8 %collective-permute-start.14 = (f32[10,64,128]{2,1,0:T(8,128)S(1)}, f32[10,64,128]{2,1,0:T(8,128)S(1)}, u32[]{:S(2)}, u32[]{:S(2)}) collective-permute-start(f32[10,64,128]{2,1,0:T(8,128)S(1)} %get-tuple-element.33.own_ahead), channel_id=1, source_target_pairs={{0,96},{32,128},{64,160},{96,192},{128,224},{160,0},{192,32},{224,... | collective-permute-start | bytes 983048 | tf_op jit(solution)/shard_map/ppermute | solution.py:517
  124.0 28.6 %collective-permute-start.17 = (f32[10,64,128]{2,1,0:T(8,128)S(1)}, f32[10,64,128]{2,1,0:T(8,128)S(1)}, u32[]{:S(2)}, u32[]{:S(2)}) collective-permute-start(f32[10,64,128]{2,1,0:T(8,128)S(1)} %get-tuple-element.34.own_wrapped), channel_id=1, source_target_pairs={{0,96},{32,128},{64,160},{96,192},{256,352},{288,384},{320,416},{3... | collective-permute-start | bytes 983048 | tf_op jit(solution)/shard_map/ppermute | solution.py:517
  137.5 10.6 %collective-permute-start.15 = (f32[8,64,128]{2,1,0:T(8,128)}, f32[8,64,128]{2,1,0:T(8,128)S(1)}, u32[]{:S(2)}, u32[]{:S(2)}) collective-permute-start(f32[8,64,128]{2,1,0:T(8,128)} %slice.22), channel_id=1, source_target_pairs={{0,64},{32,96},{64,128},{96,160},{128,192},{160,224},{192,0},{224,... | collective-permute-start | bytes 786440 | tf_op jit(solution)/shard_map/ppermute | solution.py:517
  140.1 12.5 %collective-permute-start.18 = (f32[8,64,128]{2,1,0:T(8,128)}, f32[8,64,128]{2,1,0:T(8,128)}, u32[]{:S(2)}, u32[]{:S(2)}) collective-permute-start(f32[8,64,128]{2,1,0:T(8,128)} %slice.24), channel_id=1, source_target_pairs={{0,64},{32,96},{64,128},{96,160},{256,320},{288,352},{320,384},{35... | collective-permute-start | bytes 786440 | tf_op jit(solution)/shard_map/ppermute | solution.py:517
  142.1 30.4 %copy-start.14 = (f32[8,128,128]{2,1,0:T(8,128)S(1)}, f32[8,128,128]{2,1,0:T(8,128)}, u32[]{:S(2)}) copy-start(f32[8,128,128]{2,1,0:T(8,128)} %copy-done.13) | copy-start | bytes 1572868
  157.1 16.3 %collective-permute-start.20 = (f32[4,64,128]{2,1,0:T(8,128)S(1)}, f32[4,64,128]{2,1,0:T(8,128)S(1)}, u32[]{:S(2)}, u32[]{:S(2)}) collective-permute-start(f32[4,64,128]{2,1,0:T(8,128)S(1)} %get-tuple-element.35.last), channel_id=1, source_target_pairs={{0,2},{1,3},{2,4},{3,5},{4,6},{5,7},{6,8},{7,9},{8,10},{9,11},{10,... | collective-permute-start | bytes 393224 | tf_op jit(solution)/shard_map/ppermute | solution.py:514
  162.4 11.0 %collective-permute-start.21 = (f32[4,64,128]{2,1,0:T(8,128)S(1)}, f32[4,64,128]{2,1,0:T(8,128)S(1)}, u32[]{:S(2)}, u32[]{:S(2)}) collective-permute-start(f32[4,64,128]{2,1,0:T(8,128)S(1)} %get-tuple-element.35.last), channel_id=1, source_target_pairs={{0,1},{1,2},{2,3},{3,4},{4,5},{5,6},{6,7},{7,8},{8,9},{9,10},{10,1... | collective-permute-start | bytes 393224 | tf_op jit(solution)/shard_map/ppermute | solution.py:514
  167.3 8.1 %collective-permute-start.22 = (f32[4,64,128]{2,1,0:T(8,128)S(1)}, f32[4,64,128]{2,1,0:T(8,128)S(1)}, u32[]{:S(2)}, u32[]{:S(2)}) collective-permute-start(f32[4,64,128]{2,1,0:T(8,128)S(1)} %get-tuple-element.35.last), channel_id=1, source_target_pairs={{1,0},{2,1},{3,2},{4,3},{5,4},{6,5},{7,6},{8,7},{9,8},{10,9},{11,1... | collective-permute-start | bytes 393224 | tf_op jit(solution)/shard_map/ppermute | solution.py:514
  169.8 10.1 %collective-permute-start.23 = (f32[4,64,128]{2,1,0:T(8,128)S(1)}, f32[4,64,128]{2,1,0:T(8,128)S(1)}, u32[]{:S(2)}, u32[]{:S(2)}) collective-permute-start(f32[4,64,128]{2,1,0:T(8,128)S(1)} %get-tuple-element.35.last), channel_id=1, source_target_pairs={{2,0},{3,1},{4,2},{5,3},{6,4},{7,5},{8,6},{9,7},{10,8},{11,9},{12,... | collective-permute-start | bytes 393224 | tf_op jit(solution)/shard_map/ppermute | solution.py:514
  179.9 23.0 %copy-start.12 = (f32[8,128,128]{2,1,0:T(8,128)S(1)}, f32[8,128,128]{2,1,0:T(8,128)}, u32[]{:S(2)}) copy-start(f32[8,128,128]{2,1,0:T(8,128)} %copy-done.11) | copy-start | bytes 1572868
  183.7 19.2 %collective-permute-start.26 = (f32[8,128,128]{2,1,0:T(8,128)}, f32[8,128,128]{2,1,0:T(8,128)S(1)}, u32[]{:S(2)}, u32[]{:S(2)}) collective-permute-start(f32[8,128,128]{2,1,0:T(8,128)} %broadcast_select_fusion), channel_id=1, source_target_pairs={{0,96},{32,128},{64,160},{96,192},{128,224},{160,0},{192,32},{224,... | collective-permute-start | bytes 1572872 | tf_op jit(solution)/shard_map/ppermute | solution.py:517
  190.1 22.2 %collective-permute-start.24 = (f32[4,64,128]{2,1,0:T(8,128)S(1)}, f32[4,64,128]{2,1,0:T(8,128)S(1)}, u32[]{:S(2)}, u32[]{:S(2)}) collective-permute-start(f32[4,64,128]{2,1,0:T(8,128)S(1)} %get-tuple-element.38), channel_id=1, source_target_pairs={{0,352},{32,384},{64,416},{96,448},{128,480},{160,256},{192,288},{... | collective-permute-start | bytes 393224 | tf_op jit(solution)/shard_map/ppermute | solution.py:517
  197.0 15.3 %collective-permute-start.25 = (f32[4,64,128]{2,1,0:T(8,128)S(1)}, f32[4,64,128]{2,1,0:T(8,128)S(1)}, u32[]{:S(2)}, u32[]{:S(2)}) collective-permute-start(f32[4,64,128]{2,1,0:T(8,128)S(1)} %get-tuple-element.39), channel_id=1, source_target_pairs={{0,96},{32,128},{64,160},{96,192},{128,224},{160,0},{192,32},{224,... | collective-permute-start | bytes 393224 | tf_op jit(solution)/shard_map/ppermute | solution.py:517
  (15 other events, 118.4 us)

commit v9 on v8

--- a/solution.py
+++ b/solution.py
@@ -339,7 +339,7 @@
 
 def far_sums_kernel(
     slabs, where, got_a, got_b, wide_a, wide_b, up_2, down_2, up_3, down_3, kappa_c,
-    ahead_out, wrapped_out, *scratch,
+    ahead_out, wrapped_out, ahead_2, wrapped_2, ahead_1, wrapped_1, *scratch,
 ):
     field, spare, kappa_wide, *weights = scratch
     block = kappa_c.shape[0]
@@ -372,6 +372,12 @@
     cut = part - block
     ahead_out[:cut] = ahead_out[:cut] + wide_a[block + 1 :]
     ahead_out[cut:] = ahead_out[cut:] + wide_b[: rows - 2 * block - cut]
+    for full, two, one in (
+        (ahead_out, ahead_2, ahead_1),
+        (wrapped_out, wrapped_2, wrapped_1),
+    ):
+        two[...] = full[1:-1]
+        one[...] = full[2:-2]
 
 
 def near_sums_kernel(
@@ -504,9 +510,6 @@
     local = tm % GROUP
     where = jnp.stack([tm, sp]).astype(jnp.int32)
 
-    def cut(array, have, want):
-        return array[have - want : array.shape[0] - (have - want)]
-
     def along_space(block, distance):
         pairs = [
             (i, i + distance) for i in range(slabs) if 0 <= i + distance < slabs
@@ -561,7 +564,6 @@
         second_near,
     )
 
-    deep = 2 * crows - 1
     far = (along_space(tau, 2), along_space(tau, -2))
     near = neighbours(tau, tau)
     tau_wide = jnp.concatenate([far[0], near[0], tau, near[1], far[1]], 0)
@@ -573,17 +575,20 @@
         [(i, i ^ GROUP) for i in range(2 * GROUP) if i % GROUP in (0, 1, 5, 6, 7)],
     )
     got_b = along_time(wide[1], ring(4))
-    wide_shape = (deep + 3,) + coarse_shape[1:]
-    ahead, wrapped = call(
-        far_sums_kernel, slabs, [wide_shape] * 2,
+    ahead, wrapped, *narrow = call(
+        far_sums_kernel, slabs,
+        [
+            (crows + 2 * d,) + coarse_shape[1:] for d in (3, 2, 1) for _ in range(2)
+        ],
         coarse_scratch(5 * crows, half, width_three, 2),
         where, got_a, got_b, *wide, *sides_2, *sides_3, kappa_c,
     )
     behind_pairs = lambda d: [
         (g * GROUP + i, g * GROUP + i + d) for g in (0, 1) for i in range(4)
     ]
-    got = [along_time(cut(ahead, 3, d), ring(d)) for d in (3, 2, 1)]
-    behind = [along_time(cut(wrapped, 3, d), behind_pairs(d)) for d in (3, 2, 1)]
+    sent = dict(zip((3, 2, 1), ((ahead, wrapped), narrow[:2], narrow[2:])))
+    got = [along_time(sent[d][0], ring(d)) for d in (3, 2, 1)]
+    behind = [along_time(sent[d][1], behind_pairs(d)) for d in (3, 2, 1)]
     ahead, wrapped, last = call(
         near_sums_kernel, slabs, [coarse_shape] * 3,
         coarse_scratch(3 * crows, half, width_three, 3),

time: 214 us -> 213 us (level)
  the two profiles are of different devices: /device:TPU:97 before, /device:TPU:105 now
where the time goes in v9:
time: 213 us; the launch traced here: 212 us
  starting transfers between devices  109 us (51%)
  waiting for transfers between devices  68.8 us (32%)
  Pallas kernels  26.3 us (12%)
  local copies, waits for them, and re-layouts  4.02 us (2%)
  other arithmetic  3.24 us (2%)
    ppermute x13, starting transfers between devices, along_time(): return lax.ppermute(block, 'tm', pairs)  59 us
    ppermute x14, starting transfers between devices, along_space(): return lax.ppermute(block, 'space', pairs)  49.8 us
    ppermute x14, waiting for transfers between devices, along_space(): return lax.ppermute(block, 'space', pairs)  42 us
    ppermute x13, waiting for transfers between devices, along_time(): return lax.ppermute(block, 'tm', pairs)  26.8 us
    pallas_call x7, Pallas kernels, call(): pl.pallas_call(kernel if slabs is None else functools.partial(kernel, sla...  26.3 us
  transfers between devices with their start and end apart: 27, of which 14 were waited for; matrix products, arithmetic and copies ran while one was open for 1% of the time, Pallas kernels for 3%

profile of v9, /device:TPU:105, one launch (start us, length us, event | category | flops | bytes accessed | tf_op | source)
XLA Modules:
  0.0 212.5 jit_solution(6448338273358753879)
XLA Ops:
  1.2 3.3 %shard_map.59 = (f32[11,128,128]{2,1,0:T(8,128)}, f32[11,128,128]{2,1,0:T(8,128)}) custom-call(s32[2]{0:T(128)} %pad_add_fusion.where, f32[8,128,128]{2,1,0:T(8,128)} %bitcast.12, f32[8,128,128]{2,1,0:T(8,128)} %initial.7, f32[8,128,128]{2,1,0:T(8,128)} %kappa.7, f32[8,128,128]{2,1,0:T(8,128)} %source.7), custom_call_target="tpu_custom_call" | custom-call | tf_op jit(solution)/shard_map/pallas_call | solution.py:491
  4.6 3.3 %collective-permute-start = (f32[11,128,128]{2,1,0:T(8,128)}, f32[11,128,128]{2,1,0:T(8,128)S(1)}, u32[]{:S(2)}, u32[]{:S(2)}) collective-permute-start(f32[11,128,128]{2,1,0:T(8,128)} %get-tuple-element.26), channel_id=1, source_target_pairs={{0,1},{1,2},{2,3},{3,4},{4,5},{5,6},{6,7},{7,8},{8,9},{9,10},{10,1... | collective-permute-start | bytes 2162696 | tf_op jit(solution)/shard_map/ppermute | solution.py:517
  10.4 13.4 %collective-permute-done.up_1 = f32[11,128,128]{2,1,0:T(8,128)S(1)} collective-permute-done((f32[11,128,128]{2,1,0:T(8,128)}, f32[11,128,128]{2,1,0:T(8,128)S(1)}, u32[]{:S(2)}, u32[]{:S(2)}) %collective-permute-start) | collective-permute-done | bytes 720928 | tf_op jit(solution)/shard_map/ppermute | solution.py:517
  23.8 2.9 %collective-permute-done.1.down_1 = f32[11,128,128]{2,1,0:T(8,128)S(1)} collective-permute-done((f32[11,128,128]{2,1,0:T(8,128)}, f32[11,128,128]{2,1,0:T(8,128)S(1)}, u32[]{:S(2)}, u32[]{:S(2)}) %collective-permute-start.1) | collective-permute-done | bytes 720928 | tf_op jit(solution)/shard_map/ppermute | solution.py:517
  27.7 4.1 %shard_map.60 = (f32[8,128,128]{2,1,0:T(8,128)S(1)}, f32[6,128,128]{2,1,0:T(8,128)S(1)}, f32[6,128,128]{2,1,0:T(8,128)S(1)}) custom-call(s32[2]{0:T(128)S(1)} %copy-done.17, f32[11,128,128]{2,1,0:T(8,128)S(1)} %collective-permute-done.up_1, f32[11,128,128]{2,1,0:T(8,128)S(1)} %collective-permute-done.1.down_1, f32[8,128,128]{2,1,0:T(8,128)S(1)} %bitcast.13, ...), custom_call_target="tpu_custom_call" | custom-call | tf_op jit(solution)/shard_map/pallas_call | solution.py:491
  31.9 4.3 %collective-permute-start.2 = (f32[6,128,128]{2,1,0:T(8,128)S(1)}, f32[6,128,128]{2,1,0:T(8,128)S(1)}, u32[]{:S(2)}, u32[]{:S(2)}) collective-permute-start(f32[6,128,128]{2,1,0:T(8,128)S(1)} %get-tuple-element.28), channel_id=1, source_target_pairs={{0,1},{1,2},{2,3},{3,4},{4,5},{5,6},{6,7},{7,8},{8,9},{9,10},{10,1... | collective-permute-start | bytes 1179656 | tf_op jit(solution)/shard_map/ppermute | solution.py:517
  38.1 4.9 %collective-permute-done.2.up_2 = f32[6,128,128]{2,1,0:T(8,128)S(1)} collective-permute-done((f32[6,128,128]{2,1,0:T(8,128)S(1)}, f32[6,128,128]{2,1,0:T(8,128)S(1)}, u32[]{:S(2)}, u32[]{:S(2)}) %collective-permute-start.2) | collective-permute-done | bytes 393248 | tf_op jit(solution)/shard_map/ppermute | solution.py:517
  43.0 6.8 %collective-permute-done.3.down_2 = f32[6,128,128]{2,1,0:T(8,128)S(1)} collective-permute-done((f32[6,128,128]{2,1,0:T(8,128)S(1)}, f32[6,128,128]{2,1,0:T(8,128)S(1)}, u32[]{:S(2)}, u32[]{:S(2)}) %collective-permute-start.3) | collective-permute-done | bytes 393248 | tf_op jit(solution)/shard_map/ppermute | solution.py:517
  51.0 4.1 %shard_map.61 = (f32[8,128,128]{2,1,0:T(8,128)S(1)}, f32[6,128,128]{2,1,0:T(8,128)S(1)}, f32[6,128,128]{2,1,0:T(8,128)S(1)}) custom-call(s32[2]{0:T(128)S(1)} %copy-done.17, f32[11,128,128]{2,1,0:T(8,128)S(1)} %collective-permute-done.up_1, f32[11,128,128]{2,1,0:T(8,128)S(1)} %copy-done.4, f32[6,128,128]{2,1,0:T(8,128)S(1)} %collective-permute-done.2.up_2, ...), custom_call_target="tpu_custom_call" | custom-call | tf_op jit(solution)/shard_map/pallas_call | solution.py:491
  55.1 3.1 %collective-permute-start.6 = (f32[8,128,128]{2,1,0:T(8,128)S(1)}, f32[8,128,128]{2,1,0:T(8,128)S(1)}, u32[]{:S(2)}, u32[]{:S(2)}) collective-permute-start(f32[8,128,128]{2,1,0:T(8,128)S(1)} %get-tuple-element.33.second), channel_id=1, source_target_pairs={{0,64},{32,96},{64,128},{96,160},{128,192},{160,224},{192,0},{224,... | collective-permute-start | bytes 1572872 | tf_op jit(solution)/shard_map/ppermute | solution.py:520
  58.2 3.1 %collective-permute-start.4 = (f32[6,128,128]{2,1,0:T(8,128)S(1)}, f32[6,128,128]{2,1,0:T(8,128)S(1)}, u32[]{:S(2)}, u32[]{:S(2)}) collective-permute-start(f32[6,128,128]{2,1,0:T(8,128)S(1)} %get-tuple-element.31), channel_id=1, source_target_pairs={{0,1},{1,2},{2,3},{3,4},{4,5},{5,6},{6,7},{7,8},{8,9},{9,10},{10,1... | collective-permute-start | bytes 1179656 | tf_op jit(solution)/shard_map/ppermute | solution.py:517
  63.5 4.1 %collective-permute-done.4.up_3 = f32[6,128,128]{2,1,0:T(8,128)S(1)} collective-permute-done((f32[6,128,128]{2,1,0:T(8,128)S(1)}, f32[6,128,128]{2,1,0:T(8,128)S(1)}, u32[]{:S(2)}, u32[]{:S(2)}) %collective-permute-start.4) | collective-permute-done | bytes 393248 | tf_op jit(solution)/shard_map/ppermute | solution.py:517
  67.7 5.2 %collective-permute-done.5.down_3 = f32[6,128,128]{2,1,0:T(8,128)S(1)} collective-permute-done((f32[6,128,128]{2,1,0:T(8,128)S(1)}, f32[6,128,128]{2,1,0:T(8,128)S(1)}, u32[]{:S(2)}, u32[]{:S(2)}) %collective-permute-start.5) | collective-permute-done | bytes 393248 | tf_op jit(solution)/shard_map/ppermute | solution.py:517
  72.9 5.4 %shard_map.62 = (f32[8,128,128]{2,1,0:T(8,128)S(1)}, f32[4,64,128]{2,1,0:T(8,128)S(1)}, f32[8,128,128]{2,1,0:T(8,128)}) custom-call(s32[2]{0:T(128)S(1)} %copy-done.17, f32[11,128,128]{2,1,0:T(8,128)S(1)} %collective-permute-done.up_1, f32[11,128,128]{2,1,0:T(8,128)S(1)} %copy-done.5, f32[6,128,128]{2,1,0:T(8,128)S(1)} %collective-permute-done.2.up_2, ...), custom_call_target="tpu_custom_call" | custom-call | tf_op jit(solution)/shard_map/pallas_call | solution.py:491
  82.1 3.4 %collective-permute-start.8 = (f32[4,64,128]{2,1,0:T(8,128)S(1)}, f32[4,64,128]{2,1,0:T(8,128)S(1)}, u32[]{:S(2)}, u32[]{:S(2)}) collective-permute-start(f32[4,64,128]{2,1,0:T(8,128)S(1)} %get-tuple-element.35), channel_id=1, source_target_pairs={{0,1},{1,2},{2,3},{3,4},{4,5},{5,6},{6,7},{7,8},{8,9},{9,10},{10,1... | collective-permute-start | bytes 393224 | tf_op jit(solution)/shard_map/ppermute | solution.py:517
  85.5 9.7 %collective-permute-start.7 = (f32[4,64,128]{2,1,0:T(8,128)S(1)}, f32[4,64,128]{2,1,0:T(8,128)S(1)}, u32[]{:S(2)}, u32[]{:S(2)}) collective-permute-start(f32[4,64,128]{2,1,0:T(8,128)S(1)} %get-tuple-element.35), channel_id=1, source_target_pairs={{0,2},{1,3},{2,4},{3,5},{4,6},{5,7},{6,8},{7,9},{8,10},{9,11},{10,... | collective-permute-start | bytes 393224 | tf_op jit(solution)/shard_map/ppermute | solution.py:517
  97.2 4.4 %collective-permute-start.9 = (f32[10,64,128]{2,1,0:T(8,128)S(1)}, f32[10,64,128]{2,1,0:T(8,128)S(1)}, u32[]{:S(2)}, u32[]{:S(2)}) collective-permute-start(f32[10,64,128]{2,1,0:T(8,128)S(1)} %get-tuple-element.53.wide_a), channel_id=1, source_target_pairs={{0,128},{32,160},{64,192},{96,224},{128,0},{160,32},{192,64},{224,... | collective-permute-start | bytes 983048 | tf_op jit(solution)/shard_map/ppermute | solution.py:520
  104.0 2.5 %collective-permute-done.9.got_a = f32[10,64,128]{2,1,0:T(8,128)S(1)} collective-permute-done((f32[10,64,128]{2,1,0:T(8,128)S(1)}, f32[10,64,128]{2,1,0:T(8,128)S(1)}, u32[]{:S(2)}, u32[]{:S(2)}) %collective-permute-start.9) | collective-permute-done | bytes 327712 | tf_op jit(solution)/shard_map/ppermute | solution.py:520
  106.6 10.6 %collective-permute-start.10 = (f32[8,128,128]{2,1,0:T(8,128)}, f32[8,128,128]{2,1,0:T(8,128)S(1)}, u32[]{:S(2)}, u32[]{:S(2)}) collective-permute-start(f32[8,128,128]{2,1,0:T(8,128)} %get-tuple-element.36), channel_id=1, source_target_pairs={{0,256},{32,288},{160,416},{192,448},{224,480},{256,0},{288,32},{4... | collective-permute-start | bytes 1572872 | tf_op jit(solution)/shard_map/ppermute | solution.py:520
  117.2 3.4 %shard_map.63 = (f32[10,64,128]{2,1,0:T(8,128)S(1)}, f32[10,64,128]{2,1,0:T(8,128)S(1)}, f32[8,64,128]{2,1,0:T(8,128)}, f32[8,64,128]{2,1,0:T(8,128)}, f32[6,64,...) custom-call(s32[2]{0:T(128)S(1)} %copy-done.17, f32[10,64,128]{2,1,0:T(8,128)S(1)} %collective-permute-done.9.got_a, ...), custom_call_target="tpu_custom_call" | custom-call | tf_op jit(solution)/shard_map/pallas_call | solution.py:491
  124.2 2.5 %collective-permute-start.14 = (f32[10,64,128]{2,1,0:T(8,128)S(1)}, f32[10,64,128]{2,1,0:T(8,128)S(1)}, u32[]{:S(2)}, u32[]{:S(2)}) collective-permute-start(f32[10,64,128]{2,1,0:T(8,128)S(1)} %get-tuple-element.37.own_ahead), channel_id=1, source_target_pairs={{0,96},{32,128},{64,160},{96,192},{128,224},{160,0},{192,32},{224,... | collective-permute-start | bytes 983048 | tf_op jit(solution)/shard_map/ppermute | solution.py:520
  126.7 11.1 %collective-permute-start.17 = (f32[10,64,128]{2,1,0:T(8,128)S(1)}, f32[10,64,128]{2,1,0:T(8,128)S(1)}, u32[]{:S(2)}, u32[]{:S(2)}) collective-permute-start(f32[10,64,128]{2,1,0:T(8,128)S(1)} %get-tuple-element.40.own_wrapped), channel_id=1, source_target_pairs={{0,96},{32,128},{64,160},{96,192},{256,352},{288,384},{320,416},{3... | collective-permute-start | bytes 983048 | tf_op jit(solution)/shard_map/ppermute | solution.py:520
  141.9 9.3 %collective-permute-done.15.got_2 = f32[8,64,128]{2,1,0:T(8,128)S(1)} collective-permute-done((f32[8,64,128]{2,1,0:T(8,128)}, f32[8,64,128]{2,1,0:T(8,128)S(1)}, u32[]{:S(2)}, u32[]{:S(2)}) %collective-permute-start.15) | collective-permute-done | bytes 262176 | tf_op jit(solution)/shard_map/ppermute | solution.py:520
  151.2 3.9 %collective-permute-done.18.behind_2 = f32[8,64,128]{2,1,0:T(8,128)S(1)} collective-permute-done((f32[8,64,128]{2,1,0:T(8,128)}, f32[8,64,128]{2,1,0:T(8,128)S(1)}, u32[]{:S(2)}, u32[]{:S(2)}) %collective-permute-start.18) | collective-permute-done | bytes 262176 | tf_op jit(solution)/shard_map/ppermute | solution.py:520
  162.1 3.4 %collective-permute-start.21 = (f32[4,64,128]{2,1,0:T(8,128)S(1)}, f32[4,64,128]{2,1,0:T(8,128)S(1)}, u32[]{:S(2)}, u32[]{:S(2)}) collective-permute-start(f32[4,64,128]{2,1,0:T(8,128)S(1)} %get-tuple-element.43.last), channel_id=1, source_target_pairs={{0,1},{1,2},{2,3},{3,4},{4,5},{5,6},{6,7},{7,8},{8,9},{9,10},{10,1... | collective-permute-start | bytes 393224 | tf_op jit(solution)/shard_map/ppermute | solution.py:517
  165.4 8.8 %collective-permute-start.20 = (f32[4,64,128]{2,1,0:T(8,128)S(1)}, f32[4,64,128]{2,1,0:T(8,128)S(1)}, u32[]{:S(2)}, u32[]{:S(2)}) collective-permute-start(f32[4,64,128]{2,1,0:T(8,128)S(1)} %get-tuple-element.43.last), channel_id=1, source_target_pairs={{0,2},{1,3},{2,4},{3,5},{4,6},{5,7},{6,8},{7,9},{8,10},{9,11},{10,... | collective-permute-start | bytes 393224 | tf_op jit(solution)/shard_map/ppermute | solution.py:517
  174.4 2.7 %collective-permute-done.20.far_up = f32[4,64,128]{2,1,0:T(8,128)S(1)} collective-permute-done((f32[4,64,128]{2,1,0:T(8,128)S(1)}, f32[4,64,128]{2,1,0:T(8,128)S(1)}, u32[]{:S(2)}, u32[]{:S(2)}) %collective-permute-start.20) | collective-permute-done | bytes 131104 | tf_op jit(solution)/shard_map/ppermute | solution.py:517
  177.1 3.8 %shard_map.65 = (f32[4,64,128]{2,1,0:T(8,128)S(1)}, f32[4,64,128]{2,1,0:T(8,128)S(1)}) custom-call(s32[2]{0:T(128)S(1)} %copy-done.17, f32[4,64,128]{2,1,0:T(8,128)S(1)} %collective-permute-done.20.far_up, f32[4,64,128]{2,1,0:T(8,128)S(1)} %collective-permute-done.21.near_up, f32[4,64,128]{2,1,0:T(8,128)S(1)} %get-tuple-element.43.last, ...), custom_call_target="tpu_custom_call" | custom-call | tf_op jit(solution)/shard_map/pallas_call | solution.py:491
  180.9 6.7 %collective-permute-start.26 = (f32[8,128,128]{2,1,0:T(8,128)S(1)}, f32[8,128,128]{2,1,0:T(8,128)S(1)}, u32[]{:S(2)}, u32[]{:S(2)}) collective-permute-start(f32[8,128,128]{2,1,0:T(8,128)S(1)} %broadcast_select_fusion), channel_id=1, source_target_pairs={{0,96},{32,128},{64,160},{96,192},{128,224},{160,0},{192,32},{224,... | collective-permute-start | bytes 1572872 | tf_op jit(solution)/shard_map/ppermute | solution.py:520
  187.6 6.9 %collective-permute-start.24 = (f32[4,64,128]{2,1,0:T(8,128)S(1)}, f32[4,64,128]{2,1,0:T(8,128)S(1)}, u32[]{:S(2)}, u32[]{:S(2)}) collective-permute-start(f32[4,64,128]{2,1,0:T(8,128)S(1)} %get-tuple-element.46), channel_id=1, source_target_pairs={{0,352},{32,384},{64,416},{96,448},{128,480},{160,256},{192,288},{... | collective-permute-start | bytes 393224 | tf_op jit(solution)/shard_map/ppermute | solution.py:520
  194.6 4.4 %collective-permute-start.25 = (f32[4,64,128]{2,1,0:T(8,128)S(1)}, f32[4,64,128]{2,1,0:T(8,128)S(1)}, u32[]{:S(2)}, u32[]{:S(2)}) collective-permute-start(f32[4,64,128]{2,1,0:T(8,128)S(1)} %get-tuple-element.47), channel_id=1, source_target_pairs={{0,96},{32,128},{64,160},{96,192},{128,224},{160,0},{192,32},{224,... | collective-permute-start | bytes 393224 | tf_op jit(solution)/shard_map/ppermute | solution.py:520
  202.4 9.0 %collective-permute-done.24 = f32[4,64,128]{2,1,0:T(8,128)S(1)} collective-permute-done((f32[4,64,128]{2,1,0:T(8,128)S(1)}, f32[4,64,128]{2,1,0:T(8,128)S(1)}, u32[]{:S(2)}, u32[]{:S(2)}) %collective-permute-start.24) | collective-permute-done | bytes 131104 | tf_op jit(solution)/shard_map/ppermute | solution.py:520
  (76 shorter events, 36.5 us)
Async XLA Ops:
  1.2 25.5 %copy-start.2 = (f32[8,128,128]{2,1,0:T(8,128)S(1)}, f32[8,128,128]{2,1,0:T(8,128)}, u32[]{:S(2)}) copy-start(f32[8,128,128]{2,1,0:T(8,128)} %source.7) | copy-start | bytes 1572868
  4.5 22.2 %copy-start.1 = (f32[8,128,128]{2,1,0:T(8,128)S(1)}, f32[8,128,128]{2,1,0:T(8,128)}, u32[]{:S(2)}) copy-start(f32[8,128,128]{2,1,0:T(8,128)} %initial.7) | copy-start | bytes 1572868
  4.6 19.2 %collective-permute-start = (f32[11,128,128]{2,1,0:T(8,128)}, f32[11,128,128]{2,1,0:T(8,128)S(1)}, u32[]{:S(2)}, u32[]{:S(2)}) collective-permute-start(f32[11,128,128]{2,1,0:T(8,128)} %get-tuple-element.26), channel_id=1, source_target_pairs={{0,1},{1,2},{2,3},{3,4},{4,5},{5,6},{6,7},{7,8},{8,9},{9,10},{10,1... | collective-permute-start | bytes 2162696 | tf_op jit(solution)/shard_map/ppermute | solution.py:517
  7.9 18.8 %collective-permute-start.1 = (f32[11,128,128]{2,1,0:T(8,128)}, f32[11,128,128]{2,1,0:T(8,128)S(1)}, u32[]{:S(2)}, u32[]{:S(2)}) collective-permute-start(f32[11,128,128]{2,1,0:T(8,128)} %get-tuple-element.27), channel_id=1, source_target_pairs={{1,0},{2,1},{3,2},{4,3},{5,4},{6,5},{7,6},{8,7},{9,8},{10,9},{11,1... | collective-permute-start | bytes 2162696 | tf_op jit(solution)/shard_map/ppermute | solution.py:517
  31.9 11.1 %collective-permute-start.2 = (f32[6,128,128]{2,1,0:T(8,128)S(1)}, f32[6,128,128]{2,1,0:T(8,128)S(1)}, u32[]{:S(2)}, u32[]{:S(2)}) collective-permute-start(f32[6,128,128]{2,1,0:T(8,128)S(1)} %get-tuple-element.28), channel_id=1, source_target_pairs={{0,1},{1,2},{2,3},{3,4},{4,5},{5,6},{6,7},{7,8},{8,9},{9,10},{10,1... | collective-permute-start | bytes 1179656 | tf_op jit(solution)/shard_map/ppermute | solution.py:517
  36.2 13.6 %collective-permute-start.3 = (f32[6,128,128]{2,1,0:T(8,128)S(1)}, f32[6,128,128]{2,1,0:T(8,128)S(1)}, u32[]{:S(2)}, u32[]{:S(2)}) collective-permute-start(f32[6,128,128]{2,1,0:T(8,128)S(1)} %get-tuple-element.29), channel_id=1, source_target_pairs={{1,0},{2,1},{3,2},{4,3},{5,4},{6,5},{7,6},{8,7},{9,8},{10,9},{11,1... | collective-permute-start | bytes 1179656 | tf_op jit(solution)/shard_map/ppermute | solution.py:517
  55.1 17.8 %collective-permute-start.6 = (f32[8,128,128]{2,1,0:T(8,128)S(1)}, f32[8,128,128]{2,1,0:T(8,128)S(1)}, u32[]{:S(2)}, u32[]{:S(2)}) collective-permute-start(f32[8,128,128]{2,1,0:T(8,128)S(1)} %get-tuple-element.33.second), channel_id=1, source_target_pairs={{0,64},{32,96},{64,128},{96,160},{128,192},{160,224},{192,0},{224,... | collective-permute-start | bytes 1572872 | tf_op jit(solution)/shard_map/ppermute | solution.py:520
  58.2 9.4 %collective-permute-start.4 = (f32[6,128,128]{2,1,0:T(8,128)S(1)}, f32[6,128,128]{2,1,0:T(8,128)S(1)}, u32[]{:S(2)}, u32[]{:S(2)}) collective-permute-start(f32[6,128,128]{2,1,0:T(8,128)S(1)} %get-tuple-element.31), channel_id=1, source_target_pairs={{0,1},{1,2},{2,3},{3,4},{4,5},{5,6},{6,7},{7,8},{8,9},{9,10},{10,1... | collective-permute-start | bytes 1179656 | tf_op jit(solution)/shard_map/ppermute | solution.py:517
  61.3 11.6 %collective-permute-start.5 = (f32[6,128,128]{2,1,0:T(8,128)S(1)}, f32[6,128,128]{2,1,0:T(8,128)S(1)}, u32[]{:S(2)}, u32[]{:S(2)}) collective-permute-start(f32[6,128,128]{2,1,0:T(8,128)S(1)} %get-tuple-element.32), channel_id=1, source_target_pairs={{1,0},{2,1},{3,2},{4,3},{5,4},{6,5},{7,6},{8,7},{9,8},{10,9},{11,1... | collective-permute-start | bytes 1179656 | tf_op jit(solution)/shard_map/ppermute | solution.py:517
  67.7 49.5 %copy-start.6 = (f32[6,128,128]{2,1,0:T(8,128)}, f32[6,128,128]{2,1,0:T(8,128)S(1)}, u32[]{:S(2)}) copy-start(f32[6,128,128]{2,1,0:T(8,128)S(1)} %collective-permute-done.4.up_3) | copy-start | bytes 1179652
  72.9 44.3 %copy-start.8 = (f32[6,128,128]{2,1,0:T(8,128)}, f32[6,128,128]{2,1,0:T(8,128)S(1)}, u32[]{:S(2)}) copy-start(f32[6,128,128]{2,1,0:T(8,128)S(1)} %collective-permute-done.5.down_3) | copy-start | bytes 1179652
  78.3 17.0 %collective-permute-start.12 = (f32[4,64,128]{2,1,0:T(8,128)S(1)}, f32[4,64,128]{2,1,0:T(8,128)S(1)}, u32[]{:S(2)}, u32[]{:S(2)}) collective-permute-start(f32[4,64,128]{2,1,0:T(8,128)S(1)} %get-tuple-element.35), channel_id=1, source_target_pairs={{2,0},{3,1},{4,2},{5,3},{6,4},{7,5},{8,6},{9,7},{10,8},{11,9},{12,... | collective-permute-start | bytes 393224 | tf_op jit(solution)/shard_map/ppermute | solution.py:517
  80.2 15.1 %collective-permute-start.11 = (f32[4,64,128]{2,1,0:T(8,128)S(1)}, f32[4,64,128]{2,1,0:T(8,128)S(1)}, u32[]{:S(2)}, u32[]{:S(2)}) collective-permute-start(f32[4,64,128]{2,1,0:T(8,128)S(1)} %get-tuple-element.35), channel_id=1, source_target_pairs={{1,0},{2,1},{3,2},{4,3},{5,4},{6,5},{7,6},{8,7},{9,8},{10,9},{11,1... | collective-permute-start | bytes 393224 | tf_op jit(solution)/shard_map/ppermute | solution.py:517
  82.1 13.1 %collective-permute-start.8 = (f32[4,64,128]{2,1,0:T(8,128)S(1)}, f32[4,64,128]{2,1,0:T(8,128)S(1)}, u32[]{:S(2)}, u32[]{:S(2)}) collective-permute-start(f32[4,64,128]{2,1,0:T(8,128)S(1)} %get-tuple-element.35), channel_id=1, source_target_pairs={{0,1},{1,2},{2,3},{3,4},{4,5},{5,6},{6,7},{7,8},{8,9},{9,10},{10,1... | collective-permute-start | bytes 393224 | tf_op jit(solution)/shard_map/ppermute | solution.py:517
  85.5 11.7 %collective-permute-start.7 = (f32[4,64,128]{2,1,0:T(8,128)S(1)}, f32[4,64,128]{2,1,0:T(8,128)S(1)}, u32[]{:S(2)}, u32[]{:S(2)}) collective-permute-start(f32[4,64,128]{2,1,0:T(8,128)S(1)} %get-tuple-element.35), channel_id=1, source_target_pairs={{0,2},{1,3},{2,4},{3,5},{4,6},{5,7},{6,8},{7,9},{8,10},{9,11},{10,... | collective-permute-start | bytes 393224 | tf_op jit(solution)/shard_map/ppermute | solution.py:517
  97.2 9.3 %collective-permute-start.9 = (f32[10,64,128]{2,1,0:T(8,128)S(1)}, f32[10,64,128]{2,1,0:T(8,128)S(1)}, u32[]{:S(2)}, u32[]{:S(2)}) collective-permute-start(f32[10,64,128]{2,1,0:T(8,128)S(1)} %get-tuple-element.53.wide_a), channel_id=1, source_target_pairs={{0,128},{32,160},{64,192},{96,224},{128,0},{160,32},{192,64},{224,... | collective-permute-start | bytes 983048 | tf_op jit(solution)/shard_map/ppermute | solution.py:520
  101.6 15.6 %collective-permute-start.13 = (f32[10,64,128]{2,1,0:T(8,128)S(1)}, f32[10,64,128]{2,1,0:T(8,128)S(1)}, u32[]{:S(2)}, u32[]{:S(2)}) collective-permute-start(f32[10,64,128]{2,1,0:T(8,128)S(1)} %get-tuple-element.52.wide_b), channel_id=1, source_target_pairs={{0,128},{32,160},{64,192},{96,224},{128,0},{160,32},{192,64},{224,... | collective-permute-start | bytes 983048 | tf_op jit(solution)/shard_map/ppermute | solution.py:520
  106.6 67.7 %collective-permute-start.10 = (f32[8,128,128]{2,1,0:T(8,128)}, f32[8,128,128]{2,1,0:T(8,128)S(1)}, u32[]{:S(2)}, u32[]{:S(2)}) collective-permute-start(f32[8,128,128]{2,1,0:T(8,128)} %get-tuple-element.36), channel_id=1, source_target_pairs={{0,256},{32,288},{160,416},{192,448},{224,480},{256,0},{288,32},{4... | collective-permute-start | bytes 1572872 | tf_op jit(solution)/shard_map/ppermute | solution.py:520
  120.6 17.3 %collective-permute-start.16 = (f32[6,64,128]{2,1,0:T(8,128)S(1)}, f32[6,64,128]{2,1,0:T(8,128)S(1)}, u32[]{:S(2)}, u32[]{:S(2)}) collective-permute-start(f32[6,64,128]{2,1,0:T(8,128)S(1)} %get-tuple-element.39), channel_id=1, source_target_pairs={{0,32},{32,64},{64,96},{96,128},{128,160},{160,192},{192,224},{224... | collective-permute-start | bytes 589832 | tf_op jit(solution)/shard_map/ppermute | solution.py:520
  122.3 17.5 %collective-permute-start.19 = (f32[6,64,128]{2,1,0:T(8,128)S(1)}, f32[6,64,128]{2,1,0:T(8,128)S(1)}, u32[]{:S(2)}, u32[]{:S(2)}) collective-permute-start(f32[6,64,128]{2,1,0:T(8,128)S(1)} %get-tuple-element.42), channel_id=1, source_target_pairs={{0,32},{32,64},{64,96},{96,128},{256,288},{288,320},{320,352},{352... | collective-permute-start | bytes 589832 | tf_op jit(solution)/shard_map/ppermute | solution.py:520
  124.2 30.9 %collective-permute-start.14 = (f32[10,64,128]{2,1,0:T(8,128)S(1)}, f32[10,64,128]{2,1,0:T(8,128)S(1)}, u32[]{:S(2)}, u32[]{:S(2)}) collective-permute-start(f32[10,64,128]{2,1,0:T(8,128)S(1)} %get-tuple-element.37.own_ahead), channel_id=1, source_target_pairs={{0,96},{32,128},{64,160},{96,192},{128,224},{160,0},{192,32},{224,... | collective-permute-start | bytes 983048 | tf_op jit(solution)/shard_map/ppermute | solution.py:520
  126.7 28.4 %collective-permute-start.17 = (f32[10,64,128]{2,1,0:T(8,128)S(1)}, f32[10,64,128]{2,1,0:T(8,128)S(1)}, u32[]{:S(2)}, u32[]{:S(2)}) collective-permute-start(f32[10,64,128]{2,1,0:T(8,128)S(1)} %get-tuple-element.40.own_wrapped), channel_id=1, source_target_pairs={{0,96},{32,128},{64,160},{96,192},{256,352},{288,384},{320,416},{3... | collective-permute-start | bytes 983048 | tf_op jit(solution)/shard_map/ppermute | solution.py:520
  137.9 13.3 %collective-permute-start.15 = (f32[8,64,128]{2,1,0:T(8,128)}, f32[8,64,128]{2,1,0:T(8,128)S(1)}, u32[]{:S(2)}, u32[]{:S(2)}) collective-permute-start(f32[8,64,128]{2,1,0:T(8,128)} %get-tuple-element.38), channel_id=1, source_target_pairs={{0,64},{32,96},{64,128},{96,160},{128,192},{160,224},{192,0},{224,... | collective-permute-start | bytes 786440 | tf_op jit(solution)/shard_map/ppermute | solution.py:520
  140.5 14.6 %collective-permute-start.18 = (f32[8,64,128]{2,1,0:T(8,128)}, f32[8,64,128]{2,1,0:T(8,128)S(1)}, u32[]{:S(2)}, u32[]{:S(2)}) collective-permute-start(f32[8,64,128]{2,1,0:T(8,128)} %get-tuple-element.41), channel_id=1, source_target_pairs={{0,64},{32,96},{64,128},{96,160},{256,320},{288,352},{320,384},{35... | collective-permute-start | bytes 786440 | tf_op jit(solution)/shard_map/ppermute | solution.py:520
  141.8 32.4 %copy-start.14 = (f32[8,128,128]{2,1,0:T(8,128)S(1)}, f32[8,128,128]{2,1,0:T(8,128)}, u32[]{:S(2)}) copy-start(f32[8,128,128]{2,1,0:T(8,128)} %copy-done.13) | copy-start | bytes 1572868
  158.2 16.2 %collective-permute-start.23 = (f32[4,64,128]{2,1,0:T(8,128)S(1)}, f32[4,64,128]{2,1,0:T(8,128)S(1)}, u32[]{:S(2)}, u32[]{:S(2)}) collective-permute-start(f32[4,64,128]{2,1,0:T(8,128)S(1)} %get-tuple-element.43.last), channel_id=1, source_target_pairs={{2,0},{3,1},{4,2},{5,3},{6,4},{7,5},{8,6},{9,7},{10,8},{11,9},{12,... | collective-permute-start | bytes 393224 | tf_op jit(solution)/shard_map/ppermute | solution.py:517
  160.1 14.2 %collective-permute-start.22 = (f32[4,64,128]{2,1,0:T(8,128)S(1)}, f32[4,64,128]{2,1,0:T(8,128)S(1)}, u32[]{:S(2)}, u32[]{:S(2)}) collective-permute-start(f32[4,64,128]{2,1,0:T(8,128)S(1)} %get-tuple-element.43.last), channel_id=1, source_target_pairs={{1,0},{2,1},{3,2},{4,3},{5,4},{6,5},{7,6},{8,7},{9,8},{10,9},{11,1... | collective-permute-start | bytes 393224 | tf_op jit(solution)/shard_map/ppermute | solution.py:517
  162.1 12.3 %collective-permute-start.21 = (f32[4,64,128]{2,1,0:T(8,128)S(1)}, f32[4,64,128]{2,1,0:T(8,128)S(1)}, u32[]{:S(2)}, u32[]{:S(2)}) collective-permute-start(f32[4,64,128]{2,1,0:T(8,128)S(1)} %get-tuple-element.43.last), channel_id=1, source_target_pairs={{0,1},{1,2},{2,3},{3,4},{4,5},{5,6},{6,7},{7,8},{8,9},{9,10},{10,1... | collective-permute-start | bytes 393224 | tf_op jit(solution)/shard_map/ppermute | solution.py:517
  165.4 11.6 %collective-permute-start.20 = (f32[4,64,128]{2,1,0:T(8,128)S(1)}, f32[4,64,128]{2,1,0:T(8,128)S(1)}, u32[]{:S(2)}, u32[]{:S(2)}) collective-permute-start(f32[4,64,128]{2,1,0:T(8,128)S(1)} %get-tuple-element.43.last), channel_id=1, source_target_pairs={{0,2},{1,3},{2,4},{3,5},{4,6},{5,7},{6,8},{7,9},{8,10},{9,11},{10,... | collective-permute-start | bytes 393224 | tf_op jit(solution)/shard_map/ppermute | solution.py:517
  180.9 18.3 %collective-permute-start.26 = (f32[8,128,128]{2,1,0:T(8,128)S(1)}, f32[8,128,128]{2,1,0:T(8,128)S(1)}, u32[]{:S(2)}, u32[]{:S(2)}) collective-permute-start(f32[8,128,128]{2,1,0:T(8,128)S(1)} %broadcast_select_fusion), channel_id=1, source_target_pairs={{0,96},{32,128},{64,160},{96,192},{128,224},{160,0},{192,32},{224,... | collective-permute-start | bytes 1572872 | tf_op jit(solution)/shard_map/ppermute | solution.py:520
  187.6 23.7 %collective-permute-start.24 = (f32[4,64,128]{2,1,0:T(8,128)S(1)}, f32[4,64,128]{2,1,0:T(8,128)S(1)}, u32[]{:S(2)}, u32[]{:S(2)}) collective-permute-start(f32[4,64,128]{2,1,0:T(8,128)S(1)} %get-tuple-element.46), channel_id=1, source_target_pairs={{0,352},{32,384},{64,416},{96,448},{128,480},{160,256},{192,288},{... | collective-permute-start | bytes 393224 | tf_op jit(solution)/shard_map/ppermute | solution.py:520
  194.6 7.8 %collective-permute-start.25 = (f32[4,64,128]{2,1,0:T(8,128)S(1)}, f32[4,64,128]{2,1,0:T(8,128)S(1)}, u32[]{:S(2)}, u32[]{:S(2)}) collective-permute-start(f32[4,64,128]{2,1,0:T(8,128)S(1)} %get-tuple-element.47), channel_id=1, source_target_pairs={{0,96},{32,128},{64,160},{96,192},{128,224},{160,0},{192,32},{224,... | collective-permute-start | bytes 393224 | tf_op jit(solution)/shard_map/ppermute | solution.py:520
  (13 other events, 107.0 us)

commit v10 on v9

--- a/solution.py
+++ b/solution.py
@@ -345,14 +345,14 @@
     block = kappa_c.shape[0]
     deep = 2 * block - 1
     rows = block + 2 * deep
-    part = rows // 2
+    part = got_a.shape[0] - 1
     local = lax.rem(where[0], GROUP)
     high = where[0] >= GROUP
     clear_edges(field)
     clear_edges(spare)
     coarse_kappa_8(kappa_wide, up_2, down_2, up_3, down_3, kappa_c)
     face_weights(kappa_wide, weights, 4.0 * ALONG_THIRD)
-    fill(field, [(got_a, 1, part, 0), (got_b, 0, part, part)])
+    fill(field, [(got_a, 1, part, 0), (got_b, 0, rows - part, part)])
     inside = inside_of(where[1], slabs, deep, block)
     late = local >= 4
     to_ahead = jnp.where(late & ~(high & (local >= 5)), 1.0, 0.0)
@@ -567,7 +567,7 @@
     far = (along_space(tau, 2), along_space(tau, -2))
     near = neighbours(tau, tau)
     tau_wide = jnp.concatenate([far[0], near[0], tau, near[1], far[1]], 0)
-    part = tau_wide.shape[0] // 2
+    part = crows + 2
     wide = (tau_wide[:part], tau_wide[part:])
     got_a = along_time(wide[0], ring(4))
     crossed = along_time(

time: 213 us -> 212 us (level)
  the two profiles are of different devices: /device:TPU:105 before, /device:TPU:97 now
where the time goes in v10:
time: 212 us; the launch traced here: 211 us
  starting transfers between devices  110 us (52%)
  waiting for transfers between devices  65.8 us (31%)
  Pallas kernels  26.3 us (12%)
  local copies, waits for them, and re-layouts  4.01 us (2%)
  other arithmetic  3.24 us (2%)
    ppermute x14, starting transfers between devices, along_space(): return lax.ppermute(block, 'space', pairs)  55.8 us
    ppermute x13, starting transfers between devices, along_time(): return lax.ppermute(block, 'tm', pairs)  54.6 us
    ppermute x14, waiting for transfers between devices, along_space(): return lax.ppermute(block, 'space', pairs)  35 us
    ppermute x13, waiting for transfers between devices, along_time(): return lax.ppermute(block, 'tm', pairs)  30.8 us
    pallas_call x7, Pallas kernels, call(): pl.pallas_call(kernel if slabs is None else functools.partial(kernel, sla...  26.3 us
  transfers between devices with their start and end apart: 27, of which 13 were waited for; matrix products, arithmetic and copies ran while one was open for 1% of the time, Pallas kernels for 3%

profile of v10, /device:TPU:97, one launch (start us, length us, event | category | flops | bytes accessed | tf_op | source)
XLA Modules:
  0.0 211.0 jit_solution(11354738018067402917)
XLA Ops:
  1.2 3.3 %shard_map.59 = (f32[11,128,128]{2,1,0:T(8,128)}, f32[11,128,128]{2,1,0:T(8,128)}) custom-call(s32[2]{0:T(128)} %pad_add_fusion.where, f32[8,128,128]{2,1,0:T(8,128)} %bitcast.12, f32[8,128,128]{2,1,0:T(8,128)} %initial.7, f32[8,128,128]{2,1,0:T(8,128)} %kappa.7, f32[8,128,128]{2,1,0:T(8,128)} %source.7), custom_call_target="tpu_custom_call" | custom-call | tf_op jit(solution)/shard_map/pallas_call | solution.py:491
  4.6 3.3 %collective-permute-start = (f32[11,128,128]{2,1,0:T(8,128)}, f32[11,128,128]{2,1,0:T(8,128)S(1)}, u32[]{:S(2)}, u32[]{:S(2)}) collective-permute-start(f32[11,128,128]{2,1,0:T(8,128)} %get-tuple-element.26), channel_id=1, source_target_pairs={{0,1},{1,2},{2,3},{3,4},{4,5},{5,6},{6,7},{7,8},{8,9},{9,10},{10,1... | collective-permute-start | bytes 2162696 | tf_op jit(solution)/shard_map/ppermute | solution.py:517
  7.9 4.2 %collective-permute-start.1 = (f32[11,128,128]{2,1,0:T(8,128)}, f32[11,128,128]{2,1,0:T(8,128)S(1)}, u32[]{:S(2)}, u32[]{:S(2)}) collective-permute-start(f32[11,128,128]{2,1,0:T(8,128)} %get-tuple-element.27), channel_id=1, source_target_pairs={{1,0},{2,1},{3,2},{4,3},{5,4},{6,5},{7,6},{8,7},{9,8},{10,9},{11,1... | collective-permute-start | bytes 2162696 | tf_op jit(solution)/shard_map/ppermute | solution.py:517
  12.5 13.4 %collective-permute-done.up_1 = f32[11,128,128]{2,1,0:T(8,128)S(1)} collective-permute-done((f32[11,128,128]{2,1,0:T(8,128)}, f32[11,128,128]{2,1,0:T(8,128)S(1)}, u32[]{:S(2)}, u32[]{:S(2)}) %collective-permute-start) | collective-permute-done | bytes 720928 | tf_op jit(solution)/shard_map/ppermute | solution.py:517
  27.9 4.1 %shard_map.60 = (f32[8,128,128]{2,1,0:T(8,128)S(1)}, f32[6,128,128]{2,1,0:T(8,128)S(1)}, f32[6,128,128]{2,1,0:T(8,128)S(1)}) custom-call(s32[2]{0:T(128)S(1)} %copy-done.17, f32[11,128,128]{2,1,0:T(8,128)S(1)} %collective-permute-done.up_1, f32[11,128,128]{2,1,0:T(8,128)S(1)} %collective-permute-done.1.down_1, f32[8,128,128]{2,1,0:T(8,128)S(1)} %bitcast.13, ...), custom_call_target="tpu_custom_call" | custom-call | tf_op jit(solution)/shard_map/pallas_call | solution.py:491
  35.1 5.0 %collective-permute-start.3 = (f32[6,128,128]{2,1,0:T(8,128)S(1)}, f32[6,128,128]{2,1,0:T(8,128)S(1)}, u32[]{:S(2)}, u32[]{:S(2)}) collective-permute-start(f32[6,128,128]{2,1,0:T(8,128)S(1)} %get-tuple-element.29), channel_id=1, source_target_pairs={{1,0},{2,1},{3,2},{4,3},{5,4},{6,5},{7,6},{8,7},{9,8},{10,9},{11,1... | collective-permute-start | bytes 1179656 | tf_op jit(solution)/shard_map/ppermute | solution.py:517
  40.1 5.6 %collective-permute-done.2.up_2 = f32[6,128,128]{2,1,0:T(8,128)S(1)} collective-permute-done((f32[6,128,128]{2,1,0:T(8,128)S(1)}, f32[6,128,128]{2,1,0:T(8,128)S(1)}, u32[]{:S(2)}, u32[]{:S(2)}) %collective-permute-start.2) | collective-permute-done | bytes 393248 | tf_op jit(solution)/shard_map/ppermute | solution.py:517
  48.1 4.1 %shard_map.61 = (f32[8,128,128]{2,1,0:T(8,128)S(1)}, f32[6,128,128]{2,1,0:T(8,128)S(1)}, f32[6,128,128]{2,1,0:T(8,128)S(1)}) custom-call(s32[2]{0:T(128)S(1)} %copy-done.17, f32[11,128,128]{2,1,0:T(8,128)S(1)} %collective-permute-done.up_1, f32[11,128,128]{2,1,0:T(8,128)S(1)} %copy-done.4, f32[6,128,128]{2,1,0:T(8,128)S(1)} %collective-permute-done.2.up_2, ...), custom_call_target="tpu_custom_call" | custom-call | tf_op jit(solution)/shard_map/pallas_call | solution.py:491
  52.3 3.1 %collective-permute-start.6 = (f32[8,128,128]{2,1,0:T(8,128)S(1)}, f32[8,128,128]{2,1,0:T(8,128)S(1)}, u32[]{:S(2)}, u32[]{:S(2)}) collective-permute-start(f32[8,128,128]{2,1,0:T(8,128)S(1)} %get-tuple-element.33.second), channel_id=1, source_target_pairs={{0,64},{32,96},{64,128},{96,160},{128,192},{160,224},{192,0},{224,... | collective-permute-start | bytes 1572872 | tf_op jit(solution)/shard_map/ppermute | solution.py:520
  55.4 6.0 %collective-permute-start.4 = (f32[6,128,128]{2,1,0:T(8,128)S(1)}, f32[6,128,128]{2,1,0:T(8,128)S(1)}, u32[]{:S(2)}, u32[]{:S(2)}) collective-permute-start(f32[6,128,128]{2,1,0:T(8,128)S(1)} %get-tuple-element.31), channel_id=1, source_target_pairs={{0,1},{1,2},{2,3},{3,4},{4,5},{5,6},{6,7},{7,8},{8,9},{9,10},{10,1... | collective-permute-start | bytes 1179656 | tf_op jit(solution)/shard_map/ppermute | solution.py:517
  63.4 4.3 %collective-permute-done.4.up_3 = f32[6,128,128]{2,1,0:T(8,128)S(1)} collective-permute-done((f32[6,128,128]{2,1,0:T(8,128)S(1)}, f32[6,128,128]{2,1,0:T(8,128)S(1)}, u32[]{:S(2)}, u32[]{:S(2)}) %collective-permute-start.4) | collective-permute-done | bytes 393248 | tf_op jit(solution)/shard_map/ppermute | solution.py:517
  70.6 5.4 %shard_map.62 = (f32[8,128,128]{2,1,0:T(8,128)S(1)}, f32[4,64,128]{2,1,0:T(8,128)S(1)}, f32[8,128,128]{2,1,0:T(8,128)}) custom-call(s32[2]{0:T(128)S(1)} %copy-done.17, f32[11,128,128]{2,1,0:T(8,128)S(1)} %collective-permute-done.up_1, f32[11,128,128]{2,1,0:T(8,128)S(1)} %copy-done.5, f32[6,128,128]{2,1,0:T(8,128)S(1)} %collective-permute-done.2.up_2, ...), custom_call_target="tpu_custom_call" | custom-call | tf_op jit(solution)/shard_map/pallas_call | solution.py:491
  76.0 5.5 %collective-permute-start.8 = (f32[4,64,128]{2,1,0:T(8,128)S(1)}, f32[4,64,128]{2,1,0:T(8,128)S(1)}, u32[]{:S(2)}, u32[]{:S(2)}) collective-permute-start(f32[4,64,128]{2,1,0:T(8,128)S(1)} %get-tuple-element.35), channel_id=1, source_target_pairs={{0,1},{1,2},{2,3},{3,4},{4,5},{5,6},{6,7},{7,8},{8,9},{9,10},{10,1... | collective-permute-start | bytes 393224 | tf_op jit(solution)/shard_map/ppermute | solution.py:517
  85.4 7.0 %collective-permute-start.7 = (f32[4,64,128]{2,1,0:T(8,128)S(1)}, f32[4,64,128]{2,1,0:T(8,128)S(1)}, u32[]{:S(2)}, u32[]{:S(2)}) collective-permute-start(f32[4,64,128]{2,1,0:T(8,128)S(1)} %get-tuple-element.35), channel_id=1, source_target_pairs={{0,2},{1,3},{2,4},{3,5},{4,6},{5,7},{6,8},{7,9},{8,10},{9,11},{10,... | collective-permute-start | bytes 393224 | tf_op jit(solution)/shard_map/ppermute | solution.py:517
  92.5 4.4 %collective-permute-start.13 = (f32[14,64,128]{2,1,0:T(8,128)S(1)}, f32[14,64,128]{2,1,0:T(8,128)S(1)}, u32[]{:S(2)}, u32[]{:S(2)}) collective-permute-start(f32[14,64,128]{2,1,0:T(8,128)S(1)} %pad_maximum_fusion.wide_b), channel_id=1, source_target_pairs={{0,128},{32,160},{64,192},{96,224},{128,0},{160,32},{192,64},{224,... | collective-permute-start | bytes 1376264 | tf_op jit(solution)/shard_map/ppermute | solution.py:520
  99.3 8.2 %collective-permute-done.9.got_a = f32[6,64,128]{2,1,0:T(8,128)S(1)} collective-permute-done((f32[6,64,128]{2,1,0:T(8,128)S(1)}, f32[6,64,128]{2,1,0:T(8,128)S(1)}, u32[]{:S(2)}, u32[]{:S(2)}) %collective-permute-start.9) | collective-permute-done | bytes 196640 | tf_op jit(solution)/shard_map/ppermute | solution.py:520
  107.5 8.4 %collective-permute-start.10 = (f32[8,128,128]{2,1,0:T(8,128)}, f32[8,128,128]{2,1,0:T(8,128)S(1)}, u32[]{:S(2)}, u32[]{:S(2)}) collective-permute-start(f32[8,128,128]{2,1,0:T(8,128)} %get-tuple-element.36), channel_id=1, source_target_pairs={{0,256},{32,288},{160,416},{192,448},{224,480},{256,0},{288,32},{4... | collective-permute-start | bytes 1572872 | tf_op jit(solution)/shard_map/ppermute | solution.py:520
  115.9 3.4 %shard_map.63 = (f32[10,64,128]{2,1,0:T(8,128)S(1)}, f32[10,64,128]{2,1,0:T(8,128)S(1)}, f32[8,64,128]{2,1,0:T(8,128)}, f32[8,64,128]{2,1,0:T(8,128)}, f32[6,64,...) custom-call(s32[2]{0:T(128)S(1)} %copy-done.17, f32[6,64,128]{2,1,0:T(8,128)S(1)} %collective-permute-done.9.got_a, ...), custom_call_target="tpu_custom_call" | custom-call | tf_op jit(solution)/shard_map/pallas_call | solution.py:491
  121.3 4.0 %collective-permute-start.14 = (f32[10,64,128]{2,1,0:T(8,128)S(1)}, f32[10,64,128]{2,1,0:T(8,128)S(1)}, u32[]{:S(2)}, u32[]{:S(2)}) collective-permute-start(f32[10,64,128]{2,1,0:T(8,128)S(1)} %get-tuple-element.37.own_ahead), channel_id=1, source_target_pairs={{0,96},{32,128},{64,160},{96,192},{128,224},{160,0},{192,32},{224,... | collective-permute-start | bytes 983048 | tf_op jit(solution)/shard_map/ppermute | solution.py:520
  125.3 11.2 %collective-permute-start.17 = (f32[10,64,128]{2,1,0:T(8,128)S(1)}, f32[10,64,128]{2,1,0:T(8,128)S(1)}, u32[]{:S(2)}, u32[]{:S(2)}) collective-permute-start(f32[10,64,128]{2,1,0:T(8,128)S(1)} %get-tuple-element.40.own_wrapped), channel_id=1, source_target_pairs={{0,96},{32,128},{64,160},{96,192},{256,352},{288,384},{320,416},{3... | collective-permute-start | bytes 983048 | tf_op jit(solution)/shard_map/ppermute | solution.py:520
  140.4 9.3 %collective-permute-done.15.got_2 = f32[8,64,128]{2,1,0:T(8,128)S(1)} collective-permute-done((f32[8,64,128]{2,1,0:T(8,128)}, f32[8,64,128]{2,1,0:T(8,128)S(1)}, u32[]{:S(2)}, u32[]{:S(2)}) %collective-permute-start.15) | collective-permute-done | bytes 262176 | tf_op jit(solution)/shard_map/ppermute | solution.py:520
  149.7 4.0 %collective-permute-done.18.behind_2 = f32[8,64,128]{2,1,0:T(8,128)S(1)} collective-permute-done((f32[8,64,128]{2,1,0:T(8,128)}, f32[8,64,128]{2,1,0:T(8,128)S(1)}, u32[]{:S(2)}, u32[]{:S(2)}) %collective-permute-start.18) | collective-permute-done | bytes 262176 | tf_op jit(solution)/shard_map/ppermute | solution.py:520
  156.9 6.4 %collective-permute-start.20 = (f32[4,64,128]{2,1,0:T(8,128)S(1)}, f32[4,64,128]{2,1,0:T(8,128)S(1)}, u32[]{:S(2)}, u32[]{:S(2)}) collective-permute-start(f32[4,64,128]{2,1,0:T(8,128)S(1)} %get-tuple-element.43.last), channel_id=1, source_target_pairs={{0,2},{1,3},{2,4},{3,5},{4,6},{5,7},{6,8},{7,9},{8,10},{9,11},{10,... | collective-permute-start | bytes 393224 | tf_op jit(solution)/shard_map/ppermute | solution.py:517
  163.3 3.4 %collective-permute-start.21 = (f32[4,64,128]{2,1,0:T(8,128)S(1)}, f32[4,64,128]{2,1,0:T(8,128)S(1)}, u32[]{:S(2)}, u32[]{:S(2)}) collective-permute-start(f32[4,64,128]{2,1,0:T(8,128)S(1)} %get-tuple-element.43.last), channel_id=1, source_target_pairs={{0,1},{1,2},{2,3},{3,4},{4,5},{5,6},{6,7},{7,8},{8,9},{9,10},{10,1... | collective-permute-start | bytes 393224 | tf_op jit(solution)/shard_map/ppermute | solution.py:517
  166.6 4.0 %collective-permute-start.22 = (f32[4,64,128]{2,1,0:T(8,128)S(1)}, f32[4,64,128]{2,1,0:T(8,128)S(1)}, u32[]{:S(2)}, u32[]{:S(2)}) collective-permute-start(f32[4,64,128]{2,1,0:T(8,128)S(1)} %get-tuple-element.43.last), channel_id=1, source_target_pairs={{1,0},{2,1},{3,2},{4,3},{5,4},{6,5},{7,6},{8,7},{9,8},{10,9},{11,1... | collective-permute-start | bytes 393224 | tf_op jit(solution)/shard_map/ppermute | solution.py:517
  174.0 5.5 %collective-permute-done.23.far_down = f32[4,64,128]{2,1,0:T(8,128)S(1)} collective-permute-done((f32[4,64,128]{2,1,0:T(8,128)S(1)}, f32[4,64,128]{2,1,0:T(8,128)S(1)}, u32[]{:S(2)}, u32[]{:S(2)}) %collective-permute-start.23) | collective-permute-done | bytes 131104 | tf_op jit(solution)/shard_map/ppermute | solution.py:517
  179.5 3.8 %shard_map.65 = (f32[4,64,128]{2,1,0:T(8,128)S(1)}, f32[4,64,128]{2,1,0:T(8,128)S(1)}) custom-call(s32[2]{0:T(128)S(1)} %copy-done.17, f32[4,64,128]{2,1,0:T(8,128)S(1)} %collective-permute-done.20.far_up, f32[4,64,128]{2,1,0:T(8,128)S(1)} %collective-permute-done.21.near_up, f32[4,64,128]{2,1,0:T(8,128)S(1)} %get-tuple-element.43.last, ...), custom_call_target="tpu_custom_call" | custom-call | tf_op jit(solution)/shard_map/pallas_call | solution.py:491
  183.3 6.9 %collective-permute-start.26 = (f32[8,128,128]{2,1,0:T(8,128)S(1)}, f32[8,128,128]{2,1,0:T(8,128)S(1)}, u32[]{:S(2)}, u32[]{:S(2)}) collective-permute-start(f32[8,128,128]{2,1,0:T(8,128)S(1)} %broadcast_select_fusion), channel_id=1, source_target_pairs={{0,96},{32,128},{64,160},{96,192},{128,224},{160,0},{192,32},{224,... | collective-permute-start | bytes 1572872 | tf_op jit(solution)/shard_map/ppermute | solution.py:520
  190.2 5.3 %collective-permute-start.24 = (f32[4,64,128]{2,1,0:T(8,128)S(1)}, f32[4,64,128]{2,1,0:T(8,128)S(1)}, u32[]{:S(2)}, u32[]{:S(2)}) collective-permute-start(f32[4,64,128]{2,1,0:T(8,128)S(1)} %get-tuple-element.46), channel_id=1, source_target_pairs={{0,352},{32,384},{64,416},{96,448},{128,480},{160,256},{192,288},{... | collective-permute-start | bytes 393224 | tf_op jit(solution)/shard_map/ppermute | solution.py:520
  195.5 3.9 %collective-permute-start.25 = (f32[4,64,128]{2,1,0:T(8,128)S(1)}, f32[4,64,128]{2,1,0:T(8,128)S(1)}, u32[]{:S(2)}, u32[]{:S(2)}) collective-permute-start(f32[4,64,128]{2,1,0:T(8,128)S(1)} %get-tuple-element.47), channel_id=1, source_target_pairs={{0,96},{32,128},{64,160},{96,192},{128,224},{160,0},{192,32},{224,... | collective-permute-start | bytes 393224 | tf_op jit(solution)/shard_map/ppermute | solution.py:520
  199.4 3.1 %collective-permute-done.26 = f32[8,128,128]{2,1,0:T(8,128)S(1)} collective-permute-done((f32[8,128,128]{2,1,0:T(8,128)S(1)}, f32[8,128,128]{2,1,0:T(8,128)S(1)}, u32[]{:S(2)}, u32[]{:S(2)}) %collective-permute-start.26) | collective-permute-done | bytes 524320 | tf_op jit(solution)/shard_map/ppermute | solution.py:520
  203.7 6.1 %collective-permute-done.24 = f32[4,64,128]{2,1,0:T(8,128)S(1)} collective-permute-done((f32[4,64,128]{2,1,0:T(8,128)S(1)}, f32[4,64,128]{2,1,0:T(8,128)S(1)}, u32[]{:S(2)}, u32[]{:S(2)}) %collective-permute-start.24) | collective-permute-done | bytes 131104 | tf_op jit(solution)/shard_map/ppermute | solution.py:520
  (77 shorter events, 34.1 us)
Async XLA Ops:
  1.2 25.7 %copy-start.2 = (f32[8,128,128]{2,1,0:T(8,128)S(1)}, f32[8,128,128]{2,1,0:T(8,128)}, u32[]{:S(2)}) copy-start(f32[8,128,128]{2,1,0:T(8,128)} %source.7) | copy-start | bytes 1572868
  4.6 21.4 %collective-permute-start = (f32[11,128,128]{2,1,0:T(8,128)}, f32[11,128,128]{2,1,0:T(8,128)S(1)}, u32[]{:S(2)}, u32[]{:S(2)}) collective-permute-start(f32[11,128,128]{2,1,0:T(8,128)} %get-tuple-element.26), channel_id=1, source_target_pairs={{0,1},{1,2},{2,3},{3,4},{4,5},{5,6},{6,7},{7,8},{8,9},{9,10},{10,1... | collective-permute-start | bytes 2162696 | tf_op jit(solution)/shard_map/ppermute | solution.py:517
  7.9 19.0 %collective-permute-start.1 = (f32[11,128,128]{2,1,0:T(8,128)}, f32[11,128,128]{2,1,0:T(8,128)S(1)}, u32[]{:S(2)}, u32[]{:S(2)}) collective-permute-start(f32[11,128,128]{2,1,0:T(8,128)} %get-tuple-element.27), channel_id=1, source_target_pairs={{1,0},{2,1},{3,2},{4,3},{5,4},{6,5},{7,6},{8,7},{9,8},{10,9},{11,1... | collective-permute-start | bytes 2162696 | tf_op jit(solution)/shard_map/ppermute | solution.py:517
  32.1 13.7 %collective-permute-start.2 = (f32[6,128,128]{2,1,0:T(8,128)S(1)}, f32[6,128,128]{2,1,0:T(8,128)S(1)}, u32[]{:S(2)}, u32[]{:S(2)}) collective-permute-start(f32[6,128,128]{2,1,0:T(8,128)S(1)} %get-tuple-element.28), channel_id=1, source_target_pairs={{0,1},{1,2},{2,3},{3,4},{4,5},{5,6},{6,7},{7,8},{8,9},{9,10},{10,1... | collective-permute-start | bytes 1179656 | tf_op jit(solution)/shard_map/ppermute | solution.py:517
  35.1 11.9 %collective-permute-start.3 = (f32[6,128,128]{2,1,0:T(8,128)S(1)}, f32[6,128,128]{2,1,0:T(8,128)S(1)}, u32[]{:S(2)}, u32[]{:S(2)}) collective-permute-start(f32[6,128,128]{2,1,0:T(8,128)S(1)} %get-tuple-element.29), channel_id=1, source_target_pairs={{1,0},{2,1},{3,2},{4,3},{5,4},{6,5},{7,6},{8,7},{9,8},{10,9},{11,1... | collective-permute-start | bytes 1179656 | tf_op jit(solution)/shard_map/ppermute | solution.py:517
  52.3 18.3 %collective-permute-start.6 = (f32[8,128,128]{2,1,0:T(8,128)S(1)}, f32[8,128,128]{2,1,0:T(8,128)S(1)}, u32[]{:S(2)}, u32[]{:S(2)}) collective-permute-start(f32[8,128,128]{2,1,0:T(8,128)S(1)} %get-tuple-element.33.second), channel_id=1, source_target_pairs={{0,64},{32,96},{64,128},{96,160},{128,192},{160,224},{192,0},{224,... | collective-permute-start | bytes 1572872 | tf_op jit(solution)/shard_map/ppermute | solution.py:520
  55.4 12.2 %collective-permute-start.4 = (f32[6,128,128]{2,1,0:T(8,128)S(1)}, f32[6,128,128]{2,1,0:T(8,128)S(1)}, u32[]{:S(2)}, u32[]{:S(2)}) collective-permute-start(f32[6,128,128]{2,1,0:T(8,128)S(1)} %get-tuple-element.31), channel_id=1, source_target_pairs={{0,1},{1,2},{2,3},{3,4},{4,5},{5,6},{6,7},{7,8},{8,9},{9,10},{10,1... | collective-permute-start | bytes 1179656 | tf_op jit(solution)/shard_map/ppermute | solution.py:517
  61.4 9.2 %collective-permute-start.5 = (f32[6,128,128]{2,1,0:T(8,128)S(1)}, f32[6,128,128]{2,1,0:T(8,128)S(1)}, u32[]{:S(2)}, u32[]{:S(2)}) collective-permute-start(f32[6,128,128]{2,1,0:T(8,128)S(1)} %get-tuple-element.32), channel_id=1, source_target_pairs={{1,0},{2,1},{3,2},{4,3},{5,4},{6,5},{7,6},{8,7},{9,8},{10,9},{11,1... | collective-permute-start | bytes 1179656 | tf_op jit(solution)/shard_map/ppermute | solution.py:517
  67.6 48.3 %copy-start.6 = (f32[6,128,128]{2,1,0:T(8,128)}, f32[6,128,128]{2,1,0:T(8,128)S(1)}, u32[]{:S(2)}) copy-start(f32[6,128,128]{2,1,0:T(8,128)S(1)} %collective-permute-done.4.up_3) | copy-start | bytes 1179652
  70.6 45.3 %copy-start.8 = (f32[6,128,128]{2,1,0:T(8,128)}, f32[6,128,128]{2,1,0:T(8,128)S(1)}, u32[]{:S(2)}) copy-start(f32[6,128,128]{2,1,0:T(8,128)S(1)} %collective-permute-done.5.down_3) | copy-start | bytes 1179652
  76.0 16.4 %collective-permute-start.8 = (f32[4,64,128]{2,1,0:T(8,128)S(1)}, f32[4,64,128]{2,1,0:T(8,128)S(1)}, u32[]{:S(2)}, u32[]{:S(2)}) collective-permute-start(f32[4,64,128]{2,1,0:T(8,128)S(1)} %get-tuple-element.35), channel_id=1, source_target_pairs={{0,1},{1,2},{2,3},{3,4},{4,5},{5,6},{6,7},{7,8},{8,9},{9,10},{10,1... | collective-permute-start | bytes 393224 | tf_op jit(solution)/shard_map/ppermute | solution.py:517
  81.5 10.9 %collective-permute-start.12 = (f32[4,64,128]{2,1,0:T(8,128)S(1)}, f32[4,64,128]{2,1,0:T(8,128)S(1)}, u32[]{:S(2)}, u32[]{:S(2)}) collective-permute-start(f32[4,64,128]{2,1,0:T(8,128)S(1)} %get-tuple-element.35), channel_id=1, source_target_pairs={{2,0},{3,1},{4,2},{5,3},{6,4},{7,5},{8,6},{9,7},{10,8},{11,9},{12,... | collective-permute-start | bytes 393224 | tf_op jit(solution)/shard_map/ppermute | solution.py:517
  83.4 9.0 %collective-permute-start.11 = (f32[4,64,128]{2,1,0:T(8,128)S(1)}, f32[4,64,128]{2,1,0:T(8,128)S(1)}, u32[]{:S(2)}, u32[]{:S(2)}) collective-permute-start(f32[4,64,128]{2,1,0:T(8,128)S(1)} %get-tuple-element.35), channel_id=1, source_target_pairs={{1,0},{2,1},{3,2},{4,3},{5,4},{6,5},{7,6},{8,7},{9,8},{10,9},{11,1... | collective-permute-start | bytes 393224 | tf_op jit(solution)/shard_map/ppermute | solution.py:517
  85.4 11.5 %collective-permute-start.7 = (f32[4,64,128]{2,1,0:T(8,128)S(1)}, f32[4,64,128]{2,1,0:T(8,128)S(1)}, u32[]{:S(2)}, u32[]{:S(2)}) collective-permute-start(f32[4,64,128]{2,1,0:T(8,128)S(1)} %get-tuple-element.35), channel_id=1, source_target_pairs={{0,2},{1,3},{2,4},{3,5},{4,6},{5,7},{6,8},{7,9},{8,10},{9,11},{10,... | collective-permute-start | bytes 393224 | tf_op jit(solution)/shard_map/ppermute | solution.py:517
  92.5 23.5 %collective-permute-start.13 = (f32[14,64,128]{2,1,0:T(8,128)S(1)}, f32[14,64,128]{2,1,0:T(8,128)S(1)}, u32[]{:S(2)}, u32[]{:S(2)}) collective-permute-start(f32[14,64,128]{2,1,0:T(8,128)S(1)} %pad_maximum_fusion.wide_b), channel_id=1, source_target_pairs={{0,128},{32,160},{64,192},{96,224},{128,0},{160,32},{192,64},{224,... | collective-permute-start | bytes 1376264 | tf_op jit(solution)/shard_map/ppermute | solution.py:520
  96.9 10.7 %collective-permute-start.9 = (f32[6,64,128]{2,1,0:T(8,128)S(1)}, f32[6,64,128]{2,1,0:T(8,128)S(1)}, u32[]{:S(2)}, u32[]{:S(2)}) collective-permute-start(f32[6,64,128]{2,1,0:T(8,128)S(1)} %pad_maximum_fusion.3.wide_a), channel_id=1, source_target_pairs={{0,128},{32,160},{64,192},{96,224},{128,0},{160,32},{192,64},{224,... | collective-permute-start | bytes 589832 | tf_op jit(solution)/shard_map/ppermute | solution.py:520
  107.5 65.3 %collective-permute-start.10 = (f32[8,128,128]{2,1,0:T(8,128)}, f32[8,128,128]{2,1,0:T(8,128)S(1)}, u32[]{:S(2)}, u32[]{:S(2)}) collective-permute-start(f32[8,128,128]{2,1,0:T(8,128)} %get-tuple-element.36), channel_id=1, source_target_pairs={{0,256},{32,288},{160,416},{192,448},{224,480},{256,0},{288,32},{4... | collective-permute-start | bytes 1572872 | tf_op jit(solution)/shard_map/ppermute | solution.py:520
  119.3 17.1 %collective-permute-start.16 = (f32[6,64,128]{2,1,0:T(8,128)S(1)}, f32[6,64,128]{2,1,0:T(8,128)S(1)}, u32[]{:S(2)}, u32[]{:S(2)}) collective-permute-start(f32[6,64,128]{2,1,0:T(8,128)S(1)} %get-tuple-element.39), channel_id=1, source_target_pairs={{0,32},{32,64},{64,96},{96,128},{128,160},{160,192},{192,224},{224... | collective-permute-start | bytes 589832 | tf_op jit(solution)/shard_map/ppermute | solution.py:520
  119.3 19.0 %collective-permute-start.19 = (f32[6,64,128]{2,1,0:T(8,128)S(1)}, f32[6,64,128]{2,1,0:T(8,128)S(1)}, u32[]{:S(2)}, u32[]{:S(2)}) collective-permute-start(f32[6,64,128]{2,1,0:T(8,128)S(1)} %get-tuple-element.42), channel_id=1, source_target_pairs={{0,32},{32,64},{64,96},{96,128},{256,288},{288,320},{320,352},{352... | collective-permute-start | bytes 589832 | tf_op jit(solution)/shard_map/ppermute | solution.py:520
  121.3 32.5 %collective-permute-start.14 = (f32[10,64,128]{2,1,0:T(8,128)S(1)}, f32[10,64,128]{2,1,0:T(8,128)S(1)}, u32[]{:S(2)}, u32[]{:S(2)}) collective-permute-start(f32[10,64,128]{2,1,0:T(8,128)S(1)} %get-tuple-element.37.own_ahead), channel_id=1, source_target_pairs={{0,96},{32,128},{64,160},{96,192},{128,224},{160,0},{192,32},{224,... | collective-permute-start | bytes 983048 | tf_op jit(solution)/shard_map/ppermute | solution.py:520
  125.3 28.5 %collective-permute-start.17 = (f32[10,64,128]{2,1,0:T(8,128)S(1)}, f32[10,64,128]{2,1,0:T(8,128)S(1)}, u32[]{:S(2)}, u32[]{:S(2)}) collective-permute-start(f32[10,64,128]{2,1,0:T(8,128)S(1)} %get-tuple-element.40.own_wrapped), channel_id=1, source_target_pairs={{0,96},{32,128},{64,160},{96,192},{256,352},{288,384},{320,416},{3... | collective-permute-start | bytes 983048 | tf_op jit(solution)/shard_map/ppermute | solution.py:520
  136.5 13.3 %collective-permute-start.15 = (f32[8,64,128]{2,1,0:T(8,128)}, f32[8,64,128]{2,1,0:T(8,128)S(1)}, u32[]{:S(2)}, u32[]{:S(2)}) collective-permute-start(f32[8,64,128]{2,1,0:T(8,128)} %get-tuple-element.38), channel_id=1, source_target_pairs={{0,64},{32,96},{64,128},{96,160},{128,192},{160,224},{192,0},{224,... | collective-permute-start | bytes 786440 | tf_op jit(solution)/shard_map/ppermute | solution.py:520
  139.1 14.7 %collective-permute-start.18 = (f32[8,64,128]{2,1,0:T(8,128)}, f32[8,64,128]{2,1,0:T(8,128)S(1)}, u32[]{:S(2)}, u32[]{:S(2)}) collective-permute-start(f32[8,64,128]{2,1,0:T(8,128)} %get-tuple-element.41), channel_id=1, source_target_pairs={{0,64},{32,96},{64,128},{96,160},{256,320},{288,352},{320,384},{35... | collective-permute-start | bytes 786440 | tf_op jit(solution)/shard_map/ppermute | solution.py:520
  140.4 32.5 %copy-start.14 = (f32[8,128,128]{2,1,0:T(8,128)S(1)}, f32[8,128,128]{2,1,0:T(8,128)}, u32[]{:S(2)}) copy-start(f32[8,128,128]{2,1,0:T(8,128)} %copy-done.13) | copy-start | bytes 1572868
  156.9 16.1 %collective-permute-start.20 = (f32[4,64,128]{2,1,0:T(8,128)S(1)}, f32[4,64,128]{2,1,0:T(8,128)S(1)}, u32[]{:S(2)}, u32[]{:S(2)}) collective-permute-start(f32[4,64,128]{2,1,0:T(8,128)S(1)} %get-tuple-element.43.last), channel_id=1, source_target_pairs={{0,2},{1,3},{2,4},{3,5},{4,6},{5,7},{6,8},{7,9},{8,10},{9,11},{10,... | collective-permute-start | bytes 393224 | tf_op jit(solution)/shard_map/ppermute | solution.py:517
  163.3 9.7 %collective-permute-start.21 = (f32[4,64,128]{2,1,0:T(8,128)S(1)}, f32[4,64,128]{2,1,0:T(8,128)S(1)}, u32[]{:S(2)}, u32[]{:S(2)}) collective-permute-start(f32[4,64,128]{2,1,0:T(8,128)S(1)} %get-tuple-element.43.last), channel_id=1, source_target_pairs={{0,1},{1,2},{2,3},{3,4},{4,5},{5,6},{6,7},{7,8},{8,9},{9,10},{10,1... | collective-permute-start | bytes 393224 | tf_op jit(solution)/shard_map/ppermute | solution.py:517
  166.6 7.3 %collective-permute-start.22 = (f32[4,64,128]{2,1,0:T(8,128)S(1)}, f32[4,64,128]{2,1,0:T(8,128)S(1)}, u32[]{:S(2)}, u32[]{:S(2)}) collective-permute-start(f32[4,64,128]{2,1,0:T(8,128)S(1)} %get-tuple-element.43.last), channel_id=1, source_target_pairs={{1,0},{2,1},{3,2},{4,3},{5,4},{6,5},{7,6},{8,7},{9,8},{10,9},{11,1... | collective-permute-start | bytes 393224 | tf_op jit(solution)/shard_map/ppermute | solution.py:517
  170.7 8.8 %collective-permute-start.23 = (f32[4,64,128]{2,1,0:T(8,128)S(1)}, f32[4,64,128]{2,1,0:T(8,128)S(1)}, u32[]{:S(2)}, u32[]{:S(2)}) collective-permute-start(f32[4,64,128]{2,1,0:T(8,128)S(1)} %get-tuple-element.43.last), channel_id=1, source_target_pairs={{2,0},{3,1},{4,2},{5,3},{6,4},{7,5},{8,6},{9,7},{10,8},{11,9},{12,... | collective-permute-start | bytes 393224 | tf_op jit(solution)/shard_map/ppermute | solution.py:517
  179.5 23.0 %copy-start.12 = (f32[8,128,128]{2,1,0:T(8,128)S(1)}, f32[8,128,128]{2,1,0:T(8,128)}, u32[]{:S(2)}) copy-start(f32[8,128,128]{2,1,0:T(8,128)} %copy-done.11) | copy-start | bytes 1572868
  183.3 19.1 %collective-permute-start.26 = (f32[8,128,128]{2,1,0:T(8,128)S(1)}, f32[8,128,128]{2,1,0:T(8,128)S(1)}, u32[]{:S(2)}, u32[]{:S(2)}) collective-permute-start(f32[8,128,128]{2,1,0:T(8,128)S(1)} %broadcast_select_fusion), channel_id=1, source_target_pairs={{0,96},{32,128},{64,160},{96,192},{128,224},{160,0},{192,32},{224,... | collective-permute-start | bytes 1572872 | tf_op jit(solution)/shard_map/ppermute | solution.py:520
  190.2 19.6 %collective-permute-start.24 = (f32[4,64,128]{2,1,0:T(8,128)S(1)}, f32[4,64,128]{2,1,0:T(8,128)S(1)}, u32[]{:S(2)}, u32[]{:S(2)}) collective-permute-start(f32[4,64,128]{2,1,0:T(8,128)S(1)} %get-tuple-element.46), channel_id=1, source_target_pairs={{0,352},{32,384},{64,416},{96,448},{128,480},{160,256},{192,288},{... | collective-permute-start | bytes 393224 | tf_op jit(solution)/shard_map/ppermute | solution.py:520
  195.5 14.3 %collective-permute-start.25 = (f32[4,64,128]{2,1,0:T(8,128)S(1)}, f32[4,64,128]{2,1,0:T(8,128)S(1)}, u32[]{:S(2)}, u32[]{:S(2)}) collective-permute-start(f32[4,64,128]{2,1,0:T(8,128)S(1)} %get-tuple-element.47), channel_id=1, source_target_pairs={{0,96},{32,128},{64,160},{96,192},{128,224},{160,0},{192,32},{224,... | collective-permute-start | bytes 393224 | tf_op jit(solution)/shard_map/ppermute | solution.py:520
  (13 other events, 117.5 us)
